TPU v7x, 32 devices: a whole 2x2x4 slice. The times are simulated.
32 devices in a mesh: rows: 8 (over y, x, core), cols: 4 (over z).
Axes of the slice: x: 2, y: 2, z: 4, core: 2. Of those that a mesh axis runs over, the one named last changes fastest.
Arguments:
- cross_kernel: float32 [8192, 512], P('rows', 'cols'), may hold values from -6 to 6
- factor_panels: float32 [2, 512, 8192], P(None, 'cols', 'rows'), may hold values from -0.25 to 0.25
- block_inverses: float32 [2, 512, 512], P(None, 'cols'), may hold values from -0.5 to 1.5, as said below
Outputs:
- solved: float32 [8192, 512], P('rows', 'cols')
Inputs may be any that keep to these rules, and one draw needn't show every extreme that they name: `block_inverses`: each block is lower triangular, with diagonal entries from 0.5 to 1.5.
All inputs are finite; a program needn't handle non-finite values.
Results may differ from a plain program's by a relative error of at most 0.000084.
Values sent between devices are 32-bit elements; how exact they have to be, the bound alone decides.
No kernel may reach another device: no remote copies, remote signals or barrier semaphores. Data moves between devices by JAX's collectives and lax.ppermute only.
A program may use at most 64 MiB of HBM per device.

v0:
```python
import jax
import jax.numpy as jnp
from jax import lax
from jax.sharding import PartitionSpec as P

highest = lax.Precision.HIGHEST


def spread(array, axis, root):
    mine = lax.axis_index(axis) == root
    return lax.psum(jnp.where(mine, array, jnp.zeros_like(array)), axis)


def contract_rows(left, right):
    return lax.dot_general(
        left, right, (((0,), (0,)), ((), ())), precision=highest, preferred_element_type=jnp.float32
    )


def diagonal_solve(inverse_rows, rhs_block):
    return jnp.dot(
        lax.all_gather(inverse_rows, "cols", axis=0, tiled=True),
        rhs_block,
        precision=highest,
        preferred_element_type=jnp.float32,
    )


def second_update(factor_rows, solved_rows, initial):
    return initial + contract_rows(
        lax.all_gather(factor_rows, "cols", axis=0, tiled=True), solved_rows
    )


def on_device(cross_kernel, factor_panels, block_inverses):
    width = block_inverses.shape[2]
    is_zero = lax.axis_index("rows") == 0
    first_factor = lax.all_gather(factor_panels[0], "cols", axis=0, tiled=True)
    first = diagonal_solve(block_inverses[0], cross_kernel[:width])
    rest_rows = cross_kernel[width : 2 * width] - contract_rows(
        first_factor[:, width : 2 * width], first
    )
    second = diagonal_solve(block_inverses[1], rest_rows)
    first, second = (spread(first, "rows", 0), spread(second, "rows", 0))
    update = second_update(factor_panels[1], second, contract_rows(first_factor, first))
    fresh = cross_kernel - update
    top = jnp.where(is_zero, first, fresh[:width])
    middle = jnp.where(is_zero, second, fresh[width : 2 * width])
    return jnp.concatenate([top, middle, fresh[2 * width :]], axis=0)


def solution(mesh):
    in_specs = (P("rows", "cols"), P(None, "cols", "rows"), P(None, "cols", None))
    out_specs = P("rows", "cols")
    return jax.shard_map(
        on_device, mesh=mesh, in_specs=in_specs, out_specs=out_specs, check_vma=False
    )
```

profile of v0, /device:TPU:2, one launch (start us, length us, event | category | flops | bytes accessed | tf_op | source)
XLA Modules:
  0.0 229.8 jit_solution(1420202897743146658)
XLA Ops:
  6.5 0.0 copy-start.1
  6.5 0.0 all-gather.9.cloned.1.call-start
  6.5 1.9 fusion.21
  8.5 0.0 all-gather.9.cloned.1.call-update
  8.5 0.0 all-gather.11.cloned.1.call-start
  8.6 2.3 fusion.20
  10.8 0.0 all-gather.11.cloned.1.call-update
  10.9 0.0 all-gather.13.cloned.1.call-start
  10.9 0.7 all-gather.13.cloned.1.call-update
  11.6 0.0 all-reduce.3.cloned.1.call-start
  11.7 26.5 %all-gather.9.cloned.1.call-done = f32[1,512,512]{2,1,0:T(8,128)} async-done(((f32[1,128,512]{2,1,0:T(8,128)}), f32[1,512,512]{2,1,0:T(8,128)}) %all-gather.9.cloned.1.call-update) | async-done | bytes 1048592 | tf_op jit(solution)/shard_map/all_gather | solution.py:22
  38.1 0.0 copy-done.1
  38.1 2.9 %broadcast_select_fusion = (f32[512,128]{1,0:T(8,128)}, f32[512,128]{1,0:T(8,128)S(1)}) fusion(pred[]{:T(512)S(6)} %eq.2, f32[1024,128]{1,0:T(8,128)S(1)} %copy-done.1, f32[1,512,512]{2,1,0:T(8,128)} %all-gather.9.cloned.1.call-done), kind=kOutput, calls=%fused_computation.17 | convolution fusion | flops 402718720 | bytes 1835009 | tf_op jit(solution)/shard_map/dot_general | solution.py:21
  41.0 44.1 %all-gather.11.cloned.1.call-done = f32[1,512,1024]{2,1,0:T(8,128)} async-done(((f32[1,128,1024]{2,1,0:T(8,128)}), f32[1,512,1024]{2,1,0:T(8,128)}) %all-gather.11.cloned.1.call-update) | async-done | bytes 2097168 | tf_op jit(solution)/shard_map/all_gather | solution.py:38
  85.1 0.0 copy-start
  85.1 3.2 %fusion.11 = f32[512,128]{1,0:T(8,128)S(1)} fusion(f32[512,128]{1,0:T(8,128)S(1)} %get-tuple-element.14, f32[512,1024]{1,0:T(8,128)} %bitcast.34, f32[1024,128]{1,0:T(8,128)S(1)} %copy-done.1), kind=kOutput, calls=%fused_computation.6 | convolution fusion | flops 402718720 | bytes 1835008 | tf_op jit(solution)/shard_map/dot_general | solution.py:15
  88.3 25.1 %all-gather.13.cloned.1.call-done = f32[1,512,512]{2,1,0:T(8,128)} async-done(((f32[1,128,512]{2,1,0:T(8,128)}), f32[1,512,512]{2,1,0:T(8,128)}) %all-gather.13.cloned.1.call-update) | async-done | bytes 1048592 | tf_op jit(solution)/shard_map/all_gather | solution.py:22
  113.4 2.9 %fusion.12 = f32[512,128]{1,0:T(8,128)} fusion(f32[512,128]{1,0:T(8,128)S(1)} %fusion.11, f32[1,512,512]{2,1,0:T(8,128)} %all-gather.13.cloned.1.call-done, pred[]{:T(512)S(6)} %eq.2), kind=kOutput, calls=%fused_computation.8 | convolution fusion | flops 402718720 | bytes 1572865 | tf_op jit(solution)/shard_map/dot_general | solution.py:21
  116.3 0.0 all-reduce.3.cloned.1.call-update
  116.3 0.0 all-gather.15.cloned.1.call-start
  116.4 0.5 all-gather.15.cloned.1.call-update
  116.9 53.0 %all-reduce.3.cloned.1.call-done = (f32[512,128]{1,0:T(8,128)}, f32[512,128]{1,0:T(8,128)}) async-done(((f32[512,128]{1,0:T(8,128)}, f32[512,128]{1,0:T(8,128)}), (f32[512,128]{1,0:T(8,128)}, f32[512,128]{1,0:T(8,128)})) %all-reduce.3.cloned.1.call-update) | async-done | bytes 524304 | tf_op jit(solution)/shard_map/psum | solution.py:11
  169.9 0.0 copy-start.3
  169.9 0.0 copy-done
  169.9 4.4 %fusion.18 = f32[128,1024]{0,1:T(8,128)S(1)} fusion(f32[512,128]{1,0:T(8,128)} %get-tuple-element.6, f32[1,512,1024]{2,1,0:T(8,128)S(1)} %copy-done), kind=kOutput, calls=%fused_computation.18 | convolution fusion | flops 805306368 | bytes 2883584 | tf_op jit(solution)/shard_map/dot_general | solution.py:15
  174.4 0.0 copy-start.2
  174.4 0.0 copy-start.4
  174.4 43.0 %all-gather.15.cloned.1.call-done = f32[1,512,1024]{2,1,0:T(8,128)} async-done(((f32[1,128,1024]{2,1,0:T(8,128)}), f32[1,512,1024]{2,1,0:T(8,128)}) %all-gather.15.cloned.1.call-update) | async-done | bytes 2097168 | tf_op jit(solution)/shard_map/all_gather | solution.py:31
  217.4 0.0 copy-done.3
  217.4 5.0 %fusion.8 = f32[1024,128]{1,0:T(8,128)S(1)} fusion(f32[1024,128]{1,0:T(8,128)S(1)} %copy-done.1, f32[128,1024]{0,1:T(8,128)S(1)} %fusion.18, f32[512,128]{1,0:T(8,128)S(1)} %copy-done.3, f32[1,512,1024]{2,1,0:T(8,128)} %all-gather.15.cloned.1.call-done), kind=kOutput, calls=%fused_computation.4 | convolution fusion | flops 805568512 | bytes 3932160 | tf_op jit(solution)/shard_map/dot_general | solution.py:15
  222.4 0.0 copy-done.2
  222.4 0.0 copy-done.4
  222.4 0.1 slice_select_fusion.1
  222.5 0.0 copy-start.5
  222.5 0.8 copy-done.5
  (1 shorter events, 0.0 us)
Async XLA Ops:
  6.5 31.6 %copy-start.1 = (f32[1024,128]{1,0:T(8,128)S(1)}, f32[1024,128]{1,0:T(8,128)}, u32[]{:S(2)}) copy-start(f32[1024,128]{1,0:T(8,128)} %param.3) | copy-start | bytes 1572868
  6.5 31.6 %all-gather.9.cloned.1.call-start = ((), (), s32[]{:S(2)}) async-start(), calls=%async_computation | async-start | bytes 1310720 | tf_op jit(solution)/shard_map/all_gather | solution.py:22
  8.5 76.6 %all-gather.11.cloned.1.call-start = ((), (), s32[]{:S(2)}) async-start(), calls=%async_computation.1 | async-start | bytes 2621440 | tf_op jit(solution)/shard_map/all_gather | solution.py:38
  10.9 102.5 %all-gather.13.cloned.1.call-start = ((), (), s32[]{:S(2)}) async-start(), calls=%async_computation.2 | async-start | bytes 1310720 | tf_op jit(solution)/shard_map/all_gather | solution.py:22
  11.6 158.3 %all-reduce.3.cloned.1.call-start = ((), (), s32[]{:S(2)}) async-start(), calls=%async_computation.4 | async-start | bytes 1048576 | tf_op jit(solution)/shard_map/psum | solution.py:11
  85.1 84.8 %copy-start = (f32[1,512,1024]{2,1,0:T(8,128)S(1)}, f32[1,512,1024]{2,1,0:T(8,128)}, u32[]{:S(2)}) copy-start(f32[1,512,1024]{2,1,0:T(8,128)} %all-gather.11.cloned.1.call-done) | copy-start | bytes 6291460
  116.3 101.1 %all-gather.15.cloned.1.call-start = ((), (), s32[]{:S(2)}) async-start(), calls=%async_computation.3 | async-start | bytes 2621440 | tf_op jit(solution)/shard_map/all_gather | solution.py:31
  169.9 47.5 %copy-start.3 = (f32[512,128]{1,0:T(8,128)S(1)}, f32[512,128]{1,0:T(8,128)}, u32[]{:S(2)}) copy-start(f32[512,128]{1,0:T(8,128)} %get-tuple-element.5) | copy-start | bytes 786436
  174.4 48.1 %copy-start.2 = (f32[512,128]{1,0:T(8,128)S(1)}, f32[512,128]{1,0:T(8,128)}, u32[]{:S(2)}) copy-start(f32[512,128]{1,0:T(8,128)} %get-tuple-element.6) | copy-start | bytes 786436
  174.4 48.1 %copy-start.4 = (f32[1024,128]{1,0:T(8,128)S(1)}, f32[1024,128]{1,0:T(8,128)}, u32[]{:S(2)}) copy-start(f32[1024,128]{1,0:T(8,128)} %custom-call) | copy-start | bytes 1572868
  222.5 0.8 copy-start.5
Sparse Core Ops, SparseCore 0:
  8.9 29.1 all-gather.8
  39.7 45.3 all-gather.10
  86.7 26.6 all-gather.12
  116.5 53.4 all-reduce.2
  171.4 45.9 all-gather.14
where the time goes:
time: 232 us; the launch traced here: 230 us
  waiting for transfers between devices  193 us (83%)
  matrix products  18.4 us (8%)
  between operations  13.2 us (6%)
  local copies, waits for them, and re-layouts  5.03 us (2%)
    psum x1, waiting for transfers between devices, spread(): return lax.psum(jnp.where(mine, array, jnp.zeros_like(array)), axis)  53 us
    all_gather x2, waiting for transfers between devices, diagonal_solve(): lax.all_gather(inverse_rows, 'cols', axis=0, tiled=True)  51.6 us
    all_gather x1, waiting for transfers between devices, on_device(): first_factor = lax.all_gather(factor_panels[0], 'cols', axis=0, tiled=True)  44.1 us
    all_gather x1, waiting for transfers between devices, second_update(): lax.all_gather(factor_rows, 'cols', axis=0, tiled=True)  43 us
    dot_general x3, matrix products, contract_rows(): lax.dot_general(left, right, (((0,), (0,)), ((), ())), precision=highest,...  12.6 us
    dot_general x2, matrix products, diagonal_solve(): jnp.dot(lax.all_gather(inverse_rows, 'cols', axis=0, tiled=True), rhs_blo...  5.81 us
  transfers between devices with their start and end apart: 5, of which 5 were waited for; matrix products, arithmetic and copies ran while one was open for 6% of the time, Pallas kernels for 0%

commit v1 on v0

v1 whole, which is shorter than its diff:
```python
import jax
import jax.numpy as jnp
from jax import lax
from jax.sharding import PartitionSpec as P

AXES = ("rows", "cols")


def dot(left, right, left_dim):
    return lax.dot_general(
        left,
        right,
        (((left_dim,), (0,)), ((), ())),
        precision=lax.Precision.HIGH,
        preferred_element_type=jnp.float32,
    )


def make_on_device(n_rows, n_cols):
    groups = n_cols // 2

    def swap(array, flip, rows):
        pairs = [
            (row * n_cols + col, row * n_cols + (col ^ flip))
            for row in rows
            for col in range(n_cols)
        ]
        return lax.ppermute(array, AXES, pairs)

    def step_down(array, bit, have):
        pairs = [
            (row * n_cols + col, (row | bit) * n_cols + col) for row in have for col in range(n_cols)
        ]
        return lax.ppermute(array, AXES, pairs)

    def broadcast(array, row_id, bits):
        have = [0]
        for bit in bits:
            got = step_down(array, bit, have)
            array = jnp.where((row_id & bit) != 0, got, array)
            have = have + [row | bit for row in have]
        return array

    def broadcast_halves(array, row_id):
        bits = []
        bit = 1
        while bit < n_rows:
            bits.append(bit)
            bit *= 2
        outer, inner = bits[1:], bits[:1]
        half = array.shape[0] // 2
        upper = broadcast(array[:half], row_id, outer + inner)
        lower = broadcast(array[half:], row_id, outer[::-1] + inner)
        return jnp.concatenate([upper, lower], axis=0)

    def on_device(cross_kernel, factor_panels, block_inverses):
        row_id = lax.axis_index("rows")
        col_id = lax.axis_index("cols")
        width = block_inverses.shape[2]
        cands = cross_kernel.shape[1]
        top = [0]
        below = range(1, n_rows)

        inverse = block_inverses[0]
        inverse_pair = jnp.concatenate([inverse, swap(inverse, 1, top)], axis=0)
        rhs = cross_kernel[:width]
        rhs_blocks = jnp.concatenate(
            [rhs] + [swap(rhs, 2 * step, top) for step in range(1, groups)], axis=1
        )
        first_pair = dot(inverse_pair, rhs_blocks, 1)
        first_all = [first_pair]
        for step in range(1, groups):
            got = swap(first_pair, 2 * step, top)
            order = [place ^ step for place in range(groups)]
            first_all.append(
                jnp.concatenate([got[:, at * cands : (at + 1) * cands] for at in order], axis=1)
            )
        first_all = jnp.concatenate(first_all, axis=0)
        corner = factor_panels[0, :, width : 2 * width]
        corner_all = jnp.concatenate(
            [corner] + [swap(corner, flip, top) for flip in range(1, n_cols)], axis=0
        )
        rhs = cross_kernel[width : 2 * width]
        rhs_blocks = jnp.concatenate(
            [rhs] + [swap(rhs, 2 * step, top) for step in range(1, groups)], axis=1
        )
        inverse = block_inverses[1]
        inverse_pair = jnp.concatenate([inverse, swap(inverse, 1, top)], axis=0)
        second_pair = dot(inverse_pair, rhs_blocks - dot(corner_all, first_all, 0), 1)

        solved_pair = jnp.concatenate(
            [broadcast_halves(first_pair, row_id), broadcast_halves(second_pair, row_id)], axis=0
        )
        factors = factor_panels
        factors_other = swap(factors, 1, below)
        stacked = jnp.concatenate(
            [factors[0], factors_other[0], factors[1], factors_other[1]], axis=0
        )
        fresh = cross_kernel
        partials = []
        for step in range(1, groups):
            block = solved_pair[:, step * cands : (step + 1) * cands]
            partials.append(swap(dot(stacked, block, 0), 2 * step, below))
        fresh = fresh - dot(stacked, solved_pair[:, :cands], 0)
        for partial in partials:
            fresh = fresh - partial

        second_all = jnp.concatenate(
            [second_pair[:, :cands]]
            + [
                swap(second_pair[:, step * cands : (step + 1) * cands], 2 * step, top)
                for step in range(1, groups)
            ],
            axis=0,
        )
        order = jnp.arange(n_cols) ^ col_id
        both = jnp.stack([first_all[:, :cands], second_all])
        both = both.reshape(2, n_cols, width // n_cols, cands)
        both = jnp.take(both, order, axis=1).reshape(2 * width, cands)
        head = jnp.where(row_id == 0, both, fresh[: 2 * width])
        return jnp.concatenate([head, fresh[2 * width :]], axis=0)

    return on_device


def solution(mesh):
    in_specs = (P("rows", "cols"), P(None, "cols", "rows"), P(None, "cols", None))
    out_specs = P("rows", "cols")
    return jax.shard_map(
        make_on_device(mesh.shape["rows"], mesh.shape["cols"]),
        mesh=mesh,
        in_specs=in_specs,
        out_specs=out_specs,
        check_vma=False,
    )
```

time: 232 us -> 111 us (0.48)
  waiting for transfers between devices: 193 us -> 57.8 us
  starting transfers between devices: 0.17 us -> 33.1 us
  between operations: 13.2 us -> 0.45 us
  matrix products: 18.4 us -> 9.25 us
  other arithmetic: 0.06 us -> 3.04 us
    all_gather x4 -> x0, waiting for transfers between devices: 139 us -> none  [the longest x2 51.6 us: diagonal_solve(): lax.all_gather(inverse_rows, 'cols', axis=0, tiled=True)]
    ppermute x0 -> x23, waiting for transfers between devices: none -> 57.8 us  [the longest x12 35.6 us: step_down(): return lax.ppermute(array, AXES, pairs)]
    psum x1 -> x0, waiting for transfers between devices: 53 us -> none  [spread(): return lax.psum(jnp.where(mine, array, jnp.zeros_like(array)), axis)]
    ppermute x0 -> x23, starting transfers between devices: none -> 33.1 us  [the longest x11 17.5 us: swap(): return lax.ppermute(array, AXES, pairs)]
    dot_general x5, matrix products: 18.4 us -> 9.25 us  [dot(): lax.dot_general(left, right, (((left_dim,), (0,)), ((), ())), precision=l...]
    slice x2 -> x5, local copies, waits for them, and re-layouts: 4.23 us -> 0.77 us  [the longest x2 0.69 us: broadcast_halves(): upper = broadcast(array[:half], row_id, outer + inner)]
    select_n x2 -> x12, other arithmetic: 0.06 us -> 2.9 us  [the longest x10 2.69 us: broadcast(): array = jnp.where(row_id & bit != 0, got, array)]
    gather x0 -> x2, local copies, waits for them, and re-layouts: none -> 2.51 us  [on_device(): both = jnp.take(both, order, axis=1).reshape(2 * width, cands)]
  transfers between devices with their start and end apart: 5 -> 23, of which waited for: 5 -> 8; matrix products, arithmetic and copies ran while one was open for 6% -> 12% of each run, Pallas kernels for 0% -> 0%
where the time goes in v1:
time: 111 us; the launch traced here: 110 us
  waiting for transfers between devices  57.8 us (52%)
  starting transfers between devices  33.1 us (30%)
  matrix products  9.25 us (8%)
  local copies, waits for them, and re-layouts  6.11 us (6%)
  other arithmetic  3.04 us (3%)
    ppermute x12, waiting for transfers between devices, step_down(): return lax.ppermute(array, AXES, pairs)  35.6 us
    ppermute x11, waiting for transfers between devices, swap(): return lax.ppermute(array, AXES, pairs)  22.3 us
    ppermute x11, starting transfers between devices, swap(): return lax.ppermute(array, AXES, pairs)  17.5 us
    ppermute x12, starting transfers between devices, step_down(): return lax.ppermute(array, AXES, pairs)  15.6 us
    dot_general x5, matrix products, dot(): lax.dot_general(left, right, (((left_dim,), (0,)), ((), ())), precision=l...  9.25 us
    select_n x10, other arithmetic, broadcast(): array = jnp.where(row_id & bit != 0, got, array)  2.69 us
    gather x2, local copies, waits for them, and re-layouts, on_device(): both = jnp.take(both, order, axis=1).reshape(2 * width, cands)  2.51 us
  transfers between devices with their start and end apart: 23, of which 8 were waited for; matrix products, arithmetic and copies ran while one was open for 12% of the time, Pallas kernels for 0%

profile of v1, /device:TPU:2, one launch (start us, length us, event | category | flops | bytes accessed | tf_op | source)
XLA Modules:
  0.0 109.7 jit_solution(16932954725145777337)
XLA Ops:
  0.0 1.2 %slice_bitcast_fusion.6 = (f32[128,512]{1,0:T(8,128)S(1)}, f32[128,512]{1,0:T(8,128)S(1)}) fusion(f32[2,128,512]{2,1,0:T(8,128)} %param.5), kind=kLoop, calls=%fused_computation.46 | loop fusion | bytes 1048576 | tf_op jit(solution)/shard_map/squeeze | solution.py:64
  1.2 0.7 collective-permute-start
  1.9 0.7 collective-permute-start.1
  2.6 0.7 slice_bitcast_fusion.4
  3.4 1.4 %collective-permute-start.7 = (f32[128,512]{1,0:T(8,128)}, f32[128,512]{1,0:T(8,128)}, u32[]{:S(2)}, u32[]{:S(2)}) collective-permute-start(f32[128,512]{1,0:T(8,128)} %slice_bitcast_fusion.4), channel_id=1, source_target_pairs={{0,3},{1,2},{2,1},{3,0}} | collective-permute-start | bytes 786440 | tf_op jit(solution)/shard_map/ppermute | solution.py:28
  4.7 1.4 %collective-permute-start.6 = (f32[128,512]{1,0:T(8,128)}, f32[128,512]{1,0:T(8,128)}, u32[]{:S(2)}, u32[]{:S(2)}) collective-permute-start(f32[128,512]{1,0:T(8,128)} %slice_bitcast_fusion.4), channel_id=1, source_target_pairs={{0,2},{1,3},{2,0},{3,1}} | collective-permute-start | bytes 786440 | tf_op jit(solution)/shard_map/ppermute | solution.py:28
  6.1 1.4 %collective-permute-start.5 = (f32[128,512]{1,0:T(8,128)}, f32[128,512]{1,0:T(8,128)}, u32[]{:S(2)}, u32[]{:S(2)}) collective-permute-start(f32[128,512]{1,0:T(8,128)} %slice_bitcast_fusion.4), channel_id=1, source_target_pairs={{0,1},{1,0},{2,3},{3,2}} | collective-permute-start | bytes 786440 | tf_op jit(solution)/shard_map/ppermute | solution.py:28
  7.4 0.4 fusion.11
  7.8 0.7 fusion.38
  8.5 1.3 %collective-permute-start.10 = (f32[128,256]{1,0:T(8,128)}, f32[128,256]{1,0:T(8,128)}, u32[]{:S(2)}, u32[]{:S(2)}) collective-permute-start(f32[128,256]{1,0:T(8,128)} %get-tuple-element.15), channel_id=1, source_target_pairs={{0,8},{1,9},{2,10},{3,11}} | collective-permute-start | bytes 393224 | tf_op jit(solution)/shard_map/ppermute | solution.py:34
  9.8 1.3 %collective-permute-start.13 = (f32[128,256]{1,0:T(8,128)S(1)}, f32[128,256]{1,0:T(8,128)}, u32[]{:S(2)}, u32[]{:S(2)}) collective-permute-start(f32[128,256]{1,0:T(8,128)S(1)} %get-tuple-element.16), channel_id=1, source_target_pairs={{0,16},{1,17},{2,18},{3,19}} | collective-permute-start | bytes 393224 | tf_op jit(solution)/shard_map/ppermute | solution.py:34
  11.1 0.1 slice_bitcast_fusion.3
  11.2 15.1 %collective-permute-done.10 = f32[128,256]{1,0:T(8,128)} collective-permute-done((f32[128,256]{1,0:T(8,128)}, f32[128,256]{1,0:T(8,128)}, u32[]{:S(2)}, u32[]{:S(2)}) %collective-permute-start.10) | collective-permute-done | bytes 131104 | tf_op jit(solution)/shard_map/ppermute | solution.py:34
  26.3 1.6 %broadcast_select_fusion.3 = (f32[128,256]{1,0:T(8,128)}, f32[128,256]{1,0:T(8,128)S(1)}) fusion(f32[128,256]{1,0:T(8,128)} %collective-permute-done.10, pred[]{:T(512)S(6)} %ne.8, f32[256,256]{1,0:T(8,128)S(1)} %fusion.11, f32[128,256]{1,0:T(8,128)} %collective-permute-done.13, pred[]{:T(512)S(6)} %ne.7), kind=kLoop, calls=%fused_computation.50 | loop fusion | flops 65536 | bytes 786434 | tf_op jit(solution)/shard_map/jit(_where)/select_n | solution.py:40
  27.9 1.9 %collective-permute-start.11 = (f32[128,256]{1,0:T(8,128)}, f32[128,256]{1,0:T(8,128)}, u32[]{:S(2)}, u32[]{:S(2)}) collective-permute-start(f32[128,256]{1,0:T(8,128)} %get-tuple-element.13), channel_id=1, source_target_pairs={{0,16},{1,17},{2,18},{3,19},{8,24},{9,25},{10,26},{11,27}} | collective-permute-start | bytes 393224 | tf_op jit(solution)/shard_map/ppermute | solution.py:34
  29.8 0.7 collective-permute-start.2
  30.5 1.5 %collective-permute-done.11 = f32[128,256]{1,0:T(8,128)} collective-permute-done((f32[128,256]{1,0:T(8,128)}, f32[128,256]{1,0:T(8,128)}, u32[]{:S(2)}, u32[]{:S(2)}) %collective-permute-start.11) | collective-permute-done | bytes 131104 | tf_op jit(solution)/shard_map/ppermute | solution.py:34
  32.0 1.3 %collective-permute-start.14 = (f32[128,256]{1,0:T(8,128)S(1)}, f32[128,256]{1,0:T(8,128)S(1)}, u32[]{:S(2)}, u32[]{:S(2)}) collective-permute-start(f32[128,256]{1,0:T(8,128)S(1)} %get-tuple-element.14), channel_id=1, source_target_pairs={{0,8},{1,9},{2,10},{3,11},{16,24},{17,25},{18,26},{19,27}} | collective-permute-start | bytes 393224 | tf_op jit(solution)/shard_map/ppermute | solution.py:34
  33.3 0.9 broadcast_select_fusion.7
  34.2 6.3 %collective-permute-done.14 = f32[128,256]{1,0:T(8,128)S(1)} collective-permute-done((f32[128,256]{1,0:T(8,128)S(1)}, f32[128,256]{1,0:T(8,128)S(1)}, u32[]{:S(2)}, u32[]{:S(2)}) %collective-permute-start.14) | collective-permute-done | bytes 131104 | tf_op jit(solution)/shard_map/ppermute | solution.py:34
  40.5 0.7 collective-permute-start.3
  41.2 0.7 collective-permute-start.4
  42.0 7.0 %collective-permute-start.9 = (f32[2,128,1024]{2,1,0:T(8,128)S(1)}, f32[2,128,1024]{2,1,0:T(8,128)S(1)}, u32[]{:S(2)}, u32[]{:S(2)}) collective-permute-start(f32[2,128,1024]{2,1,0:T(8,128)S(1)} %copy-done.1), channel_id=1, source_target_pairs={{4,5},{5,4},{6,7},{7,6},{8,9},{9,8},{10,11},{11,10},{12,13},{13,12... | collective-permute-start | bytes 3145736 | tf_op jit(solution)/shard_map/ppermute | solution.py:28
  49.0 1.3 %collective-permute-start.12 = (f32[128,256]{1,0:T(8,128)S(1)}, f32[128,256]{1,0:T(8,128)S(1)}, u32[]{:S(2)}, u32[]{:S(2)}) collective-permute-start(f32[128,256]{1,0:T(8,128)S(1)} %broadcast_select_fusion.7), channel_id=1, source_target_pairs={{0,4},{1,5},{2,6},{3,7},{8,12},{9,13},{10,14},{11,15},{16,20},{17,... | collective-permute-start | bytes 393224 | tf_op jit(solution)/shard_map/ppermute | solution.py:34
  50.3 1.3 %collective-permute-start.15 = (f32[128,256]{1,0:T(8,128)S(1)}, f32[128,256]{1,0:T(8,128)S(1)}, u32[]{:S(2)}, u32[]{:S(2)}) collective-permute-start(f32[128,256]{1,0:T(8,128)S(1)} %broadcast_select_fusion.2), channel_id=1, source_target_pairs={{0,4},{1,5},{2,6},{3,7},{16,20},{17,21},{18,22},{19,23},{8,12},{9,... | collective-permute-start | bytes 393224 | tf_op jit(solution)/shard_map/ppermute | solution.py:34
  51.6 2.2 %fusion.3 = f32[512,256]{1,0:T(8,128)S(1)} fusion(f32[128,512]{1,0:T(8,128)} %collective-permute-done.7, f32[128,512]{1,0:T(8,128)} %collective-permute-done.6, f32[128,512]{1,0:T(8,128)} %collective-permute-done.5, f32[128,512]{1,0:T(8,128)} %slice_bitcast_fusion.4, f32[256,128]{1,0:T(8,128)S(1)} %get-tuple-element.24, ...), kind=kOutput, calls=%fused_computation.6 | convolution fusion | flops 403701760 | bytes 2097152 | tf_op jit(solution)/shard_map/dot_general | solution.py:10
  53.9 0.4 fusion.23
  54.3 1.3 %collective-permute-start.16 = (f32[128,256]{1,0:T(8,128)S(1)}, f32[128,256]{1,0:T(8,128)S(1)}, u32[]{:S(2)}, u32[]{:S(2)}) collective-permute-start(f32[128,256]{1,0:T(8,128)S(1)} %get-tuple-element.19), channel_id=1, source_target_pairs={{0,8},{1,9},{2,10},{3,11}} | collective-permute-start | bytes 393224 | tf_op jit(solution)/shard_map/ppermute | solution.py:34
  55.6 0.7 collective-permute-start.19
  56.3 6.9 %collective-permute-done.16 = f32[128,256]{1,0:T(8,128)S(1)} collective-permute-done((f32[128,256]{1,0:T(8,128)S(1)}, f32[128,256]{1,0:T(8,128)S(1)}, u32[]{:S(2)}, u32[]{:S(2)}) %collective-permute-start.16) | collective-permute-done | bytes 131104 | tf_op jit(solution)/shard_map/ppermute | solution.py:34
  63.3 0.7 collective-permute-start.8
  64.0 1.3 %collective-permute-start.17 = (f32[128,256]{1,0:T(8,128)S(1)}, f32[128,256]{1,0:T(8,128)S(1)}, u32[]{:S(2)}, u32[]{:S(2)}) collective-permute-start(f32[128,256]{1,0:T(8,128)S(1)} %get-tuple-element.17), channel_id=1, source_target_pairs={{0,16},{1,17},{2,18},{3,19},{8,24},{9,25},{10,26},{11,27}} | collective-permute-start | bytes 393224 | tf_op jit(solution)/shard_map/ppermute | solution.py:34
  65.3 1.3 %collective-permute-start.20 = (f32[128,256]{1,0:T(8,128)S(1)}, f32[128,256]{1,0:T(8,128)S(1)}, u32[]{:S(2)}, u32[]{:S(2)}) collective-permute-start(f32[128,256]{1,0:T(8,128)S(1)} %get-tuple-element.18), channel_id=1, source_target_pairs={{0,8},{1,9},{2,10},{3,11},{16,24},{17,25},{18,26},{19,27}} | collective-permute-start | bytes 393224 | tf_op jit(solution)/shard_map/ppermute | solution.py:34
  66.7 1.1 %collective-permute-done.17 = f32[128,256]{1,0:T(8,128)S(1)} collective-permute-done((f32[128,256]{1,0:T(8,128)S(1)}, f32[128,256]{1,0:T(8,128)S(1)}, u32[]{:S(2)}, u32[]{:S(2)}) %collective-permute-start.17) | collective-permute-done | bytes 131104 | tf_op jit(solution)/shard_map/ppermute | solution.py:34
  67.8 1.3 %collective-permute-start.18 = (f32[128,256]{1,0:T(8,128)S(1)}, f32[128,256]{1,0:T(8,128)S(1)}, u32[]{:S(2)}, u32[]{:S(2)}) collective-permute-start(f32[128,256]{1,0:T(8,128)S(1)} %broadcast_select_fusion.5), channel_id=1, source_target_pairs={{0,4},{1,5},{2,6},{3,7},{8,12},{9,13},{10,14},{11,15},{16,20},{17,... | collective-permute-start | bytes 393224 | tf_op jit(solution)/shard_map/ppermute | solution.py:34
  69.1 3.7 %collective-permute-done.20 = f32[128,256]{1,0:T(8,128)S(1)} collective-permute-done((f32[128,256]{1,0:T(8,128)S(1)}, f32[128,256]{1,0:T(8,128)S(1)}, u32[]{:S(2)}, u32[]{:S(2)}) %collective-permute-start.20) | collective-permute-done | bytes 131104 | tf_op jit(solution)/shard_map/ppermute | solution.py:34
  72.8 1.3 %collective-permute-start.21 = (f32[128,256]{1,0:T(8,128)S(1)}, f32[128,256]{1,0:T(8,128)S(1)}, u32[]{:S(2)}, u32[]{:S(2)}) collective-permute-start(f32[128,256]{1,0:T(8,128)S(1)} %broadcast_select_fusion), channel_id=1, source_target_pairs={{0,4},{1,5},{2,6},{3,7},{16,20},{17,21},{18,22},{19,23},{8,12},{9,... | collective-permute-start | bytes 393224 | tf_op jit(solution)/shard_map/ppermute | solution.py:34
  74.2 0.9 collective-permute-done.21
  75.2 0.1 slice_bitcast_fusion.1
  75.3 0.7 copy-done.2
  75.9 2.6 %fusion.2 = f32[1024,128]{1,0:T(8,128)} fusion(f32[128,1024]{1,0:T(8,128)S(1)} %get-tuple-element.8, f32[128,1024]{1,0:T(8,128)S(1)} %get-tuple-element.6, f32[128,1024]{1,0:T(8,128)S(1)} %get-tuple-element.7, f32[128,1024]{1,0:T(8,128)S(1)} %get-tuple-element.5, f32[512,256]{1,0:T(8,128)S(1)} %pad_maximum_fusion.4), kind=kOutput, calls=%fused_computation.5 | convolution fusion | flops 404226048 | bytes 2883584 | tf_op jit(solution)/shard_map/dot_general | solution.py:10
  78.5 2.4 %collective-permute-start.22 = (f32[1024,128]{1,0:T(8,128)}, f32[1024,128]{1,0:T(8,128)}, u32[]{:S(2)}, u32[]{:S(2)}) collective-permute-start(f32[1024,128]{1,0:T(8,128)} %fusion.2), channel_id=1, source_target_pairs={{4,6},{5,7},{6,4},{7,5},{8,10},{9,11},{10,8},{11,9},{12,14},{13,15... | collective-permute-start | bytes 1572872 | tf_op jit(solution)/shard_map/ppermute | solution.py:28
  81.1 1.4 %gather_fusion = f32[4,2,128,128]{3,2,1,0:T(8,128)} fusion(f32[2,4,128,128]{3,2,1,0:T(8,128)S(1)} %pad_maximum_fusion.3, s32[1024]{0:T(1024)S(1)} %pad_clamp_fusion), kind=kCustom, calls=%fused_computation | custom fusion | bytes 1048592 | tf_op jit(solution)/shard_map/jit(_take)/gather | solution.py:119
  82.4 1.1 %copy.4 = f32[2,4,128,128]{3,2,1,0:T(8,128)S(1)} copy(f32[2,4,128,128]{3,2,0,1:T(8,128)} %bitcast.22) | data formatting | bytes 1048576 | tf_op jit(solution)/shard_map/jit(_take)/gather | solution.py:119
  83.6 0.1 broadcast_in_dim.14
  83.6 0.2 bitcast_select_fusion
  83.8 22.2 %collective-permute-done.22 = f32[1024,128]{1,0:T(8,128)} collective-permute-done((f32[1024,128]{1,0:T(8,128)}, f32[1024,128]{1,0:T(8,128)}, u32[]{:S(2)}, u32[]{:S(2)}) %collective-permute-start.22) | collective-permute-done | bytes 524320 | tf_op jit(solution)/shard_map/ppermute | solution.py:28
  106.1 3.7 %fusion.1 = f32[1024,128]{1,0:T(8,128)} fusion(f32[1024,128]{1,0:T(8,128)S(1)} %bitcast_select_fusion, f32[1024,128]{1,0:T(8,128)} %collective-permute-done.22, f32[1024,128]{1,0:T(8,128)S(1)} %copy-done, f32[128,1024]{1,0:T(8,128)S(1)} %get-tuple-element.8, f32[128,1024]{1,0:T(8,128)S(1)} %get-tuple-element.6, f32[128,1024]{1,0:T(8,128)S(1)} %get-tuple-element.7, ...), kind=kOutput, calls=%fused_computation.4 | convolution fusion | flops 404619264 | bytes 4456449 | tf_op jit(solution)/shard_map/dot_general | solution.py:10
  (41 shorter events, 0.5 us)
Async XLA Ops:
  0.0 1.9 %copy-start = (f32[1024,128]{1,0:T(8,128)S(1)}, f32[1024,128]{1,0:T(8,128)}, u32[]{:S(2)}) copy-start(f32[1024,128]{1,0:T(8,128)} %param.3) | copy-start | bytes 1572868
  0.0 2.6 %copy-start.1 = (f32[2,128,1024]{2,1,0:T(8,128)S(1)}, f32[2,128,1024]{2,1,0:T(8,128)}, u32[]{:S(2)}) copy-start(f32[2,128,1024]{2,1,0:T(8,128)} %param.4) | copy-start | bytes 3145732
  1.2 6.2 %collective-permute-start = (f32[128,512]{1,0:T(8,128)S(1)}, f32[128,512]{1,0:T(8,128)S(1)}, u32[]{:S(2)}, u32[]{:S(2)}) collective-permute-start(f32[128,512]{1,0:T(8,128)S(1)} %get-tuple-element.11), channel_id=1, source_target_pairs={{0,1},{1,0},{2,3},{3,2}} | collective-permute-start | bytes 786440 | tf_op jit(solution)/shard_map/ppermute | solution.py:28
  1.9 5.5 %collective-permute-start.1 = (f32[512,128]{1,0:T(8,128)S(1)}, f32[512,128]{1,0:T(8,128)S(1)}, u32[]{:S(2)}, u32[]{:S(2)}) collective-permute-start(f32[512,128]{1,0:T(8,128)S(1)} %get-tuple-element.10), channel_id=1, source_target_pairs={{0,2},{1,3},{2,0},{3,1}} | collective-permute-start | bytes 786440 | tf_op jit(solution)/shard_map/ppermute | solution.py:28
  3.4 38.6 %collective-permute-start.7 = (f32[128,512]{1,0:T(8,128)}, f32[128,512]{1,0:T(8,128)}, u32[]{:S(2)}, u32[]{:S(2)}) collective-permute-start(f32[128,512]{1,0:T(8,128)} %slice_bitcast_fusion.4), channel_id=1, source_target_pairs={{0,3},{1,2},{2,1},{3,0}} | collective-permute-start | bytes 786440 | tf_op jit(solution)/shard_map/ppermute | solution.py:28
  4.7 44.3 %collective-permute-start.6 = (f32[128,512]{1,0:T(8,128)}, f32[128,512]{1,0:T(8,128)}, u32[]{:S(2)}, u32[]{:S(2)}) collective-permute-start(f32[128,512]{1,0:T(8,128)} %slice_bitcast_fusion.4), channel_id=1, source_target_pairs={{0,2},{1,3},{2,0},{3,1}} | collective-permute-start | bytes 786440 | tf_op jit(solution)/shard_map/ppermute | solution.py:28
  6.1 44.3 %collective-permute-start.5 = (f32[128,512]{1,0:T(8,128)}, f32[128,512]{1,0:T(8,128)}, u32[]{:S(2)}, u32[]{:S(2)}) collective-permute-start(f32[128,512]{1,0:T(8,128)} %slice_bitcast_fusion.4), channel_id=1, source_target_pairs={{0,1},{1,0},{2,3},{3,2}} | collective-permute-start | bytes 786440 | tf_op jit(solution)/shard_map/ppermute | solution.py:28
  8.5 17.8 %collective-permute-start.10 = (f32[128,256]{1,0:T(8,128)}, f32[128,256]{1,0:T(8,128)}, u32[]{:S(2)}, u32[]{:S(2)}) collective-permute-start(f32[128,256]{1,0:T(8,128)} %get-tuple-element.15), channel_id=1, source_target_pairs={{0,8},{1,9},{2,10},{3,11}} | collective-permute-start | bytes 393224 | tf_op jit(solution)/shard_map/ppermute | solution.py:34
  9.8 16.5 %collective-permute-start.13 = (f32[128,256]{1,0:T(8,128)S(1)}, f32[128,256]{1,0:T(8,128)}, u32[]{:S(2)}, u32[]{:S(2)}) collective-permute-start(f32[128,256]{1,0:T(8,128)S(1)} %get-tuple-element.16), channel_id=1, source_target_pairs={{0,16},{1,17},{2,18},{3,19}} | collective-permute-start | bytes 393224 | tf_op jit(solution)/shard_map/ppermute | solution.py:34
  27.9 4.1 %collective-permute-start.11 = (f32[128,256]{1,0:T(8,128)}, f32[128,256]{1,0:T(8,128)}, u32[]{:S(2)}, u32[]{:S(2)}) collective-permute-start(f32[128,256]{1,0:T(8,128)} %get-tuple-element.13), channel_id=1, source_target_pairs={{0,16},{1,17},{2,18},{3,19},{8,24},{9,25},{10,26},{11,27}} | collective-permute-start | bytes 393224 | tf_op jit(solution)/shard_map/ppermute | solution.py:34
  29.8 11.4 %collective-permute-start.2 = (f32[256,256]{1,0:T(8,128)S(1)}, f32[256,256]{1,0:T(8,128)S(1)}, u32[]{:S(2)}, u32[]{:S(2)}) collective-permute-start(f32[256,256]{1,0:T(8,128)S(1)} %fusion.11), channel_id=1, source_target_pairs={{0,2},{1,3},{2,0},{3,1}} | collective-permute-start | bytes 786440 | tf_op jit(solution)/shard_map/ppermute | solution.py:28
  32.0 8.6 %collective-permute-start.14 = (f32[128,256]{1,0:T(8,128)S(1)}, f32[128,256]{1,0:T(8,128)S(1)}, u32[]{:S(2)}, u32[]{:S(2)}) collective-permute-start(f32[128,256]{1,0:T(8,128)S(1)} %get-tuple-element.14), channel_id=1, source_target_pairs={{0,8},{1,9},{2,10},{3,11},{16,24},{17,25},{18,26},{19,27}} | collective-permute-start | bytes 393224 | tf_op jit(solution)/shard_map/ppermute | solution.py:34
  40.5 13.3 %collective-permute-start.3 = (f32[128,512]{1,0:T(8,128)S(1)}, f32[128,512]{1,0:T(8,128)S(1)}, u32[]{:S(2)}, u32[]{:S(2)}) collective-permute-start(f32[128,512]{1,0:T(8,128)S(1)} %get-tuple-element.12), channel_id=1, source_target_pairs={{0,1},{1,0},{2,3},{3,2}} | collective-permute-start | bytes 786440 | tf_op jit(solution)/shard_map/ppermute | solution.py:28
  41.2 12.6 %collective-permute-start.4 = (f32[512,128]{1,0:T(8,128)S(1)}, f32[512,128]{1,0:T(8,128)S(1)}, u32[]{:S(2)}, u32[]{:S(2)}) collective-permute-start(f32[512,128]{1,0:T(8,128)S(1)} %get-tuple-element.9), channel_id=1, source_target_pairs={{0,2},{1,3},{2,0},{3,1}} | collective-permute-start | bytes 786440 | tf_op jit(solution)/shard_map/ppermute | solution.py:28
  42.0 33.2 %collective-permute-start.9 = (f32[2,128,1024]{2,1,0:T(8,128)S(1)}, f32[2,128,1024]{2,1,0:T(8,128)S(1)}, u32[]{:S(2)}, u32[]{:S(2)}) collective-permute-start(f32[2,128,1024]{2,1,0:T(8,128)S(1)} %copy-done.1), channel_id=1, source_target_pairs={{4,5},{5,4},{6,7},{7,6},{8,9},{9,8},{10,11},{11,10},{12,13},{13,12... | collective-permute-start | bytes 3145736 | tf_op jit(solution)/shard_map/ppermute | solution.py:28
  49.0 16.3 %collective-permute-start.12 = (f32[128,256]{1,0:T(8,128)S(1)}, f32[128,256]{1,0:T(8,128)S(1)}, u32[]{:S(2)}, u32[]{:S(2)}) collective-permute-start(f32[128,256]{1,0:T(8,128)S(1)} %broadcast_select_fusion.7), channel_id=1, source_target_pairs={{0,4},{1,5},{2,6},{3,7},{8,12},{9,13},{10,14},{11,15},{16,20},{17,... | collective-permute-start | bytes 393224 | tf_op jit(solution)/shard_map/ppermute | solution.py:34
  50.3 16.3 %collective-permute-start.15 = (f32[128,256]{1,0:T(8,128)S(1)}, f32[128,256]{1,0:T(8,128)S(1)}, u32[]{:S(2)}, u32[]{:S(2)}) collective-permute-start(f32[128,256]{1,0:T(8,128)S(1)} %broadcast_select_fusion.2), channel_id=1, source_target_pairs={{0,4},{1,5},{2,6},{3,7},{16,20},{17,21},{18,22},{19,23},{8,12},{9,... | collective-permute-start | bytes 393224 | tf_op jit(solution)/shard_map/ppermute | solution.py:34
  54.3 9.0 %collective-permute-start.16 = (f32[128,256]{1,0:T(8,128)S(1)}, f32[128,256]{1,0:T(8,128)S(1)}, u32[]{:S(2)}, u32[]{:S(2)}) collective-permute-start(f32[128,256]{1,0:T(8,128)S(1)} %get-tuple-element.19), channel_id=1, source_target_pairs={{0,8},{1,9},{2,10},{3,11}} | collective-permute-start | bytes 393224 | tf_op jit(solution)/shard_map/ppermute | solution.py:34
  55.6 8.3 %collective-permute-start.19 = (f32[128,256]{1,0:T(8,128)S(1)}, f32[128,256]{1,0:T(8,128)S(1)}, u32[]{:S(2)}, u32[]{:S(2)}) collective-permute-start(f32[128,256]{1,0:T(8,128)S(1)} %get-tuple-element.20), channel_id=1, source_target_pairs={{0,16},{1,17},{2,18},{3,19}} | collective-permute-start | bytes 393224 | tf_op jit(solution)/shard_map/ppermute | solution.py:34
  63.3 17.7 %collective-permute-start.8 = (f32[256,128]{1,0:T(8,128)S(1)}, f32[256,128]{1,0:T(8,128)S(1)}, u32[]{:S(2)}, u32[]{:S(2)}) collective-permute-start(f32[256,128]{1,0:T(8,128)S(1)} %get-tuple-element.22), channel_id=1, source_target_pairs={{0,2},{1,3},{2,0},{3,1}} | collective-permute-start | bytes 393224 | tf_op jit(solution)/shard_map/ppermute | solution.py:28
  64.0 3.8 %collective-permute-start.17 = (f32[128,256]{1,0:T(8,128)S(1)}, f32[128,256]{1,0:T(8,128)S(1)}, u32[]{:S(2)}, u32[]{:S(2)}) collective-permute-start(f32[128,256]{1,0:T(8,128)S(1)} %get-tuple-element.17), channel_id=1, source_target_pairs={{0,16},{1,17},{2,18},{3,19},{8,24},{9,25},{10,26},{11,27}} | collective-permute-start | bytes 393224 | tf_op jit(solution)/shard_map/ppermute | solution.py:34
  65.3 7.5 %collective-permute-start.20 = (f32[128,256]{1,0:T(8,128)S(1)}, f32[128,256]{1,0:T(8,128)S(1)}, u32[]{:S(2)}, u32[]{:S(2)}) collective-permute-start(f32[128,256]{1,0:T(8,128)S(1)} %get-tuple-element.18), channel_id=1, source_target_pairs={{0,8},{1,9},{2,10},{3,11},{16,24},{17,25},{18,26},{19,27}} | collective-permute-start | bytes 393224 | tf_op jit(solution)/shard_map/ppermute | solution.py:34
  67.8 6.3 %collective-permute-start.18 = (f32[128,256]{1,0:T(8,128)S(1)}, f32[128,256]{1,0:T(8,128)S(1)}, u32[]{:S(2)}, u32[]{:S(2)}) collective-permute-start(f32[128,256]{1,0:T(8,128)S(1)} %broadcast_select_fusion.5), channel_id=1, source_target_pairs={{0,4},{1,5},{2,6},{3,7},{8,12},{9,13},{10,14},{11,15},{16,20},{17,... | collective-permute-start | bytes 393224 | tf_op jit(solution)/shard_map/ppermute | solution.py:34
  72.8 2.3 %collective-permute-start.21 = (f32[128,256]{1,0:T(8,128)S(1)}, f32[128,256]{1,0:T(8,128)S(1)}, u32[]{:S(2)}, u32[]{:S(2)}) collective-permute-start(f32[128,256]{1,0:T(8,128)S(1)} %broadcast_select_fusion), channel_id=1, source_target_pairs={{0,4},{1,5},{2,6},{3,7},{16,20},{17,21},{18,22},{19,23},{8,12},{9,... | collective-permute-start | bytes 393224 | tf_op jit(solution)/shard_map/ppermute | solution.py:34
  75.1 0.8 copy-start.2
  78.5 27.5 %collective-permute-start.22 = (f32[1024,128]{1,0:T(8,128)}, f32[1024,128]{1,0:T(8,128)}, u32[]{:S(2)}, u32[]{:S(2)}) collective-permute-start(f32[1024,128]{1,0:T(8,128)} %fusion.2), channel_id=1, source_target_pairs={{4,6},{5,7},{6,4},{7,5},{8,10},{9,11},{10,8},{11,9},{12,14},{13,15... | collective-permute-start | bytes 1572872 | tf_op jit(solution)/shard_map/ppermute | solution.py:28
  82.4 23.7 %copy-start.3 = (f32[512,256]{1,0:T(8,128)S(1)}, f32[512,256]{1,0:T(8,128)}, u32[]{:S(2)}) copy-start(f32[512,256]{1,0:T(8,128)} %copy-done.2) | copy-start | bytes 1572868

commit v2 on v0

v2 whole, which is shorter than its diff:
```python
import jax
import jax.numpy as jnp
from jax import lax
from jax.sharding import PartitionSpec as P

AXES = ("rows", "cols")
CHUNKS = 4


def dot(left, right, left_dim):
    return lax.dot_general(
        left,
        right,
        (((left_dim,), (0,)), ((), ())),
        precision=lax.Precision.HIGH,
        preferred_element_type=jnp.float32,
    )


def make_on_device(n_rows, n_cols):
    half = n_cols // 2

    def swap(array, flip, rows):
        pairs = [
            (row * n_cols + col, row * n_cols + (col ^ flip))
            for row in rows
            for col in range(n_cols)
        ]
        return lax.ppermute(array, AXES, pairs)

    def send_down(array, offset, have):
        pairs = [
            (row * n_cols + col, (row + offset) * n_cols + col) for row in have for col in range(n_cols)
        ]
        return lax.ppermute(array, AXES, pairs)

    def spread(array, row_id, stages, have):
        for low, radix in stages:
            digit = (row_id // low) % radix
            result = array
            for step in range(radix - 1, 0, -1):
                result = jnp.where(digit == step, send_down(array, step * low, have), result)
            array = result
            have = [row + step * low for row in have for step in range(radix)]
        return array

    def broadcast_outer(array, row_id):
        stages = []
        low = 2
        while low < n_rows:
            radix = min(4, n_rows // low)
            stages.append((low, radix))
            low *= radix
        return spread(array, row_id, stages[::-1], [0])

    def broadcast_inner(array, row_id):
        return spread(array, row_id, [(1, 2)], range(0, n_rows, 2))

    def block(array, place, cands):
        return array[:, place * cands : (place + 1) * cands]

    def shuffle(array, flip, cands):
        return jnp.concatenate([block(array, at ^ flip, cands) for at in range(half)], axis=1)

    def in_order(pieces, col_id):
        offsets = [at for step in range(half) for at in (step, step ^ half)]
        pieces = [pieces[offsets.index(at)] for at in range(n_cols)]
        bit = 1
        while bit < n_cols:
            flipped = (col_id & bit) != 0
            pieces = [
                jnp.where(flipped, pieces[at ^ bit], pieces[at]) for at in range(n_cols)
            ]
            bit *= 2
        return pieces

    def on_device(cross_kernel, factor_panels, block_inverses):
        row_id = lax.axis_index("rows")
        col_id = lax.axis_index("cols")
        width = block_inverses.shape[2]
        depth = block_inverses.shape[1]
        n_design, cands = cross_kernel.shape
        piece = n_design // CHUNKS
        top = [0]
        below = range(1, n_rows)

        def with_other(array, rows):
            return jnp.concatenate([array, swap(array, half, rows)], axis=0)

        def with_blocks(array):
            return jnp.concatenate(
                [array] + [swap(array, step, top) for step in range(1, half)], axis=1
            )

        def others(pair):
            got = [swap(block(pair, step, cands), step, top) for step in range(1, half)]
            return [block(pair, 0, cands)] + got

        arrived = []
        for at in range(CHUNKS):
            mine = factor_panels[:, :, at * piece : (at + 1) * piece]
            arrived.append(swap(mine, half, below))

        rhs = with_blocks(cross_kernel[: 2 * width])
        lead = jnp.concatenate(
            [block_inverses[0], factor_panels[0, :, width : 2 * width]], axis=1
        )
        lead = with_other(lead, top)
        inverse = with_other(block_inverses[1], top)
        first = dot(lead[:, :width], rhs[:width], 1)
        update = dot(lead[:, width:], first, 0)
        update, arrived[0] = lax.optimization_barrier((update, arrived[0]))
        bit = 1
        while bit < half:
            update = update + shuffle(swap(update, bit, top), bit, cands)
            bit *= 2
        first_half = broadcast_outer(first, row_id)
        rest = rhs[width:] - update
        rest, first_half, arrived[1] = lax.optimization_barrier((rest, first_half, arrived[1]))
        second = dot(inverse, rest, 1)
        second_half = broadcast_outer(second, row_id)
        second_half, arrived[2] = lax.optimization_barrier((second_half, arrived[2]))
        solved = jnp.concatenate(
            [broadcast_inner(first_half, row_id), broadcast_inner(second_half, row_id)], axis=0
        )

        pair = jnp.concatenate([first, second], axis=0)
        pieces = [[], []]
        for got in others(pair):
            for at in range(4):
                pieces[at // 2].append(got[at * depth : (at + 1) * depth])
        top_rows = jnp.concatenate(
            in_order(pieces[0], col_id) + in_order(pieces[1], col_id), axis=0
        )

        fresh = []
        for at in range(CHUNKS):
            part = slice(at * piece, (at + 1) * piece)
            mine = factor_panels[:, :, part]
            other, solved = lax.optimization_barrier((arrived[at], solved))
            stacked = jnp.concatenate([mine[0], other[0], mine[1], other[1]], axis=0)
            partial = dot(stacked, solved, 0)
            total = cross_kernel[part] - block(partial, 0, cands)
            for step in range(1, half):
                total = total - swap(block(partial, step, cands), step, below)
            fresh.append(total)
        fresh = jnp.concatenate(fresh, axis=0)
        head = jnp.where(row_id == 0, top_rows, fresh[: 2 * width])
        return jnp.concatenate([head, fresh[2 * width :]], axis=0)

    return on_device


def solution(mesh):
    in_specs = (P("rows", "cols"), P(None, "cols", "rows"), P(None, "cols", None))
    out_specs = P("rows", "cols")
    return jax.shard_map(
        make_on_device(mesh.shape["rows"], mesh.shape["cols"]),
        mesh=mesh,
        in_specs=in_specs,
        out_specs=out_specs,
        check_vma=False,
    )
```

time: 232 us -> 92.3 us (0.40)
  waiting for transfers between devices: 193 us -> 32.3 us
  starting transfers between devices: 0.17 us -> 41.6 us
  matrix products: 18.4 us -> 4.59 us
  between operations: 13.2 us -> 0.59 us
  other arithmetic: 0.06 us -> 4.27 us
  local copies, waits for them, and re-layouts: 5.03 us -> 8.21 us
    all_gather x4 -> x0, waiting for transfers between devices: 139 us -> none  [the longest x2 51.6 us: diagonal_solve(): lax.all_gather(inverse_rows, 'cols', axis=0, tiled=True)]
    psum x1 -> x0, waiting for transfers between devices: 53 us -> none  [spread(): return lax.psum(jnp.where(mine, array, jnp.zeros_like(array)), axis)]
    ppermute x0 -> x21, starting transfers between devices: none -> 41.6 us  [the longest x13 30.9 us: swap(): return lax.ppermute(array, AXES, pairs)]
    ppermute x0 -> x21, waiting for transfers between devices: none -> 32.3 us  [the longest x13 18.9 us: swap(): return lax.ppermute(array, AXES, pairs)]
    dot_general x5 -> x7, matrix products: 18.4 us -> 4.59 us  [dot(): lax.dot_general(left, right, (((left_dim,), (0,)), ((), ())), precision=l...]
    squeeze x0 -> x7, local copies, waits for them, and re-layouts: none -> 3.91 us  [the longest x5 2.85 us: on_device(): stacked = jnp.concatenate([mine[0], other[0], mine[1], other[1]], axis=0)]
    select_n x2 -> x5, other arithmetic: 0.06 us -> 2.74 us  [the longest x4 1.88 us: spread(): jnp.where(digit == step, send_down(array, step * low, have), result)]
  transfers between devices with their start and end apart: 5 -> 21, of which waited for: 5 -> 7; matrix products, arithmetic and copies ran while one was open for 6% -> 14% of each run, Pallas kernels for 0% -> 0%
where the time goes in v2:
time: 92.3 us; the launch traced here: 91.6 us
  starting transfers between devices  41.6 us (45%)
  waiting for transfers between devices  32.3 us (35%)
  local copies, waits for them, and re-layouts  8.21 us (9%)
  matrix products  4.59 us (5%)
  other arithmetic  4.27 us (5%)
    ppermute x13, starting transfers between devices, swap(): return lax.ppermute(array, AXES, pairs)  30.9 us
    ppermute x13, waiting for transfers between devices, swap(): return lax.ppermute(array, AXES, pairs)  18.9 us
    ppermute x8, waiting for transfers between devices, send_down(): return lax.ppermute(array, AXES, pairs)  13.4 us
    ppermute x8, starting transfers between devices, send_down(): return lax.ppermute(array, AXES, pairs)  10.7 us
    dot_general x7, matrix products, dot(): lax.dot_general(left, right, (((left_dim,), (0,)), ((), ())), precision=l...  4.59 us
    squeeze x5, local copies, waits for them, and re-layouts, on_device(): stacked = jnp.concatenate([mine[0], other[0], mine[1], other[1]], axis=0)  2.85 us
    unnamed x23, local copies, waits for them, and re-layouts  2.23 us
    select_n x4, other arithmetic, spread(): jnp.where(digit == step, send_down(array, step * low, have), result)  1.88 us
  transfers between devices with their start and end apart: 21, of which 7 were waited for; matrix products, arithmetic and copies ran while one was open for 14% of the time, Pallas kernels for 0%

profile of v2, /device:TPU:2, one launch (start us, length us, event | category | flops | bytes accessed | tf_op | source)
XLA Modules:
  0.0 91.6 jit_solution(11938273720660110636)
XLA Ops:
  0.0 1.0 %slice_bitcast_fusion.1 = f32[128,512]{1,0:T(8,128)S(1)} fusion(f32[2,128,1024]{2,1,0:T(8,128)} %param.4), kind=kLoop, calls=%fused_computation.51 | loop fusion | bytes 524288 | tf_op jit(solution)/shard_map/squeeze | solution.py:106
  1.0 0.1 copy-done.8
  1.2 0.8 collective-permute-start
  2.1 0.2 copy-done.1
  2.3 0.7 collective-permute-start.1
  3.0 0.9 %fusion.50 = (f32[2,128,256]{2,1,0:T(8,128)}, f32[2,128,256]{2,1,0:T(8,128)}, f32[2,128,256]{2,1,0:T(8,128)S(1)}, f32[2,128,256]{2,1,0:T(8,128)}) fusion(f32[2,128,1024]{2,1,0:T(8,128)S(1)} %copy-done), kind=kLoop, calls=%fused_computation.102 | loop fusion | bytes 2097152 | tf_op jit(solution)/shard_map/slice | solution.py:101
  3.9 4.5 %collective-permute-start.3 = (f32[2,128,256]{2,1,0:T(8,128)S(1)}, f32[2,128,256]{2,1,0:T(8,128)S(1)}, u32[]{:S(2)}, u32[]{:S(2)}) collective-permute-start(f32[2,128,256]{2,1,0:T(8,128)S(1)} %get-tuple-element.45), channel_id=1, source_target_pairs={{4,6},{5,7},{6,4},{7,5},{8,10},{9,11},{10,8},{11,9},{12,14},{13,15... | collective-permute-start | bytes 786440 | tf_op jit(solution)/shard_map/ppermute | solution.py:29
  8.5 0.1 pad_maximum_fusion
  8.6 0.4 fusion.2
  9.0 1.4 %fusion = f32[512,256]{1,0:T(8,128)} fusion(f32[256,256]{1,0:T(8,128)S(1)} %fusion.2, f32[256,1024]{1,0:T(8,128)S(1)} %pad_maximum_fusion), kind=kOutput, calls=%fused_computation.1 | convolution fusion | flops 201326592 | bytes 1310720 | tf_op jit(solution)/shard_map/dot_general | solution.py:11
  10.4 9.9 %collective-permute-done.3 = f32[2,128,256]{2,1,0:T(8,128)S(1)} collective-permute-done((f32[2,128,256]{2,1,0:T(8,128)S(1)}, f32[2,128,256]{2,1,0:T(8,128)S(1)}, u32[]{:S(2)}, u32[]{:S(2)}) %collective-permute-start.3) | collective-permute-done | bytes 262176 | tf_op jit(solution)/shard_map/ppermute | solution.py:29
  20.4 1.5 %collective-permute-start.4 = (f32[512,256]{1,0:T(8,128)}, f32[512,256]{1,0:T(8,128)}, u32[]{:S(2)}, u32[]{:S(2)}) collective-permute-start(f32[512,256]{1,0:T(8,128)} %fusion), channel_id=1, source_target_pairs={{0,1},{1,0},{2,3},{3,2}} | collective-permute-start | bytes 1572872 | tf_op jit(solution)/shard_map/ppermute | solution.py:29
  21.8 1.3 %collective-permute-start.5 = (f32[256,256]{1,0:T(8,128)S(1)}, f32[256,256]{1,0:T(8,128)}, u32[]{:S(2)}, u32[]{:S(2)}) collective-permute-start(f32[256,256]{1,0:T(8,128)S(1)} %fusion.2), channel_id=1, source_target_pairs={{0,8},{1,9},{2,10},{3,11}} | collective-permute-start | bytes 786440 | tf_op jit(solution)/shard_map/ppermute | solution.py:35
  23.1 1.4 %collective-permute-start.6 = (f32[256,256]{1,0:T(8,128)S(1)}, f32[256,256]{1,0:T(8,128)}, u32[]{:S(2)}, u32[]{:S(2)}) collective-permute-start(f32[256,256]{1,0:T(8,128)S(1)} %fusion.2), channel_id=1, source_target_pairs={{0,16},{1,17},{2,18},{3,19}} | collective-permute-start | bytes 786440 | tf_op jit(solution)/shard_map/ppermute | solution.py:35
  24.5 1.4 %collective-permute-start.7 = (f32[256,256]{1,0:T(8,128)S(1)}, f32[256,256]{1,0:T(8,128)}, u32[]{:S(2)}, u32[]{:S(2)}) collective-permute-start(f32[256,256]{1,0:T(8,128)S(1)} %fusion.2), channel_id=1, source_target_pairs={{0,24},{1,25},{2,26},{3,27}} | collective-permute-start | bytes 786440 | tf_op jit(solution)/shard_map/ppermute | solution.py:35
  25.8 1.9 %collective-permute-start.8 = (f32[2,128,256]{2,1,0:T(8,128)}, f32[2,128,256]{2,1,0:T(8,128)}, u32[]{:S(2)}, u32[]{:S(2)}) collective-permute-start(f32[2,128,256]{2,1,0:T(8,128)} %get-tuple-element.44), channel_id=1, source_target_pairs={{4,6},{5,7},{6,4},{7,5},{8,10},{9,11},{10,8},{11,9},{12,14},{13,15... | collective-permute-start | bytes 786440 | tf_op jit(solution)/shard_map/ppermute | solution.py:29
  27.8 7.6 %collective-permute-done.5 = f32[256,256]{1,0:T(8,128)} collective-permute-done((f32[256,256]{1,0:T(8,128)S(1)}, f32[256,256]{1,0:T(8,128)}, u32[]{:S(2)}, u32[]{:S(2)}) %collective-permute-start.5) | collective-permute-done | bytes 262176 | tf_op jit(solution)/shard_map/ppermute | solution.py:35
  35.4 0.7 collective-permute-start.2
  36.1 5.3 %collective-permute-start.14 = (f32[2,128,256]{2,1,0:T(8,128)}, f32[2,128,256]{2,1,0:T(8,128)}, u32[]{:S(2)}, u32[]{:S(2)}) collective-permute-start(f32[2,128,256]{2,1,0:T(8,128)} %get-tuple-element.43), channel_id=1, source_target_pairs={{4,6},{5,7},{6,4},{7,5},{8,10},{9,11},{10,8},{11,9},{12,14},{13,15... | collective-permute-start | bytes 786440 | tf_op jit(solution)/shard_map/ppermute | solution.py:29
  41.4 1.7 %select_select_fusion.1 = f32[256,256]{1,0:T(8,128)} fusion(f32[256,256]{1,0:T(8,128)} %collective-permute-done.5, f32[256,256]{1,0:T(8,128)} %collective-permute-done.6, f32[256,256]{1,0:T(8,128)} %collective-permute-done.7, f32[256,256]{1,0:T(8,128)S(1)} %fusion.2, pred[]{:T(512)S(6)} %eq.27, pred[]{:T(512)S(6)} %eq.26, pred[]{:T(512)S(6)} %eq.25), kind=kLoop, calls=%fused_computation.49 | loop fusion | flops 196608 | bytes 1310723 | tf_op jit(solution)/shard_map/jit(_where)/select_n | solution.py:42
  43.1 1.1 %fusion.51 = (f32[512,128]{1,0:T(8,128)S(1)}, f32[512,128]{1,0:T(8,128)S(1)}) fusion(f32[512,256]{1,0:T(8,128)} %collective-permute-done.4), kind=kLoop, calls=%fused_computation.103 | loop fusion | bytes 1048576 | tf_op jit(solution)/shard_map/slice | solution.py:60
  44.2 1.1 %slice_subtract_fusion = f32[512,256]{1,0:T(8,128)S(1)} fusion(f32[1024,256]{1,0:T(8,128)S(1)} %constant_dynamic-update-slice_fusion, f32[512,256]{1,0:T(8,128)} %fusion, f32[512,128]{1,0:T(8,128)S(1)} %get-tuple-element.54, f32[512,128]{1,0:T(8,128)S(1)} %get-tuple-element.53), kind=kLoop, calls=%fused_computation.3 | loop fusion | flops 393216 | bytes 2097152 | tf_op jit(solution)/shard_map/sub | solution.py:118
  45.3 4.1 %collective-permute-done.8 = f32[2,128,256]{2,1,0:T(8,128)} collective-permute-done((f32[2,128,256]{2,1,0:T(8,128)}, f32[2,128,256]{2,1,0:T(8,128)}, u32[]{:S(2)}, u32[]{:S(2)}) %collective-permute-start.8) | collective-permute-done | bytes 262176 | tf_op jit(solution)/shard_map/ppermute | solution.py:29
  49.4 0.4 fusion.5
  49.8 1.3 %collective-permute-start.11 = (f32[256,256]{1,0:T(8,128)S(1)}, f32[256,256]{1,0:T(8,128)S(1)}, u32[]{:S(2)}, u32[]{:S(2)}) collective-permute-start(f32[256,256]{1,0:T(8,128)S(1)} %fusion.5), channel_id=1, source_target_pairs={{0,8},{1,9},{2,10},{3,11}} | collective-permute-start | bytes 786440 | tf_op jit(solution)/shard_map/ppermute | solution.py:35
  51.1 1.4 %collective-permute-start.12 = (f32[256,256]{1,0:T(8,128)S(1)}, f32[256,256]{1,0:T(8,128)}, u32[]{:S(2)}, u32[]{:S(2)}) collective-permute-start(f32[256,256]{1,0:T(8,128)S(1)} %fusion.5), channel_id=1, source_target_pairs={{0,16},{1,17},{2,18},{3,19}} | collective-permute-start | bytes 786440 | tf_op jit(solution)/shard_map/ppermute | solution.py:35
  52.5 1.4 %collective-permute-start.13 = (f32[256,256]{1,0:T(8,128)S(1)}, f32[256,256]{1,0:T(8,128)}, u32[]{:S(2)}, u32[]{:S(2)}) collective-permute-start(f32[256,256]{1,0:T(8,128)S(1)} %fusion.5), channel_id=1, source_target_pairs={{0,24},{1,25},{2,26},{3,27}} | collective-permute-start | bytes 786440 | tf_op jit(solution)/shard_map/ppermute | solution.py:35
  53.9 0.8 collective-permute-start.9
  54.7 0.8 slice_bitcast_fusion.18
  55.5 4.9 %collective-permute-done.11 = f32[256,256]{1,0:T(8,128)S(1)} collective-permute-done((f32[256,256]{1,0:T(8,128)S(1)}, f32[256,256]{1,0:T(8,128)S(1)}, u32[]{:S(2)}, u32[]{:S(2)}) %collective-permute-start.11) | collective-permute-done | bytes 262176 | tf_op jit(solution)/shard_map/ppermute | solution.py:35
  60.4 1.9 %collective-permute-start.19 = (f32[2,128,256]{2,1,0:T(8,128)}, f32[2,128,256]{2,1,0:T(8,128)S(1)}, u32[]{:S(2)}, u32[]{:S(2)}) collective-permute-start(f32[2,128,256]{2,1,0:T(8,128)} %get-tuple-element.46), channel_id=1, source_target_pairs={{4,6},{5,7},{6,4},{7,5},{8,10},{9,11},{10,8},{11,9},{12,14},{13,15... | collective-permute-start | bytes 786440 | tf_op jit(solution)/shard_map/ppermute | solution.py:29
  62.4 1.3 %collective-permute-start.10 = (f32[256,256]{1,0:T(8,128)S(1)}, f32[256,256]{1,0:T(8,128)S(1)}, u32[]{:S(2)}, u32[]{:S(2)}) collective-permute-start(f32[256,256]{1,0:T(8,128)S(1)} %copy-done.2), channel_id=1, source_target_pairs={{0,4},{1,5},{2,6},{3,7},{8,12},{9,13},{10,14},{11,15},{16,20},{17,... | collective-permute-start | bytes 786440 | tf_op jit(solution)/shard_map/ppermute | solution.py:35
  63.8 1.3 %collective-permute-start.15 = (f32[256,256]{1,0:T(8,128)S(1)}, f32[256,256]{1,0:T(8,128)S(1)}, u32[]{:S(2)}, u32[]{:S(2)}) collective-permute-start(f32[256,256]{1,0:T(8,128)S(1)} %select_select_fusion), channel_id=1, source_target_pairs={{0,4},{1,5},{2,6},{3,7},{8,12},{9,13},{10,14},{11,15},{16,20},{17,... | collective-permute-start | bytes 786440 | tf_op jit(solution)/shard_map/ppermute | solution.py:35
  65.4 0.9 collective-permute-done.15
  66.3 0.9 copy-done.10
  67.3 0.9 copy-done.6
  68.2 0.6 fusion.9
  68.9 5.0 %collective-permute-start.16 = (f32[256,128]{1,0:T(8,128)S(1)}, f32[256,128]{1,0:T(8,128)S(1)}, u32[]{:S(2)}, u32[]{:S(2)}) collective-permute-start(f32[256,128]{1,0:T(8,128)S(1)} %slice.236), channel_id=1, source_target_pairs={{4,5},{5,4},{6,7},{7,6},{8,9},{9,8},{10,11},{11,10},{12,13},{13,12... | collective-permute-start | bytes 393224 | tf_op jit(solution)/shard_map/ppermute | solution.py:29
  73.8 1.0 %slice_bitcast_fusion.13 = (f32[128,256]{1,0:T(8,128)S(1)}, f32[128,256]{1,0:T(8,128)S(1)}) fusion(f32[2,128,256]{2,1,0:T(8,128)} %collective-permute-done.8), kind=kLoop, calls=%fused_computation.71 | loop fusion | bytes 524288 | tf_op jit(solution)/shard_map/squeeze | solution.py:141
  74.8 0.6 fusion.17
  75.5 2.1 %collective-permute-start.17 = (f32[256,128]{1,0:T(8,128)S(1)}, f32[256,128]{1,0:T(8,128)S(1)}, u32[]{:S(2)}, u32[]{:S(2)}) collective-permute-start(f32[256,128]{1,0:T(8,128)S(1)} %slice.238), channel_id=1, source_target_pairs={{4,5},{5,4},{6,7},{7,6},{8,9},{9,8},{10,11},{11,10},{12,13},{13,12... | collective-permute-start | bytes 393224 | tf_op jit(solution)/shard_map/ppermute | solution.py:29
  77.6 0.6 fusion.33
  78.2 3.9 %collective-permute-start.20 = (f32[256,128]{1,0:T(8,128)S(1)}, f32[256,128]{1,0:T(8,128)S(1)}, u32[]{:S(2)}, u32[]{:S(2)}) collective-permute-start(f32[256,128]{1,0:T(8,128)S(1)} %slice.242), channel_id=1, source_target_pairs={{4,5},{5,4},{6,7},{7,6},{8,9},{9,8},{10,11},{11,10},{12,13},{13,12... | collective-permute-start | bytes 393224 | tf_op jit(solution)/shard_map/ppermute | solution.py:29
  82.1 1.0 %slice_bitcast_fusion.9 = (f32[128,256]{1,0:T(8,128)S(1)}, f32[128,256]{1,0:T(8,128)S(1)}) fusion(f32[2,128,256]{2,1,0:T(8,128)} %collective-permute-done.14), kind=kLoop, calls=%fused_computation.67 | loop fusion | bytes 524288 | tf_op jit(solution)/shard_map/squeeze | solution.py:141
  83.1 0.6 fusion.25
  83.8 1.9 %collective-permute-start.18 = (f32[256,128]{1,0:T(8,128)S(1)}, f32[256,128]{1,0:T(8,128)S(1)}, u32[]{:S(2)}, u32[]{:S(2)}) collective-permute-start(f32[256,128]{1,0:T(8,128)S(1)} %slice.240), channel_id=1, source_target_pairs={{4,5},{5,4},{6,7},{7,6},{8,9},{9,8},{10,11},{11,10},{12,13},{13,12... | collective-permute-start | bytes 393224 | tf_op jit(solution)/shard_map/ppermute | solution.py:29
  85.8 4.8 %collective-permute-done.18 = f32[256,128]{1,0:T(8,128)S(1)} collective-permute-done((f32[256,128]{1,0:T(8,128)S(1)}, f32[256,128]{1,0:T(8,128)S(1)}, u32[]{:S(2)}, u32[]{:S(2)}) %collective-permute-start.18) | collective-permute-done | bytes 131104 | tf_op jit(solution)/shard_map/ppermute | solution.py:29
  90.7 0.9 maximum_select_fusion
  (57 shorter events, 0.8 us)
Async XLA Ops:
  0.0 1.1 %copy-start.8 = (f32[2,128,512]{2,1,0:T(8,128)S(1)}, f32[2,128,512]{2,1,0:T(8,128)}, u32[]{:S(2)}) copy-start(f32[2,128,512]{2,1,0:T(8,128)} %param.5) | copy-start | bytes 1572868
  1.1 1.9 %copy-start = (f32[2,128,1024]{2,1,0:T(8,128)S(1)}, f32[2,128,1024]{2,1,0:T(8,128)}, u32[]{:S(2)}) copy-start(f32[2,128,1024]{2,1,0:T(8,128)} %param.4) | copy-start | bytes 3145732
  1.2 1.1 %copy-start.1 = (f32[1024,128]{1,0:T(8,128)S(1)}, f32[1024,128]{1,0:T(8,128)}, u32[]{:S(2)}) copy-start(f32[1024,128]{1,0:T(8,128)} %param.3) | copy-start | bytes 1572868
  1.2 7.2 %collective-permute-start = (f32[128,1024]{1,0:T(8,128)S(1)}, f32[128,1024]{1,0:T(8,128)S(1)}, u32[]{:S(2)}, u32[]{:S(2)}) collective-permute-start(f32[128,1024]{1,0:T(8,128)S(1)} %pad_maximum_fusion.1), channel_id=1, source_target_pairs={{0,2},{1,3},{2,0},{3,1}} | collective-permute-start | bytes 1572872 | tf_op jit(solution)/shard_map/ppermute | solution.py:29
  2.3 6.3 %collective-permute-start.1 = (f32[1024,128]{1,0:T(8,128)S(1)}, f32[1024,128]{1,0:T(8,128)S(1)}, u32[]{:S(2)}, u32[]{:S(2)}) collective-permute-start(f32[1024,128]{1,0:T(8,128)S(1)} %copy-done.1), channel_id=1, source_target_pairs={{0,1},{1,0},{2,3},{3,2}} | collective-permute-start | bytes 1572872 | tf_op jit(solution)/shard_map/ppermute | solution.py:29
  3.9 16.4 %collective-permute-start.3 = (f32[2,128,256]{2,1,0:T(8,128)S(1)}, f32[2,128,256]{2,1,0:T(8,128)S(1)}, u32[]{:S(2)}, u32[]{:S(2)}) collective-permute-start(f32[2,128,256]{2,1,0:T(8,128)S(1)} %get-tuple-element.45), channel_id=1, source_target_pairs={{4,6},{5,7},{6,4},{7,5},{8,10},{9,11},{10,8},{11,9},{12,14},{13,15... | collective-permute-start | bytes 786440 | tf_op jit(solution)/shard_map/ppermute | solution.py:29
  20.4 22.7 %copy-start.9 = (f32[2,128,256]{2,1,0:T(8,128)}, f32[2,128,256]{2,1,0:T(8,128)S(1)}, u32[]{:S(2)}) copy-start(f32[2,128,256]{2,1,0:T(8,128)S(1)} %collective-permute-done.3) | copy-start | bytes 786436
  20.4 22.7 %collective-permute-start.4 = (f32[512,256]{1,0:T(8,128)}, f32[512,256]{1,0:T(8,128)}, u32[]{:S(2)}, u32[]{:S(2)}) collective-permute-start(f32[512,256]{1,0:T(8,128)} %fusion), channel_id=1, source_target_pairs={{0,1},{1,0},{2,3},{3,2}} | collective-permute-start | bytes 1572872 | tf_op jit(solution)/shard_map/ppermute | solution.py:29
  21.8 13.6 %collective-permute-start.5 = (f32[256,256]{1,0:T(8,128)S(1)}, f32[256,256]{1,0:T(8,128)}, u32[]{:S(2)}, u32[]{:S(2)}) collective-permute-start(f32[256,256]{1,0:T(8,128)S(1)} %fusion.2), channel_id=1, source_target_pairs={{0,8},{1,9},{2,10},{3,11}} | collective-permute-start | bytes 786440 | tf_op jit(solution)/shard_map/ppermute | solution.py:35
  23.1 12.9 %collective-permute-start.6 = (f32[256,256]{1,0:T(8,128)S(1)}, f32[256,256]{1,0:T(8,128)}, u32[]{:S(2)}, u32[]{:S(2)}) collective-permute-start(f32[256,256]{1,0:T(8,128)S(1)} %fusion.2), channel_id=1, source_target_pairs={{0,16},{1,17},{2,18},{3,19}} | collective-permute-start | bytes 786440 | tf_op jit(solution)/shard_map/ppermute | solution.py:35
  24.5 16.9 %collective-permute-start.7 = (f32[256,256]{1,0:T(8,128)S(1)}, f32[256,256]{1,0:T(8,128)}, u32[]{:S(2)}, u32[]{:S(2)}) collective-permute-start(f32[256,256]{1,0:T(8,128)S(1)} %fusion.2), channel_id=1, source_target_pairs={{0,24},{1,25},{2,26},{3,27}} | collective-permute-start | bytes 786440 | tf_op jit(solution)/shard_map/ppermute | solution.py:35
  25.8 23.6 %collective-permute-start.8 = (f32[2,128,256]{2,1,0:T(8,128)}, f32[2,128,256]{2,1,0:T(8,128)}, u32[]{:S(2)}, u32[]{:S(2)}) collective-permute-start(f32[2,128,256]{2,1,0:T(8,128)} %get-tuple-element.44), channel_id=1, source_target_pairs={{4,6},{5,7},{6,4},{7,5},{8,10},{9,11},{10,8},{11,9},{12,14},{13,15... | collective-permute-start | bytes 786440 | tf_op jit(solution)/shard_map/ppermute | solution.py:29
  35.4 14.0 %collective-permute-start.2 = (f32[128,512]{1,0:T(8,128)S(1)}, f32[128,512]{1,0:T(8,128)S(1)}, u32[]{:S(2)}, u32[]{:S(2)}) collective-permute-start(f32[128,512]{1,0:T(8,128)S(1)} %get-tuple-element.51), channel_id=1, source_target_pairs={{0,2},{1,3},{2,0},{3,1}} | collective-permute-start | bytes 786440 | tf_op jit(solution)/shard_map/ppermute | solution.py:29
  36.1 27.7 %collective-permute-start.14 = (f32[2,128,256]{2,1,0:T(8,128)}, f32[2,128,256]{2,1,0:T(8,128)}, u32[]{:S(2)}, u32[]{:S(2)}) collective-permute-start(f32[2,128,256]{2,1,0:T(8,128)} %get-tuple-element.43), channel_id=1, source_target_pairs={{4,6},{5,7},{6,4},{7,5},{8,10},{9,11},{10,8},{11,9},{12,14},{13,15... | collective-permute-start | bytes 786440 | tf_op jit(solution)/shard_map/ppermute | solution.py:29
  49.8 10.6 %collective-permute-start.11 = (f32[256,256]{1,0:T(8,128)S(1)}, f32[256,256]{1,0:T(8,128)S(1)}, u32[]{:S(2)}, u32[]{:S(2)}) collective-permute-start(f32[256,256]{1,0:T(8,128)S(1)} %fusion.5), channel_id=1, source_target_pairs={{0,8},{1,9},{2,10},{3,11}} | collective-permute-start | bytes 786440 | tf_op jit(solution)/shard_map/ppermute | solution.py:35
  51.1 11.3 %collective-permute-start.12 = (f32[256,256]{1,0:T(8,128)S(1)}, f32[256,256]{1,0:T(8,128)}, u32[]{:S(2)}, u32[]{:S(2)}) collective-permute-start(f32[256,256]{1,0:T(8,128)S(1)} %fusion.5), channel_id=1, source_target_pairs={{0,16},{1,17},{2,18},{3,19}} | collective-permute-start | bytes 786440 | tf_op jit(solution)/shard_map/ppermute | solution.py:35
  52.5 11.2 %collective-permute-start.13 = (f32[256,256]{1,0:T(8,128)S(1)}, f32[256,256]{1,0:T(8,128)}, u32[]{:S(2)}, u32[]{:S(2)}) collective-permute-start(f32[256,256]{1,0:T(8,128)S(1)} %fusion.5), channel_id=1, source_target_pairs={{0,24},{1,25},{2,26},{3,27}} | collective-permute-start | bytes 786440 | tf_op jit(solution)/shard_map/ppermute | solution.py:35
  53.9 8.5 %copy-start.2 = (f32[256,256]{1,0:T(8,128)S(1)}, f32[256,256]{1,0:T(8,128)}, u32[]{:S(2)}) copy-start(f32[256,256]{1,0:T(8,128)} %select_select_fusion.1) | copy-start | bytes 786436
  53.9 11.2 %collective-permute-start.9 = (f32[512,128]{1,0:T(8,128)S(1)}, f32[512,128]{1,0:T(8,128)S(1)}, u32[]{:S(2)}, u32[]{:S(2)}) collective-permute-start(f32[512,128]{1,0:T(8,128)S(1)} %pad_maximum_fusion.3), channel_id=1, source_target_pairs={{0,1},{1,0},{2,3},{3,2}} | collective-permute-start | bytes 786440 | tf_op jit(solution)/shard_map/ppermute | solution.py:29
  60.4 17.1 %collective-permute-start.19 = (f32[2,128,256]{2,1,0:T(8,128)}, f32[2,128,256]{2,1,0:T(8,128)S(1)}, u32[]{:S(2)}, u32[]{:S(2)}) collective-permute-start(f32[2,128,256]{2,1,0:T(8,128)} %get-tuple-element.46), channel_id=1, source_target_pairs={{4,6},{5,7},{6,4},{7,5},{8,10},{9,11},{10,8},{11,9},{12,14},{13,15... | collective-permute-start | bytes 786440 | tf_op jit(solution)/shard_map/ppermute | solution.py:29
  62.4 2.9 %collective-permute-start.10 = (f32[256,256]{1,0:T(8,128)S(1)}, f32[256,256]{1,0:T(8,128)S(1)}, u32[]{:S(2)}, u32[]{:S(2)}) collective-permute-start(f32[256,256]{1,0:T(8,128)S(1)} %copy-done.2), channel_id=1, source_target_pairs={{0,4},{1,5},{2,6},{3,7},{8,12},{9,13},{10,14},{11,15},{16,20},{17,... | collective-permute-start | bytes 786440 | tf_op jit(solution)/shard_map/ppermute | solution.py:35
  63.8 2.4 %collective-permute-start.15 = (f32[256,256]{1,0:T(8,128)S(1)}, f32[256,256]{1,0:T(8,128)S(1)}, u32[]{:S(2)}, u32[]{:S(2)}) collective-permute-start(f32[256,256]{1,0:T(8,128)S(1)} %select_select_fusion), channel_id=1, source_target_pairs={{0,4},{1,5},{2,6},{3,7},{8,12},{9,13},{10,14},{11,15},{16,20},{17,... | collective-permute-start | bytes 786440 | tf_op jit(solution)/shard_map/ppermute | solution.py:35
  66.3 1.0 %copy-start.10 = (f32[2,128,256]{2,1,0:T(8,128)S(1)}, f32[2,128,256]{2,1,0:T(8,128)}, u32[]{:S(2)}) copy-start(f32[2,128,256]{2,1,0:T(8,128)} %copy-done.9) | copy-start | bytes 786436
  67.2 0.9 copy-start.6
  67.2 1.0 %copy-start.7 = (f32[128,256]{1,0:T(8,128)S(1)}, f32[128,256]{1,0:T(8,128)}, u32[]{:S(2)}) copy-start(f32[128,256]{1,0:T(8,128)} %get-tuple-element.41) | copy-start | bytes 393220
  68.8 6.0 %copy-start.4 = (f32[128,256]{1,0:T(8,128)S(1)}, f32[128,256]{1,0:T(8,128)}, u32[]{:S(2)}) copy-start(f32[128,256]{1,0:T(8,128)} %get-tuple-element.39) | copy-start | bytes 393220
  68.8 6.0 %copy-start.5 = (f32[128,256]{1,0:T(8,128)S(1)}, f32[128,256]{1,0:T(8,128)}, u32[]{:S(2)}) copy-start(f32[128,256]{1,0:T(8,128)} %get-tuple-element.40) | copy-start | bytes 393220
  68.9 16.9 %collective-permute-start.16 = (f32[256,128]{1,0:T(8,128)S(1)}, f32[256,128]{1,0:T(8,128)S(1)}, u32[]{:S(2)}, u32[]{:S(2)}) collective-permute-start(f32[256,128]{1,0:T(8,128)S(1)} %slice.236), channel_id=1, source_target_pairs={{4,5},{5,4},{6,7},{7,6},{8,9},{9,8},{10,11},{11,10},{12,13},{13,12... | collective-permute-start | bytes 393224 | tf_op jit(solution)/shard_map/ppermute | solution.py:29
  75.5 2.1 %copy-start.3 = (f32[128,256]{1,0:T(8,128)S(1)}, f32[128,256]{1,0:T(8,128)}, u32[]{:S(2)}) copy-start(f32[128,256]{1,0:T(8,128)} %get-tuple-element.42) | copy-start | bytes 393220
  75.5 10.3 %collective-permute-start.17 = (f32[256,128]{1,0:T(8,128)S(1)}, f32[256,128]{1,0:T(8,128)S(1)}, u32[]{:S(2)}, u32[]{:S(2)}) collective-permute-start(f32[256,128]{1,0:T(8,128)S(1)} %slice.238), channel_id=1, source_target_pairs={{4,5},{5,4},{6,7},{7,6},{8,9},{9,8},{10,11},{11,10},{12,13},{13,12... | collective-permute-start | bytes 393224 | tf_op jit(solution)/shard_map/ppermute | solution.py:29
  78.2 7.6 %collective-permute-start.20 = (f32[256,128]{1,0:T(8,128)S(1)}, f32[256,128]{1,0:T(8,128)S(1)}, u32[]{:S(2)}, u32[]{:S(2)}) collective-permute-start(f32[256,128]{1,0:T(8,128)S(1)} %slice.242), channel_id=1, source_target_pairs={{4,5},{5,4},{6,7},{7,6},{8,9},{9,8},{10,11},{11,10},{12,13},{13,12... | collective-permute-start | bytes 393224 | tf_op jit(solution)/shard_map/ppermute | solution.py:29
  83.8 6.9 %collective-permute-start.18 = (f32[256,128]{1,0:T(8,128)S(1)}, f32[256,128]{1,0:T(8,128)S(1)}, u32[]{:S(2)}, u32[]{:S(2)}) collective-permute-start(f32[256,128]{1,0:T(8,128)S(1)} %slice.240), channel_id=1, source_target_pairs={{4,5},{5,4},{6,7},{7,6},{8,9},{9,8},{10,11},{11,10},{12,13},{13,12... | collective-permute-start | bytes 393224 | tf_op jit(solution)/shard_map/ppermute | solution.py:29

commit v3 on v2

--- a/solution.py
+++ b/solution.py
@@ -4,7 +4,6 @@
 from jax.sharding import PartitionSpec as P
 
 AXES = ("rows", "cols")
-CHUNKS = 4
 
 
 def dot(left, right, left_dim):
@@ -80,7 +79,8 @@
         width = block_inverses.shape[2]
         depth = block_inverses.shape[1]
         n_design, cands = cross_kernel.shape
-        piece = n_design // CHUNKS
+        cuts = [0, 3 * n_design // 8, 5 * n_design // 8, n_design]
+        parts = [slice(start, stop) for start, stop in zip(cuts, cuts[1:])]
         top = [0]
         below = range(1, n_rows)
 
@@ -96,19 +96,22 @@
             got = [swap(block(pair, step, cands), step, top) for step in range(1, half)]
             return [block(pair, 0, cands)] + got
 
-        arrived = []
-        for at in range(CHUNKS):
-            mine = factor_panels[:, :, at * piece : (at + 1) * piece]
-            arrived.append(swap(mine, half, below))
+        flat = factor_panels.reshape(2 * depth, n_design)
 
-        rhs = with_blocks(cross_kernel[: 2 * width])
-        lead = jnp.concatenate(
-            [block_inverses[0], factor_panels[0, :, width : 2 * width]], axis=1
-        )
-        lead = with_other(lead, top)
-        inverse = with_other(block_inverses[1], top)
-        first = dot(lead[:, :width], rhs[:width], 1)
-        update = dot(lead[:, width:], first, 0)
+        inverses = block_inverses.reshape(2 * depth, width)
+        inverses_other = swap(inverses, half, top)
+        corner = factor_panels[0, :, width : 2 * width]
+        rhs, corner = lax.optimization_barrier((cross_kernel, corner))
+        rhs = with_blocks(rhs[: 2 * width])
+        corner = with_other(corner, top)
+        arrived = [swap(flat[:, parts[0]], half, range(2, n_rows))]
+        arrived += [swap(flat[:, part], half, below) for part in parts[1:]]
+
+        inverse = jnp.concatenate([inverses[:depth], inverses_other[:depth]], axis=0)
+        first = dot(inverse, rhs[:width], 1)
+        first, late = lax.optimization_barrier((first, flat[:, parts[0]]))
+        late = swap(late, half, range(1, min(2, n_rows)))
+        update = dot(corner, first, 0)
         update, arrived[0] = lax.optimization_barrier((update, arrived[0]))
         bit = 1
         while bit < half:
@@ -117,11 +120,12 @@
         first_half = broadcast_outer(first, row_id)
         rest = rhs[width:] - update
         rest, first_half, arrived[1] = lax.optimization_barrier((rest, first_half, arrived[1]))
+        inverse = jnp.concatenate([inverses[depth:], inverses_other[depth:]], axis=0)
         second = dot(inverse, rest, 1)
         second_half = broadcast_outer(second, row_id)
-        second_half, arrived[2] = lax.optimization_barrier((second_half, arrived[2]))
+        halves = [broadcast_inner(first_half, row_id), broadcast_inner(second_half, row_id)]
         solved = jnp.concatenate(
-            [broadcast_inner(first_half, row_id), broadcast_inner(second_half, row_id)], axis=0
+            [got[at : at + depth] for at in (0, depth) for got in halves], axis=0
         )
 
         pair = jnp.concatenate([first, second], axis=0)
@@ -134,12 +138,12 @@
         )
 
         fresh = []
-        for at in range(CHUNKS):
-            part = slice(at * piece, (at + 1) * piece)
-            mine = factor_panels[:, :, part]
-            other, solved = lax.optimization_barrier((arrived[at], solved))
-            stacked = jnp.concatenate([mine[0], other[0], mine[1], other[1]], axis=0)
+        arrived[0], late, solved = lax.optimization_barrier((arrived[0], late, solved))
+        arrived[0] = jnp.where(row_id == 1, late, arrived[0])
+        for part, other in zip(parts, arrived):
+            stacked = jnp.concatenate([flat[:, part], other], axis=0)
             partial = dot(stacked, solved, 0)
+            partial, solved = lax.optimization_barrier((partial, solved))
             total = cross_kernel[part] - block(partial, 0, cands)
             for step in range(1, half):
                 total = total - swap(block(partial, step, cands), step, below)

time: 92.3 us -> 87.2 us (0.945)
  the two profiles are of different devices: /device:TPU:2 before, /device:TPU:1 now
where the time goes in v3:
time: 87.2 us; the launch traced here: 86.5 us
  waiting for transfers between devices  38.1 us (44%)
  starting transfers between devices  33 us (38%)
  local copies, waits for them, and re-layouts  7.1 us (8%)
  matrix products  5.51 us (6%)
  other arithmetic  2.19 us (3%)
    ppermute x12, starting transfers between devices, swap(): return lax.ppermute(array, AXES, pairs)  23.4 us
    ppermute x8, waiting for transfers between devices, send_down(): return lax.ppermute(array, AXES, pairs)  23 us
    ppermute x12, waiting for transfers between devices, swap(): return lax.ppermute(array, AXES, pairs)  15.1 us
    ppermute x8, starting transfers between devices, send_down(): return lax.ppermute(array, AXES, pairs)  9.56 us
    dot_general x6, matrix products, dot(): lax.dot_general(left, right, (((left_dim,), (0,)), ((), ())), precision=l...  5.51 us
  transfers between devices with their start and end apart: 20, of which 4 were waited for; matrix products, arithmetic and copies ran while one was open for 13% of the time, Pallas kernels for 0%

profile of v3, /device:TPU:1, one launch (start us, length us, event | category | flops | bytes accessed | tf_op | source)
XLA Modules:
  0.0 86.5 jit_solution(4403855441156142221)
XLA Ops:
  0.0 1.0 %slice_bitcast_fusion.1 = f32[128,512]{1,0:T(8,128)S(1)} fusion(f32[2,128,1024]{2,1,0:T(8,128)} %param.4), kind=kLoop, calls=%fused_computation.33 | loop fusion | bytes 524288 | tf_op jit(solution)/shard_map/squeeze | solution.py:103
  1.0 0.1 copy-done
  1.1 0.7 collective-permute-start.1
  1.8 0.7 collective-permute-start
  2.5 0.7 collective-permute-start.2
  3.2 1.2 %fusion.31 = (f32[256,384]{1,0:T(8,128)S(1)}, f32[256,384]{1,0:T(8,128)S(1)}) fusion(f32[256,1024]{1,0:T(8,128)} %bitcast.13), kind=kLoop, calls=%fused_computation.65 | loop fusion | bytes 1572864 | tf_op jit(solution)/shard_map/slice | solution.py:144
  4.4 0.0 copy-start.4
  4.4 0.8 collective-permute-start.3
  5.3 0.2 copy-done.4
  5.4 0.8 slice_bitcast_fusion
  6.2 0.8 fusion.32
  6.9 0.0 collective-permute-done.1
  7.0 0.4 fusion.8
  7.4 0.6 fusion.17
  8.0 0.0 copy-start.5
  8.0 1.5 %collective-permute-start.4 = (f32[512,256]{1,0:T(8,128)S(1)}, f32[512,256]{1,0:T(8,128)}, u32[]{:S(2)}, u32[]{:S(2)}) collective-permute-start(f32[512,256]{1,0:T(8,128)S(1)} %fusion.17), channel_id=1, source_target_pairs={{0,1},{1,0},{2,3},{3,2}} | collective-permute-start | bytes 1572872 | tf_op jit(solution)/shard_map/ppermute | solution.py:28
  9.5 1.4 %collective-permute-start.5 = (f32[256,256]{1,0:T(8,128)S(1)}, f32[256,256]{1,0:T(8,128)}, u32[]{:S(2)}, u32[]{:S(2)}) collective-permute-start(f32[256,256]{1,0:T(8,128)S(1)} %fusion.8), channel_id=1, source_target_pairs={{0,8},{1,9},{2,10},{3,11}} | collective-permute-start | bytes 786440 | tf_op jit(solution)/shard_map/ppermute | solution.py:34
  10.9 1.4 %collective-permute-start.6 = (f32[256,256]{1,0:T(8,128)S(1)}, f32[256,256]{1,0:T(8,128)}, u32[]{:S(2)}, u32[]{:S(2)}) collective-permute-start(f32[256,256]{1,0:T(8,128)S(1)} %fusion.8), channel_id=1, source_target_pairs={{0,16},{1,17},{2,18},{3,19}} | collective-permute-start | bytes 786440 | tf_op jit(solution)/shard_map/ppermute | solution.py:34
  12.2 1.4 %collective-permute-start.7 = (f32[256,256]{1,0:T(8,128)S(1)}, f32[256,256]{1,0:T(8,128)}, u32[]{:S(2)}, u32[]{:S(2)}) collective-permute-start(f32[256,256]{1,0:T(8,128)S(1)} %fusion.8), channel_id=1, source_target_pairs={{0,24},{1,25},{2,26},{3,27}} | collective-permute-start | bytes 786440 | tf_op jit(solution)/shard_map/ppermute | solution.py:34
  13.6 1.0 %slice.164 = f32[256,256]{1,0:T(8,128)S(1)} slice(f32[256,1024]{1,0:T(8,128)} %bitcast.14), slice={[0:256], [384:640]} | slice | bytes 524288 | tf_op jit(solution)/shard_map/slice | solution.py:108
  14.6 5.0 %collective-permute-start.8 = (f32[256,256]{1,0:T(8,128)S(1)}, f32[256,256]{1,0:T(8,128)}, u32[]{:S(2)}, u32[]{:S(2)}) collective-permute-start(f32[256,256]{1,0:T(8,128)S(1)} %slice.164), channel_id=1, source_target_pairs={{4,6},{5,7},{6,4},{7,5},{8,10},{9,11},{10,8},{11,9},{12,14},{13,15... | collective-permute-start | bytes 786440 | tf_op jit(solution)/shard_map/ppermute | solution.py:28
  19.7 0.8 select_select_fusion.1
  20.5 1.1 %fusion.33 = (f32[512,128]{1,0:T(8,128)S(1)}, f32[512,128]{1,0:T(8,128)S(1)}) fusion(f32[512,256]{1,0:T(8,128)} %collective-permute-done.4), kind=kLoop, calls=%fused_computation.67 | loop fusion | bytes 1048576 | tf_op jit(solution)/shard_map/slice | solution.py:59
  21.6 0.1 slice_subtract_fusion
  21.7 10.6 %collective-permute-done.8 = f32[256,256]{1,0:T(8,128)} collective-permute-done((f32[256,256]{1,0:T(8,128)S(1)}, f32[256,256]{1,0:T(8,128)}, u32[]{:S(2)}, u32[]{:S(2)}) %collective-permute-start.8) | collective-permute-done | bytes 262176 | tf_op jit(solution)/shard_map/ppermute | solution.py:28
  32.3 0.4 fusion.13
  32.7 0.8 collective-permute-start.12
  33.6 0.7 collective-permute-start.13
  34.2 1.4 %collective-permute-start.14 = (f32[256,256]{1,0:T(8,128)S(1)}, f32[256,256]{1,0:T(8,128)}, u32[]{:S(2)}, u32[]{:S(2)}) collective-permute-start(f32[256,256]{1,0:T(8,128)S(1)} %fusion.13), channel_id=1, source_target_pairs={{0,24},{1,25},{2,26},{3,27}} | collective-permute-start | bytes 786440 | tf_op jit(solution)/shard_map/ppermute | solution.py:34
  35.6 0.7 collective-permute-start.9
  36.3 1.9 %collective-permute-start.18 = (f32[256,384]{1,0:T(8,128)S(1)}, f32[256,384]{1,0:T(8,128)}, u32[]{:S(2)}, u32[]{:S(2)}) collective-permute-start(f32[256,384]{1,0:T(8,128)S(1)} %get-tuple-element.39), channel_id=1, source_target_pairs={{4,6},{5,7},{6,4},{7,5},{8,10},{9,11},{10,8},{11,9},{12,14},{13,15... | collective-permute-start | bytes 1179656 | tf_op jit(solution)/shard_map/ppermute | solution.py:28
  38.3 4.3 %collective-permute-start.10 = (f32[256,384]{1,0:T(8,128)S(1)}, f32[256,384]{1,0:T(8,128)S(1)}, u32[]{:S(2)}, u32[]{:S(2)}) collective-permute-start(f32[256,384]{1,0:T(8,128)S(1)} %get-tuple-element.28), channel_id=1, source_target_pairs={{4,6},{5,7},{6,4},{7,5}} | collective-permute-start | bytes 1179656 | tf_op jit(solution)/shard_map/ppermute | solution.py:28
  42.6 1.3 %collective-permute-start.11 = (f32[256,256]{1,0:T(8,128)S(1)}, f32[256,256]{1,0:T(8,128)S(1)}, u32[]{:S(2)}, u32[]{:S(2)}) collective-permute-start(f32[256,256]{1,0:T(8,128)S(1)} %copy-done.3), channel_id=1, source_target_pairs={{0,4},{1,5},{2,6},{3,7},{8,12},{9,13},{10,14},{11,15},{16,20},{17,... | collective-permute-start | bytes 786440 | tf_op jit(solution)/shard_map/ppermute | solution.py:34
  43.9 0.1 select_select_fusion
  44.0 1.3 %collective-permute-start.15 = (f32[256,256]{1,0:T(8,128)S(1)}, f32[256,256]{1,0:T(8,128)S(1)}, u32[]{:S(2)}, u32[]{:S(2)}) collective-permute-start(f32[256,256]{1,0:T(8,128)S(1)} %select_select_fusion), channel_id=1, source_target_pairs={{0,4},{1,5},{2,6},{3,7},{8,12},{9,13},{10,14},{11,15},{16,20},{17,... | collective-permute-start | bytes 786440 | tf_op jit(solution)/shard_map/ppermute | solution.py:34
  45.5 21.7 %collective-permute-done.11 = f32[256,256]{1,0:T(8,128)S(1)} collective-permute-done((f32[256,256]{1,0:T(8,128)S(1)}, f32[256,256]{1,0:T(8,128)S(1)}, u32[]{:S(2)}, u32[]{:S(2)}) %collective-permute-start.11) | collective-permute-done | bytes 262176 | tf_op jit(solution)/shard_map/ppermute | solution.py:34
  67.2 1.3 %collective-permute-done.15 = f32[256,256]{1,0:T(8,128)S(1)} collective-permute-done((f32[256,256]{1,0:T(8,128)S(1)}, f32[256,256]{1,0:T(8,128)S(1)}, u32[]{:S(2)}, u32[]{:S(2)}) %collective-permute-start.15) | collective-permute-done | bytes 262176 | tf_op jit(solution)/shard_map/ppermute | solution.py:34
  68.6 0.0 copy-start.6
  68.7 0.9 %copy-done.6 = f32[256,384]{1,0:T(8,128)S(1)} copy-done((f32[256,384]{1,0:T(8,128)S(1)}, f32[256,384]{1,0:T(8,128)}, u32[]{:S(2)}) %copy-start.6) | copy-done | bytes 393240
  69.7 0.8 fusion
  70.5 1.9 %collective-permute-start.16 = (f32[384,128]{1,0:T(8,128)S(1)}, f32[384,128]{1,0:T(8,128)S(1)}, u32[]{:S(2)}, u32[]{:S(2)}) collective-permute-start(f32[384,128]{1,0:T(8,128)S(1)} %slice.149), channel_id=1, source_target_pairs={{4,5},{5,4},{6,7},{7,6},{8,9},{9,8},{10,11},{11,10},{12,13},{13,12... | collective-permute-start | bytes 589832 | tf_op jit(solution)/shard_map/ppermute | solution.py:28
  72.4 1.5 %fusion.21 = f32[256,256]{1,0:T(8,128)S(1)} fusion(f32[512,256]{1,0:T(8,128)S(1)} %pad_maximum_fusion, f32[256,256]{1,0:T(8,128)} %collective-permute-done.8, f32[256,256]{1,0:T(8,128)S(1)} %slice.164), kind=kOutput, calls=%fused_computation.24 | convolution fusion | flops 201457664 | bytes 1310720 | tf_op jit(solution)/shard_map/dot_general | solution.py:10
  74.0 3.4 %collective-permute-start.17 = (f32[256,128]{1,0:T(8,128)S(1)}, f32[256,128]{1,0:T(8,128)S(1)}, u32[]{:S(2)}, u32[]{:S(2)}) collective-permute-start(f32[256,128]{1,0:T(8,128)S(1)} %slice.152), channel_id=1, source_target_pairs={{4,5},{5,4},{6,7},{7,6},{8,9},{9,8},{10,11},{11,10},{12,13},{13,12... | collective-permute-start | bytes 393224 | tf_op jit(solution)/shard_map/ppermute | solution.py:28
  77.4 1.8 %fusion.4 = f32[384,256]{1,0:T(8,128)S(1)} fusion(f32[512,256]{1,0:T(8,128)S(1)} %pad_maximum_fusion, f32[256,384]{1,0:T(8,128)} %collective-permute-done.18, f32[256,384]{1,0:T(8,128)S(1)} %get-tuple-element.39), kind=kOutput, calls=%fused_computation.4 | convolution fusion | flops 302186496 | bytes 1703936 | tf_op jit(solution)/shard_map/dot_general | solution.py:10
  79.2 1.9 %collective-permute-start.19 = (f32[384,128]{1,0:T(8,128)S(1)}, f32[384,128]{1,0:T(8,128)S(1)}, u32[]{:S(2)}, u32[]{:S(2)}) collective-permute-start(f32[384,128]{1,0:T(8,128)S(1)} %slice.156), channel_id=1, source_target_pairs={{4,5},{5,4},{6,7},{7,6},{8,9},{9,8},{10,11},{11,10},{12,13},{13,12... | collective-permute-start | bytes 589832 | tf_op jit(solution)/shard_map/ppermute | solution.py:28
  81.2 4.4 %collective-permute-done.19 = f32[384,128]{1,0:T(8,128)S(1)} collective-permute-done((f32[384,128]{1,0:T(8,128)S(1)}, f32[384,128]{1,0:T(8,128)S(1)}, u32[]{:S(2)}, u32[]{:S(2)}) %collective-permute-start.19) | collective-permute-done | bytes 196640 | tf_op jit(solution)/shard_map/ppermute | solution.py:28
  85.6 0.1 subtract_subtract_fusion.1
  85.7 0.9 maximum_select_fusion
  (44 shorter events, 0.5 us)
Async XLA Ops:
  0.0 1.1 %copy-start = (f32[1024,128]{1,0:T(8,128)S(1)}, f32[1024,128]{1,0:T(8,128)}, u32[]{:S(2)}) copy-start(f32[1024,128]{1,0:T(8,128)} %param.3) | copy-start | bytes 1572868
  1.1 5.8 %collective-permute-start.1 = (f32[1024,128]{1,0:T(8,128)S(1)}, f32[1024,128]{1,0:T(8,128)S(1)}, u32[]{:S(2)}, u32[]{:S(2)}) collective-permute-start(f32[1024,128]{1,0:T(8,128)S(1)} %copy-done), channel_id=1, source_target_pairs={{0,1},{1,0},{2,3},{3,2}} | collective-permute-start | bytes 1572872 | tf_op jit(solution)/shard_map/ppermute | solution.py:28
  1.8 4.4 %collective-permute-start = (f32[256,512]{1,0:T(8,128)}, f32[256,512]{1,0:T(8,128)S(1)}, u32[]{:S(2)}, u32[]{:S(2)}) collective-permute-start(f32[256,512]{1,0:T(8,128)} %bitcast.15), channel_id=1, source_target_pairs={{0,2},{1,3},{2,0},{3,1}} | collective-permute-start | bytes 1572872 | tf_op jit(solution)/shard_map/ppermute | solution.py:28
  2.5 4.9 %collective-permute-start.2 = (f32[128,512]{1,0:T(8,128)S(1)}, f32[128,512]{1,0:T(8,128)S(1)}, u32[]{:S(2)}, u32[]{:S(2)}) collective-permute-start(f32[128,512]{1,0:T(8,128)S(1)} %slice_bitcast_fusion.1), channel_id=1, source_target_pairs={{0,2},{1,3},{2,0},{3,1}} | collective-permute-start | bytes 786440 | tf_op jit(solution)/shard_map/ppermute | solution.py:28
  4.4 1.0 %copy-start.4 = (f32[2,128,512]{2,1,0:T(8,128)S(1)}, f32[2,128,512]{2,1,0:T(8,128)}, u32[]{:S(2)}) copy-start(f32[2,128,512]{2,1,0:T(8,128)} %param.5) | copy-start | bytes 1572868
  4.4 3.6 %collective-permute-start.3 = (f32[256,384]{1,0:T(8,128)S(1)}, f32[256,384]{1,0:T(8,128)S(1)}, u32[]{:S(2)}, u32[]{:S(2)}) collective-permute-start(f32[256,384]{1,0:T(8,128)S(1)} %get-tuple-element.28), channel_id=1, source_target_pairs={{8,10},{9,11},{10,8},{11,9},{12,14},{13,15},{14,12},{15,13},{16,18... | collective-permute-start | bytes 1179656 | tf_op jit(solution)/shard_map/ppermute | solution.py:28
  8.0 5.6 %copy-start.5 = (f32[256,384]{1,0:T(8,128)}, f32[256,384]{1,0:T(8,128)S(1)}, u32[]{:S(2)}) copy-start(f32[256,384]{1,0:T(8,128)S(1)} %collective-permute-done.3) | copy-start | bytes 1179652
  8.0 12.5 %collective-permute-start.4 = (f32[512,256]{1,0:T(8,128)S(1)}, f32[512,256]{1,0:T(8,128)}, u32[]{:S(2)}, u32[]{:S(2)}) collective-permute-start(f32[512,256]{1,0:T(8,128)S(1)} %fusion.17), channel_id=1, source_target_pairs={{0,1},{1,0},{2,3},{3,2}} | collective-permute-start | bytes 1572872 | tf_op jit(solution)/shard_map/ppermute | solution.py:28
  9.5 10.2 %collective-permute-start.5 = (f32[256,256]{1,0:T(8,128)S(1)}, f32[256,256]{1,0:T(8,128)}, u32[]{:S(2)}, u32[]{:S(2)}) collective-permute-start(f32[256,256]{1,0:T(8,128)S(1)} %fusion.8), channel_id=1, source_target_pairs={{0,8},{1,9},{2,10},{3,11}} | collective-permute-start | bytes 786440 | tf_op jit(solution)/shard_map/ppermute | solution.py:34
  10.9 8.8 %collective-permute-start.6 = (f32[256,256]{1,0:T(8,128)S(1)}, f32[256,256]{1,0:T(8,128)}, u32[]{:S(2)}, u32[]{:S(2)}) collective-permute-start(f32[256,256]{1,0:T(8,128)S(1)} %fusion.8), channel_id=1, source_target_pairs={{0,16},{1,17},{2,18},{3,19}} | collective-permute-start | bytes 786440 | tf_op jit(solution)/shard_map/ppermute | solution.py:34
  12.2 7.5 %collective-permute-start.7 = (f32[256,256]{1,0:T(8,128)S(1)}, f32[256,256]{1,0:T(8,128)}, u32[]{:S(2)}, u32[]{:S(2)}) collective-permute-start(f32[256,256]{1,0:T(8,128)S(1)} %fusion.8), channel_id=1, source_target_pairs={{0,24},{1,25},{2,26},{3,27}} | collective-permute-start | bytes 786440 | tf_op jit(solution)/shard_map/ppermute | solution.py:34
  14.6 17.7 %collective-permute-start.8 = (f32[256,256]{1,0:T(8,128)S(1)}, f32[256,256]{1,0:T(8,128)}, u32[]{:S(2)}, u32[]{:S(2)}) collective-permute-start(f32[256,256]{1,0:T(8,128)S(1)} %slice.164), channel_id=1, source_target_pairs={{4,6},{5,7},{6,4},{7,5},{8,10},{9,11},{10,8},{11,9},{12,14},{13,15... | collective-permute-start | bytes 786440 | tf_op jit(solution)/shard_map/ppermute | solution.py:28
  21.6 10.8 %copy-start.1 = (f32[128,512]{1,0:T(8,128)S(1)}, f32[128,512]{1,0:T(8,128)}, u32[]{:S(2)}) copy-start(f32[128,512]{1,0:T(8,128)} %get-tuple-element.43) | copy-start | bytes 786436
  21.6 10.8 %copy-start.2 = (f32[128,512]{1,0:T(8,128)S(1)}, f32[128,512]{1,0:T(8,128)}, u32[]{:S(2)}) copy-start(f32[128,512]{1,0:T(8,128)} %get-tuple-element.45) | copy-start | bytes 786436
  32.7 9.8 %copy-start.3 = (f32[256,256]{1,0:T(8,128)S(1)}, f32[256,256]{1,0:T(8,128)}, u32[]{:S(2)}) copy-start(f32[256,256]{1,0:T(8,128)} %select_select_fusion.1) | copy-start | bytes 786436
  32.7 5.5 %collective-permute-start.12 = (f32[256,256]{1,0:T(8,128)S(1)}, f32[256,256]{1,0:T(8,128)S(1)}, u32[]{:S(2)}, u32[]{:S(2)}) collective-permute-start(f32[256,256]{1,0:T(8,128)S(1)} %fusion.13), channel_id=1, source_target_pairs={{0,8},{1,9},{2,10},{3,11}} | collective-permute-start | bytes 786440 | tf_op jit(solution)/shard_map/ppermute | solution.py:34
  33.6 9.0 %collective-permute-start.13 = (f32[256,256]{1,0:T(8,128)S(1)}, f32[256,256]{1,0:T(8,128)S(1)}, u32[]{:S(2)}, u32[]{:S(2)}) collective-permute-start(f32[256,256]{1,0:T(8,128)S(1)} %fusion.13), channel_id=1, source_target_pairs={{0,16},{1,17},{2,18},{3,19}} | collective-permute-start | bytes 786440 | tf_op jit(solution)/shard_map/ppermute | solution.py:34
  34.2 9.6 %collective-permute-start.14 = (f32[256,256]{1,0:T(8,128)S(1)}, f32[256,256]{1,0:T(8,128)}, u32[]{:S(2)}, u32[]{:S(2)}) collective-permute-start(f32[256,256]{1,0:T(8,128)S(1)} %fusion.13), channel_id=1, source_target_pairs={{0,24},{1,25},{2,26},{3,27}} | collective-permute-start | bytes 786440 | tf_op jit(solution)/shard_map/ppermute | solution.py:34
  35.6 9.6 %collective-permute-start.9 = (f32[512,128]{1,0:T(8,128)S(1)}, f32[512,128]{1,0:T(8,128)S(1)}, u32[]{:S(2)}, u32[]{:S(2)}) collective-permute-start(f32[512,128]{1,0:T(8,128)S(1)} %pad_maximum_fusion.1), channel_id=1, source_target_pairs={{0,1},{1,0},{2,3},{3,2}} | collective-permute-start | bytes 786440 | tf_op jit(solution)/shard_map/ppermute | solution.py:28
  36.3 41.0 %collective-permute-start.18 = (f32[256,384]{1,0:T(8,128)S(1)}, f32[256,384]{1,0:T(8,128)}, u32[]{:S(2)}, u32[]{:S(2)}) collective-permute-start(f32[256,384]{1,0:T(8,128)S(1)} %get-tuple-element.39), channel_id=1, source_target_pairs={{4,6},{5,7},{6,4},{7,5},{8,10},{9,11},{10,8},{11,9},{12,14},{13,15... | collective-permute-start | bytes 1179656 | tf_op jit(solution)/shard_map/ppermute | solution.py:28
  38.3 30.4 %collective-permute-start.10 = (f32[256,384]{1,0:T(8,128)S(1)}, f32[256,384]{1,0:T(8,128)S(1)}, u32[]{:S(2)}, u32[]{:S(2)}) collective-permute-start(f32[256,384]{1,0:T(8,128)S(1)} %get-tuple-element.28), channel_id=1, source_target_pairs={{4,6},{5,7},{6,4},{7,5}} | collective-permute-start | bytes 1179656 | tf_op jit(solution)/shard_map/ppermute | solution.py:28
  42.6 24.6 %collective-permute-start.11 = (f32[256,256]{1,0:T(8,128)S(1)}, f32[256,256]{1,0:T(8,128)S(1)}, u32[]{:S(2)}, u32[]{:S(2)}) collective-permute-start(f32[256,256]{1,0:T(8,128)S(1)} %copy-done.3), channel_id=1, source_target_pairs={{0,4},{1,5},{2,6},{3,7},{8,12},{9,13},{10,14},{11,15},{16,20},{17,... | collective-permute-start | bytes 786440 | tf_op jit(solution)/shard_map/ppermute | solution.py:34
  44.0 24.6 %collective-permute-start.15 = (f32[256,256]{1,0:T(8,128)S(1)}, f32[256,256]{1,0:T(8,128)S(1)}, u32[]{:S(2)}, u32[]{:S(2)}) collective-permute-start(f32[256,256]{1,0:T(8,128)S(1)} %select_select_fusion), channel_id=1, source_target_pairs={{0,4},{1,5},{2,6},{3,7},{8,12},{9,13},{10,14},{11,15},{16,20},{17,... | collective-permute-start | bytes 786440 | tf_op jit(solution)/shard_map/ppermute | solution.py:34
  68.6 1.0 %copy-start.6 = (f32[256,384]{1,0:T(8,128)S(1)}, f32[256,384]{1,0:T(8,128)}, u32[]{:S(2)}) copy-start(f32[256,384]{1,0:T(8,128)} %copy-done.5) | copy-start | bytes 1179652
  70.5 10.7 %collective-permute-start.16 = (f32[384,128]{1,0:T(8,128)S(1)}, f32[384,128]{1,0:T(8,128)S(1)}, u32[]{:S(2)}, u32[]{:S(2)}) collective-permute-start(f32[384,128]{1,0:T(8,128)S(1)} %slice.149), channel_id=1, source_target_pairs={{4,5},{5,4},{6,7},{7,6},{8,9},{9,8},{10,11},{11,10},{12,13},{13,12... | collective-permute-start | bytes 589832 | tf_op jit(solution)/shard_map/ppermute | solution.py:28
  74.0 7.1 %collective-permute-start.17 = (f32[256,128]{1,0:T(8,128)S(1)}, f32[256,128]{1,0:T(8,128)S(1)}, u32[]{:S(2)}, u32[]{:S(2)}) collective-permute-start(f32[256,128]{1,0:T(8,128)S(1)} %slice.152), channel_id=1, source_target_pairs={{4,5},{5,4},{6,7},{7,6},{8,9},{9,8},{10,11},{11,10},{12,13},{13,12... | collective-permute-start | bytes 393224 | tf_op jit(solution)/shard_map/ppermute | solution.py:28
  79.2 6.4 %collective-permute-start.19 = (f32[384,128]{1,0:T(8,128)S(1)}, f32[384,128]{1,0:T(8,128)S(1)}, u32[]{:S(2)}, u32[]{:S(2)}) collective-permute-start(f32[384,128]{1,0:T(8,128)S(1)} %slice.156), channel_id=1, source_target_pairs={{4,5},{5,4},{6,7},{7,6},{8,9},{9,8},{10,11},{11,10},{12,13},{13,12... | collective-permute-start | bytes 589832 | tf_op jit(solution)/shard_map/ppermute | solution.py:28

commit v4 on v2

v4 whole, which is shorter than its diff:
```python
import functools
import jax
import jax.numpy as jnp
from jax import lax
from jax.experimental import pallas as pl
from jax.experimental.pallas import tpu as pltpu
from jax.sharding import PartitionSpec as P

AXES = ("rows", "cols")
EIGHTHS = (0, 2, 3, 5, 8)
PARAMS = pltpu.CompilerParams(vmem_limit_bytes=24 * 1024 * 1024)


def split(array):
    high = array.astype(jnp.bfloat16)
    return high, (array - high.astype(jnp.float32)).astype(jnp.bfloat16)


def dot(left, right, left_dim):
    def one(a, b):
        return lax.dot_general(
            a, b, (((left_dim,), (0,)), ((), ())), preferred_element_type=jnp.float32
        )

    left_high, left_low = split(left)
    right_high, right_low = split(right)
    return one(left_high, right_high) + (one(left_high, right_low) + one(left_low, right_high))


def call(kernel, shapes, n_in, flops, *args):
    return pl.pallas_call(
        kernel,
        out_shape=[jax.ShapeDtypeStruct(shape, jnp.float32) for shape in shapes],
        in_specs=[pl.BlockSpec(memory_space=pltpu.VMEM)] * n_in
        + [pl.BlockSpec(memory_space=pltpu.SMEM)] * (len(args) - n_in),
        out_specs=[pl.BlockSpec(memory_space=pltpu.VMEM)] * len(shapes),
        compiler_params=PARAMS,
        cost_estimate=pl.CostEstimate(flops=flops, bytes_accessed=0, transcendentals=0),
    )(*args)


def first_kernel(places, width, lead, lead_other, rhs, *refs):
    others, (low, solved, update, shuffled) = refs[:-4], refs[-4:]
    cands = rhs.shape[1]
    blocks = [rhs[...]] + [other[...] for other in others]
    blocks = jnp.concatenate(blocks, axis=1)
    inverse = jnp.concatenate([lead[:, :width], lead_other[:, :width]], axis=0)
    first = dot(inverse, blocks, 1)
    solved[...] = first
    corner = jnp.concatenate([lead[:, width:], lead_other[:, width:]], axis=0)
    total = dot(corner, first, 0)
    pieces = [total[:, at * cands : (at + 1) * cands] for at in range(len(places))]
    pieces[0] = pieces[0] - low[...]
    for at, place in enumerate(places):
        update[:, at * cands : (at + 1) * cands] = pieces[at]
        shuffled[:, at * cands : (at + 1) * cands] = pieces[place]


def second_kernel(inverse, inverse_other, update, got, solved):
    both = jnp.concatenate([inverse[...], inverse_other[...]], axis=0)
    solved[...] = dot(both, -(update[...] + got[...]), 1)


def chunk_kernel(part, mine, other, late, first, second, base, beside, own, send):
    cands = base.shape[1]
    depth = first.shape[0] // 2
    other = other[...]
    if late is not None:
        other = jnp.where(beside[0] == 1, late[:, part], other)
    factors = jnp.concatenate([mine[...], other], axis=0)
    solved = jnp.concatenate(
        [first[:depth], second[:depth], first[depth:], second[depth:]], axis=0
    )
    partial = dot(factors, solved, 0)
    own[...] = base[...] - partial[:, :cands]
    send[...] = partial[:, cands:]


def chunk_kernel_plain(part, mine, other, first, second, base, beside, own, send):
    chunk_kernel(part, mine, other, None, first, second, base, beside, own, send)


def make_on_device(n_rows, n_cols):
    half = n_cols // 2

    def swap(array, flip, rows):
        pairs = [
            (row * n_cols + col, row * n_cols + (col ^ flip))
            for row in rows
            for col in range(n_cols)
        ]
        return lax.ppermute(array, AXES, pairs)

    def send_down(array, offset, have):
        pairs = [
            (row * n_cols + col, (row + offset) * n_cols + col) for row in have for col in range(n_cols)
        ]
        return lax.ppermute(array, AXES, pairs)

    def spread(array, row_id, stages, have):
        for low, radix in stages:
            digit = (row_id // low) % radix
            result = array
            for step in range(radix - 1, 0, -1):
                result = jnp.where(digit == step, send_down(array, step * low, have), result)
            array = result
            have = [row + step * low for row in have for step in range(radix)]
        return array

    def broadcast_outer(array, row_id):
        stages = []
        low = 2
        while low < n_rows:
            radix = min(4, n_rows // low)
            stages.append((low, radix))
            low *= radix
        return spread(array, row_id, stages[::-1], [0])

    def broadcast_inner(array, row_id):
        return spread(array, row_id, [(1, 2)], range(0, n_rows, 2))

    def block(array, place, cands):
        return array[:, place * cands : (place + 1) * cands]

    def shuffle(array, flip, cands):
        return jnp.concatenate([block(array, at ^ flip, cands) for at in range(half)], axis=1)

    def in_order(pieces, col_id):
        offsets = [at for step in range(half) for at in (step, step ^ half)]
        pieces = [pieces[offsets.index(at)] for at in range(n_cols)]
        bit = 1
        while bit < n_cols:
            flipped = (col_id & bit) != 0
            pieces = [
                jnp.where(flipped, pieces[at ^ bit], pieces[at]) for at in range(n_cols)
            ]
            bit *= 2
        return pieces

    def on_device(cross_kernel, factor_panels, block_inverses):
        row_id = lax.axis_index("rows")
        col_id = lax.axis_index("cols")
        width = block_inverses.shape[2]
        depth = block_inverses.shape[1]
        n_design, cands = cross_kernel.shape
        cuts = [n_design * at // 8 for at in EIGHTHS]
        parts = [slice(start, stop) for start, stop in zip(cuts, cuts[1:])]
        early = slice(0, cuts[-2])
        top = [0]
        beside = range(1, min(2, n_rows))
        below = range(2, n_rows)
        flat = factor_panels.reshape(2 * depth, n_design)
        mine = [flat[:, part] for part in parts]

        lead = jnp.concatenate(
            [block_inverses[0], factor_panels[0, :, width : 2 * width]], axis=1
        )
        lead, rhs = lax.optimization_barrier((lead, cross_kernel[:width]))
        lead_other = swap(lead, half, top)
        rhs_others = [swap(rhs, step, top) for step in range(1, half)]
        arrived = [swap(piece, half, below) for piece in mine[:-1]]
        arrived.append(swap(mine[-1], half, range(1, n_rows)))

        first, update, shuffled = call(
            functools.partial(first_kernel, [at ^ 1 for at in range(half)], width),
            [(2 * depth, half * cands)] + [(width, half * cands)] * 2,
            4 + len(rhs_others),
            6 * width * half * cands * (2 * depth + 2 * depth),
            lead,
            lead_other,
            rhs,
            *rhs_others,
            cross_kernel[width : 2 * width],
        )
        first, inverse, late = lax.optimization_barrier((first, block_inverses[1], flat[:, early]))
        late = swap(late, half, beside)
        inverse_other = swap(inverse, half, top)
        shuffled, arrived[0] = lax.optimization_barrier((shuffled, arrived[0]))
        got = swap(shuffled, 1, top)
        bit = 2
        while bit < half:
            update = update + got
            got = swap(shuffle(update, bit, cands), bit, top)
            bit *= 2
        first_half = broadcast_outer(first, row_id)
        got, first_half, arrived[1] = lax.optimization_barrier((got, first_half, arrived[1]))
        (second,) = call(
            second_kernel,
            [(2 * depth, half * cands)],
            4,
            6 * 2 * depth * width * half * cands,
            inverse,
            inverse_other,
            update,
            got,
        )
        second_half = broadcast_outer(second, row_id)
        second_half, arrived[2] = lax.optimization_barrier((second_half, arrived[2]))
        solved = [broadcast_inner(first_half, row_id), broadcast_inner(second_half, row_id)]

        pair = jnp.concatenate([first, second], axis=0)
        others = [block(pair, 0, cands)]
        others += [swap(block(pair, step, cands), step, top) for step in range(1, half)]
        pieces = [[], []]
        for got in others:
            for at in range(4):
                pieces[at // 2].append(got[at * depth : (at + 1) * depth])
        top_rows = jnp.concatenate(
            in_order(pieces[0], col_id) + in_order(pieces[1], col_id), axis=0
        )

        is_beside = (row_id == 1).astype(jnp.int32).reshape(1)
        fresh = []
        for at, part in enumerate(parts):
            last = at == len(parts) - 1
            args = [mine[at], arrived[at]] + ([] if last else [late])
            args += [*solved, cross_kernel[part]]
            count = part.stop - part.start
            own, send = call(
                functools.partial(chunk_kernel_plain if last else chunk_kernel, part),
                [(count, cands), (count, (half - 1) * cands)],
                len(args),
                6 * count * 4 * depth * half * cands,
                *args,
                is_beside,
            )
            own, send, solved[0], solved[1] = lax.optimization_barrier((own, send, *solved))
            for step in range(1, half):
                own = own - swap(block(send, step - 1, cands), step, range(1, n_rows))
            fresh.append(own)
        fresh = jnp.concatenate(fresh, axis=0)
        head = jnp.where(row_id == 0, top_rows, fresh[: 2 * width])
        return jnp.concatenate([head, fresh[2 * width :]], axis=0)

    return on_device


def solution(mesh):
    in_specs = (P("rows", "cols"), P(None, "cols", "rows"), P(None, "cols", None))
    out_specs = P("rows", "cols")
    return jax.shard_map(
        make_on_device(mesh.shape["rows"], mesh.shape["cols"]),
        mesh=mesh,
        in_specs=in_specs,
        out_specs=out_specs,
        check_vma=False,
    )
```

time: 92.3 us -> 88.2 us (0.956)
  matrix products: 4.59 us -> 0 us
  Pallas kernels: 0 us -> 4 us
  local copies, waits for them, and re-layouts: 8.21 us -> 6.03 us
  starting transfers between devices: 41.6 us -> 40.6 us
    dot_general x7 -> x0, matrix products: 4.59 us -> none  [dot(): lax.dot_general(left, right, (((left_dim,), (0,)), ((), ())), precision=l...]
    pallas_call x0 -> x6, Pallas kernels: none -> 4 us  [call(): pl.pallas_call(kernel, out_shape=[jax.ShapeDtypeStruct(shape, jnp.float32...]
    squeeze x6 -> x1, local copies, waits for them, and re-layouts: 2.89 us -> 1.18 us  [on_device(): block_inverses[1]]
    sub x2 -> x4, other arithmetic: 1.21 us -> 0.07 us  [on_device(): own = own - swap(block(send, step - 1, cands), step, range(1, n_rows))]
    squeeze x1, local copies, waits for them, and re-layouts: 1.03 us -> 0.02 us  [on_device(): factor_panels[0, :, width:2 * width]]
    slice x6 -> x8, local copies, waits for them, and re-layouts: 2.03 us -> 2.95 us  [the longest x3 1.98 us: on_device(): mine = [flat[:, part] for part in parts]]
    ppermute x13 -> x14, starting transfers between devices: 30.9 us -> 30.5 us  [swap(): return lax.ppermute(array, AXES, pairs)]
    unnamed x23 -> x10, local copies, waits for them, and re-layouts: 2.23 us -> 1.88 us
  transfers between devices with their start and end apart: 21 -> 22, of which waited for: 7 -> 6; matrix products, arithmetic and copies ran while one was open for 14% -> 7% of each run, Pallas kernels for 0% -> 5%
where the time goes in v4:
time: 88.2 us; the launch traced here: 87.6 us
  starting transfers between devices  40.6 us (46%)
  waiting for transfers between devices  32.7 us (37%)
  local copies, waits for them, and re-layouts  6.03 us (7%)
  Pallas kernels  4 us (5%)
  other arithmetic  3.7 us (4%)
    ppermute x14, starting transfers between devices, swap(): return lax.ppermute(array, AXES, pairs)  30.5 us
    ppermute x14, waiting for transfers between devices, swap(): return lax.ppermute(array, AXES, pairs)  19.2 us
    ppermute x8, waiting for transfers between devices, send_down(): return lax.ppermute(array, AXES, pairs)  13.5 us
    ppermute x8, starting transfers between devices, send_down(): return lax.ppermute(array, AXES, pairs)  10.1 us
    pallas_call x6, Pallas kernels, call(): pl.pallas_call(kernel, out_shape=[jax.ShapeDtypeStruct(shape, jnp.float32...  4 us
    slice x3, local copies, waits for them, and re-layouts, on_device(): mine = [flat[:, part] for part in parts]  1.98 us
    select_n x4, other arithmetic, spread(): jnp.where(digit == step, send_down(array, step * low, have), result)  1.89 us
    unnamed x10, local copies, waits for them, and re-layouts  1.88 us
  transfers between devices with their start and end apart: 22, of which 6 were waited for; matrix products, arithmetic and copies ran while one was open for 7% of the time, Pallas kernels for 5%

profile of v4, /device:TPU:2, one launch (start us, length us, event | category | flops | bytes accessed | tf_op | source)
XLA Modules:
  0.0 87.6 jit_solution(2364548260180530981)
XLA Ops:
  0.0 1.2 %slice_bitcast_fusion = (f32[128,512]{1,0:T(8,128)S(1)}, f32[128,512]{1,0:T(8,128)S(1)}) fusion(f32[2,128,512]{2,1,0:T(8,128)} %param.5), kind=kLoop, calls=%fused_computation.5 | loop fusion | bytes 1048576 | tf_op jit(solution)/shard_map/squeeze | solution.py:175
  1.2 0.2 copy-done
  1.4 0.1 copy-done.1
  1.6 0.7 collective-permute-start
  2.3 0.7 collective-permute-start.1
  3.0 4.5 %collective-permute-start.3 = (f32[256,256]{1,0:T(8,128)S(1)}, f32[256,256]{1,0:T(8,128)S(1)}, u32[]{:S(2)}, u32[]{:S(2)}) collective-permute-start(f32[256,256]{1,0:T(8,128)S(1)} %get-tuple-element.80.mine), channel_id=1, source_target_pairs={{8,10},{9,11},{10,8},{11,9},{12,14},{13,15},{14,12},{15,13},{16,18... | collective-permute-start | bytes 786440 | tf_op jit(solution)/shard_map/ppermute | solution.py:92
  7.6 1.9 %shard_map.37 = (f32[256,256]{1,0:T(8,128)S(1)}, f32[512,256]{1,0:T(8,128)S(1)}, f32[512,256]{1,0:T(8,128)}) custom-call(f32[128,1024]{1,0:T(8,128)S(1)} %pad_maximum_fusion.lead, f32[128,1024]{1,0:T(8,128)S(1)} %collective-permute-done.lead_other, f32[512,128]{1,0:T(8,128)S(1)} %get-tuple-element.43.rhs, f32[512,128]{1,0:T(8,128)S(1)} %collective-permute-done.1.refs_0_, ...), custom_call_target="tpu_custom_call" | custom-call | flops 402653184 | tf_op jit(solution)/shard_map/pallas_call | solution.py:31
  9.4 10.1 %collective-permute-done.3.other = f32[256,256]{1,0:T(8,128)S(1)} collective-permute-done((f32[256,256]{1,0:T(8,128)S(1)}, f32[256,256]{1,0:T(8,128)S(1)}, u32[]{:S(2)}, u32[]{:S(2)}) %collective-permute-start.3) | collective-permute-done | bytes 262176 | tf_op jit(solution)/shard_map/ppermute | solution.py:92
  19.5 0.7 collective-permute-start.4
  20.2 0.9 %slice.101 = f32[256,640]{1,0:T(8,128)} slice(f32[256,1024]{1,0:T(8,128)S(1)} %bitcast.11), slice={[0:256], [0:640]} | slice | bytes 1310720 | tf_op jit(solution)/shard_map/slice | solution.py:175
  21.1 1.3 %collective-permute-start.5 = (f32[256,256]{1,0:T(8,128)S(1)}, f32[256,256]{1,0:T(8,128)S(1)}, u32[]{:S(2)}, u32[]{:S(2)}) collective-permute-start(f32[256,256]{1,0:T(8,128)S(1)} %get-tuple-element.45), channel_id=1, source_target_pairs={{0,8},{1,9},{2,10},{3,11}} | collective-permute-start | bytes 786440 | tf_op jit(solution)/shard_map/ppermute | solution.py:98
  22.4 0.7 collective-permute-start.6
  23.0 1.4 %collective-permute-start.7 = (f32[256,256]{1,0:T(8,128)S(1)}, f32[256,256]{1,0:T(8,128)}, u32[]{:S(2)}, u32[]{:S(2)}) collective-permute-start(f32[256,256]{1,0:T(8,128)S(1)} %get-tuple-element.45), channel_id=1, source_target_pairs={{0,24},{1,25},{2,26},{3,27}} | collective-permute-start | bytes 786440 | tf_op jit(solution)/shard_map/ppermute | solution.py:98
  24.4 0.7 collective-permute-start.2
  25.1 0.9 %slice.103.mine = f32[256,128]{1,0:T(8,128)S(1)} slice(f32[256,1024]{1,0:T(8,128)} %bitcast.8), slice={[0:256], [256:384]} | slice | bytes 262144 | tf_op jit(solution)/shard_map/slice | solution.py:153
  26.1 4.6 %collective-permute-done.5 = f32[256,256]{1,0:T(8,128)S(1)} collective-permute-done((f32[256,256]{1,0:T(8,128)S(1)}, f32[256,256]{1,0:T(8,128)S(1)}, u32[]{:S(2)}, u32[]{:S(2)}) %collective-permute-start.5) | collective-permute-done | bytes 262176 | tf_op jit(solution)/shard_map/ppermute | solution.py:98
  30.7 5.3 %collective-permute-start.8 = (f32[256,128]{1,0:T(8,128)S(1)}, f32[256,128]{1,0:T(8,128)S(1)}, u32[]{:S(2)}, u32[]{:S(2)}) collective-permute-start(f32[256,128]{1,0:T(8,128)S(1)} %slice.103.mine), channel_id=1, source_target_pairs={{8,10},{9,11},{10,8},{11,9},{12,14},{13,15},{14,12},{15,13},{16,18... | collective-permute-start | bytes 393224 | tf_op jit(solution)/shard_map/ppermute | solution.py:92
  36.0 0.7 copy-done.4
  36.7 1.9 %collective-permute-start.15 = (f32[256,256]{1,0:T(8,128)S(1)}, f32[256,256]{1,0:T(8,128)S(1)}, u32[]{:S(2)}, u32[]{:S(2)}) collective-permute-start(f32[256,256]{1,0:T(8,128)S(1)} %get-tuple-element.79.mine), channel_id=1, source_target_pairs={{8,10},{9,11},{10,8},{11,9},{12,14},{13,15},{14,12},{15,13},{16,18... | collective-permute-start | bytes 786440 | tf_op jit(solution)/shard_map/ppermute | solution.py:92
  38.6 0.8 select_select_fusion.1
  39.4 2.9 %collective-permute-done.8.other = f32[256,128]{1,0:T(8,128)S(1)} collective-permute-done((f32[256,128]{1,0:T(8,128)S(1)}, f32[256,128]{1,0:T(8,128)S(1)}, u32[]{:S(2)}, u32[]{:S(2)}) %collective-permute-start.8) | collective-permute-done | bytes 131104 | tf_op jit(solution)/shard_map/ppermute | solution.py:92
  42.3 0.4 shard_map.38
  42.7 0.0 copy-start.2
  42.7 1.4 %collective-permute-start.12 = (f32[256,256]{1,0:T(8,128)S(1)}, f32[256,256]{1,0:T(8,128)}, u32[]{:S(2)}, u32[]{:S(2)}) collective-permute-start(f32[256,256]{1,0:T(8,128)S(1)} %shard_map.38), channel_id=1, source_target_pairs={{0,8},{1,9},{2,10},{3,11}} | collective-permute-start | bytes 786440 | tf_op jit(solution)/shard_map/ppermute | solution.py:98
  44.2 1.4 %collective-permute-start.13 = (f32[256,256]{1,0:T(8,128)S(1)}, f32[256,256]{1,0:T(8,128)}, u32[]{:S(2)}, u32[]{:S(2)}) collective-permute-start(f32[256,256]{1,0:T(8,128)S(1)} %shard_map.38), channel_id=1, source_target_pairs={{0,16},{1,17},{2,18},{3,19}} | collective-permute-start | bytes 786440 | tf_op jit(solution)/shard_map/ppermute | solution.py:98
  45.5 1.4 %collective-permute-start.14 = (f32[256,256]{1,0:T(8,128)S(1)}, f32[256,256]{1,0:T(8,128)}, u32[]{:S(2)}, u32[]{:S(2)}) collective-permute-start(f32[256,256]{1,0:T(8,128)S(1)} %shard_map.38), channel_id=1, source_target_pairs={{0,24},{1,25},{2,26},{3,27}} | collective-permute-start | bytes 786440 | tf_op jit(solution)/shard_map/ppermute | solution.py:98
  46.9 0.7 pad_maximum_fusion.1
  47.6 0.7 collective-permute-start.9
  48.4 1.0 %slice.111.mine = f32[256,384]{1,0:T(8,128)S(1)} slice(f32[256,1024]{1,0:T(8,128)} %bitcast.9), slice={[0:256], [640:1024]} | slice | bytes 786432 | tf_op jit(solution)/shard_map/slice | solution.py:153
  49.4 8.9 %collective-permute-done.12 = f32[256,256]{1,0:T(8,128)} collective-permute-done((f32[256,256]{1,0:T(8,128)S(1)}, f32[256,256]{1,0:T(8,128)}, u32[]{:S(2)}, u32[]{:S(2)}) %collective-permute-start.12) | collective-permute-done | bytes 262176 | tf_op jit(solution)/shard_map/ppermute | solution.py:98
  58.3 1.9 %collective-permute-start.20 = (f32[256,384]{1,0:T(8,128)S(1)}, f32[256,384]{1,0:T(8,128)S(1)}, u32[]{:S(2)}, u32[]{:S(2)}) collective-permute-start(f32[256,384]{1,0:T(8,128)S(1)} %slice.111.mine), channel_id=1, source_target_pairs={{4,6},{5,7},{6,4},{7,5},{8,10},{9,11},{10,8},{11,9},{12,14},{13,15... | collective-permute-start | bytes 1179656 | tf_op jit(solution)/shard_map/ppermute | solution.py:92
  60.3 0.7 collective-permute-start.10
  61.0 1.3 %collective-permute-start.11 = (f32[256,256]{1,0:T(8,128)}, f32[256,256]{1,0:T(8,128)S(1)}, u32[]{:S(2)}, u32[]{:S(2)}) collective-permute-start(f32[256,256]{1,0:T(8,128)} %select_select_fusion.1), channel_id=1, source_target_pairs={{0,4},{1,5},{2,6},{3,7},{8,12},{9,13},{10,14},{11,15},{16,20},{17,... | collective-permute-start | bytes 786440 | tf_op jit(solution)/shard_map/ppermute | solution.py:98
  62.3 1.0 %select_select_fusion = f32[256,256]{1,0:T(8,128)S(1)} fusion(f32[256,256]{1,0:T(8,128)} %collective-permute-done.12, f32[256,256]{1,0:T(8,128)} %collective-permute-done.13, f32[256,256]{1,0:T(8,128)} %collective-permute-done.14, f32[256,256]{1,0:T(8,128)S(1)} %shard_map.38, pred[]{:T(512)S(6)} %eq.30, pred[]{:T(512)S(6)} %eq.29, pred[]{:T(512)S(6)} %eq.28), kind=kLoop, calls=%fused_computation.3 | loop fusion | flops 196608 | bytes 1310723 | tf_op jit(solution)/shard_map/jit(_where)/select_n | solution.py:105
  63.3 1.3 %collective-permute-start.16 = (f32[256,256]{1,0:T(8,128)S(1)}, f32[256,256]{1,0:T(8,128)S(1)}, u32[]{:S(2)}, u32[]{:S(2)}) collective-permute-start(f32[256,256]{1,0:T(8,128)S(1)} %select_select_fusion), channel_id=1, source_target_pairs={{0,4},{1,5},{2,6},{3,7},{8,12},{9,13},{10,14},{11,15},{16,20},{17,... | collective-permute-start | bytes 786440 | tf_op jit(solution)/shard_map/ppermute | solution.py:98
  64.8 0.9 %copy-done.3 = f32[256,256]{1,0:T(8,128)S(1)} copy-done((f32[256,256]{1,0:T(8,128)S(1)}, f32[256,256]{1,0:T(8,128)}, u32[]{:S(2)}) %copy-start.3) | copy-done | bytes 262168
  65.8 0.0 collective-permute-done.16
  65.8 0.4 shard_map.39
  66.3 5.1 %collective-permute-start.17 = (f32[256,128]{1,0:T(8,128)S(1)}, f32[256,128]{1,0:T(8,128)S(1)}, u32[]{:S(2)}, u32[]{:S(2)}) collective-permute-start(f32[256,128]{1,0:T(8,128)S(1)} %get-tuple-element.58), channel_id=1, source_target_pairs={{4,5},{5,4},{6,7},{7,6},{8,9},{9,8},{10,11},{11,10},{12,13},{13,12... | collective-permute-start | bytes 393224 | tf_op jit(solution)/shard_map/ppermute | solution.py:92
  71.3 0.3 shard_map.40
  71.7 1.9 %collective-permute-start.18 = (f32[128,128]{1,0:T(8,128)S(1)}, f32[128,128]{1,0:T(8,128)S(1)}, u32[]{:S(2)}, u32[]{:S(2)}) collective-permute-start(f32[128,128]{1,0:T(8,128)S(1)} %get-tuple-element.65), channel_id=1, source_target_pairs={{4,5},{5,4},{6,7},{7,6},{8,9},{9,8},{10,11},{11,10},{12,13},{13,12... | collective-permute-start | bytes 196616 | tf_op jit(solution)/shard_map/ppermute | solution.py:92
  73.6 0.4 shard_map.41
  74.0 3.9 %collective-permute-start.19 = (f32[256,128]{1,0:T(8,128)S(1)}, f32[256,128]{1,0:T(8,128)S(1)}, u32[]{:S(2)}, u32[]{:S(2)}) collective-permute-start(f32[256,128]{1,0:T(8,128)S(1)} %get-tuple-element.72), channel_id=1, source_target_pairs={{4,5},{5,4},{6,7},{7,6},{8,9},{9,8},{10,11},{11,10},{12,13},{13,12... | collective-permute-start | bytes 393224 | tf_op jit(solution)/shard_map/ppermute | solution.py:92
  78.0 0.5 shard_map.42
  78.5 1.9 %collective-permute-start.21 = (f32[384,128]{1,0:T(8,128)S(1)}, f32[384,128]{1,0:T(8,128)S(1)}, u32[]{:S(2)}, u32[]{:S(2)}) collective-permute-start(f32[384,128]{1,0:T(8,128)S(1)} %get-tuple-element.78), channel_id=1, source_target_pairs={{4,5},{5,4},{6,7},{7,6},{8,9},{9,8},{10,11},{11,10},{12,13},{13,12... | collective-permute-start | bytes 589832 | tf_op jit(solution)/shard_map/ppermute | solution.py:92
  80.5 0.9 %collective-permute-done.19 = f32[256,128]{1,0:T(8,128)S(1)} collective-permute-done((f32[256,128]{1,0:T(8,128)S(1)}, f32[256,128]{1,0:T(8,128)S(1)}, u32[]{:S(2)}, u32[]{:S(2)}) %collective-permute-start.19) | collective-permute-done | bytes 131104 | tf_op jit(solution)/shard_map/ppermute | solution.py:92
  81.4 5.3 %collective-permute-done.21 = f32[384,128]{1,0:T(8,128)S(1)} collective-permute-done((f32[384,128]{1,0:T(8,128)S(1)}, f32[384,128]{1,0:T(8,128)S(1)}, u32[]{:S(2)}, u32[]{:S(2)}) %collective-permute-start.21) | collective-permute-done | bytes 196640 | tf_op jit(solution)/shard_map/ppermute | solution.py:92
  86.8 0.9 maximum_select_fusion
  (41 shorter events, 0.5 us)
Async XLA Ops:
  0.0 1.4 %copy-start = (f32[2,128,1024]{2,1,0:T(8,128)S(1)}, f32[2,128,1024]{2,1,0:T(8,128)}, u32[]{:S(2)}) copy-start(f32[2,128,1024]{2,1,0:T(8,128)} %param.4) | copy-start | bytes 3145732
  0.0 1.5 %copy-start.1 = (f32[1024,128]{1,0:T(8,128)S(1)}, f32[1024,128]{1,0:T(8,128)}, u32[]{:S(2)}) copy-start(f32[1024,128]{1,0:T(8,128)} %param.3) | copy-start | bytes 1572868
  1.6 6.0 %collective-permute-start = (f32[128,1024]{1,0:T(8,128)S(1)}, f32[128,1024]{1,0:T(8,128)S(1)}, u32[]{:S(2)}, u32[]{:S(2)}) collective-permute-start(f32[128,1024]{1,0:T(8,128)S(1)} %pad_maximum_fusion.lead), channel_id=1, source_target_pairs={{0,2},{1,3},{2,0},{3,1}} | collective-permute-start | bytes 1572872 | tf_op jit(solution)/shard_map/ppermute | solution.py:92
  2.3 5.2 %collective-permute-start.1 = (f32[512,128]{1,0:T(8,128)S(1)}, f32[512,128]{1,0:T(8,128)S(1)}, u32[]{:S(2)}, u32[]{:S(2)}) collective-permute-start(f32[512,128]{1,0:T(8,128)S(1)} %get-tuple-element.43.rhs), channel_id=1, source_target_pairs={{0,1},{1,0},{2,3},{3,2}} | collective-permute-start | bytes 786440 | tf_op jit(solution)/shard_map/ppermute | solution.py:92
  3.0 16.5 %collective-permute-start.3 = (f32[256,256]{1,0:T(8,128)S(1)}, f32[256,256]{1,0:T(8,128)S(1)}, u32[]{:S(2)}, u32[]{:S(2)}) collective-permute-start(f32[256,256]{1,0:T(8,128)S(1)} %get-tuple-element.80.mine), channel_id=1, source_target_pairs={{8,10},{9,11},{10,8},{11,9},{12,14},{13,15},{14,12},{15,13},{16,18... | collective-permute-start | bytes 786440 | tf_op jit(solution)/shard_map/ppermute | solution.py:92
  19.5 22.8 %collective-permute-start.4 = (f32[512,256]{1,0:T(8,128)}, f32[512,256]{1,0:T(8,128)S(1)}, u32[]{:S(2)}, u32[]{:S(2)}) collective-permute-start(f32[512,256]{1,0:T(8,128)} %get-tuple-element.49), channel_id=1, source_target_pairs={{0,1},{1,0},{2,3},{3,2}} | collective-permute-start | bytes 1572872 | tf_op jit(solution)/shard_map/ppermute | solution.py:92
  21.1 9.6 %collective-permute-start.5 = (f32[256,256]{1,0:T(8,128)S(1)}, f32[256,256]{1,0:T(8,128)S(1)}, u32[]{:S(2)}, u32[]{:S(2)}) collective-permute-start(f32[256,256]{1,0:T(8,128)S(1)} %get-tuple-element.45), channel_id=1, source_target_pairs={{0,8},{1,9},{2,10},{3,11}} | collective-permute-start | bytes 786440 | tf_op jit(solution)/shard_map/ppermute | solution.py:98
  22.4 13.6 %collective-permute-start.6 = (f32[256,256]{1,0:T(8,128)S(1)}, f32[256,256]{1,0:T(8,128)S(1)}, u32[]{:S(2)}, u32[]{:S(2)}) collective-permute-start(f32[256,256]{1,0:T(8,128)S(1)} %get-tuple-element.45), channel_id=1, source_target_pairs={{0,16},{1,17},{2,18},{3,19}} | collective-permute-start | bytes 786440 | tf_op jit(solution)/shard_map/ppermute | solution.py:98
  23.0 15.5 %collective-permute-start.7 = (f32[256,256]{1,0:T(8,128)S(1)}, f32[256,256]{1,0:T(8,128)}, u32[]{:S(2)}, u32[]{:S(2)}) collective-permute-start(f32[256,256]{1,0:T(8,128)S(1)} %get-tuple-element.45), channel_id=1, source_target_pairs={{0,24},{1,25},{2,26},{3,27}} | collective-permute-start | bytes 786440 | tf_op jit(solution)/shard_map/ppermute | solution.py:98
  24.4 17.9 %collective-permute-start.2 = (f32[128,512]{1,0:T(8,128)S(1)}, f32[128,512]{1,0:T(8,128)S(1)}, u32[]{:S(2)}, u32[]{:S(2)}) collective-permute-start(f32[128,512]{1,0:T(8,128)S(1)} %get-tuple-element.46.inverse), channel_id=1, source_target_pairs={{0,2},{1,3},{2,0},{3,1}} | collective-permute-start | bytes 786440 | tf_op jit(solution)/shard_map/ppermute | solution.py:92
  30.7 11.6 %collective-permute-start.8 = (f32[256,128]{1,0:T(8,128)S(1)}, f32[256,128]{1,0:T(8,128)S(1)}, u32[]{:S(2)}, u32[]{:S(2)}) collective-permute-start(f32[256,128]{1,0:T(8,128)S(1)} %slice.103.mine), channel_id=1, source_target_pairs={{8,10},{9,11},{10,8},{11,9},{12,14},{13,15},{14,12},{15,13},{16,18... | collective-permute-start | bytes 393224 | tf_op jit(solution)/shard_map/ppermute | solution.py:92
  36.0 0.7 copy-start.4
  36.7 26.6 %collective-permute-start.15 = (f32[256,256]{1,0:T(8,128)S(1)}, f32[256,256]{1,0:T(8,128)S(1)}, u32[]{:S(2)}, u32[]{:S(2)}) collective-permute-start(f32[256,256]{1,0:T(8,128)S(1)} %get-tuple-element.79.mine), channel_id=1, source_target_pairs={{8,10},{9,11},{10,8},{11,9},{12,14},{13,15},{14,12},{15,13},{16,18... | collective-permute-start | bytes 786440 | tf_op jit(solution)/shard_map/ppermute | solution.py:92
  42.7 5.6 %copy-start.2 = (f32[1024,128]{1,0:T(8,128)S(1)}, f32[1024,128]{1,0:T(8,128)}, u32[]{:S(2)}) copy-start(f32[1024,128]{1,0:T(8,128)} %param.3) | copy-start | bytes 1572868
  42.7 15.6 %collective-permute-start.12 = (f32[256,256]{1,0:T(8,128)S(1)}, f32[256,256]{1,0:T(8,128)}, u32[]{:S(2)}, u32[]{:S(2)}) collective-permute-start(f32[256,256]{1,0:T(8,128)S(1)} %shard_map.38), channel_id=1, source_target_pairs={{0,8},{1,9},{2,10},{3,11}} | collective-permute-start | bytes 786440 | tf_op jit(solution)/shard_map/ppermute | solution.py:98
  44.2 16.1 %collective-permute-start.13 = (f32[256,256]{1,0:T(8,128)S(1)}, f32[256,256]{1,0:T(8,128)}, u32[]{:S(2)}, u32[]{:S(2)}) collective-permute-start(f32[256,256]{1,0:T(8,128)S(1)} %shard_map.38), channel_id=1, source_target_pairs={{0,16},{1,17},{2,18},{3,19}} | collective-permute-start | bytes 786440 | tf_op jit(solution)/shard_map/ppermute | solution.py:98
  45.5 15.4 %collective-permute-start.14 = (f32[256,256]{1,0:T(8,128)S(1)}, f32[256,256]{1,0:T(8,128)}, u32[]{:S(2)}, u32[]{:S(2)}) collective-permute-start(f32[256,256]{1,0:T(8,128)S(1)} %shard_map.38), channel_id=1, source_target_pairs={{0,24},{1,25},{2,26},{3,27}} | collective-permute-start | bytes 786440 | tf_op jit(solution)/shard_map/ppermute | solution.py:98
  47.6 17.0 %collective-permute-start.9 = (f32[512,128]{1,0:T(8,128)}, f32[512,128]{1,0:T(8,128)S(1)}, u32[]{:S(2)}, u32[]{:S(2)}) collective-permute-start(f32[512,128]{1,0:T(8,128)} %pad_maximum_fusion.1), channel_id=1, source_target_pairs={{0,1},{1,0},{2,3},{3,2}} | collective-permute-start | bytes 786440 | tf_op jit(solution)/shard_map/ppermute | solution.py:92
  58.3 19.6 %collective-permute-start.20 = (f32[256,384]{1,0:T(8,128)S(1)}, f32[256,384]{1,0:T(8,128)S(1)}, u32[]{:S(2)}, u32[]{:S(2)}) collective-permute-start(f32[256,384]{1,0:T(8,128)S(1)} %slice.111.mine), channel_id=1, source_target_pairs={{4,6},{5,7},{6,4},{7,5},{8,10},{9,11},{10,8},{11,9},{12,14},{13,15... | collective-permute-start | bytes 1179656 | tf_op jit(solution)/shard_map/ppermute | solution.py:92
  60.3 5.6 %collective-permute-start.10 = (f32[256,640]{1,0:T(8,128)}, f32[256,640]{1,0:T(8,128)S(1)}, u32[]{:S(2)}, u32[]{:S(2)}) collective-permute-start(f32[256,640]{1,0:T(8,128)} %slice.101), channel_id=1, source_target_pairs={{4,6},{5,7},{6,4},{7,5}} | collective-permute-start | bytes 1966088 | tf_op jit(solution)/shard_map/ppermute | solution.py:92
  61.0 3.8 %collective-permute-start.11 = (f32[256,256]{1,0:T(8,128)}, f32[256,256]{1,0:T(8,128)S(1)}, u32[]{:S(2)}, u32[]{:S(2)}) collective-permute-start(f32[256,256]{1,0:T(8,128)} %select_select_fusion.1), channel_id=1, source_target_pairs={{0,4},{1,5},{2,6},{3,7},{8,12},{9,13},{10,14},{11,15},{16,20},{17,... | collective-permute-start | bytes 786440 | tf_op jit(solution)/shard_map/ppermute | solution.py:98
  63.3 2.4 %collective-permute-start.16 = (f32[256,256]{1,0:T(8,128)S(1)}, f32[256,256]{1,0:T(8,128)S(1)}, u32[]{:S(2)}, u32[]{:S(2)}) collective-permute-start(f32[256,256]{1,0:T(8,128)S(1)} %select_select_fusion), channel_id=1, source_target_pairs={{0,4},{1,5},{2,6},{3,7},{8,12},{9,13},{10,14},{11,15},{16,20},{17,... | collective-permute-start | bytes 786440 | tf_op jit(solution)/shard_map/ppermute | solution.py:98
  64.7 1.0 %copy-start.3 = (f32[256,256]{1,0:T(8,128)S(1)}, f32[256,256]{1,0:T(8,128)}, u32[]{:S(2)}) copy-start(f32[256,256]{1,0:T(8,128)} %select_select_fusion.1) | copy-start | bytes 786436
  66.3 14.2 %collective-permute-start.17 = (f32[256,128]{1,0:T(8,128)S(1)}, f32[256,128]{1,0:T(8,128)S(1)}, u32[]{:S(2)}, u32[]{:S(2)}) collective-permute-start(f32[256,128]{1,0:T(8,128)S(1)} %get-tuple-element.58), channel_id=1, source_target_pairs={{4,5},{5,4},{6,7},{7,6},{8,9},{9,8},{10,11},{11,10},{12,13},{13,12... | collective-permute-start | bytes 393224 | tf_op jit(solution)/shard_map/ppermute | solution.py:92
  71.7 8.8 %collective-permute-start.18 = (f32[128,128]{1,0:T(8,128)S(1)}, f32[128,128]{1,0:T(8,128)S(1)}, u32[]{:S(2)}, u32[]{:S(2)}) collective-permute-start(f32[128,128]{1,0:T(8,128)S(1)} %get-tuple-element.65), channel_id=1, source_target_pairs={{4,5},{5,4},{6,7},{7,6},{8,9},{9,8},{10,11},{11,10},{12,13},{13,12... | collective-permute-start | bytes 196616 | tf_op jit(solution)/shard_map/ppermute | solution.py:92
  74.0 7.4 %collective-permute-start.19 = (f32[256,128]{1,0:T(8,128)S(1)}, f32[256,128]{1,0:T(8,128)S(1)}, u32[]{:S(2)}, u32[]{:S(2)}) collective-permute-start(f32[256,128]{1,0:T(8,128)S(1)} %get-tuple-element.72), channel_id=1, source_target_pairs={{4,5},{5,4},{6,7},{7,6},{8,9},{9,8},{10,11},{11,10},{12,13},{13,12... | collective-permute-start | bytes 393224 | tf_op jit(solution)/shard_map/ppermute | solution.py:92
  78.5 8.2 %collective-permute-start.21 = (f32[384,128]{1,0:T(8,128)S(1)}, f32[384,128]{1,0:T(8,128)S(1)}, u32[]{:S(2)}, u32[]{:S(2)}) collective-permute-start(f32[384,128]{1,0:T(8,128)S(1)} %get-tuple-element.78), channel_id=1, source_target_pairs={{4,5},{5,4},{6,7},{7,6},{8,9},{9,8},{10,11},{11,10},{12,13},{13,12... | collective-permute-start | bytes 589832 | tf_op jit(solution)/shard_map/ppermute | solution.py:92

commit v5 on v4

--- a/solution.py
+++ b/solution.py
@@ -7,7 +7,7 @@
 from jax.sharding import PartitionSpec as P
 
 AXES = ("rows", "cols")
-EIGHTHS = (0, 2, 3, 5, 8)
+EIGHTHS = (0, 4, 5, 8)
 PARAMS = pltpu.CompilerParams(vmem_limit_bytes=24 * 1024 * 1024)
 
 
@@ -47,7 +47,7 @@
     inverse = jnp.concatenate([lead[:, :width], lead_other[:, :width]], axis=0)
     first = dot(inverse, blocks, 1)
     solved[...] = first
-    corner = jnp.concatenate([lead[:, width:], lead_other[:, width:]], axis=0)
+    corner = jnp.concatenate([lead[:, width : 2 * width], lead_other[:, width : 2 * width]], axis=0)
     total = dot(corner, first, 0)
     pieces = [total[:, at * cands : (at + 1) * cands] for at in range(len(places))]
     pieces[0] = pieces[0] - low[...]
@@ -56,17 +56,17 @@
         shuffled[:, at * cands : (at + 1) * cands] = pieces[place]
 
 
-def second_kernel(inverse, inverse_other, update, got, solved):
-    both = jnp.concatenate([inverse[...], inverse_other[...]], axis=0)
+def second_kernel(start, lead, lead_other, update, got, solved):
+    both = jnp.concatenate([lead[:, start:], lead_other[:, start:]], axis=0)
     solved[...] = dot(both, -(update[...] + got[...]), 1)
 
 
-def chunk_kernel(part, mine, other, late, first, second, base, beside, own, send):
+def chunk_kernel(mine, others, late, first, second, base, beside, own, send):
     cands = base.shape[1]
     depth = first.shape[0] // 2
-    other = other[...]
+    other = jnp.concatenate([piece[...] for piece in others], axis=1)
     if late is not None:
-        other = jnp.where(beside[0] == 1, late[:, part], other)
+        other = jnp.where(beside[0] == 1, late[...], other)
     factors = jnp.concatenate([mine[...], other], axis=0)
     solved = jnp.concatenate(
         [first[:depth], second[:depth], first[depth:], second[depth:]], axis=0
@@ -76,8 +76,12 @@
     send[...] = partial[:, cands:]
 
 
-def chunk_kernel_plain(part, mine, other, first, second, base, beside, own, send):
-    chunk_kernel(part, mine, other, None, first, second, base, beside, own, send)
+def early_kernel(mine, one, two, late, *refs):
+    chunk_kernel(mine, [one, two], late, *refs)
+
+
+def late_kernel(mine, one, *refs):
+    chunk_kernel(mine, [one], None, *refs)
 
 
 def make_on_device(n_rows, n_cols):
@@ -97,27 +101,24 @@
         ]
         return lax.ppermute(array, AXES, pairs)
 
-    def spread(array, row_id, stages, have):
-        for low, radix in stages:
-            digit = (row_id // low) % radix
-            result = array
-            for step in range(radix - 1, 0, -1):
-                result = jnp.where(digit == step, send_down(array, step * low, have), result)
-            array = result
-            have = [row + step * low for row in have for step in range(radix)]
+    def spread(array, row_id, low, radix, have):
+        digit = (row_id // low) % radix
+        result = array
+        for step in range(radix - 1, 0, -1):
+            result = jnp.where(digit == step, send_down(array, step * low, have), result)
+        return result, [row + step * low for row in have for step in range(radix)]
+
+    def broadcast_outer(array, row_id):
+        low = n_rows
+        have = [0]
+        while low > 2:
+            radix = min(4, low // 2)
+            low //= radix
+            array, have = spread(array, row_id, low, radix, have)
         return array
 
-    def broadcast_outer(array, row_id):
-        stages = []
-        low = 2
-        while low < n_rows:
-            radix = min(4, n_rows // low)
-            stages.append((low, radix))
-            low *= radix
-        return spread(array, row_id, stages[::-1], [0])
-
-    def broadcast_inner(array, row_id):
-        return spread(array, row_id, [(1, 2)], range(0, n_rows, 2))
+    def broadcast_inner(array, row_id, start=0):
+        return jnp.where(row_id % 2 == 1, send_down(array, 1, range(start, n_rows, 2)), array)
 
     def block(array, place, cands):
         return array[:, place * cands : (place + 1) * cands]
@@ -150,16 +151,19 @@
         beside = range(1, min(2, n_rows))
         below = range(2, n_rows)
         flat = factor_panels.reshape(2 * depth, n_design)
-        mine = [flat[:, part] for part in parts]
 
         lead = jnp.concatenate(
-            [block_inverses[0], factor_panels[0, :, width : 2 * width]], axis=1
+            [block_inverses[0], factor_panels[0, :, width : 2 * width], block_inverses[1]], axis=1
         )
         lead, rhs = lax.optimization_barrier((lead, cross_kernel[:width]))
         lead_other = swap(lead, half, top)
         rhs_others = [swap(rhs, step, top) for step in range(1, half)]
-        arrived = [swap(piece, half, below) for piece in mine[:-1]]
-        arrived.append(swap(mine[-1], half, range(1, n_rows)))
+        mine = [flat[:, part] for part in parts]
+        arrived = [swap(mine[0], half, below)]
+        lead_other, mine_early, mine[1], mine[2] = lax.optimization_barrier(
+            (lead_other, flat[:, early], mine[1], mine[2])
+        )
+        arrived.append(swap(mine[1], half, below))
 
         first, update, shuffled = call(
             functools.partial(first_kernel, [at ^ 1 for at in range(half)], width),
@@ -172,9 +176,6 @@
             *rhs_others,
             cross_kernel[width : 2 * width],
         )
-        first, inverse, late = lax.optimization_barrier((first, block_inverses[1], flat[:, early]))
-        late = swap(late, half, beside)
-        inverse_other = swap(inverse, half, top)
         shuffled, arrived[0] = lax.optimization_barrier((shuffled, arrived[0]))
         got = swap(shuffled, 1, top)
         bit = 2
@@ -182,21 +183,33 @@
             update = update + got
             got = swap(shuffle(update, bit, cands), bit, top)
             bit *= 2
+        first_beside = first
+        late = mine_early
+        if n_rows > 1:
+            first_beside = send_down(first, 1, top)
+            first_beside, late = lax.optimization_barrier((first_beside, late))
+        late = swap(late, half, beside)
         first_half = broadcast_outer(first, row_id)
-        got, first_half, arrived[1] = lax.optimization_barrier((got, first_half, arrived[1]))
+        got, first_half = lax.optimization_barrier((got, first_half))
         (second,) = call(
-            second_kernel,
+            functools.partial(second_kernel, 2 * width),
             [(2 * depth, half * cands)],
             4,
             6 * 2 * depth * width * half * cands,
-            inverse,
-            inverse_other,
+            lead,
+            lead_other,
             update,
             got,
         )
         second_half = broadcast_outer(second, row_id)
-        second_half, arrived[2] = lax.optimization_barrier((second_half, arrived[2]))
-        solved = [broadcast_inner(first_half, row_id), broadcast_inner(second_half, row_id)]
+        second_half, second, arrived[1], late = lax.optimization_barrier(
+            (second_half, second, arrived[1], late)
+        )
+        first_full = jnp.where(
+            row_id == 1, first_beside, broadcast_inner(first_half, row_id, 2)
+        )
+        solved = [first_full, broadcast_inner(second_half, row_id)]
+        arrived.append(swap(mine[2], half, range(1, n_rows)))
 
         pair = jnp.concatenate([first, second], axis=0)
         others = [block(pair, 0, cands)]
@@ -211,13 +224,15 @@
 
         is_beside = (row_id == 1).astype(jnp.int32).reshape(1)
         fresh = []
-        for at, part in enumerate(parts):
-            last = at == len(parts) - 1
-            args = [mine[at], arrived[at]] + ([] if last else [late])
-            args += [*solved, cross_kernel[part]]
+        work = [
+            (early, early_kernel, [mine_early, arrived[0], arrived[1], late]),
+            (parts[2], late_kernel, [mine[2], arrived[2]]),
+        ]
+        for part, kernel, args in work:
+            args = args + [*solved, cross_kernel[part]]
             count = part.stop - part.start
             own, send = call(
-                functools.partial(chunk_kernel_plain if last else chunk_kernel, part),
+                kernel,
                 [(count, cands), (count, (half - 1) * cands)],
                 len(args),
                 6 * count * 4 * depth * half * cands,

time: 88.2 us -> 92.6 us (1.050)
  waiting for transfers between devices: 32.7 us -> 44.5 us
  starting transfers between devices: 40.6 us -> 33 us
  Pallas kernels: 4 us -> 5.69 us
  other arithmetic: 3.7 us -> 2.31 us
    ppermute x14 -> x10, waiting for transfers between devices: 19.2 us -> 40.1 us  [swap(): return lax.ppermute(array, AXES, pairs)]
    ppermute x8 -> x9, waiting for transfers between devices: 13.5 us -> 4.42 us  [send_down(): return lax.ppermute(array, AXES, pairs)]
    ppermute x14 -> x10, starting transfers between devices: 30.5 us -> 22.4 us  [swap(): return lax.ppermute(array, AXES, pairs)]
    slice x3 -> x2, local copies, waits for them, and re-layouts: 0.04 us -> 1.94 us  [on_device(): args = args + [*solved, cross_kernel[part]]]
    slice x3, local copies, waits for them, and re-layouts: 1.98 us -> 0.09 us  [on_device(): mine = [flat[:, part] for part in parts]]
    pallas_call x6 -> x4, Pallas kernels: 4 us -> 5.69 us  [call(): pl.pallas_call(kernel, out_shape=[jax.ShapeDtypeStruct(shape, jnp.float32...]
    select_n x4 -> x2, other arithmetic: 1.89 us -> 1.1 us  [spread(): jnp.where(digit == step, send_down(array, step * low, have), result)]
    unnamed x10 -> x20, local copies, waits for them, and re-layouts: 1.88 us -> 2.62 us
  transfers between devices with their start and end apart: 22 -> 19, of which waited for: 6 -> 6; matrix products, arithmetic and copies ran while one was open for 7% -> 4% of each run, Pallas kernels for 5% -> 6%
where the time goes in v5:
time: 92.6 us; the launch traced here: 91.9 us
  waiting for transfers between devices  44.5 us (48%)
  starting transfers between devices  33 us (36%)
  local copies, waits for them, and re-layouts  5.94 us (6%)
  Pallas kernels  5.69 us (6%)
  other arithmetic  2.31 us (2%)
    ppermute x10, waiting for transfers between devices, swap(): return lax.ppermute(array, AXES, pairs)  40.1 us
    ppermute x10, starting transfers between devices, swap(): return lax.ppermute(array, AXES, pairs)  22.4 us
    ppermute x9, starting transfers between devices, send_down(): return lax.ppermute(array, AXES, pairs)  10.6 us
    pallas_call x4, Pallas kernels, call(): pl.pallas_call(kernel, out_shape=[jax.ShapeDtypeStruct(shape, jnp.float32...  5.69 us
    ppermute x9, waiting for transfers between devices, send_down(): return lax.ppermute(array, AXES, pairs)  4.42 us
    unnamed x20, local copies, waits for them, and re-layouts  2.62 us
    slice x2, local copies, waits for them, and re-layouts, on_device(): args = args + [*solved, cross_kernel[part]]  1.94 us
  transfers between devices with their start and end apart: 19, of which 6 were waited for; matrix products, arithmetic and copies ran while one was open for 4% of the time, Pallas kernels for 6%

profile of v5, /device:TPU:2, one launch (start us, length us, event | category | flops | bytes accessed | tf_op | source)
XLA Modules:
  0.0 91.9 jit_solution(5133974978918823052)
XLA Ops:
  0.0 1.2 %slice_bitcast_fusion.2 = (f32[128,512]{1,0:T(8,128)S(1)}, f32[128,512]{1,0:T(8,128)S(1)}) fusion(f32[2,128,512]{2,1,0:T(8,128)} %param.5), kind=kLoop, calls=%fused_computation.8 | loop fusion | bytes 1048576 | tf_op jit(solution)/shard_map/squeeze | solution.py:156
  1.2 0.2 copy-done.4
  1.4 0.1 copy-done.5
  1.6 0.1 pad_maximum_fusion.lead
  1.6 0.7 collective-permute-start
  2.4 4.5 %collective-permute-start.2 = (f32[256,512]{1,0:T(8,128)S(1)}, f32[256,512]{1,0:T(8,128)S(1)}, u32[]{:S(2)}, u32[]{:S(2)}) collective-permute-start(f32[256,512]{1,0:T(8,128)S(1)} %slice.92), channel_id=1, source_target_pairs={{8,10},{9,11},{10,8},{11,9},{12,14},{13,15},{14,12},{15,13},{16,18... | collective-permute-start | bytes 1572872 | tf_op jit(solution)/shard_map/ppermute | solution.py:96
  6.9 0.7 collective-permute-start.1
  7.6 0.1 slice.89.mine
  7.7 0.0 collective-permute-done.1.refs_0_
  7.7 1.9 %shard_map.37 = (f32[256,256]{1,0:T(8,128)S(1)}, f32[512,256]{1,0:T(8,128)S(1)}, f32[512,256]{1,0:T(8,128)}) custom-call(f32[128,1536]{1,0:T(8,128)S(1)} %pad_maximum_fusion.lead, f32[128,1536]{1,0:T(8,128)S(1)} %collective-permute-done.lead_other, f32[512,128]{1,0:T(8,128)S(1)} %get-tuple-element.36.rhs, f32[512,128]{1,0:T(8,128)S(1)} %collective-permute-done.1.refs_0_, ...), custom_call_target="tpu_custom_call" | custom-call | flops 402653184 | tf_op jit(solution)/shard_map/pallas_call | solution.py:31
  9.6 0.8 copy-done.2
  10.4 19.7 %collective-permute-done.2.one = f32[256,512]{1,0:T(8,128)S(1)} collective-permute-done((f32[256,512]{1,0:T(8,128)S(1)}, f32[256,512]{1,0:T(8,128)S(1)}, u32[]{:S(2)}, u32[]{:S(2)}) %collective-permute-start.2) | collective-permute-done | bytes 524320 | tf_op jit(solution)/shard_map/ppermute | solution.py:96
  30.1 0.8 copy-done
  30.9 1.5 %collective-permute-start.3 = (f32[512,256]{1,0:T(8,128)}, f32[512,256]{1,0:T(8,128)}, u32[]{:S(2)}, u32[]{:S(2)}) collective-permute-start(f32[512,256]{1,0:T(8,128)} %get-tuple-element.40), channel_id=1, source_target_pairs={{0,1},{1,0},{2,3},{3,2}} | collective-permute-start | bytes 1572872 | tf_op jit(solution)/shard_map/ppermute | solution.py:96
  32.4 0.7 collective-permute-start.11
  33.0 1.3 %collective-permute-start.4 = (f32[256,256]{1,0:T(8,128)S(1)}, f32[256,256]{1,0:T(8,128)S(1)}, u32[]{:S(2)}, u32[]{:S(2)}) collective-permute-start(f32[256,256]{1,0:T(8,128)S(1)} %get-tuple-element.37), channel_id=1, source_target_pairs={{0,8},{1,9},{2,10},{3,11}} | collective-permute-start | bytes 786440 | tf_op jit(solution)/shard_map/ppermute | solution.py:102
  34.3 1.4 %collective-permute-start.5 = (f32[256,256]{1,0:T(8,128)S(1)}, f32[256,256]{1,0:T(8,128)}, u32[]{:S(2)}, u32[]{:S(2)}) collective-permute-start(f32[256,256]{1,0:T(8,128)S(1)} %get-tuple-element.37), channel_id=1, source_target_pairs={{0,16},{1,17},{2,18},{3,19}} | collective-permute-start | bytes 786440 | tf_op jit(solution)/shard_map/ppermute | solution.py:102
  35.7 1.4 %collective-permute-start.6 = (f32[256,256]{1,0:T(8,128)S(1)}, f32[256,256]{1,0:T(8,128)}, u32[]{:S(2)}, u32[]{:S(2)}) collective-permute-start(f32[256,256]{1,0:T(8,128)S(1)} %get-tuple-element.37), channel_id=1, source_target_pairs={{0,24},{1,25},{2,26},{3,27}} | collective-permute-start | bytes 786440 | tf_op jit(solution)/shard_map/ppermute | solution.py:102
  37.1 0.0 collective-permute-done.11
  37.1 1.6 %collective-permute-start.12 = (f32[256,640]{1,0:T(8,128)S(1)}, f32[256,640]{1,0:T(8,128)}, u32[]{:S(2)}, u32[]{:S(2)}) collective-permute-start(f32[256,640]{1,0:T(8,128)S(1)} %slice.89.mine), channel_id=1, source_target_pairs={{4,6},{5,7},{6,4},{7,5}} | collective-permute-start | bytes 1966088 | tf_op jit(solution)/shard_map/ppermute | solution.py:96
  38.7 2.6 %collective-permute-done.4 = f32[256,256]{1,0:T(8,128)S(1)} collective-permute-done((f32[256,256]{1,0:T(8,128)S(1)}, f32[256,256]{1,0:T(8,128)S(1)}, u32[]{:S(2)}, u32[]{:S(2)}) %collective-permute-start.4) | collective-permute-done | bytes 262176 | tf_op jit(solution)/shard_map/ppermute | solution.py:102
  41.3 0.0 collective-permute-done.5
  41.3 0.7 copy-done.8
  42.0 0.0 collective-permute-done.6
  42.0 1.0 %select_select_fusion.2 = f32[256,256]{1,0:T(8,128)S(1)} fusion(f32[256,256]{1,0:T(8,128)} %copy-done.8, f32[256,256]{1,0:T(8,128)} %collective-permute-done.5, f32[256,256]{1,0:T(8,128)} %collective-permute-done.6, f32[256,256]{1,0:T(8,128)S(1)} %get-tuple-element.37, pred[]{:T(512)S(6)} %eq.31, pred[]{:T(512)S(6)} %eq.30, pred[]{:T(512)S(6)} %eq.29), kind=kLoop, calls=%fused_computation.5 | loop fusion | flops 196608 | bytes 1310723 | tf_op jit(solution)/shard_map/jit(_where)/select_n | solution.py:108
  43.0 1.5 %shard_map.38 = f32[256,256]{1,0:T(8,128)S(1)} custom-call(f32[128,1536]{1,0:T(8,128)S(1)} %pad_maximum_fusion.lead, f32[128,1536]{1,0:T(8,128)S(1)} %collective-permute-done.lead_other, f32[512,256]{1,0:T(8,128)S(1)} %copy-done.3, f32[512,256]{1,0:T(8,128)} %collective-permute-done.3.got), custom_call_target="tpu_custom_call" | custom-call | flops 201326592 | tf_op jit(solution)/shard_map/pallas_call | solution.py:31
  44.5 1.3 %collective-permute-start.7 = (f32[256,256]{1,0:T(8,128)S(1)}, f32[256,256]{1,0:T(8,128)S(1)}, u32[]{:S(2)}, u32[]{:S(2)}) collective-permute-start(f32[256,256]{1,0:T(8,128)S(1)} %shard_map.38), channel_id=1, source_target_pairs={{0,8},{1,9},{2,10},{3,11}} | collective-permute-start | bytes 786440 | tf_op jit(solution)/shard_map/ppermute | solution.py:102
  45.8 0.7 collective-permute-start.8
  46.5 1.4 %collective-permute-start.9 = (f32[256,256]{1,0:T(8,128)S(1)}, f32[256,256]{1,0:T(8,128)}, u32[]{:S(2)}, u32[]{:S(2)}) collective-permute-start(f32[256,256]{1,0:T(8,128)S(1)} %shard_map.38), channel_id=1, source_target_pairs={{0,24},{1,25},{2,26},{3,27}} | collective-permute-start | bytes 786440 | tf_op jit(solution)/shard_map/ppermute | solution.py:102
  47.9 1.3 %collective-permute-start.14 = (f32[256,256]{1,0:T(8,128)S(1)}, f32[256,256]{1,0:T(8,128)S(1)}, u32[]{:S(2)}, u32[]{:S(2)}) collective-permute-start(f32[256,256]{1,0:T(8,128)S(1)} %select_select_fusion.2), channel_id=1, source_target_pairs={{8,12},{9,13},{10,14},{11,15},{16,20},{17,21},{18,22},{19,23},{24,... | collective-permute-start | bytes 786440 | tf_op jit(solution)/shard_map/ppermute | solution.py:102
  49.2 1.0 %slice.87.refs_2_ = f32[640,128]{1,0:T(8,128)S(1)} slice(f32[1024,128]{1,0:T(8,128)} %param.3), slice={[0:640], [0:128]} | slice | bytes 655360 | tf_op jit(solution)/shard_map/slice | solution.py:232
  50.2 0.9 %slice.88.refs_2_ = f32[384,128]{1,0:T(8,128)S(1)} slice(f32[1024,128]{1,0:T(8,128)} %param.3), slice={[640:1024], [0:128]} | slice | bytes 393216 | tf_op jit(solution)/shard_map/slice | solution.py:232
  51.2 1.6 %collective-permute-done.7 = f32[256,256]{1,0:T(8,128)S(1)} collective-permute-done((f32[256,256]{1,0:T(8,128)S(1)}, f32[256,256]{1,0:T(8,128)S(1)}, u32[]{:S(2)}, u32[]{:S(2)}) %collective-permute-start.7) | collective-permute-done | bytes 262176 | tf_op jit(solution)/shard_map/ppermute | solution.py:102
  52.8 2.3 %collective-permute-start.10 = (f32[256,128]{1,0:T(8,128)S(1)}, f32[256,128]{1,0:T(8,128)S(1)}, u32[]{:S(2)}, u32[]{:S(2)}) collective-permute-start(f32[256,128]{1,0:T(8,128)S(1)} %slice.90), channel_id=1, source_target_pairs={{8,10},{9,11},{10,8},{11,9},{12,14},{13,15},{14,12},{15,13},{16,18... | collective-permute-start | bytes 393224 | tf_op jit(solution)/shard_map/ppermute | solution.py:96
  55.1 0.0 copy-start.9
  55.2 4.4 %collective-permute-start.17 = (f32[256,384]{1,0:T(8,128)S(1)}, f32[256,384]{1,0:T(8,128)S(1)}, u32[]{:S(2)}, u32[]{:S(2)}) collective-permute-start(f32[256,384]{1,0:T(8,128)S(1)} %slice.91.mine), channel_id=1, source_target_pairs={{4,6},{5,7},{6,4},{7,5},{8,10},{9,11},{10,8},{11,9},{12,14},{13,15... | collective-permute-start | bytes 1179656 | tf_op jit(solution)/shard_map/ppermute | solution.py:96
  59.6 0.1 select_select_fusion.1
  59.7 10.9 %collective-permute-done.10.two = f32[256,128]{1,0:T(8,128)S(1)} collective-permute-done((f32[256,128]{1,0:T(8,128)S(1)}, f32[256,128]{1,0:T(8,128)S(1)}, u32[]{:S(2)}, u32[]{:S(2)}) %collective-permute-start.10) | collective-permute-done | bytes 131104 | tf_op jit(solution)/shard_map/ppermute | solution.py:96
  70.6 1.3 %collective-permute-start.15 = (f32[256,256]{1,0:T(8,128)S(1)}, f32[256,256]{1,0:T(8,128)S(1)}, u32[]{:S(2)}, u32[]{:S(2)}) collective-permute-start(f32[256,256]{1,0:T(8,128)S(1)} %select_select_fusion.1), channel_id=1, source_target_pairs={{0,4},{1,5},{2,6},{3,7},{8,12},{9,13},{10,14},{11,15},{16,20},{17,... | collective-permute-start | bytes 786440 | tf_op jit(solution)/shard_map/ppermute | solution.py:102
  71.9 0.1 select_select_fusion.refs_0_
  72.0 0.8 collective-permute-start.13
  72.8 0.2 collective-permute-done.15
  73.1 1.8 %shard_map.39 = (f32[640,128]{1,0:T(8,128)S(1)}, f32[640,128]{1,0:T(8,128)S(1)}) custom-call(f32[256,640]{1,0:T(8,128)S(1)} %slice.89.mine, f32[256,512]{1,0:T(8,128)S(1)} %copy-done.1, f32[256,128]{1,0:T(8,128)S(1)} %collective-permute-done.10.two, f32[256,640]{1,0:T(8,128)} %collective-permute-done.12.late, f32[256,256]{1,0:T(8,128)S(1)} %select_select_fusion.refs_0_, ...), custom_call_target="tpu_custom_call" | custom-call | flops 503316480 | tf_op jit(solution)/shard_map/pallas_call | solution.py:31
  74.9 1.9 %collective-permute-start.16 = (f32[640,128]{1,0:T(8,128)S(1)}, f32[640,128]{1,0:T(8,128)S(1)}, u32[]{:S(2)}, u32[]{:S(2)}) collective-permute-start(f32[640,128]{1,0:T(8,128)S(1)} %get-tuple-element.55), channel_id=1, source_target_pairs={{4,5},{5,4},{6,7},{7,6},{8,9},{9,8},{10,11},{11,10},{12,13},{13,12... | collective-permute-start | bytes 983048 | tf_op jit(solution)/shard_map/ppermute | solution.py:96
  76.8 0.5 shard_map.40
  77.4 3.9 %collective-permute-start.18 = (f32[384,128]{1,0:T(8,128)S(1)}, f32[384,128]{1,0:T(8,128)S(1)}, u32[]{:S(2)}, u32[]{:S(2)}) collective-permute-start(f32[384,128]{1,0:T(8,128)S(1)} %get-tuple-element.62), channel_id=1, source_target_pairs={{4,5},{5,4},{6,7},{7,6},{8,9},{9,8},{10,11},{11,10},{12,13},{13,12... | collective-permute-start | bytes 589832 | tf_op jit(solution)/shard_map/ppermute | solution.py:96
  81.5 9.5 %collective-permute-done.18 = f32[384,128]{1,0:T(8,128)S(1)} collective-permute-done((f32[384,128]{1,0:T(8,128)S(1)}, f32[384,128]{1,0:T(8,128)S(1)}, u32[]{:S(2)}, u32[]{:S(2)}) %collective-permute-start.18) | collective-permute-done | bytes 196640 | tf_op jit(solution)/shard_map/ppermute | solution.py:96
  91.1 0.9 maximum_select_fusion
  (40 shorter events, 0.4 us)
Async XLA Ops:
  0.0 1.4 %copy-start.4 = (f32[2,128,1024]{2,1,0:T(8,128)S(1)}, f32[2,128,1024]{2,1,0:T(8,128)}, u32[]{:S(2)}) copy-start(f32[2,128,1024]{2,1,0:T(8,128)} %param.4) | copy-start | bytes 3145732
  0.0 1.5 %copy-start.5 = (f32[1024,128]{1,0:T(8,128)S(1)}, f32[1024,128]{1,0:T(8,128)}, u32[]{:S(2)}) copy-start(f32[1024,128]{1,0:T(8,128)} %param.3) | copy-start | bytes 1572868
  1.6 6.1 %collective-permute-start = (f32[128,1536]{1,0:T(8,128)S(1)}, f32[128,1536]{1,0:T(8,128)S(1)}, u32[]{:S(2)}, u32[]{:S(2)}) collective-permute-start(f32[128,1536]{1,0:T(8,128)S(1)} %pad_maximum_fusion.lead), channel_id=1, source_target_pairs={{0,2},{1,3},{2,0},{3,1}} | collective-permute-start | bytes 2359304 | tf_op jit(solution)/shard_map/ppermute | solution.py:96
  2.4 27.7 %collective-permute-start.2 = (f32[256,512]{1,0:T(8,128)S(1)}, f32[256,512]{1,0:T(8,128)S(1)}, u32[]{:S(2)}, u32[]{:S(2)}) collective-permute-start(f32[256,512]{1,0:T(8,128)S(1)} %slice.92), channel_id=1, source_target_pairs={{8,10},{9,11},{10,8},{11,9},{12,14},{13,15},{14,12},{15,13},{16,18... | collective-permute-start | bytes 1572872 | tf_op jit(solution)/shard_map/ppermute | solution.py:96
  6.9 0.8 collective-permute-start.1
  9.6 0.8 copy-start.2
  30.1 0.8 copy-start
  30.9 12.1 %collective-permute-start.3 = (f32[512,256]{1,0:T(8,128)}, f32[512,256]{1,0:T(8,128)}, u32[]{:S(2)}, u32[]{:S(2)}) collective-permute-start(f32[512,256]{1,0:T(8,128)} %get-tuple-element.40), channel_id=1, source_target_pairs={{0,1},{1,0},{2,3},{3,2}} | collective-permute-start | bytes 1572872 | tf_op jit(solution)/shard_map/ppermute | solution.py:96
  32.4 4.7 %collective-permute-start.11 = (f32[256,256]{1,0:T(8,128)S(1)}, f32[256,256]{1,0:T(8,128)S(1)}, u32[]{:S(2)}, u32[]{:S(2)}) collective-permute-start(f32[256,256]{1,0:T(8,128)S(1)} %get-tuple-element.37), channel_id=1, source_target_pairs={{0,4},{1,5},{2,6},{3,7}} | collective-permute-start | bytes 786440 | tf_op jit(solution)/shard_map/ppermute | solution.py:102
  33.0 8.3 %collective-permute-start.4 = (f32[256,256]{1,0:T(8,128)S(1)}, f32[256,256]{1,0:T(8,128)S(1)}, u32[]{:S(2)}, u32[]{:S(2)}) collective-permute-start(f32[256,256]{1,0:T(8,128)S(1)} %get-tuple-element.37), channel_id=1, source_target_pairs={{0,8},{1,9},{2,10},{3,11}} | collective-permute-start | bytes 786440 | tf_op jit(solution)/shard_map/ppermute | solution.py:102
  34.3 7.0 %collective-permute-start.5 = (f32[256,256]{1,0:T(8,128)S(1)}, f32[256,256]{1,0:T(8,128)}, u32[]{:S(2)}, u32[]{:S(2)}) collective-permute-start(f32[256,256]{1,0:T(8,128)S(1)} %get-tuple-element.37), channel_id=1, source_target_pairs={{0,16},{1,17},{2,18},{3,19}} | collective-permute-start | bytes 786440 | tf_op jit(solution)/shard_map/ppermute | solution.py:102
  35.7 6.3 %collective-permute-start.6 = (f32[256,256]{1,0:T(8,128)S(1)}, f32[256,256]{1,0:T(8,128)}, u32[]{:S(2)}, u32[]{:S(2)}) collective-permute-start(f32[256,256]{1,0:T(8,128)S(1)} %get-tuple-element.37), channel_id=1, source_target_pairs={{0,24},{1,25},{2,26},{3,27}} | collective-permute-start | bytes 786440 | tf_op jit(solution)/shard_map/ppermute | solution.py:102
  37.1 6.0 %copy-start.3 = (f32[512,256]{1,0:T(8,128)S(1)}, f32[512,256]{1,0:T(8,128)}, u32[]{:S(2)}) copy-start(f32[512,256]{1,0:T(8,128)} %copy-done.2) | copy-start | bytes 1572868
  37.1 5.9 %copy-start.6 = (f32[256,256]{1,0:T(8,128)}, f32[256,256]{1,0:T(8,128)S(1)}, u32[]{:S(2)}) copy-start(f32[256,256]{1,0:T(8,128)S(1)} %collective-permute-done.11) | copy-start | bytes 786436
  37.1 33.5 %collective-permute-start.12 = (f32[256,640]{1,0:T(8,128)S(1)}, f32[256,640]{1,0:T(8,128)}, u32[]{:S(2)}, u32[]{:S(2)}) collective-permute-start(f32[256,640]{1,0:T(8,128)S(1)} %slice.89.mine), channel_id=1, source_target_pairs={{4,6},{5,7},{6,4},{7,5}} | collective-permute-start | bytes 1966088 | tf_op jit(solution)/shard_map/ppermute | solution.py:96
  41.3 0.7 copy-start.8
  44.5 8.3 %collective-permute-start.7 = (f32[256,256]{1,0:T(8,128)S(1)}, f32[256,256]{1,0:T(8,128)S(1)}, u32[]{:S(2)}, u32[]{:S(2)}) collective-permute-start(f32[256,256]{1,0:T(8,128)S(1)} %shard_map.38), channel_id=1, source_target_pairs={{0,8},{1,9},{2,10},{3,11}} | collective-permute-start | bytes 786440 | tf_op jit(solution)/shard_map/ppermute | solution.py:102
  45.8 9.3 %collective-permute-start.8 = (f32[256,256]{1,0:T(8,128)S(1)}, f32[256,256]{1,0:T(8,128)S(1)}, u32[]{:S(2)}, u32[]{:S(2)}) collective-permute-start(f32[256,256]{1,0:T(8,128)S(1)} %shard_map.38), channel_id=1, source_target_pairs={{0,16},{1,17},{2,18},{3,19}} | collective-permute-start | bytes 786440 | tf_op jit(solution)/shard_map/ppermute | solution.py:102
  46.5 13.1 %collective-permute-start.9 = (f32[256,256]{1,0:T(8,128)S(1)}, f32[256,256]{1,0:T(8,128)}, u32[]{:S(2)}, u32[]{:S(2)}) collective-permute-start(f32[256,256]{1,0:T(8,128)S(1)} %shard_map.38), channel_id=1, source_target_pairs={{0,24},{1,25},{2,26},{3,27}} | collective-permute-start | bytes 786440 | tf_op jit(solution)/shard_map/ppermute | solution.py:102
  47.9 24.0 %collective-permute-start.14 = (f32[256,256]{1,0:T(8,128)S(1)}, f32[256,256]{1,0:T(8,128)S(1)}, u32[]{:S(2)}, u32[]{:S(2)}) collective-permute-start(f32[256,256]{1,0:T(8,128)S(1)} %select_select_fusion.2), channel_id=1, source_target_pairs={{8,12},{9,13},{10,14},{11,15},{16,20},{17,21},{18,22},{19,23},{24,... | collective-permute-start | bytes 786440 | tf_op jit(solution)/shard_map/ppermute | solution.py:102
  51.1 20.8 %copy-start.7 = (f32[256,256]{1,0:T(8,128)S(1)}, f32[256,256]{1,0:T(8,128)}, u32[]{:S(2)}) copy-start(f32[256,256]{1,0:T(8,128)} %copy-done.6) | copy-start | bytes 786436
  52.8 17.8 %collective-permute-start.10 = (f32[256,128]{1,0:T(8,128)S(1)}, f32[256,128]{1,0:T(8,128)S(1)}, u32[]{:S(2)}, u32[]{:S(2)}) collective-permute-start(f32[256,128]{1,0:T(8,128)S(1)} %slice.90), channel_id=1, source_target_pairs={{8,10},{9,11},{10,8},{11,9},{12,14},{13,15},{14,12},{15,13},{16,18... | collective-permute-start | bytes 393224 | tf_op jit(solution)/shard_map/ppermute | solution.py:96
  55.1 4.4 %copy-start.9 = (f32[256,256]{1,0:T(8,128)}, f32[256,256]{1,0:T(8,128)S(1)}, u32[]{:S(2)}) copy-start(f32[256,256]{1,0:T(8,128)S(1)} %collective-permute-done.8) | copy-start | bytes 786436
  55.2 21.7 %collective-permute-start.17 = (f32[256,384]{1,0:T(8,128)S(1)}, f32[256,384]{1,0:T(8,128)S(1)}, u32[]{:S(2)}, u32[]{:S(2)}) collective-permute-start(f32[256,384]{1,0:T(8,128)S(1)} %slice.91.mine), channel_id=1, source_target_pairs={{4,6},{5,7},{6,4},{7,5},{8,10},{9,11},{10,8},{11,9},{12,14},{13,15... | collective-permute-start | bytes 1179656 | tf_op jit(solution)/shard_map/ppermute | solution.py:96
  70.6 2.4 %collective-permute-start.15 = (f32[256,256]{1,0:T(8,128)S(1)}, f32[256,256]{1,0:T(8,128)S(1)}, u32[]{:S(2)}, u32[]{:S(2)}) collective-permute-start(f32[256,256]{1,0:T(8,128)S(1)} %select_select_fusion.1), channel_id=1, source_target_pairs={{0,4},{1,5},{2,6},{3,7},{8,12},{9,13},{10,14},{11,15},{16,20},{17,... | collective-permute-start | bytes 786440 | tf_op jit(solution)/shard_map/ppermute | solution.py:102
  72.0 1.1 %copy-start.1 = (f32[256,512]{1,0:T(8,128)S(1)}, f32[256,512]{1,0:T(8,128)}, u32[]{:S(2)}) copy-start(f32[256,512]{1,0:T(8,128)} %copy-done) | copy-start | bytes 1572868
  72.0 9.3 %collective-permute-start.13 = (f32[512,128]{1,0:T(8,128)S(1)}, f32[512,128]{1,0:T(8,128)S(1)}, u32[]{:S(2)}, u32[]{:S(2)}) collective-permute-start(f32[512,128]{1,0:T(8,128)S(1)} %pad_maximum_fusion.1), channel_id=1, source_target_pairs={{0,1},{1,0},{2,3},{3,2}} | collective-permute-start | bytes 786440 | tf_op jit(solution)/shard_map/ppermute | solution.py:96
  74.9 16.1 %collective-permute-start.16 = (f32[640,128]{1,0:T(8,128)S(1)}, f32[640,128]{1,0:T(8,128)S(1)}, u32[]{:S(2)}, u32[]{:S(2)}) collective-permute-start(f32[640,128]{1,0:T(8,128)S(1)} %get-tuple-element.55), channel_id=1, source_target_pairs={{4,5},{5,4},{6,7},{7,6},{8,9},{9,8},{10,11},{11,10},{12,13},{13,12... | collective-permute-start | bytes 983048 | tf_op jit(solution)/shard_map/ppermute | solution.py:96
  77.4 13.6 %collective-permute-start.18 = (f32[384,128]{1,0:T(8,128)S(1)}, f32[384,128]{1,0:T(8,128)S(1)}, u32[]{:S(2)}, u32[]{:S(2)}) collective-permute-start(f32[384,128]{1,0:T(8,128)S(1)} %get-tuple-element.62), channel_id=1, source_target_pairs={{4,5},{5,4},{6,7},{7,6},{8,9},{9,8},{10,11},{11,10},{12,13},{13,12... | collective-permute-start | bytes 589832 | tf_op jit(solution)/shard_map/ppermute | solution.py:96

commit v6 on v5

--- a/solution.py
+++ b/solution.py
@@ -7,8 +7,7 @@
 from jax.sharding import PartitionSpec as P
 
 AXES = ("rows", "cols")
-EIGHTHS = (0, 4, 5, 8)
-PARAMS = pltpu.CompilerParams(vmem_limit_bytes=24 * 1024 * 1024)
+LIMIT = 20 * 1024 * 1024
 
 
 def split(array):
@@ -27,16 +26,24 @@
     return one(left_high, right_high) + (one(left_high, right_low) + one(left_low, right_high))
 
 
-def call(kernel, shapes, n_in, flops, *args):
+def call(kernel, shapes, flops, operands):
+    def spec(shape, place):
+        return pl.BlockSpec(shape, lambda step: place)
+
+    arrays, specs = [], []
+    for operand in operands:
+        array, shape, place = operand if isinstance(operand, tuple) else (operand, None, (0, 0))
+        arrays.append(array)
+        specs.append(spec(shape or array.shape, place))
     return pl.pallas_call(
         kernel,
+        grid=(1,),
         out_shape=[jax.ShapeDtypeStruct(shape, jnp.float32) for shape in shapes],
-        in_specs=[pl.BlockSpec(memory_space=pltpu.VMEM)] * n_in
-        + [pl.BlockSpec(memory_space=pltpu.SMEM)] * (len(args) - n_in),
-        out_specs=[pl.BlockSpec(memory_space=pltpu.VMEM)] * len(shapes),
-        compiler_params=PARAMS,
+        in_specs=specs,
+        out_specs=[spec(shape, (0, 0)) for shape in shapes],
+        compiler_params=pltpu.CompilerParams(vmem_limit_bytes=LIMIT),
         cost_estimate=pl.CostEstimate(flops=flops, bytes_accessed=0, transcendentals=0),
-    )(*args)
+    )(*arrays)
 
 
 def first_kernel(places, width, lead, lead_other, rhs, *refs):
@@ -56,17 +63,15 @@
         shuffled[:, at * cands : (at + 1) * cands] = pieces[place]
 
 
-def second_kernel(start, lead, lead_other, update, got, solved):
-    both = jnp.concatenate([lead[:, start:], lead_other[:, start:]], axis=0)
+def second_kernel(inverse, inverse_other, update, got, solved):
+    both = jnp.concatenate([inverse[...], inverse_other[...]], axis=0)
     solved[...] = dot(both, -(update[...] + got[...]), 1)
 
 
-def chunk_kernel(mine, others, late, first, second, base, beside, own, send):
+def chunk_kernel(mine, whole, late, piece, first, second, base, own, send):
     cands = base.shape[1]
     depth = first.shape[0] // 2
-    other = jnp.concatenate([piece[...] for piece in others], axis=1)
-    if late is not None:
-        other = jnp.where(beside[0] == 1, late[...], other)
+    other = piece[...] + (whole[...] + late[...])
     factors = jnp.concatenate([mine[...], other], axis=0)
     solved = jnp.concatenate(
         [first[:depth], second[:depth], first[depth:], second[depth:]], axis=0
@@ -74,14 +79,6 @@
     partial = dot(factors, solved, 0)
     own[...] = base[...] - partial[:, :cands]
     send[...] = partial[:, cands:]
-
-
-def early_kernel(mine, one, two, late, *refs):
-    chunk_kernel(mine, [one, two], late, *refs)
-
-
-def late_kernel(mine, one, *refs):
-    chunk_kernel(mine, [one], None, *refs)
 
 
 def make_on_device(n_rows, n_cols):
@@ -144,12 +141,10 @@
         width = block_inverses.shape[2]
         depth = block_inverses.shape[1]
         n_design, cands = cross_kernel.shape
-        cuts = [n_design * at // 8 for at in EIGHTHS]
-        parts = [slice(start, stop) for start, stop in zip(cuts, cuts[1:])]
-        early = slice(0, cuts[-2])
+        count = n_design // 2
         top = [0]
         beside = range(1, min(2, n_rows))
-        below = range(2, n_rows)
+        evens, odds = range(2, n_rows, 2), range(3, n_rows, 2)
         flat = factor_panels.reshape(2 * depth, n_design)
 
         lead = jnp.concatenate(
@@ -158,25 +153,20 @@
         lead, rhs = lax.optimization_barrier((lead, cross_kernel[:width]))
         lead_other = swap(lead, half, top)
         rhs_others = [swap(rhs, step, top) for step in range(1, half)]
-        mine = [flat[:, part] for part in parts]
-        arrived = [swap(mine[0], half, below)]
-        lead_other, mine_early, mine[1], mine[2] = lax.optimization_barrier(
-            (lead_other, flat[:, early], mine[1], mine[2])
-        )
-        arrived.append(swap(mine[1], half, below))
+        whole = swap(flat, half, odds)
+        arrived = [swap(flat[:, :count], half, evens)]
+        lead_other, rest = lax.optimization_barrier((lead_other, flat[:, count:]))
+        arrived.append(swap(rest, half, evens))
 
         first, update, shuffled = call(
             functools.partial(first_kernel, [at ^ 1 for at in range(half)], width),
             [(2 * depth, half * cands)] + [(width, half * cands)] * 2,
-            4 + len(rhs_others),
             6 * width * half * cands * (2 * depth + 2 * depth),
-            lead,
-            lead_other,
-            rhs,
-            *rhs_others,
-            cross_kernel[width : 2 * width],
-        )
-        shuffled, arrived[0] = lax.optimization_barrier((shuffled, arrived[0]))
+            [lead, lead_other, rhs, *rhs_others, cross_kernel[width : 2 * width]],
+        )
+        shuffled, first, arrived[0], whole = lax.optimization_barrier(
+            (shuffled, first, arrived[0], whole)
+        )
         got = swap(shuffled, 1, top)
         bit = 2
         while bit < half:
@@ -184,32 +174,26 @@
             got = swap(shuffle(update, bit, cands), bit, top)
             bit *= 2
         first_beside = first
-        late = mine_early
+        late = flat
         if n_rows > 1:
             first_beside = send_down(first, 1, top)
             first_beside, late = lax.optimization_barrier((first_beside, late))
         late = swap(late, half, beside)
         first_half = broadcast_outer(first, row_id)
         got, first_half = lax.optimization_barrier((got, first_half))
+        inverse = ((depth, width), (0, 2))
         (second,) = call(
-            functools.partial(second_kernel, 2 * width),
+            second_kernel,
             [(2 * depth, half * cands)],
-            4,
             6 * 2 * depth * width * half * cands,
-            lead,
-            lead_other,
-            update,
-            got,
+            [(lead, *inverse), (lead_other, *inverse), update, got],
         )
         second_half = broadcast_outer(second, row_id)
-        second_half, second, arrived[1], late = lax.optimization_barrier(
-            (second_half, second, arrived[1], late)
-        )
+        second_half, second, late = lax.optimization_barrier((second_half, second, late))
         first_full = jnp.where(
             row_id == 1, first_beside, broadcast_inner(first_half, row_id, 2)
         )
         solved = [first_full, broadcast_inner(second_half, row_id)]
-        arrived.append(swap(mine[2], half, range(1, n_rows)))
 
         pair = jnp.concatenate([first, second], axis=0)
         others = [block(pair, 0, cands)]
@@ -222,22 +206,15 @@
             in_order(pieces[0], col_id) + in_order(pieces[1], col_id), axis=0
         )
 
-        is_beside = (row_id == 1).astype(jnp.int32).reshape(1)
         fresh = []
-        work = [
-            (early, early_kernel, [mine_early, arrived[0], arrived[1], late]),
-            (parts[2], late_kernel, [mine[2], arrived[2]]),
-        ]
-        for part, kernel, args in work:
-            args = args + [*solved, cross_kernel[part]]
-            count = part.stop - part.start
+        for at, piece in enumerate(arrived):
+            window = ((2 * depth, count), (0, at))
             own, send = call(
-                kernel,
+                chunk_kernel,
                 [(count, cands), (count, (half - 1) * cands)],
-                len(args),
                 6 * count * 4 * depth * half * cands,
-                *args,
-                is_beside,
+                [(flat, *window), (whole, *window), (late, *window)]
+                + [piece, *solved, (cross_kernel, (count, cands), (at, 0))],
             )
             own, send, solved[0], solved[1] = lax.optimization_barrier((own, send, *solved))
             for step in range(1, half):

time: 92.6 us -> 92 us (level)
  the two profiles are of different devices: /device:TPU:2 before, /device:TPU:6 now
where the time goes in v6:
time: 92 us; the launch traced here: 91.4 us
  waiting for transfers between devices  45.1 us (49%)
  starting transfers between devices  29.3 us (32%)
  Pallas kernels  6.86 us (7%)
  local copies, waits for them, and re-layouts  5.71 us (6%)
  other arithmetic  3.95 us (4%)
    ppermute x10, waiting for transfers between devices, swap(): return lax.ppermute(array, AXES, pairs)  34.7 us
    ppermute x10, starting transfers between devices, swap(): return lax.ppermute(array, AXES, pairs)  19.3 us
    ppermute x9, waiting for transfers between devices, send_down(): return lax.ppermute(array, AXES, pairs)  10.4 us
    ppermute x9, starting transfers between devices, send_down(): return lax.ppermute(array, AXES, pairs)  9.94 us
    pallas_call x4, Pallas kernels, call(): pl.pallas_call(kernel, grid=(1,), out_shape=[jax.ShapeDtypeStruct(shape,...  6.86 us
    unnamed x22, local copies, waits for them, and re-layouts  3.79 us
  transfers between devices with their start and end apart: 19, of which 6 were waited for; matrix products, arithmetic and copies ran while one was open for 5% of the time, Pallas kernels for 8%

profile of v6, /device:TPU:6, one launch (start us, length us, event | category | flops | bytes accessed | tf_op | source)
XLA Modules:
  0.0 91.4 jit_solution(1060369052766988569)
XLA Ops:
  0.0 0.8 collective-permute-start.3
  0.9 1.0 %slice_bitcast_fusion.1 = f32[128,512]{1,0:T(8,128)S(1)} fusion(f32[2,128,1024]{2,1,0:T(8,128)} %param.4), kind=kLoop, calls=%fused_computation.7 | loop fusion | bytes 524288 | tf_op jit(solution)/shard_map/squeeze | solution.py:151
  1.9 0.0 copy-start.1
  1.9 0.0 copy-start
  1.9 0.1 pad_maximum_fusion.lead.inverse
  2.0 1.0 %copy-done.1 = f32[1024,128]{1,0:T(8,128)S(1)} copy-done((f32[1024,128]{1,0:T(8,128)S(1)}, f32[1024,128]{1,0:T(8,128)}, u32[]{:S(2)}) %copy-start.1) | copy-done | bytes 524312
  3.0 0.7 collective-permute-start
  3.7 0.9 fusion
  4.6 4.5 %collective-permute-start.2 = (f32[256,512]{1,0:T(8,128)S(1)}, f32[256,512]{1,0:T(8,128)S(1)}, u32[]{:S(2)}, u32[]{:S(2)}) collective-permute-start(f32[256,512]{1,0:T(8,128)S(1)} %get-tuple-element.61), channel_id=1, source_target_pairs={{8,10},{9,11},{10,8},{11,9},{16,18},{17,19},{18,16},{19,17},{24,26... | collective-permute-start | bytes 1572872 | tf_op jit(solution)/shard_map/ppermute | solution.py:93
  9.1 0.7 collective-permute-start.1
  9.8 0.0 collective-permute-done.1.refs_0_
  9.8 1.9 %shard_map.37 = (f32[256,256]{1,0:T(8,128)S(1)}, f32[512,256]{1,0:T(8,128)S(1)}, f32[512,256]{1,0:T(8,128)}) custom-call(f32[128,1536]{1,0:T(8,128)S(1)} %pad_maximum_fusion.lead.inverse, f32[128,1536]{1,0:T(8,128)S(1)} %collective-permute-done.lead_other.inverse_other, f32[512,128]{1,0:T(8,128)S(1)} %get-tuple-element.35.rhs, ...), custom_call_target="tpu_custom_call" | custom-call | flops 402653184 | tf_op jit(solution)/shard_map/pallas_call | solution.py:38
  11.7 0.8 copy-done.6
  12.5 22.4 %collective-permute-done.2.piece = f32[256,512]{1,0:T(8,128)S(1)} collective-permute-done((f32[256,512]{1,0:T(8,128)S(1)}, f32[256,512]{1,0:T(8,128)S(1)}, u32[]{:S(2)}, u32[]{:S(2)}) %collective-permute-start.2) | collective-permute-done | bytes 524320 | tf_op jit(solution)/shard_map/ppermute | solution.py:93
  34.8 0.0 collective-permute-done.3.whole
  34.8 1.0 %copy-done.2 = f32[256,1024]{1,0:T(8,128)} copy-done((f32[256,1024]{1,0:T(8,128)}, f32[256,1024]{1,0:T(8,128)S(1)}, u32[]{:S(2)}) %copy-start.2) | copy-done | bytes 1048600
  35.8 0.7 collective-permute-start.11
  36.5 1.5 %collective-permute-start.4 = (f32[512,256]{1,0:T(8,128)}, f32[512,256]{1,0:T(8,128)}, u32[]{:S(2)}, u32[]{:S(2)}) collective-permute-start(f32[512,256]{1,0:T(8,128)} %get-tuple-element.40), channel_id=1, source_target_pairs={{0,1},{1,0},{2,3},{3,2}} | collective-permute-start | bytes 1572872 | tf_op jit(solution)/shard_map/ppermute | solution.py:93
  37.9 0.7 collective-permute-start.5
  38.6 1.4 %collective-permute-start.6 = (f32[256,256]{1,0:T(8,128)S(1)}, f32[256,256]{1,0:T(8,128)}, u32[]{:S(2)}, u32[]{:S(2)}) collective-permute-start(f32[256,256]{1,0:T(8,128)S(1)} %get-tuple-element.38), channel_id=1, source_target_pairs={{0,16},{1,17},{2,18},{3,19}} | collective-permute-start | bytes 786440 | tf_op jit(solution)/shard_map/ppermute | solution.py:99
  40.0 1.3 %collective-permute-start.7 = (f32[256,256]{1,0:T(8,128)S(1)}, f32[256,256]{1,0:T(8,128)}, u32[]{:S(2)}, u32[]{:S(2)}) collective-permute-start(f32[256,256]{1,0:T(8,128)S(1)} %get-tuple-element.38), channel_id=1, source_target_pairs={{0,24},{1,25},{2,26},{3,27}} | collective-permute-start | bytes 786440 | tf_op jit(solution)/shard_map/ppermute | solution.py:99
  41.3 0.0 collective-permute-done.11
  41.3 0.7 copy-done.9
  42.0 1.6 %collective-permute-start.12 = (f32[256,1024]{1,0:T(8,128)S(1)}, f32[256,1024]{1,0:T(8,128)}, u32[]{:S(2)}, u32[]{:S(2)}) collective-permute-start(f32[256,1024]{1,0:T(8,128)S(1)} %bitcast.9), channel_id=1, source_target_pairs={{4,6},{5,7},{6,4},{7,5}} | collective-permute-start | bytes 3145736 | tf_op jit(solution)/shard_map/ppermute | solution.py:93
  43.6 0.0 collective-permute-done.5
  43.6 0.0 collective-permute-done.6
  43.7 5.9 %collective-permute-done.7 = f32[256,256]{1,0:T(8,128)} collective-permute-done((f32[256,256]{1,0:T(8,128)S(1)}, f32[256,256]{1,0:T(8,128)}, u32[]{:S(2)}, u32[]{:S(2)}) %collective-permute-start.7) | collective-permute-done | bytes 262176 | tf_op jit(solution)/shard_map/ppermute | solution.py:99
  49.6 1.7 %select_select_fusion.2 = f32[256,256]{1,0:T(8,128)} fusion(f32[256,256]{1,0:T(8,128)S(1)} %collective-permute-done.5, f32[256,256]{1,0:T(8,128)} %collective-permute-done.6, f32[256,256]{1,0:T(8,128)} %collective-permute-done.7, f32[256,256]{1,0:T(8,128)S(1)} %get-tuple-element.38, pred[]{:T(512)S(6)} %eq.30, pred[]{:T(512)S(6)} %eq.29, pred[]{:T(512)S(6)} %eq.28), kind=kLoop, calls=%fused_computation.5 | loop fusion | flops 196608 | bytes 1310723 | tf_op jit(solution)/shard_map/jit(_where)/select_n | solution.py:105
  51.3 1.5 %shard_map.38 = f32[256,256]{1,0:T(8,128)S(1)} custom-call(f32[128,1536]{1,0:T(8,128)S(1)} %pad_maximum_fusion.lead.inverse, f32[128,1536]{1,0:T(8,128)S(1)} %copy-done.5, f32[512,256]{1,0:T(8,128)S(1)} %copy-done.7, f32[512,256]{1,0:T(8,128)} %collective-permute-done.4.got), custom_call_target="tpu_custom_call" | custom-call | flops 201326592 | tf_op jit(solution)/shard_map/pallas_call | solution.py:38
  52.8 1.3 %collective-permute-start.10 = (f32[256,256]{1,0:T(8,128)S(1)}, f32[256,256]{1,0:T(8,128)S(1)}, u32[]{:S(2)}, u32[]{:S(2)}) collective-permute-start(f32[256,256]{1,0:T(8,128)S(1)} %shard_map.38), channel_id=1, source_target_pairs={{0,24},{1,25},{2,26},{3,27}} | collective-permute-start | bytes 786440 | tf_op jit(solution)/shard_map/ppermute | solution.py:99
  54.1 0.7 collective-permute-start.8
  54.8 1.4 %collective-permute-start.9 = (f32[256,256]{1,0:T(8,128)S(1)}, f32[256,256]{1,0:T(8,128)}, u32[]{:S(2)}, u32[]{:S(2)}) collective-permute-start(f32[256,256]{1,0:T(8,128)S(1)} %shard_map.38), channel_id=1, source_target_pairs={{0,16},{1,17},{2,18},{3,19}} | collective-permute-start | bytes 786440 | tf_op jit(solution)/shard_map/ppermute | solution.py:99
  56.1 1.3 %collective-permute-start.14 = (f32[256,256]{1,0:T(8,128)}, f32[256,256]{1,0:T(8,128)S(1)}, u32[]{:S(2)}, u32[]{:S(2)}) collective-permute-start(f32[256,256]{1,0:T(8,128)} %select_select_fusion.2), channel_id=1, source_target_pairs={{8,12},{9,13},{10,14},{11,15},{16,20},{17,21},{18,22},{19,23},{24,... | collective-permute-start | bytes 786440 | tf_op jit(solution)/shard_map/ppermute | solution.py:99
  57.5 4.5 %collective-permute-done.10 = f32[256,256]{1,0:T(8,128)S(1)} collective-permute-done((f32[256,256]{1,0:T(8,128)S(1)}, f32[256,256]{1,0:T(8,128)S(1)}, u32[]{:S(2)}, u32[]{:S(2)}) %collective-permute-start.10) | collective-permute-done | bytes 262176 | tf_op jit(solution)/shard_map/ppermute | solution.py:99
  61.9 1.9 %collective-permute-start.17 = (f32[256,512]{1,0:T(8,128)}, f32[256,512]{1,0:T(8,128)S(1)}, u32[]{:S(2)}, u32[]{:S(2)}) collective-permute-start(f32[256,512]{1,0:T(8,128)} %get-tuple-element.54), channel_id=1, source_target_pairs={{8,10},{9,11},{10,8},{11,9},{16,18},{17,19},{18,16},{19,17},{24,26... | collective-permute-start | bytes 1572872 | tf_op jit(solution)/shard_map/ppermute | solution.py:93
  63.9 0.1 select_select_fusion.1
  64.0 1.3 %collective-permute-start.15 = (f32[256,256]{1,0:T(8,128)S(1)}, f32[256,256]{1,0:T(8,128)S(1)}, u32[]{:S(2)}, u32[]{:S(2)}) collective-permute-start(f32[256,256]{1,0:T(8,128)S(1)} %select_select_fusion.1), channel_id=1, source_target_pairs={{0,4},{1,5},{2,6},{3,7},{8,12},{9,13},{10,14},{11,15},{16,20},{17,... | collective-permute-start | bytes 786440 | tf_op jit(solution)/shard_map/ppermute | solution.py:99
  65.3 1.0 %select_select_fusion.first = f32[256,256]{1,0:T(8,128)S(1)} fusion(f32[256,256]{1,0:T(8,128)S(1)} %copy-done.10, f32[256,256]{1,0:T(8,128)S(1)} %collective-permute-done.14, f32[256,256]{1,0:T(8,128)} %select_select_fusion.2, pred[]{:T(512)S(6)} %eq.32, pred[]{:T(512)S(6)} %eq.31), kind=kLoop, calls=%fused_computation.3 | loop fusion | flops 131072 | bytes 1048578 | tf_op jit(solution)/shard_map/jit(_where)/select_n | solution.py:193
  66.4 0.8 collective-permute-start.13
  67.2 0.3 copy-done.3
  67.6 1.8 %shard_map.39 = (f32[512,128]{1,0:T(8,128)S(1)}, f32[512,128]{1,0:T(8,128)S(1)}) custom-call(f32[256,1024]{1,0:T(8,128)S(1)} %bitcast.10, f32[256,1024]{1,0:T(8,128)S(1)} %copy-done.3, f32[256,1024]{1,0:T(8,128)} %collective-permute-done.12.late, f32[256,512]{1,0:T(8,128)S(1)} %collective-permute-done.2.piece, f32[256,256]{1,0:T(8,128)S(1)} %select_select_fusion.first, ...), custom_call_target="tpu_custom_call" | custom-call | flops 402653184 | tf_op jit(solution)/shard_map/pallas_call | solution.py:38
  69.3 4.9 %collective-permute-start.16 = (f32[512,128]{1,0:T(8,128)S(1)}, f32[512,128]{1,0:T(8,128)S(1)}, u32[]{:S(2)}, u32[]{:S(2)}) collective-permute-start(f32[512,128]{1,0:T(8,128)S(1)} %get-tuple-element.53), channel_id=1, source_target_pairs={{4,5},{5,4},{6,7},{7,6},{8,9},{9,8},{10,11},{11,10},{12,13},{13,12... | collective-permute-start | bytes 786440 | tf_op jit(solution)/shard_map/ppermute | solution.py:93
  74.2 5.1 %collective-permute-done.17.piece = f32[256,512]{1,0:T(8,128)S(1)} collective-permute-done((f32[256,512]{1,0:T(8,128)}, f32[256,512]{1,0:T(8,128)S(1)}, u32[]{:S(2)}, u32[]{:S(2)}) %collective-permute-start.17) | collective-permute-done | bytes 524320 | tf_op jit(solution)/shard_map/ppermute | solution.py:93
  79.3 1.8 %shard_map.40 = (f32[512,128]{1,0:T(8,128)S(1)}, f32[512,128]{1,0:T(8,128)S(1)}) custom-call(f32[256,1024]{1,0:T(8,128)S(1)} %bitcast.11, f32[256,1024]{1,0:T(8,128)S(1)} %copy-done.3, f32[256,1024]{1,0:T(8,128)} %collective-permute-done.12.late, f32[256,512]{1,0:T(8,128)S(1)} %collective-permute-done.17.piece, f32[256,256]{1,0:T(8,128)S(1)} %select_select_fusion.first, ...), custom_call_target="tpu_custom_call" | custom-call | flops 402653184 | tf_op jit(solution)/shard_map/pallas_call | solution.py:38
  81.1 1.9 %collective-permute-start.18 = (f32[512,128]{1,0:T(8,128)S(1)}, f32[512,128]{1,0:T(8,128)S(1)}, u32[]{:S(2)}, u32[]{:S(2)}) collective-permute-start(f32[512,128]{1,0:T(8,128)S(1)} %get-tuple-element.60), channel_id=1, source_target_pairs={{4,5},{5,4},{6,7},{7,6},{8,9},{9,8},{10,11},{11,10},{12,13},{13,12... | collective-permute-start | bytes 786440 | tf_op jit(solution)/shard_map/ppermute | solution.py:93
  83.2 1.7 %collective-permute-done.16 = f32[512,128]{1,0:T(8,128)S(1)} collective-permute-done((f32[512,128]{1,0:T(8,128)S(1)}, f32[512,128]{1,0:T(8,128)S(1)}, u32[]{:S(2)}, u32[]{:S(2)}) %collective-permute-start.16) | collective-permute-done | bytes 262176 | tf_op jit(solution)/shard_map/ppermute | solution.py:93
  85.0 5.5 %collective-permute-done.18 = f32[512,128]{1,0:T(8,128)S(1)} collective-permute-done((f32[512,128]{1,0:T(8,128)S(1)}, f32[512,128]{1,0:T(8,128)S(1)}, u32[]{:S(2)}, u32[]{:S(2)}) %collective-permute-start.18) | collective-permute-done | bytes 262176 | tf_op jit(solution)/shard_map/ppermute | solution.py:93
  90.5 0.9 maximum_select_fusion
  (37 shorter events, 0.4 us)
Async XLA Ops:
  0.0 1.8 %copy-start.8 = (f32[2,128,512]{2,1,0:T(8,128)S(1)}, f32[2,128,512]{2,1,0:T(8,128)}, u32[]{:S(2)}) copy-start(f32[2,128,512]{2,1,0:T(8,128)} %param.5) | copy-start | bytes 1572868
  0.0 34.8 %collective-permute-start.3 = (f32[256,1024]{1,0:T(8,128)}, f32[256,1024]{1,0:T(8,128)S(1)}, u32[]{:S(2)}, u32[]{:S(2)}) collective-permute-start(f32[256,1024]{1,0:T(8,128)} %bitcast.7), channel_id=1, source_target_pairs={{12,14},{13,15},{14,12},{15,13},{20,22},{21,23},{22,20},{23,21},{2... | collective-permute-start | bytes 3145736 | tf_op jit(solution)/shard_map/ppermute | solution.py:93
  1.9 1.0 %copy-start.1 = (f32[1024,128]{1,0:T(8,128)S(1)}, f32[1024,128]{1,0:T(8,128)}, u32[]{:S(2)}) copy-start(f32[1024,128]{1,0:T(8,128)} %base.3) | copy-start | bytes 1572868
  1.9 1.8 %copy-start = (f32[2,128,1024]{2,1,0:T(8,128)S(1)}, f32[2,128,1024]{2,1,0:T(8,128)}, u32[]{:S(2)}) copy-start(f32[2,128,1024]{2,1,0:T(8,128)} %param.4) | copy-start | bytes 3145732
  3.0 6.8 %collective-permute-start = (f32[128,1536]{1,0:T(8,128)S(1)}, f32[128,1536]{1,0:T(8,128)S(1)}, u32[]{:S(2)}, u32[]{:S(2)}) collective-permute-start(f32[128,1536]{1,0:T(8,128)S(1)} %pad_maximum_fusion.lead.inverse), channel_id=1, source_target_pairs={{0,2},{1,3},{2,0},{3,1}} | collective-permute-start | bytes 2359304 | tf_op jit(solution)/shard_map/ppermute | solution.py:93
  4.6 30.2 %collective-permute-start.2 = (f32[256,512]{1,0:T(8,128)S(1)}, f32[256,512]{1,0:T(8,128)S(1)}, u32[]{:S(2)}, u32[]{:S(2)}) collective-permute-start(f32[256,512]{1,0:T(8,128)S(1)} %get-tuple-element.61), channel_id=1, source_target_pairs={{8,10},{9,11},{10,8},{11,9},{16,18},{17,19},{18,16},{19,17},{24,26... | collective-permute-start | bytes 1572872 | tf_op jit(solution)/shard_map/ppermute | solution.py:93
  9.1 0.7 collective-permute-start.1
  9.8 1.9 %copy-start.4 = (f32[128,1536]{1,0:T(8,128)}, f32[128,1536]{1,0:T(8,128)S(1)}, u32[]{:S(2)}) copy-start(f32[128,1536]{1,0:T(8,128)S(1)} %collective-permute-done.lead_other.inverse_other) | copy-start | bytes 2359300
  11.7 0.8 copy-start.6
  34.8 1.0 %copy-start.2 = (f32[256,1024]{1,0:T(8,128)}, f32[256,1024]{1,0:T(8,128)S(1)}, u32[]{:S(2)}) copy-start(f32[256,1024]{1,0:T(8,128)S(1)} %collective-permute-done.3.whole) | copy-start | bytes 3145732
  35.8 5.5 %collective-permute-start.11 = (f32[256,256]{1,0:T(8,128)S(1)}, f32[256,256]{1,0:T(8,128)S(1)}, u32[]{:S(2)}, u32[]{:S(2)}) collective-permute-start(f32[256,256]{1,0:T(8,128)S(1)} %get-tuple-element.38), channel_id=1, source_target_pairs={{0,4},{1,5},{2,6},{3,7}} | collective-permute-start | bytes 786440 | tf_op jit(solution)/shard_map/ppermute | solution.py:99
  36.5 14.8 %collective-permute-start.4 = (f32[512,256]{1,0:T(8,128)}, f32[512,256]{1,0:T(8,128)}, u32[]{:S(2)}, u32[]{:S(2)}) collective-permute-start(f32[512,256]{1,0:T(8,128)} %get-tuple-element.40), channel_id=1, source_target_pairs={{0,1},{1,0},{2,3},{3,2}} | collective-permute-start | bytes 1572872 | tf_op jit(solution)/shard_map/ppermute | solution.py:93
  37.9 5.7 %collective-permute-start.5 = (f32[256,256]{1,0:T(8,128)S(1)}, f32[256,256]{1,0:T(8,128)S(1)}, u32[]{:S(2)}, u32[]{:S(2)}) collective-permute-start(f32[256,256]{1,0:T(8,128)S(1)} %get-tuple-element.38), channel_id=1, source_target_pairs={{0,8},{1,9},{2,10},{3,11}} | collective-permute-start | bytes 786440 | tf_op jit(solution)/shard_map/ppermute | solution.py:99
  38.6 5.0 %collective-permute-start.6 = (f32[256,256]{1,0:T(8,128)S(1)}, f32[256,256]{1,0:T(8,128)}, u32[]{:S(2)}, u32[]{:S(2)}) collective-permute-start(f32[256,256]{1,0:T(8,128)S(1)} %get-tuple-element.38), channel_id=1, source_target_pairs={{0,16},{1,17},{2,18},{3,19}} | collective-permute-start | bytes 786440 | tf_op jit(solution)/shard_map/ppermute | solution.py:99
  40.0 9.6 %collective-permute-start.7 = (f32[256,256]{1,0:T(8,128)S(1)}, f32[256,256]{1,0:T(8,128)}, u32[]{:S(2)}, u32[]{:S(2)}) collective-permute-start(f32[256,256]{1,0:T(8,128)S(1)} %get-tuple-element.38), channel_id=1, source_target_pairs={{0,24},{1,25},{2,26},{3,27}} | collective-permute-start | bytes 786440 | tf_op jit(solution)/shard_map/ppermute | solution.py:99
  41.3 0.7 copy-start.9
  42.0 22.0 %collective-permute-start.12 = (f32[256,1024]{1,0:T(8,128)S(1)}, f32[256,1024]{1,0:T(8,128)}, u32[]{:S(2)}, u32[]{:S(2)}) collective-permute-start(f32[256,1024]{1,0:T(8,128)S(1)} %bitcast.9), channel_id=1, source_target_pairs={{4,6},{5,7},{6,4},{7,5}} | collective-permute-start | bytes 3145736 | tf_op jit(solution)/shard_map/ppermute | solution.py:93
  43.6 7.6 %copy-start.5 = (f32[128,1536]{1,0:T(8,128)S(1)}, f32[128,1536]{1,0:T(8,128)}, u32[]{:S(2)}) copy-start(f32[128,1536]{1,0:T(8,128)} %copy-done.4) | copy-start | bytes 2359300
  43.6 7.6 %copy-start.7 = (f32[512,256]{1,0:T(8,128)S(1)}, f32[512,256]{1,0:T(8,128)}, u32[]{:S(2)}) copy-start(f32[512,256]{1,0:T(8,128)} %copy-done.6) | copy-start | bytes 1572868
  52.8 9.2 %collective-permute-start.10 = (f32[256,256]{1,0:T(8,128)S(1)}, f32[256,256]{1,0:T(8,128)S(1)}, u32[]{:S(2)}, u32[]{:S(2)}) collective-permute-start(f32[256,256]{1,0:T(8,128)S(1)} %shard_map.38), channel_id=1, source_target_pairs={{0,24},{1,25},{2,26},{3,27}} | collective-permute-start | bytes 786440 | tf_op jit(solution)/shard_map/ppermute | solution.py:99
  54.1 9.8 %collective-permute-start.8 = (f32[256,256]{1,0:T(8,128)S(1)}, f32[256,256]{1,0:T(8,128)S(1)}, u32[]{:S(2)}, u32[]{:S(2)}) collective-permute-start(f32[256,256]{1,0:T(8,128)S(1)} %shard_map.38), channel_id=1, source_target_pairs={{0,8},{1,9},{2,10},{3,11}} | collective-permute-start | bytes 786440 | tf_op jit(solution)/shard_map/ppermute | solution.py:99
  54.8 9.1 %collective-permute-start.9 = (f32[256,256]{1,0:T(8,128)S(1)}, f32[256,256]{1,0:T(8,128)}, u32[]{:S(2)}, u32[]{:S(2)}) collective-permute-start(f32[256,256]{1,0:T(8,128)S(1)} %shard_map.38), channel_id=1, source_target_pairs={{0,16},{1,17},{2,18},{3,19}} | collective-permute-start | bytes 786440 | tf_op jit(solution)/shard_map/ppermute | solution.py:99
  56.1 9.2 %collective-permute-start.14 = (f32[256,256]{1,0:T(8,128)}, f32[256,256]{1,0:T(8,128)S(1)}, u32[]{:S(2)}, u32[]{:S(2)}) collective-permute-start(f32[256,256]{1,0:T(8,128)} %select_select_fusion.2), channel_id=1, source_target_pairs={{8,12},{9,13},{10,14},{11,15},{16,20},{17,21},{18,22},{19,23},{24,... | collective-permute-start | bytes 786440 | tf_op jit(solution)/shard_map/ppermute | solution.py:99
  57.5 7.8 %copy-start.10 = (f32[256,256]{1,0:T(8,128)S(1)}, f32[256,256]{1,0:T(8,128)}, u32[]{:S(2)}) copy-start(f32[256,256]{1,0:T(8,128)} %copy-done.9) | copy-start | bytes 786436
  61.9 17.4 %collective-permute-start.17 = (f32[256,512]{1,0:T(8,128)}, f32[256,512]{1,0:T(8,128)S(1)}, u32[]{:S(2)}, u32[]{:S(2)}) collective-permute-start(f32[256,512]{1,0:T(8,128)} %get-tuple-element.54), channel_id=1, source_target_pairs={{8,10},{9,11},{10,8},{11,9},{16,18},{17,19},{18,16},{19,17},{24,26... | collective-permute-start | bytes 1572872 | tf_op jit(solution)/shard_map/ppermute | solution.py:93
  64.0 3.2 %collective-permute-start.15 = (f32[256,256]{1,0:T(8,128)S(1)}, f32[256,256]{1,0:T(8,128)S(1)}, u32[]{:S(2)}, u32[]{:S(2)}) collective-permute-start(f32[256,256]{1,0:T(8,128)S(1)} %select_select_fusion.1), channel_id=1, source_target_pairs={{0,4},{1,5},{2,6},{3,7},{8,12},{9,13},{10,14},{11,15},{16,20},{17,... | collective-permute-start | bytes 786440 | tf_op jit(solution)/shard_map/ppermute | solution.py:99
  66.3 1.2 %copy-start.3 = (f32[256,1024]{1,0:T(8,128)S(1)}, f32[256,1024]{1,0:T(8,128)}, u32[]{:S(2)}) copy-start(f32[256,1024]{1,0:T(8,128)} %copy-done.2) | copy-start | bytes 3145732
  66.4 16.7 %collective-permute-start.13 = (f32[512,128]{1,0:T(8,128)S(1)}, f32[512,128]{1,0:T(8,128)S(1)}, u32[]{:S(2)}, u32[]{:S(2)}) collective-permute-start(f32[512,128]{1,0:T(8,128)S(1)} %pad_maximum_fusion.1), channel_id=1, source_target_pairs={{0,1},{1,0},{2,3},{3,2}} | collective-permute-start | bytes 786440 | tf_op jit(solution)/shard_map/ppermute | solution.py:93
  69.3 15.6 %collective-permute-start.16 = (f32[512,128]{1,0:T(8,128)S(1)}, f32[512,128]{1,0:T(8,128)S(1)}, u32[]{:S(2)}, u32[]{:S(2)}) collective-permute-start(f32[512,128]{1,0:T(8,128)S(1)} %get-tuple-element.53), channel_id=1, source_target_pairs={{4,5},{5,4},{6,7},{7,6},{8,9},{9,8},{10,11},{11,10},{12,13},{13,12... | collective-permute-start | bytes 786440 | tf_op jit(solution)/shard_map/ppermute | solution.py:93
  81.1 9.4 %collective-permute-start.18 = (f32[512,128]{1,0:T(8,128)S(1)}, f32[512,128]{1,0:T(8,128)S(1)}, u32[]{:S(2)}, u32[]{:S(2)}) collective-permute-start(f32[512,128]{1,0:T(8,128)S(1)} %get-tuple-element.60), channel_id=1, source_target_pairs={{4,5},{5,4},{6,7},{7,6},{8,9},{9,8},{10,11},{11,10},{12,13},{13,12... | collective-permute-start | bytes 786440 | tf_op jit(solution)/shard_map/ppermute | solution.py:93

commit v7 on v6

--- a/solution.py
+++ b/solution.py
@@ -7,7 +7,8 @@
 from jax.sharding import PartitionSpec as P
 
 AXES = ("rows", "cols")
-LIMIT = 20 * 1024 * 1024
+FIRST = 3
+LIMIT = 16 * 1024 * 1024
 
 
 def split(array):
@@ -68,16 +69,22 @@
     solved[...] = dot(both, -(update[...] + got[...]), 1)
 
 
-def chunk_kernel(mine, whole, late, piece, first, second, base, own, send):
+def chunk_kernel(*refs):
+    tiles, (piece, first, second, own, send) = refs[:-5], refs[-5:]
+    each = len(tiles) // 4
+    mine, whole, late = [
+        jnp.concatenate([ref[...] for ref in tiles[at * each : (at + 1) * each]], axis=1)
+        for at in range(3)
+    ]
+    base = jnp.concatenate([ref[...] for ref in tiles[3 * each :]], axis=0)
     cands = base.shape[1]
     depth = first.shape[0] // 2
-    other = piece[...] + (whole[...] + late[...])
-    factors = jnp.concatenate([mine[...], other], axis=0)
+    factors = jnp.concatenate([mine, piece[...] + (whole + late)], axis=0)
     solved = jnp.concatenate(
         [first[:depth], second[:depth], first[depth:], second[depth:]], axis=0
     )
     partial = dot(factors, solved, 0)
-    own[...] = base[...] - partial[:, :cands]
+    own[...] = base - partial[:, :cands]
     send[...] = partial[:, cands:]
 
 
@@ -141,7 +148,8 @@
         width = block_inverses.shape[2]
         depth = block_inverses.shape[1]
         n_design, cands = cross_kernel.shape
-        count = n_design // 2
+        tile = n_design // 8
+        cuts = [0, FIRST * tile, n_design]
         top = [0]
         beside = range(1, min(2, n_rows))
         evens, odds = range(2, n_rows, 2), range(3, n_rows, 2)
@@ -154,9 +162,9 @@
         lead_other = swap(lead, half, top)
         rhs_others = [swap(rhs, step, top) for step in range(1, half)]
         whole = swap(flat, half, odds)
-        arrived = [swap(flat[:, :count], half, evens)]
-        lead_other, rest = lax.optimization_barrier((lead_other, flat[:, count:]))
-        arrived.append(swap(rest, half, evens))
+        arrived = [swap(flat[:, : cuts[1]], half, evens)]
+        lead_other, piece = lax.optimization_barrier((lead_other, flat[:, cuts[1] :]))
+        arrived.append(swap(piece, half, evens))
 
         first, update, shuffled = call(
             functools.partial(first_kernel, [at ^ 1 for at in range(half)], width),
@@ -164,9 +172,7 @@
             6 * width * half * cands * (2 * depth + 2 * depth),
             [lead, lead_other, rhs, *rhs_others, cross_kernel[width : 2 * width]],
         )
-        shuffled, first, arrived[0], whole = lax.optimization_barrier(
-            (shuffled, first, arrived[0], whole)
-        )
+        shuffled, arrived[0], whole = lax.optimization_barrier((shuffled, arrived[0], whole))
         got = swap(shuffled, 1, top)
         bit = 2
         while bit < half:
@@ -207,14 +213,18 @@
         )
 
         fresh = []
-        for at, piece in enumerate(arrived):
-            window = ((2 * depth, count), (0, at))
+        for start, stop, piece in zip(cuts, cuts[1:], arrived):
+            count = stop - start
+            tiles = range(start // tile, stop // tile)
+            windows = [
+                (array, (2 * depth, tile), (0, at)) for array in (flat, whole, late) for at in tiles
+            ]
+            windows += [(cross_kernel, (tile, cands), (at, 0)) for at in tiles]
             own, send = call(
                 chunk_kernel,
                 [(count, cands), (count, (half - 1) * cands)],
                 6 * count * 4 * depth * half * cands,
-                [(flat, *window), (whole, *window), (late, *window)]
-                + [piece, *solved, (cross_kernel, (count, cands), (at, 0))],
+                windows + [piece, *solved],
             )
             own, send, solved[0], solved[1] = lax.optimization_barrier((own, send, *solved))
             for step in range(1, half):

time: 92 us -> 92.7 us (level)
  Pallas kernels: 6.86 us -> 4.8 us
  starting transfers between devices: 29.3 us -> 31.2 us
  other arithmetic: 3.95 us -> 4.94 us
    ppermute x9, starting transfers between devices: 9.94 us -> 12.9 us  [send_down(): return lax.ppermute(array, AXES, pairs)]
    pallas_call x4, Pallas kernels: 6.86 us -> 4.8 us  [call(): pl.pallas_call(kernel, grid=(1,), out_shape=[jax.ShapeDtypeStruct(shape,...]
    squeeze x1, local copies, waits for them, and re-layouts: 0.04 us -> 1.18 us  [on_device(): block_inverses[0]]
    ppermute x10, starting transfers between devices: 19.3 us -> 18.3 us  [swap(): return lax.ppermute(array, AXES, pairs)]
    select_n x2, other arithmetic: 1.78 us -> 2.77 us  [spread(): jnp.where(digit == step, send_down(array, step * low, have), result)]
    squeeze x1, local copies, waits for them, and re-layouts: 0.97 us -> 0.02 us  [on_device(): factor_panels[0, :, width:2 * width]]
    unnamed x22 -> x26, local copies, waits for them, and re-layouts: 3.79 us -> 3.27 us
  transfers between devices with their start and end apart: 19 -> 19, of which waited for: 6 -> 6; matrix products, arithmetic and copies ran while one was open for 5% -> 5% of each run, Pallas kernels for 8% -> 5%
where the time goes in v7:
time: 92.7 us; the launch traced here: 92.1 us
  waiting for transfers between devices  45.3 us (49%)
  starting transfers between devices  31.2 us (34%)
  local copies, waits for them, and re-layouts  5.45 us (6%)
  other arithmetic  4.94 us (5%)
  Pallas kernels  4.8 us (5%)
    ppermute x10, waiting for transfers between devices, swap(): return lax.ppermute(array, AXES, pairs)  34.6 us
    ppermute x10, starting transfers between devices, swap(): return lax.ppermute(array, AXES, pairs)  18.3 us
    ppermute x9, starting transfers between devices, send_down(): return lax.ppermute(array, AXES, pairs)  12.9 us
    ppermute x9, waiting for transfers between devices, send_down(): return lax.ppermute(array, AXES, pairs)  10.7 us
    pallas_call x4, Pallas kernels, call(): pl.pallas_call(kernel, grid=(1,), out_shape=[jax.ShapeDtypeStruct(shape,...  4.8 us
    unnamed x26, local copies, waits for them, and re-layouts  3.27 us
    select_n x2, other arithmetic, spread(): jnp.where(digit == step, send_down(array, step * low, have), result)  2.77 us
  transfers between devices with their start and end apart: 19, of which 6 were waited for; matrix products, arithmetic and copies ran while one was open for 5% of the time, Pallas kernels for 5%

profile of v7, /device:TPU:6, one launch (start us, length us, event | category | flops | bytes accessed | tf_op | source)
XLA Modules:
  0.0 92.1 jit_solution(15259711609728285527)
XLA Ops:
  0.0 1.2 %slice_bitcast_fusion.2 = (f32[128,512]{1,0:T(8,128)S(1)}, f32[128,512]{1,0:T(8,128)S(1)}) fusion(f32[2,128,512]{2,1,0:T(8,128)} %param.5), kind=kLoop, calls=%fused_computation.8 | loop fusion | bytes 1048576 | tf_op jit(solution)/shard_map/squeeze | solution.py:159
  1.2 0.2 copy-done
  1.4 0.1 copy-done.1
  1.6 0.1 pad_maximum_fusion.lead.inverse
  1.6 0.7 collective-permute-start
  2.3 0.7 collective-permute-start.3
  3.1 0.7 collective-permute-start.1
  3.8 4.5 %collective-permute-start.2 = (f32[256,384]{1,0:T(8,128)S(1)}, f32[256,384]{1,0:T(8,128)S(1)}, u32[]{:S(2)}, u32[]{:S(2)}) collective-permute-start(f32[256,384]{1,0:T(8,128)S(1)} %slice.74), channel_id=1, source_target_pairs={{8,10},{9,11},{10,8},{11,9},{16,18},{17,19},{18,16},{19,17},{24,26... | collective-permute-start | bytes 1179656 | tf_op jit(solution)/shard_map/ppermute | solution.py:100
  8.3 0.9 slice.73
  9.2 1.9 %shard_map.37 = (f32[256,256]{1,0:T(8,128)S(1)}, f32[512,256]{1,0:T(8,128)S(1)}, f32[512,256]{1,0:T(8,128)}) custom-call(f32[128,1536]{1,0:T(8,128)S(1)} %pad_maximum_fusion.lead.inverse, f32[128,1536]{1,0:T(8,128)S(1)} %collective-permute-done.lead_other.inverse_other, f32[512,128]{1,0:T(8,128)S(1)} %get-tuple-element.34.rhs, ...), custom_call_target="tpu_custom_call" | custom-call | flops 402653184 | tf_op jit(solution)/shard_map/pallas_call | solution.py:39
  11.1 0.8 copy-done.9
  11.9 1.4 %collective-permute-start.11 = (f32[256,256]{1,0:T(8,128)S(1)}, f32[256,256]{1,0:T(8,128)}, u32[]{:S(2)}, u32[]{:S(2)}) collective-permute-start(f32[256,256]{1,0:T(8,128)S(1)} %get-tuple-element.35), channel_id=1, source_target_pairs={{0,4},{1,5},{2,6},{3,7}} | collective-permute-start | bytes 786440 | tf_op jit(solution)/shard_map/ppermute | solution.py:106
  13.3 19.3 %collective-permute-done.2.refs_12_ = f32[256,384]{1,0:T(8,128)S(1)} collective-permute-done((f32[256,384]{1,0:T(8,128)S(1)}, f32[256,384]{1,0:T(8,128)S(1)}, u32[]{:S(2)}, u32[]{:S(2)}) %collective-permute-start.2) | collective-permute-done | bytes 393248 | tf_op jit(solution)/shard_map/ppermute | solution.py:100
  32.6 0.7 copy-done.11
  33.4 0.0 collective-permute-done.3.refs_3_.refs_4_.refs_5_.refs_6_.refs_7_.refs_8_.refs_9_
  33.4 1.5 %collective-permute-start.4 = (f32[512,256]{1,0:T(8,128)}, f32[512,256]{1,0:T(8,128)}, u32[]{:S(2)}, u32[]{:S(2)}) collective-permute-start(f32[512,256]{1,0:T(8,128)} %get-tuple-element.38), channel_id=1, source_target_pairs={{0,1},{1,0},{2,3},{3,2}} | collective-permute-start | bytes 1572872 | tf_op jit(solution)/shard_map/ppermute | solution.py:100
  34.8 1.4 %collective-permute-start.5 = (f32[256,256]{1,0:T(8,128)S(1)}, f32[256,256]{1,0:T(8,128)}, u32[]{:S(2)}, u32[]{:S(2)}) collective-permute-start(f32[256,256]{1,0:T(8,128)S(1)} %get-tuple-element.35), channel_id=1, source_target_pairs={{0,8},{1,9},{2,10},{3,11}} | collective-permute-start | bytes 786440 | tf_op jit(solution)/shard_map/ppermute | solution.py:106
  36.2 1.3 %collective-permute-start.6 = (f32[256,256]{1,0:T(8,128)S(1)}, f32[256,256]{1,0:T(8,128)}, u32[]{:S(2)}, u32[]{:S(2)}) collective-permute-start(f32[256,256]{1,0:T(8,128)S(1)} %get-tuple-element.35), channel_id=1, source_target_pairs={{0,16},{1,17},{2,18},{3,19}} | collective-permute-start | bytes 786440 | tf_op jit(solution)/shard_map/ppermute | solution.py:106
  37.6 1.3 %collective-permute-start.7 = (f32[256,256]{1,0:T(8,128)S(1)}, f32[256,256]{1,0:T(8,128)}, u32[]{:S(2)}, u32[]{:S(2)}) collective-permute-start(f32[256,256]{1,0:T(8,128)S(1)} %get-tuple-element.35), channel_id=1, source_target_pairs={{0,24},{1,25},{2,26},{3,27}} | collective-permute-start | bytes 786440 | tf_op jit(solution)/shard_map/ppermute | solution.py:106
  38.9 0.7 collective-permute-start.12
  39.7 7.5 %collective-permute-done.7 = f32[256,256]{1,0:T(8,128)} collective-permute-done((f32[256,256]{1,0:T(8,128)S(1)}, f32[256,256]{1,0:T(8,128)}, u32[]{:S(2)}, u32[]{:S(2)}) %collective-permute-start.7) | collective-permute-done | bytes 262176 | tf_op jit(solution)/shard_map/ppermute | solution.py:106
  47.1 1.7 %select_select_fusion.2 = f32[256,256]{1,0:T(8,128)} fusion(f32[256,256]{1,0:T(8,128)} %collective-permute-done.5, f32[256,256]{1,0:T(8,128)} %collective-permute-done.6, f32[256,256]{1,0:T(8,128)} %collective-permute-done.7, f32[256,256]{1,0:T(8,128)S(1)} %get-tuple-element.35, pred[]{:T(512)S(6)} %eq.30, pred[]{:T(512)S(6)} %eq.29, pred[]{:T(512)S(6)} %eq.28), kind=kLoop, calls=%fused_computation.5 | loop fusion | flops 196608 | bytes 1310723 | tf_op jit(solution)/shard_map/jit(_where)/select_n | solution.py:112
  48.9 1.1 %copy-done.8 = f32[128,1536]{1,0:T(8,128)S(1)} copy-done((f32[128,1536]{1,0:T(8,128)S(1)}, f32[128,1536]{1,0:T(8,128)}, u32[]{:S(2)}) %copy-start.8) | copy-done | bytes 786456
  50.0 1.5 %shard_map.38 = f32[256,256]{1,0:T(8,128)S(1)} custom-call(f32[128,1536]{1,0:T(8,128)S(1)} %copy-done.4, f32[128,1536]{1,0:T(8,128)S(1)} %copy-done.8, f32[512,256]{1,0:T(8,128)S(1)} %copy-done.10, f32[512,256]{1,0:T(8,128)} %collective-permute-done.4.got), custom_call_target="tpu_custom_call" | custom-call | flops 201326592 | tf_op jit(solution)/shard_map/pallas_call | solution.py:39
  51.5 1.3 %collective-permute-start.10 = (f32[256,256]{1,0:T(8,128)S(1)}, f32[256,256]{1,0:T(8,128)}, u32[]{:S(2)}, u32[]{:S(2)}) collective-permute-start(f32[256,256]{1,0:T(8,128)S(1)} %shard_map.38), channel_id=1, source_target_pairs={{0,24},{1,25},{2,26},{3,27}} | collective-permute-start | bytes 786440 | tf_op jit(solution)/shard_map/ppermute | solution.py:106
  52.8 1.4 %collective-permute-start.8 = (f32[256,256]{1,0:T(8,128)S(1)}, f32[256,256]{1,0:T(8,128)}, u32[]{:S(2)}, u32[]{:S(2)}) collective-permute-start(f32[256,256]{1,0:T(8,128)S(1)} %shard_map.38), channel_id=1, source_target_pairs={{0,8},{1,9},{2,10},{3,11}} | collective-permute-start | bytes 786440 | tf_op jit(solution)/shard_map/ppermute | solution.py:106
  54.2 1.4 %collective-permute-start.9 = (f32[256,256]{1,0:T(8,128)S(1)}, f32[256,256]{1,0:T(8,128)}, u32[]{:S(2)}, u32[]{:S(2)}) collective-permute-start(f32[256,256]{1,0:T(8,128)S(1)} %shard_map.38), channel_id=1, source_target_pairs={{0,16},{1,17},{2,18},{3,19}} | collective-permute-start | bytes 786440 | tf_op jit(solution)/shard_map/ppermute | solution.py:106
  55.6 2.0 %collective-permute-start.14 = (f32[256,256]{1,0:T(8,128)}, f32[256,256]{1,0:T(8,128)}, u32[]{:S(2)}, u32[]{:S(2)}) collective-permute-start(f32[256,256]{1,0:T(8,128)} %select_select_fusion.2), channel_id=1, source_target_pairs={{8,12},{9,13},{10,14},{11,15},{16,20},{17,21},{18,22},{19,23},{24,... | collective-permute-start | bytes 786440 | tf_op jit(solution)/shard_map/ppermute | solution.py:106
  57.6 3.2 %collective-permute-done.10 = f32[256,256]{1,0:T(8,128)} collective-permute-done((f32[256,256]{1,0:T(8,128)S(1)}, f32[256,256]{1,0:T(8,128)}, u32[]{:S(2)}, u32[]{:S(2)}) %collective-permute-start.10) | collective-permute-done | bytes 262176 | tf_op jit(solution)/shard_map/ppermute | solution.py:106
  60.8 1.9 %collective-permute-start.17 = (f32[256,640]{1,0:T(8,128)}, f32[256,640]{1,0:T(8,128)S(1)}, u32[]{:S(2)}, u32[]{:S(2)}) collective-permute-start(f32[256,640]{1,0:T(8,128)} %slice.73), channel_id=1, source_target_pairs={{8,10},{9,11},{10,8},{11,9},{16,18},{17,19},{18,16},{19,17},{24,26... | collective-permute-start | bytes 1966088 | tf_op jit(solution)/shard_map/ppermute | solution.py:100
  62.7 0.0 collective-permute-done.9
  62.7 1.0 %select_select_fusion.1 = f32[256,256]{1,0:T(8,128)S(1)} fusion(f32[256,256]{1,0:T(8,128)} %collective-permute-done.8, f32[256,256]{1,0:T(8,128)} %collective-permute-done.9, f32[256,256]{1,0:T(8,128)} %collective-permute-done.10, f32[256,256]{1,0:T(8,128)S(1)} %shard_map.38, pred[]{:T(512)S(6)} %eq.30, pred[]{:T(512)S(6)} %eq.29, pred[]{:T(512)S(6)} %eq.28), kind=kLoop, calls=%fused_computation.4 | loop fusion | flops 196608 | bytes 1310723 | tf_op jit(solution)/shard_map/jit(_where)/select_n | solution.py:112
  63.8 1.4 %collective-permute-start.15 = (f32[256,256]{1,0:T(8,128)S(1)}, f32[256,256]{1,0:T(8,128)S(1)}, u32[]{:S(2)}, u32[]{:S(2)}) collective-permute-start(f32[256,256]{1,0:T(8,128)S(1)} %select_select_fusion.1), channel_id=1, source_target_pairs={{0,4},{1,5},{2,6},{3,7},{8,12},{9,13},{10,14},{11,15},{16,20},{17,... | collective-permute-start | bytes 786440 | tf_op jit(solution)/shard_map/ppermute | solution.py:106
  65.2 0.0 collective-permute-done.14
  65.2 1.0 %select_select_fusion.refs_13_.refs_21_ = f32[256,256]{1,0:T(8,128)S(1)} fusion(f32[256,256]{1,0:T(8,128)} %collective-permute-done.11, f32[256,256]{1,0:T(8,128)} %collective-permute-done.14, f32[256,256]{1,0:T(8,128)} %select_select_fusion.2, pred[]{:T(512)S(6)} %eq.32, pred[]{:T(512)S(6)} %eq.31), kind=kLoop, calls=%fused_computation.3 | loop fusion | flops 131072 | bytes 1048578 | tf_op jit(solution)/shard_map/jit(_where)/select_n | solution.py:199
  66.3 0.0 copy-start.2
  66.3 0.8 collective-permute-start.13
  67.1 0.0 collective-permute-done.15
  67.2 0.1 copy-done.12
  67.3 0.2 copy-done.2
  67.4 0.6 shard_map.39
  68.0 4.9 %collective-permute-start.16 = (f32[384,128]{1,0:T(8,128)S(1)}, f32[384,128]{1,0:T(8,128)S(1)}, u32[]{:S(2)}, u32[]{:S(2)}) collective-permute-start(f32[384,128]{1,0:T(8,128)S(1)} %get-tuple-element.51), channel_id=1, source_target_pairs={{4,5},{5,4},{6,7},{7,6},{8,9},{9,8},{10,11},{11,10},{12,13},{13,12... | collective-permute-start | bytes 589832 | tf_op jit(solution)/shard_map/ppermute | solution.py:100
  72.9 8.1 %collective-permute-done.17.refs_20_ = f32[256,640]{1,0:T(8,128)S(1)} collective-permute-done((f32[256,640]{1,0:T(8,128)}, f32[256,640]{1,0:T(8,128)S(1)}, u32[]{:S(2)}, u32[]{:S(2)}) %collective-permute-start.17) | collective-permute-done | bytes 655392 | tf_op jit(solution)/shard_map/ppermute | solution.py:100
  81.0 0.9 shard_map.40
  81.9 1.9 %collective-permute-start.18 = (f32[640,128]{1,0:T(8,128)S(1)}, f32[640,128]{1,0:T(8,128)S(1)}, u32[]{:S(2)}, u32[]{:S(2)}) collective-permute-start(f32[640,128]{1,0:T(8,128)S(1)} %get-tuple-element.58), channel_id=1, source_target_pairs={{4,5},{5,4},{6,7},{7,6},{8,9},{9,8},{10,11},{11,10},{12,13},{13,12... | collective-permute-start | bytes 983048 | tf_op jit(solution)/shard_map/ppermute | solution.py:100
  84.0 1.2 %collective-permute-done.16 = f32[384,128]{1,0:T(8,128)S(1)} collective-permute-done((f32[384,128]{1,0:T(8,128)S(1)}, f32[384,128]{1,0:T(8,128)S(1)}, u32[]{:S(2)}, u32[]{:S(2)}) %collective-permute-start.16) | collective-permute-done | bytes 196640 | tf_op jit(solution)/shard_map/ppermute | solution.py:100
  85.3 6.0 %collective-permute-done.18 = f32[640,128]{1,0:T(8,128)S(1)} collective-permute-done((f32[640,128]{1,0:T(8,128)S(1)}, f32[640,128]{1,0:T(8,128)S(1)}, u32[]{:S(2)}, u32[]{:S(2)}) %collective-permute-start.18) | collective-permute-done | bytes 327712 | tf_op jit(solution)/shard_map/ppermute | solution.py:100
  91.3 0.9 maximum_select_fusion
  (42 shorter events, 0.4 us)
Async XLA Ops:
  0.0 1.4 %copy-start = (f32[2,128,1024]{2,1,0:T(8,128)S(1)}, f32[2,128,1024]{2,1,0:T(8,128)}, u32[]{:S(2)}) copy-start(f32[2,128,1024]{2,1,0:T(8,128)} %param.4) | copy-start | bytes 3145732
  0.0 1.5 %copy-start.1 = (f32[1024,128]{1,0:T(8,128)S(1)}, f32[1024,128]{1,0:T(8,128)}, u32[]{:S(2)}) copy-start(f32[1024,128]{1,0:T(8,128)} %refs_19_.1) | copy-start | bytes 1572868
  1.6 7.6 %copy-start.3 = (f32[128,1536]{1,0:T(8,128)}, f32[128,1536]{1,0:T(8,128)S(1)}, u32[]{:S(2)}) copy-start(f32[128,1536]{1,0:T(8,128)S(1)} %pad_maximum_fusion.lead.inverse) | copy-start | bytes 2359300
  1.6 7.6 %collective-permute-start = (f32[128,1536]{1,0:T(8,128)S(1)}, f32[128,1536]{1,0:T(8,128)S(1)}, u32[]{:S(2)}, u32[]{:S(2)}) collective-permute-start(f32[128,1536]{1,0:T(8,128)S(1)} %pad_maximum_fusion.lead.inverse), channel_id=1, source_target_pairs={{0,2},{1,3},{2,0},{3,1}} | collective-permute-start | bytes 2359304 | tf_op jit(solution)/shard_map/ppermute | solution.py:100
  2.3 31.0 %collective-permute-start.3 = (f32[256,1024]{1,0:T(8,128)S(1)}, f32[256,1024]{1,0:T(8,128)S(1)}, u32[]{:S(2)}, u32[]{:S(2)}) collective-permute-start(f32[256,1024]{1,0:T(8,128)S(1)} %bitcast.7), channel_id=1, source_target_pairs={{12,14},{13,15},{14,12},{15,13},{20,22},{21,23},{22,20},{23,21},{2... | collective-permute-start | bytes 3145736 | tf_op jit(solution)/shard_map/ppermute | solution.py:100
  3.1 6.2 %collective-permute-start.1 = (f32[512,128]{1,0:T(8,128)S(1)}, f32[512,128]{1,0:T(8,128)S(1)}, u32[]{:S(2)}, u32[]{:S(2)}) collective-permute-start(f32[512,128]{1,0:T(8,128)S(1)} %get-tuple-element.34.rhs), channel_id=1, source_target_pairs={{0,1},{1,0},{2,3},{3,2}} | collective-permute-start | bytes 786440 | tf_op jit(solution)/shard_map/ppermute | solution.py:100
  3.8 28.8 %collective-permute-start.2 = (f32[256,384]{1,0:T(8,128)S(1)}, f32[256,384]{1,0:T(8,128)S(1)}, u32[]{:S(2)}, u32[]{:S(2)}) collective-permute-start(f32[256,384]{1,0:T(8,128)S(1)} %slice.74), channel_id=1, source_target_pairs={{8,10},{9,11},{10,8},{11,9},{16,18},{17,19},{18,16},{19,17},{24,26... | collective-permute-start | bytes 1179656 | tf_op jit(solution)/shard_map/ppermute | solution.py:100
  9.2 1.9 %copy-start.7 = (f32[128,1536]{1,0:T(8,128)}, f32[128,1536]{1,0:T(8,128)S(1)}, u32[]{:S(2)}) copy-start(f32[128,1536]{1,0:T(8,128)S(1)} %collective-permute-done.lead_other.inverse_other) | copy-start | bytes 2359300
  11.1 0.8 copy-start.9
  11.9 36.9 %copy-start.5 = (f32[256,256]{1,0:T(8,128)}, f32[256,256]{1,0:T(8,128)S(1)}, u32[]{:S(2)}) copy-start(f32[256,256]{1,0:T(8,128)S(1)} %get-tuple-element.35) | copy-start | bytes 786436
  11.9 26.9 %collective-permute-start.11 = (f32[256,256]{1,0:T(8,128)S(1)}, f32[256,256]{1,0:T(8,128)}, u32[]{:S(2)}, u32[]{:S(2)}) collective-permute-start(f32[256,256]{1,0:T(8,128)S(1)} %get-tuple-element.35), channel_id=1, source_target_pairs={{0,4},{1,5},{2,6},{3,7}} | collective-permute-start | bytes 786440 | tf_op jit(solution)/shard_map/ppermute | solution.py:106
  32.6 0.7 copy-start.11
  33.4 15.5 %collective-permute-start.4 = (f32[512,256]{1,0:T(8,128)}, f32[512,256]{1,0:T(8,128)}, u32[]{:S(2)}, u32[]{:S(2)}) collective-permute-start(f32[512,256]{1,0:T(8,128)} %get-tuple-element.38), channel_id=1, source_target_pairs={{0,1},{1,0},{2,3},{3,2}} | collective-permute-start | bytes 1572872 | tf_op jit(solution)/shard_map/ppermute | solution.py:100
  34.8 4.8 %collective-permute-start.5 = (f32[256,256]{1,0:T(8,128)S(1)}, f32[256,256]{1,0:T(8,128)}, u32[]{:S(2)}, u32[]{:S(2)}) collective-permute-start(f32[256,256]{1,0:T(8,128)S(1)} %get-tuple-element.35), channel_id=1, source_target_pairs={{0,8},{1,9},{2,10},{3,11}} | collective-permute-start | bytes 786440 | tf_op jit(solution)/shard_map/ppermute | solution.py:106
  36.2 3.5 %collective-permute-start.6 = (f32[256,256]{1,0:T(8,128)S(1)}, f32[256,256]{1,0:T(8,128)}, u32[]{:S(2)}, u32[]{:S(2)}) collective-permute-start(f32[256,256]{1,0:T(8,128)S(1)} %get-tuple-element.35), channel_id=1, source_target_pairs={{0,16},{1,17},{2,18},{3,19}} | collective-permute-start | bytes 786440 | tf_op jit(solution)/shard_map/ppermute | solution.py:106
  37.6 9.6 %collective-permute-start.7 = (f32[256,256]{1,0:T(8,128)S(1)}, f32[256,256]{1,0:T(8,128)}, u32[]{:S(2)}, u32[]{:S(2)}) collective-permute-start(f32[256,256]{1,0:T(8,128)S(1)} %get-tuple-element.35), channel_id=1, source_target_pairs={{0,24},{1,25},{2,26},{3,27}} | collective-permute-start | bytes 786440 | tf_op jit(solution)/shard_map/ppermute | solution.py:106
  38.9 24.9 %collective-permute-start.12 = (f32[256,1024]{1,0:T(8,128)S(1)}, f32[256,1024]{1,0:T(8,128)S(1)}, u32[]{:S(2)}, u32[]{:S(2)}) collective-permute-start(f32[256,1024]{1,0:T(8,128)S(1)} %bitcast.10), channel_id=1, source_target_pairs={{4,6},{5,7},{6,4},{7,5}} | collective-permute-start | bytes 3145736 | tf_op jit(solution)/shard_map/ppermute | solution.py:100
  39.6 9.2 %copy-start.4 = (f32[128,1536]{1,0:T(8,128)S(1)}, f32[128,1536]{1,0:T(8,128)}, u32[]{:S(2)}) copy-start(f32[128,1536]{1,0:T(8,128)} %copy-done.3) | copy-start | bytes 2359300
  39.6 9.2 %copy-start.10 = (f32[512,256]{1,0:T(8,128)S(1)}, f32[512,256]{1,0:T(8,128)}, u32[]{:S(2)}) copy-start(f32[512,256]{1,0:T(8,128)} %copy-done.9) | copy-start | bytes 1572868
  48.9 1.1 %copy-start.8 = (f32[128,1536]{1,0:T(8,128)S(1)}, f32[128,1536]{1,0:T(8,128)}, u32[]{:S(2)}) copy-start(f32[128,1536]{1,0:T(8,128)} %copy-done.7) | copy-start | bytes 2359300
  51.5 9.3 %collective-permute-start.10 = (f32[256,256]{1,0:T(8,128)S(1)}, f32[256,256]{1,0:T(8,128)}, u32[]{:S(2)}, u32[]{:S(2)}) collective-permute-start(f32[256,256]{1,0:T(8,128)S(1)} %shard_map.38), channel_id=1, source_target_pairs={{0,24},{1,25},{2,26},{3,27}} | collective-permute-start | bytes 786440 | tf_op jit(solution)/shard_map/ppermute | solution.py:106
  52.8 9.9 %collective-permute-start.8 = (f32[256,256]{1,0:T(8,128)S(1)}, f32[256,256]{1,0:T(8,128)}, u32[]{:S(2)}, u32[]{:S(2)}) collective-permute-start(f32[256,256]{1,0:T(8,128)S(1)} %shard_map.38), channel_id=1, source_target_pairs={{0,8},{1,9},{2,10},{3,11}} | collective-permute-start | bytes 786440 | tf_op jit(solution)/shard_map/ppermute | solution.py:106
  54.2 8.5 %collective-permute-start.9 = (f32[256,256]{1,0:T(8,128)S(1)}, f32[256,256]{1,0:T(8,128)}, u32[]{:S(2)}, u32[]{:S(2)}) collective-permute-start(f32[256,256]{1,0:T(8,128)S(1)} %shard_map.38), channel_id=1, source_target_pairs={{0,16},{1,17},{2,18},{3,19}} | collective-permute-start | bytes 786440 | tf_op jit(solution)/shard_map/ppermute | solution.py:106
  55.6 9.6 %collective-permute-start.14 = (f32[256,256]{1,0:T(8,128)}, f32[256,256]{1,0:T(8,128)}, u32[]{:S(2)}, u32[]{:S(2)}) collective-permute-start(f32[256,256]{1,0:T(8,128)} %select_select_fusion.2), channel_id=1, source_target_pairs={{8,12},{9,13},{10,14},{11,15},{16,20},{17,21},{18,22},{19,23},{24,... | collective-permute-start | bytes 786440 | tf_op jit(solution)/shard_map/ppermute | solution.py:106
  60.8 20.2 %collective-permute-start.17 = (f32[256,640]{1,0:T(8,128)}, f32[256,640]{1,0:T(8,128)S(1)}, u32[]{:S(2)}, u32[]{:S(2)}) collective-permute-start(f32[256,640]{1,0:T(8,128)} %slice.73), channel_id=1, source_target_pairs={{8,10},{9,11},{10,8},{11,9},{16,18},{17,19},{18,16},{19,17},{24,26... | collective-permute-start | bytes 1966088 | tf_op jit(solution)/shard_map/ppermute | solution.py:100
  63.8 2.5 %copy-start.6 = (f32[256,256]{1,0:T(8,128)S(1)}, f32[256,256]{1,0:T(8,128)}, u32[]{:S(2)}) copy-start(f32[256,256]{1,0:T(8,128)} %copy-done.5) | copy-start | bytes 786436
  63.8 3.4 %collective-permute-start.15 = (f32[256,256]{1,0:T(8,128)S(1)}, f32[256,256]{1,0:T(8,128)S(1)}, u32[]{:S(2)}, u32[]{:S(2)}) collective-permute-start(f32[256,256]{1,0:T(8,128)S(1)} %select_select_fusion.1), channel_id=1, source_target_pairs={{0,4},{1,5},{2,6},{3,7},{8,12},{9,13},{10,14},{11,15},{16,20},{17,... | collective-permute-start | bytes 786440 | tf_op jit(solution)/shard_map/ppermute | solution.py:106
  66.3 1.0 %copy-start.12 = (f32[256,384]{1,0:T(8,128)S(1)}, f32[256,384]{1,0:T(8,128)}, u32[]{:S(2)}) copy-start(f32[256,384]{1,0:T(8,128)} %copy-done.11) | copy-start | bytes 1179652
  66.3 1.1 %copy-start.2 = (f32[1024,128]{1,0:T(8,128)S(1)}, f32[1024,128]{1,0:T(8,128)}, u32[]{:S(2)}) copy-start(f32[1024,128]{1,0:T(8,128)} %refs_19_.1) | copy-start | bytes 1572868
  66.3 17.5 %collective-permute-start.13 = (f32[512,128]{1,0:T(8,128)S(1)}, f32[512,128]{1,0:T(8,128)S(1)}, u32[]{:S(2)}, u32[]{:S(2)}) collective-permute-start(f32[512,128]{1,0:T(8,128)S(1)} %pad_maximum_fusion.1), channel_id=1, source_target_pairs={{0,1},{1,0},{2,3},{3,2}} | collective-permute-start | bytes 786440 | tf_op jit(solution)/shard_map/ppermute | solution.py:100
  68.0 17.2 %collective-permute-start.16 = (f32[384,128]{1,0:T(8,128)S(1)}, f32[384,128]{1,0:T(8,128)S(1)}, u32[]{:S(2)}, u32[]{:S(2)}) collective-permute-start(f32[384,128]{1,0:T(8,128)S(1)} %get-tuple-element.51), channel_id=1, source_target_pairs={{4,5},{5,4},{6,7},{7,6},{8,9},{9,8},{10,11},{11,10},{12,13},{13,12... | collective-permute-start | bytes 589832 | tf_op jit(solution)/shard_map/ppermute | solution.py:100
  81.9 9.4 %collective-permute-start.18 = (f32[640,128]{1,0:T(8,128)S(1)}, f32[640,128]{1,0:T(8,128)S(1)}, u32[]{:S(2)}, u32[]{:S(2)}) collective-permute-start(f32[640,128]{1,0:T(8,128)S(1)} %get-tuple-element.58), channel_id=1, source_target_pairs={{4,5},{5,4},{6,7},{7,6},{8,9},{9,8},{10,11},{11,10},{12,13},{13,12... | collective-permute-start | bytes 983048 | tf_op jit(solution)/shard_map/ppermute | solution.py:100

commit v8 on v6

--- a/solution.py
+++ b/solution.py
@@ -7,7 +7,7 @@
 from jax.sharding import PartitionSpec as P
 
 AXES = ("rows", "cols")
-LIMIT = 20 * 1024 * 1024
+LIMIT = 36 * 1024 * 1024
 
 
 def split(array):
@@ -26,7 +26,7 @@
     return one(left_high, right_high) + (one(left_high, right_low) + one(left_low, right_high))
 
 
-def call(kernel, shapes, flops, operands):
+def call(kernel, shapes, flops, operands, flag=None):
     def spec(shape, place):
         return pl.BlockSpec(shape, lambda step: place)
 
@@ -35,6 +35,9 @@
         array, shape, place = operand if isinstance(operand, tuple) else (operand, None, (0, 0))
         arrays.append(array)
         specs.append(spec(shape or array.shape, place))
+    if flag is not None:
+        arrays.insert(0, flag.astype(jnp.int32).reshape(1))
+        specs.insert(0, pl.BlockSpec(memory_space=pltpu.SMEM))
     return pl.pallas_call(
         kernel,
         grid=(1,),
@@ -63,22 +66,32 @@
         shuffled[:, at * cands : (at + 1) * cands] = pieces[place]
 
 
-def second_kernel(inverse, inverse_other, update, got, solved):
+def second_kernel(beside, inverse, inverse_other, update, got, first, solved, bundle):
     both = jnp.concatenate([inverse[...], inverse_other[...]], axis=0)
-    solved[...] = dot(both, -(update[...] + got[...]), 1)
-
-
-def chunk_kernel(mine, whole, late, piece, first, second, base, own, send):
-    cands = base.shape[1]
-    depth = first.shape[0] // 2
-    other = piece[...] + (whole[...] + late[...])
-    factors = jnp.concatenate([mine[...], other], axis=0)
+    second = dot(both, -(update[...] + got[...]), 1)
+    solved[...] = second
+    bundle[...] = jnp.where(beside[0] == 1, first[...], second)
+
+
+def rows_kernel(odd, mine, whole, early, beside, tail, base, held, got, own, send):
+    n_design, cands = base.shape
+    depth = held.shape[0] // 2
+    is_odd = odd[0] == 1
+    first = jnp.where(is_odd, held[...], got[...])
+    second = jnp.where(is_odd, got[...], held[...])
     solved = jnp.concatenate(
         [first[:depth], second[:depth], first[depth:], second[depth:]], axis=0
     )
-    partial = dot(factors, solved, 0)
-    own[...] = base[...] - partial[:, :cands]
-    send[...] = partial[:, cands:]
+    count = n_design // 2
+    for at, parts in enumerate(([early, beside], [tail])):
+        part = slice(at * count, (at + 1) * count)
+        other = whole[:, part]
+        for array in parts:
+            other = other + array[...]
+        factors = jnp.concatenate([mine[:, part], other], axis=0)
+        partial = dot(factors, solved, 0)
+        own[part] = base[part] - partial[:, :cands]
+        send[part] = partial[:, cands:]
 
 
 def make_on_device(n_rows, n_cols):
@@ -107,15 +120,20 @@
 
     def broadcast_outer(array, row_id):
         low = n_rows
-        have = [0]
+        have = [0, 1]
         while low > 2:
             radix = min(4, low // 2)
             low //= radix
             array, have = spread(array, row_id, low, radix, have)
         return array
 
-    def broadcast_inner(array, row_id, start=0):
-        return jnp.where(row_id % 2 == 1, send_down(array, 1, range(start, n_rows, 2)), array)
+    def swap_cores(array):
+        pairs = [
+            (row * n_cols + col, (row ^ 1) * n_cols + col)
+            for row in range(n_rows)
+            for col in range(n_cols)
+        ]
+        return lax.ppermute(array, AXES, pairs)
 
     def block(array, place, cands):
         return array[:, place * cands : (place + 1) * cands]
@@ -143,7 +161,7 @@
         n_design, cands = cross_kernel.shape
         count = n_design // 2
         top = [0]
-        beside = range(1, min(2, n_rows))
+        beside = [1]
         evens, odds = range(2, n_rows, 2), range(3, n_rows, 2)
         flat = factor_panels.reshape(2 * depth, n_design)
 
@@ -154,9 +172,9 @@
         lead_other = swap(lead, half, top)
         rhs_others = [swap(rhs, step, top) for step in range(1, half)]
         whole = swap(flat, half, odds)
-        arrived = [swap(flat[:, :count], half, evens)]
-        lead_other, rest = lax.optimization_barrier((lead_other, flat[:, count:]))
-        arrived.append(swap(rest, half, evens))
+        head = flat[:, :count]
+        arrived = swap(head, half, evens)
+        lead_other, head, tail = lax.optimization_barrier((lead_other, head, flat[:, count:]))
 
         first, update, shuffled = call(
             functools.partial(first_kernel, [at ^ 1 for at in range(half)], width),
@@ -164,36 +182,28 @@
             6 * width * half * cands * (2 * depth + 2 * depth),
             [lead, lead_other, rhs, *rhs_others, cross_kernel[width : 2 * width]],
         )
-        shuffled, first, arrived[0], whole = lax.optimization_barrier(
-            (shuffled, first, arrived[0], whole)
-        )
+        shuffled, arrived, whole = lax.optimization_barrier((shuffled, arrived, whole))
         got = swap(shuffled, 1, top)
         bit = 2
         while bit < half:
             update = update + got
             got = swap(shuffle(update, bit, cands), bit, top)
             bit *= 2
-        first_beside = first
-        late = flat
-        if n_rows > 1:
-            first_beside = send_down(first, 1, top)
-            first_beside, late = lax.optimization_barrier((first_beside, late))
-        late = swap(late, half, beside)
-        first_half = broadcast_outer(first, row_id)
-        got, first_half = lax.optimization_barrier((got, first_half))
+        first_beside = send_down(first, 1, top)
         inverse = ((depth, width), (0, 2))
-        (second,) = call(
+        second, bundle = call(
             second_kernel,
-            [(2 * depth, half * cands)],
+            [(2 * depth, half * cands)] * 2,
             6 * 2 * depth * width * half * cands,
-            [(lead, *inverse), (lead_other, *inverse), update, got],
-        )
-        second_half = broadcast_outer(second, row_id)
-        second_half, second, late = lax.optimization_barrier((second_half, second, late))
-        first_full = jnp.where(
-            row_id == 1, first_beside, broadcast_inner(first_half, row_id, 2)
-        )
-        solved = [first_full, broadcast_inner(second_half, row_id)]
+            [(lead, *inverse), (lead_other, *inverse), update, got, first_beside],
+            row_id == 1,
+        )
+        first_beside, head = lax.optimization_barrier((first_beside, head))
+        late = swap(head, half, beside)
+        held = broadcast_outer(bundle, row_id)
+        held, second, late = lax.optimization_barrier((held, second, late))
+        tail = swap(tail, half, [*beside, *evens])
+        solved = [held, swap_cores(held)]
 
         pair = jnp.concatenate([first, second], axis=0)
         others = [block(pair, 0, cands)]
@@ -206,21 +216,15 @@
             in_order(pieces[0], col_id) + in_order(pieces[1], col_id), axis=0
         )
 
-        fresh = []
-        for at, piece in enumerate(arrived):
-            window = ((2 * depth, count), (0, at))
-            own, send = call(
-                chunk_kernel,
-                [(count, cands), (count, (half - 1) * cands)],
-                6 * count * 4 * depth * half * cands,
-                [(flat, *window), (whole, *window), (late, *window)]
-                + [piece, *solved, (cross_kernel, (count, cands), (at, 0))],
-            )
-            own, send, solved[0], solved[1] = lax.optimization_barrier((own, send, *solved))
-            for step in range(1, half):
-                own = own - swap(block(send, step - 1, cands), step, range(1, n_rows))
-            fresh.append(own)
-        fresh = jnp.concatenate(fresh, axis=0)
+        fresh, send = call(
+            rows_kernel,
+            [(n_design, cands), (n_design, (half - 1) * cands)],
+            6 * n_design * 4 * depth * half * cands,
+            [flat, whole, arrived, late, tail, cross_kernel, *solved],
+            row_id % 2 == 1,
+        )
+        for step in range(1, half):
+            fresh = fresh - swap(block(send, step - 1, cands), step, range(1, n_rows))
         head = jnp.where(row_id == 0, top_rows, fresh[: 2 * width])
         return jnp.concatenate([head, fresh[2 * width :]], axis=0)
 

time: 92 us -> 86.7 us (0.942)
  the two profiles are of different devices: /device:TPU:6 before, /device:TPU:1 now
where the time goes in v8:
time: 86.7 us; the launch traced here: 86.1 us
  waiting for transfers between devices  45.9 us (53%)
  starting transfers between devices  22.6 us (26%)
  local copies, waits for them, and re-layouts  9.59 us (11%)
  Pallas kernels  5.82 us (7%)
  other arithmetic  1.85 us (2%)
    ppermute x4, waiting for transfers between devices, send_down(): return lax.ppermute(array, AXES, pairs)  29.3 us
    ppermute x9, waiting for transfers between devices, swap(): return lax.ppermute(array, AXES, pairs)  16.5 us
    ppermute x9, starting transfers between devices, swap(): return lax.ppermute(array, AXES, pairs)  13.1 us
    ppermute x4, starting transfers between devices, send_down(): return lax.ppermute(array, AXES, pairs)  9.41 us
    unnamed x26, local copies, waits for them, and re-layouts  7.66 us
    pallas_call x3, Pallas kernels, call(): pl.pallas_call(kernel, grid=(1,), out_shape=[jax.ShapeDtypeStruct(shape,...  5.82 us
  transfers between devices with their start and end apart: 14, of which 5 were waited for; matrix products, arithmetic and copies ran while one was open for 3% of the time, Pallas kernels for 7%

profile of v8, /device:TPU:1, one launch (start us, length us, event | category | flops | bytes accessed | tf_op | source)
XLA Modules:
  0.0 86.1 jit_solution(8482311978201526911)
XLA Ops:
  0.0 0.8 collective-permute-start.3
  0.9 1.0 %slice_bitcast_fusion.1 = f32[128,512]{1,0:T(8,128)S(1)} fusion(f32[2,128,1024]{2,1,0:T(8,128)} %param.4), kind=kLoop, calls=%fused_computation.5 | loop fusion | bytes 524288 | tf_op jit(solution)/shard_map/squeeze | solution.py:169
  1.9 0.0 copy-start.1
  1.9 0.0 copy-start
  1.9 0.1 pad_maximum_fusion.lead.inverse
  2.0 1.0 %copy-done.1 = f32[1024,128]{1,0:T(8,128)S(1)} copy-done((f32[1024,128]{1,0:T(8,128)S(1)}, f32[1024,128]{1,0:T(8,128)}, u32[]{:S(2)}) %copy-start.1) | copy-done | bytes 524312
  3.0 0.7 collective-permute-start
  3.7 0.9 %fusion = (f32[256,512]{1,0:T(8,128)}, f32[256,512]{1,0:T(8,128)S(1)}) fusion(f32[256,1024]{1,0:T(8,128)S(1)} %bitcast.10), kind=kLoop, calls=%fused_computation.23 | loop fusion | bytes 2097152 | tf_op jit(solution)/shard_map/slice | solution.py:177
  4.6 0.7 collective-permute-start.2
  5.3 0.7 collective-permute-start.1
  6.0 0.0 collective-permute-done.lead_other.inverse_other
  6.0 0.0 collective-permute-done.1.refs_0_
  6.0 1.9 %shard_map.37 = (f32[256,256]{1,0:T(8,128)S(1)}, f32[512,256]{1,0:T(8,128)S(1)}, f32[512,256]{1,0:T(8,128)}) custom-call(f32[128,1536]{1,0:T(8,128)S(1)} %pad_maximum_fusion.lead.inverse, f32[128,1536]{1,0:T(8,128)S(1)} %collective-permute-done.lead_other.inverse_other, f32[512,128]{1,0:T(8,128)S(1)} %get-tuple-element.26.rhs, ...), custom_call_target="tpu_custom_call" | custom-call | flops 402653184 | tf_op jit(solution)/shard_map/pallas_call | solution.py:41
  7.9 0.8 copy-done.7
  8.7 0.8 copy-done.5
  9.5 0.0 collective-permute-done.3.whole
  9.5 1.0 %copy-done.3 = f32[256,1024]{1,0:T(8,128)} copy-done((f32[256,1024]{1,0:T(8,128)}, f32[256,1024]{1,0:T(8,128)S(1)}, u32[]{:S(2)}) %copy-start.3) | copy-done | bytes 1048600
  10.5 0.7 collective-permute-start.4
  11.2 1.3 %collective-permute-start.5 = (f32[256,256]{1,0:T(8,128)S(1)}, f32[256,256]{1,0:T(8,128)}, u32[]{:S(2)}, u32[]{:S(2)}) collective-permute-start(f32[256,256]{1,0:T(8,128)S(1)} %get-tuple-element.27), channel_id=1, source_target_pairs={{0,4},{1,5},{2,6},{3,7}} | collective-permute-start | bytes 786440 | tf_op jit(solution)/shard_map/ppermute | solution.py:112
  12.5 24.7 %collective-permute-done.5.first = f32[256,256]{1,0:T(8,128)} collective-permute-done((f32[256,256]{1,0:T(8,128)S(1)}, f32[256,256]{1,0:T(8,128)}, u32[]{:S(2)}, u32[]{:S(2)}) %collective-permute-start.5) | collective-permute-done | bytes 262176 | tf_op jit(solution)/shard_map/ppermute | solution.py:112
  37.2 5.0 %collective-permute-start.9 = (f32[256,512]{1,0:T(8,128)}, f32[256,512]{1,0:T(8,128)}, u32[]{:S(2)}, u32[]{:S(2)}) collective-permute-start(f32[256,512]{1,0:T(8,128)} %copy-done.12), channel_id=1, source_target_pairs={{4,6},{5,7},{6,4},{7,5}} | collective-permute-start | bytes 1572872 | tf_op jit(solution)/shard_map/ppermute | solution.py:106
  42.2 0.0 collective-permute-done.4.got
  42.2 0.0 copy-start.9
  42.2 0.8 copy-done.9
  43.0 1.0 %copy-done.8 = f32[512,256]{1,0:T(8,128)S(1)} copy-done((f32[512,256]{1,0:T(8,128)S(1)}, f32[512,256]{1,0:T(8,128)}, u32[]{:S(2)}) %copy-start.8) | copy-done | bytes 524312
  44.0 1.0 %copy-done.10 = f32[512,256]{1,0:T(8,128)S(1)} copy-done((f32[512,256]{1,0:T(8,128)S(1)}, f32[512,256]{1,0:T(8,128)}, u32[]{:S(2)}) %copy-start.10) | copy-done | bytes 524312
  45.1 1.4 %shard_map.38 = (f32[256,256]{1,0:T(8,128)S(1)}, f32[256,256]{1,0:T(8,128)S(1)}) custom-call(s32[1]{0:T(128)} %bitcast.4.beside, f32[128,1536]{1,0:T(8,128)S(1)} %pad_maximum_fusion.lead.inverse, f32[128,1536]{1,0:T(8,128)S(1)} %collective-permute-done.lead_other.inverse_other, f32[512,256]{1,0:T(8,128)S(1)} %copy-done.8, f32[512,256]{1,0:T(8,128)S(1)} %copy-done.10, ...), custom_call_target="tpu_custom_call" | custom-call | flops 201326592 | tf_op jit(solution)/shard_map/pallas_call | solution.py:41
  46.5 5.5 %collective-permute-start.6 = (f32[256,256]{1,0:T(8,128)S(1)}, f32[256,256]{1,0:T(8,128)S(1)}, u32[]{:S(2)}, u32[]{:S(2)}) collective-permute-start(f32[256,256]{1,0:T(8,128)S(1)} %get-tuple-element.31), channel_id=1, source_target_pairs={{0,8},{1,9},{2,10},{3,11},{4,12},{5,13},{6,14},{7,15}} | collective-permute-start | bytes 786440 | tf_op jit(solution)/shard_map/ppermute | solution.py:112
  52.0 1.3 %collective-permute-start.7 = (f32[256,256]{1,0:T(8,128)S(1)}, f32[256,256]{1,0:T(8,128)S(1)}, u32[]{:S(2)}, u32[]{:S(2)}) collective-permute-start(f32[256,256]{1,0:T(8,128)S(1)} %get-tuple-element.31), channel_id=1, source_target_pairs={{0,16},{1,17},{2,18},{3,19},{4,20},{5,21},{6,22},{7,23}} | collective-permute-start | bytes 786440 | tf_op jit(solution)/shard_map/ppermute | solution.py:112
  53.3 1.3 %collective-permute-start.8 = (f32[256,256]{1,0:T(8,128)S(1)}, f32[256,256]{1,0:T(8,128)S(1)}, u32[]{:S(2)}, u32[]{:S(2)}) collective-permute-start(f32[256,256]{1,0:T(8,128)S(1)} %get-tuple-element.31), channel_id=1, source_target_pairs={{0,24},{1,25},{2,26},{3,27},{4,28},{5,29},{6,30},{7,31}} | collective-permute-start | bytes 786440 | tf_op jit(solution)/shard_map/ppermute | solution.py:112
  54.7 1.9 %collective-permute-start.11 = (f32[256,512]{1,0:T(8,128)}, f32[256,512]{1,0:T(8,128)}, u32[]{:S(2)}, u32[]{:S(2)}) collective-permute-start(f32[256,512]{1,0:T(8,128)} %get-tuple-element.39), channel_id=1, source_target_pairs={{4,6},{5,7},{6,4},{7,5},{8,10},{9,11},{10,8},{11,9},{16,18},{17,19... | collective-permute-start | bytes 1572872 | tf_op jit(solution)/shard_map/ppermute | solution.py:106
  56.6 1.6 %collective-permute-done.6 = f32[256,256]{1,0:T(8,128)S(1)} collective-permute-done((f32[256,256]{1,0:T(8,128)S(1)}, f32[256,256]{1,0:T(8,128)S(1)}, u32[]{:S(2)}, u32[]{:S(2)}) %collective-permute-start.6) | collective-permute-done | bytes 262176 | tf_op jit(solution)/shard_map/ppermute | solution.py:112
  58.2 0.0 collective-permute-done.7
  58.2 3.1 %collective-permute-done.8 = f32[256,256]{1,0:T(8,128)S(1)} collective-permute-done((f32[256,256]{1,0:T(8,128)S(1)}, f32[256,256]{1,0:T(8,128)S(1)}, u32[]{:S(2)}, u32[]{:S(2)}) %collective-permute-start.8) | collective-permute-done | bytes 262176 | tf_op jit(solution)/shard_map/ppermute | solution.py:112
  61.2 0.1 select_select_fusion.held
  61.3 0.0 copy-start.2
  61.3 0.0 collective-permute-done.9.beside
  61.3 0.1 collective-permute-start.12
  61.4 0.7 pad_maximum_fusion.1
  62.1 0.7 collective-permute-start.10
  62.8 8.7 %collective-permute-done.11.tail = f32[256,512]{1,0:T(8,128)} collective-permute-done((f32[256,512]{1,0:T(8,128)}, f32[256,512]{1,0:T(8,128)}, u32[]{:S(2)}, u32[]{:S(2)}) %collective-permute-start.11) | collective-permute-done | bytes 524320 | tf_op jit(solution)/shard_map/ppermute | solution.py:106
  71.5 0.0 collective-permute-done.12.got
  71.5 1.2 %copy-done.4 = f32[256,1024]{1,0:T(8,128)S(1)} copy-done((f32[256,1024]{1,0:T(8,128)S(1)}, f32[256,1024]{1,0:T(8,128)}, u32[]{:S(2)}) %copy-start.4) | copy-done | bytes 1048600
  72.8 2.5 %shard_map.39 = (f32[1024,128]{1,0:T(8,128)S(1)}, f32[1024,128]{1,0:T(8,128)S(1)}) custom-call(s32[1]{0:T(128)} %bitcast.5.odd, f32[256,1024]{1,0:T(8,128)S(1)} %bitcast.11, f32[256,1024]{1,0:T(8,128)S(1)} %copy-done.4, f32[256,512]{1,0:T(8,128)S(1)} %copy-done.6, f32[256,512]{1,0:T(8,128)} %collective-permute-done.9.beside, ...), custom_call_target="tpu_custom_call" | custom-call | flops 805306368 | tf_op jit(solution)/shard_map/pallas_call | solution.py:41
  75.3 1.9 %collective-permute-start.13 = (f32[1024,128]{1,0:T(8,128)S(1)}, f32[1024,128]{1,0:T(8,128)S(1)}, u32[]{:S(2)}, u32[]{:S(2)}) collective-permute-start(f32[1024,128]{1,0:T(8,128)S(1)} %get-tuple-element.42), channel_id=1, source_target_pairs={{4,5},{5,4},{6,7},{7,6},{8,9},{9,8},{10,11},{11,10},{12,13},{13,12... | collective-permute-start | bytes 1572872 | tf_op jit(solution)/shard_map/ppermute | solution.py:106
  77.2 0.0 collective-permute-done.10
  77.5 7.8 %collective-permute-done.13 = f32[1024,128]{1,0:T(8,128)S(1)} collective-permute-done((f32[1024,128]{1,0:T(8,128)S(1)}, f32[1024,128]{1,0:T(8,128)S(1)}, u32[]{:S(2)}, u32[]{:S(2)}) %collective-permute-start.13) | collective-permute-done | bytes 524320 | tf_op jit(solution)/shard_map/ppermute | solution.py:106
  85.2 0.9 %subtract_select_fusion = f32[1024,128]{1,0:T(8,128)} fusion(f32[1024,128]{1,0:T(8,128)S(1)} %select_dynamic-update-slice_fusion, f32[1024,128]{1,0:T(8,128)S(1)} %get-tuple-element.41, f32[1024,128]{1,0:T(8,128)S(1)} %collective-permute-done.13, pred[]{:T(512)S(6)} %eq.21), kind=kLoop, calls=%fused_computation.1 | loop fusion | flops 262144 | bytes 2097153 | tf_op jit(solution)/shard_map/jit(_where)/select_n | solution.py:228
  (25 shorter events, 0.2 us)
Async XLA Ops:
  0.0 1.8 %copy-start.11 = (f32[2,128,512]{2,1,0:T(8,128)S(1)}, f32[2,128,512]{2,1,0:T(8,128)}, u32[]{:S(2)}) copy-start(f32[2,128,512]{2,1,0:T(8,128)} %param.5) | copy-start | bytes 1572868
  0.0 9.5 %collective-permute-start.3 = (f32[256,1024]{1,0:T(8,128)}, f32[256,1024]{1,0:T(8,128)S(1)}, u32[]{:S(2)}, u32[]{:S(2)}) collective-permute-start(f32[256,1024]{1,0:T(8,128)} %bitcast.9), channel_id=1, source_target_pairs={{12,14},{13,15},{14,12},{15,13},{20,22},{21,23},{22,20},{23,21},{2... | collective-permute-start | bytes 3145736 | tf_op jit(solution)/shard_map/ppermute | solution.py:106
  1.9 1.0 %copy-start.1 = (f32[1024,128]{1,0:T(8,128)S(1)}, f32[1024,128]{1,0:T(8,128)}, u32[]{:S(2)}) copy-start(f32[1024,128]{1,0:T(8,128)} %base.1) | copy-start | bytes 1572868
  1.9 1.8 %copy-start = (f32[2,128,1024]{2,1,0:T(8,128)S(1)}, f32[2,128,1024]{2,1,0:T(8,128)}, u32[]{:S(2)}) copy-start(f32[2,128,1024]{2,1,0:T(8,128)} %param.4) | copy-start | bytes 3145732
  3.0 3.0 %collective-permute-start = (f32[128,1536]{1,0:T(8,128)S(1)}, f32[128,1536]{1,0:T(8,128)S(1)}, u32[]{:S(2)}, u32[]{:S(2)}) collective-permute-start(f32[128,1536]{1,0:T(8,128)S(1)} %pad_maximum_fusion.lead.inverse), channel_id=1, source_target_pairs={{0,2},{1,3},{2,0},{3,1}} | collective-permute-start | bytes 2359304 | tf_op jit(solution)/shard_map/ppermute | solution.py:106
  4.6 6.6 %copy-start.12 = (f32[256,512]{1,0:T(8,128)}, f32[256,512]{1,0:T(8,128)S(1)}, u32[]{:S(2)}) copy-start(f32[256,512]{1,0:T(8,128)S(1)} %get-tuple-element.34) | copy-start | bytes 1572868
  4.6 4.1 %collective-permute-start.2 = (f32[256,512]{1,0:T(8,128)S(1)}, f32[256,512]{1,0:T(8,128)S(1)}, u32[]{:S(2)}, u32[]{:S(2)}) collective-permute-start(f32[256,512]{1,0:T(8,128)S(1)} %get-tuple-element.34), channel_id=1, source_target_pairs={{8,10},{9,11},{10,8},{11,9},{16,18},{17,19},{18,16},{19,17},{24,26... | collective-permute-start | bytes 1572872 | tf_op jit(solution)/shard_map/ppermute | solution.py:106
  5.3 0.7 collective-permute-start.1
  7.9 0.8 copy-start.7
  8.7 0.8 copy-start.5
  9.5 1.0 %copy-start.3 = (f32[256,1024]{1,0:T(8,128)}, f32[256,1024]{1,0:T(8,128)S(1)}, u32[]{:S(2)}) copy-start(f32[256,1024]{1,0:T(8,128)S(1)} %collective-permute-done.3.whole) | copy-start | bytes 3145732
  10.5 31.7 %collective-permute-start.4 = (f32[512,256]{1,0:T(8,128)}, f32[512,256]{1,0:T(8,128)S(1)}, u32[]{:S(2)}, u32[]{:S(2)}) collective-permute-start(f32[512,256]{1,0:T(8,128)} %get-tuple-element.30), channel_id=1, source_target_pairs={{0,1},{1,0},{2,3},{3,2}} | collective-permute-start | bytes 1572872 | tf_op jit(solution)/shard_map/ppermute | solution.py:106
  11.2 26.0 %collective-permute-start.5 = (f32[256,256]{1,0:T(8,128)S(1)}, f32[256,256]{1,0:T(8,128)}, u32[]{:S(2)}, u32[]{:S(2)}) collective-permute-start(f32[256,256]{1,0:T(8,128)S(1)} %get-tuple-element.27), channel_id=1, source_target_pairs={{0,4},{1,5},{2,6},{3,7}} | collective-permute-start | bytes 786440 | tf_op jit(solution)/shard_map/ppermute | solution.py:112
  37.2 24.1 %collective-permute-start.9 = (f32[256,512]{1,0:T(8,128)}, f32[256,512]{1,0:T(8,128)}, u32[]{:S(2)}, u32[]{:S(2)}) collective-permute-start(f32[256,512]{1,0:T(8,128)} %copy-done.12), channel_id=1, source_target_pairs={{4,6},{5,7},{6,4},{7,5}} | collective-permute-start | bytes 1572872 | tf_op jit(solution)/shard_map/ppermute | solution.py:106
  42.2 0.8 copy-start.9
  43.0 1.0 %copy-start.8 = (f32[512,256]{1,0:T(8,128)S(1)}, f32[512,256]{1,0:T(8,128)}, u32[]{:S(2)}) copy-start(f32[512,256]{1,0:T(8,128)} %copy-done.7) | copy-start | bytes 1572868
  44.0 1.0 %copy-start.10 = (f32[512,256]{1,0:T(8,128)S(1)}, f32[512,256]{1,0:T(8,128)}, u32[]{:S(2)}) copy-start(f32[512,256]{1,0:T(8,128)} %copy-done.9) | copy-start | bytes 1572868
  46.5 11.7 %collective-permute-start.6 = (f32[256,256]{1,0:T(8,128)S(1)}, f32[256,256]{1,0:T(8,128)S(1)}, u32[]{:S(2)}, u32[]{:S(2)}) collective-permute-start(f32[256,256]{1,0:T(8,128)S(1)} %get-tuple-element.31), channel_id=1, source_target_pairs={{0,8},{1,9},{2,10},{3,11},{4,12},{5,13},{6,14},{7,15}} | collective-permute-start | bytes 786440 | tf_op jit(solution)/shard_map/ppermute | solution.py:112
  52.0 6.2 %collective-permute-start.7 = (f32[256,256]{1,0:T(8,128)S(1)}, f32[256,256]{1,0:T(8,128)S(1)}, u32[]{:S(2)}, u32[]{:S(2)}) collective-permute-start(f32[256,256]{1,0:T(8,128)S(1)} %get-tuple-element.31), channel_id=1, source_target_pairs={{0,16},{1,17},{2,18},{3,19},{4,20},{5,21},{6,22},{7,23}} | collective-permute-start | bytes 786440 | tf_op jit(solution)/shard_map/ppermute | solution.py:112
  53.3 7.9 %collective-permute-start.8 = (f32[256,256]{1,0:T(8,128)S(1)}, f32[256,256]{1,0:T(8,128)S(1)}, u32[]{:S(2)}, u32[]{:S(2)}) collective-permute-start(f32[256,256]{1,0:T(8,128)S(1)} %get-tuple-element.31), channel_id=1, source_target_pairs={{0,24},{1,25},{2,26},{3,27},{4,28},{5,29},{6,30},{7,31}} | collective-permute-start | bytes 786440 | tf_op jit(solution)/shard_map/ppermute | solution.py:112
  54.7 16.9 %collective-permute-start.11 = (f32[256,512]{1,0:T(8,128)}, f32[256,512]{1,0:T(8,128)}, u32[]{:S(2)}, u32[]{:S(2)}) collective-permute-start(f32[256,512]{1,0:T(8,128)} %get-tuple-element.39), channel_id=1, source_target_pairs={{4,6},{5,7},{6,4},{7,5},{8,10},{9,11},{10,8},{11,9},{16,18},{17,19... | collective-permute-start | bytes 1572872 | tf_op jit(solution)/shard_map/ppermute | solution.py:106
  61.2 10.3 %copy-start.6 = (f32[256,512]{1,0:T(8,128)S(1)}, f32[256,512]{1,0:T(8,128)}, u32[]{:S(2)}) copy-start(f32[256,512]{1,0:T(8,128)} %copy-done.5) | copy-start | bytes 1572868
  61.3 10.2 %copy-start.2 = (f32[1024,128]{1,0:T(8,128)S(1)}, f32[1024,128]{1,0:T(8,128)}, u32[]{:S(2)}) copy-start(f32[1024,128]{1,0:T(8,128)} %base.1) | copy-start | bytes 1572868
  61.3 10.2 %collective-permute-start.12 = (f32[256,256]{1,0:T(8,128)S(1)}, f32[256,256]{1,0:T(8,128)S(1)}, u32[]{:S(2)}, u32[]{:S(2)}) collective-permute-start(f32[256,256]{1,0:T(8,128)S(1)} %select_select_fusion.held), channel_id=1, source_target_pairs={{0,4},{1,5},{2,6},{3,7},{4,0},{5,1},{6,2},{7,3},{8,12},{9,13},{10,... | collective-permute-start | bytes 786440 | tf_op jit(solution)/shard_map/ppermute | solution.py:136
  62.1 15.1 %collective-permute-start.10 = (f32[512,128]{1,0:T(8,128)}, f32[512,128]{1,0:T(8,128)S(1)}, u32[]{:S(2)}, u32[]{:S(2)}) collective-permute-start(f32[512,128]{1,0:T(8,128)} %pad_maximum_fusion.1), channel_id=1, source_target_pairs={{0,1},{1,0},{2,3},{3,2}} | collective-permute-start | bytes 786440 | tf_op jit(solution)/shard_map/ppermute | solution.py:106
  71.5 1.2 %copy-start.4 = (f32[256,1024]{1,0:T(8,128)S(1)}, f32[256,1024]{1,0:T(8,128)}, u32[]{:S(2)}) copy-start(f32[256,1024]{1,0:T(8,128)} %copy-done.3) | copy-start | bytes 3145732
  75.3 9.9 %collective-permute-start.13 = (f32[1024,128]{1,0:T(8,128)S(1)}, f32[1024,128]{1,0:T(8,128)S(1)}, u32[]{:S(2)}, u32[]{:S(2)}) collective-permute-start(f32[1024,128]{1,0:T(8,128)S(1)} %get-tuple-element.42), channel_id=1, source_target_pairs={{4,5},{5,4},{6,7},{7,6},{8,9},{9,8},{10,11},{11,10},{12,13},{13,12... | collective-permute-start | bytes 1572872 | tf_op jit(solution)/shard_map/ppermute | solution.py:106

commit v9 on v8

--- a/solution.py
+++ b/solution.py
@@ -7,7 +7,7 @@
 from jax.sharding import PartitionSpec as P
 
 AXES = ("rows", "cols")
-LIMIT = 36 * 1024 * 1024
+LIMIT = 12 * 1024 * 1024
 
 
 def split(array):
@@ -114,7 +114,7 @@
     def spread(array, row_id, low, radix, have):
         digit = (row_id // low) % radix
         result = array
-        for step in range(radix - 1, 0, -1):
+        for step in range(1, radix):
             result = jnp.where(digit == step, send_down(array, step * low, have), result)
         return result, [row + step * low for row in have for step in range(radix)]
 

time: 86.7 us -> 87.7 us (1.012)
  starting transfers between devices: 22.6 us -> 23.5 us
    ppermute x4, starting transfers between devices: 9.41 us -> 10.4 us  [send_down(): return lax.ppermute(array, AXES, pairs)]
where the time goes in v9:
time: 87.7 us; the launch traced here: 87.1 us
  waiting for transfers between devices  45.9 us (52%)
  starting transfers between devices  23.5 us (27%)
  local copies, waits for them, and re-layouts  9.59 us (11%)
  Pallas kernels  5.82 us (7%)
  other arithmetic  1.86 us (2%)
    ppermute x4, waiting for transfers between devices, send_down(): return lax.ppermute(array, AXES, pairs)  29.3 us
    ppermute x9, waiting for transfers between devices, swap(): return lax.ppermute(array, AXES, pairs)  16.5 us
    ppermute x9, starting transfers between devices, swap(): return lax.ppermute(array, AXES, pairs)  13.1 us
    ppermute x4, starting transfers between devices, send_down(): return lax.ppermute(array, AXES, pairs)  10.4 us
    unnamed x26, local copies, waits for them, and re-layouts  7.66 us
    pallas_call x3, Pallas kernels, call(): pl.pallas_call(kernel, grid=(1,), out_shape=[jax.ShapeDtypeStruct(shape,...  5.82 us
  transfers between devices with their start and end apart: 14, of which 5 were waited for; matrix products, arithmetic and copies ran while one was open for 3% of the time, Pallas kernels for 7%

profile of v9, /device:TPU:1, one launch (start us, length us, event | category | flops | bytes accessed | tf_op | source)
XLA Modules:
  0.0 87.1 jit_solution(7173722101433619552)
XLA Ops:
  0.0 0.8 collective-permute-start.3
  0.9 1.0 %slice_bitcast_fusion.1 = f32[128,512]{1,0:T(8,128)S(1)} fusion(f32[2,128,1024]{2,1,0:T(8,128)} %param.4), kind=kLoop, calls=%fused_computation.5 | loop fusion | bytes 524288 | tf_op jit(solution)/shard_map/squeeze | solution.py:169
  1.9 0.0 copy-start.1
  1.9 0.0 copy-start
  1.9 0.1 pad_maximum_fusion.lead.inverse
  2.0 1.0 %copy-done.1 = f32[1024,128]{1,0:T(8,128)S(1)} copy-done((f32[1024,128]{1,0:T(8,128)S(1)}, f32[1024,128]{1,0:T(8,128)}, u32[]{:S(2)}) %copy-start.1) | copy-done | bytes 524312
  3.0 0.7 collective-permute-start
  3.7 0.9 %fusion = (f32[256,512]{1,0:T(8,128)}, f32[256,512]{1,0:T(8,128)S(1)}) fusion(f32[256,1024]{1,0:T(8,128)S(1)} %bitcast.10), kind=kLoop, calls=%fused_computation.23 | loop fusion | bytes 2097152 | tf_op jit(solution)/shard_map/slice | solution.py:177
  4.6 0.7 collective-permute-start.2
  5.3 0.7 collective-permute-start.1
  6.0 0.0 collective-permute-done.lead_other.inverse_other
  6.0 0.0 collective-permute-done.1.refs_0_
  6.0 1.9 %shard_map.37 = (f32[256,256]{1,0:T(8,128)S(1)}, f32[512,256]{1,0:T(8,128)S(1)}, f32[512,256]{1,0:T(8,128)}) custom-call(f32[128,1536]{1,0:T(8,128)S(1)} %pad_maximum_fusion.lead.inverse, f32[128,1536]{1,0:T(8,128)S(1)} %collective-permute-done.lead_other.inverse_other, f32[512,128]{1,0:T(8,128)S(1)} %get-tuple-element.26.rhs, ...), custom_call_target="tpu_custom_call" | custom-call | flops 402653184 | tf_op jit(solution)/shard_map/pallas_call | solution.py:41
  7.9 0.8 copy-done.7
  8.7 0.0 collective-permute-done.2.early
  8.7 0.8 copy-done.5
  9.5 0.0 collective-permute-done.3.whole
  9.5 1.0 %copy-done.3 = f32[256,1024]{1,0:T(8,128)} copy-done((f32[256,1024]{1,0:T(8,128)}, f32[256,1024]{1,0:T(8,128)S(1)}, u32[]{:S(2)}) %copy-start.3) | copy-done | bytes 1048600
  10.5 0.7 collective-permute-start.4
  11.2 1.3 %collective-permute-start.5 = (f32[256,256]{1,0:T(8,128)S(1)}, f32[256,256]{1,0:T(8,128)}, u32[]{:S(2)}, u32[]{:S(2)}) collective-permute-start(f32[256,256]{1,0:T(8,128)S(1)} %get-tuple-element.27), channel_id=1, source_target_pairs={{0,4},{1,5},{2,6},{3,7}} | collective-permute-start | bytes 786440 | tf_op jit(solution)/shard_map/ppermute | solution.py:112
  12.5 24.7 %collective-permute-done.5.first = f32[256,256]{1,0:T(8,128)} collective-permute-done((f32[256,256]{1,0:T(8,128)S(1)}, f32[256,256]{1,0:T(8,128)}, u32[]{:S(2)}, u32[]{:S(2)}) %collective-permute-start.5) | collective-permute-done | bytes 262176 | tf_op jit(solution)/shard_map/ppermute | solution.py:112
  37.2 5.0 %collective-permute-start.9 = (f32[256,512]{1,0:T(8,128)}, f32[256,512]{1,0:T(8,128)}, u32[]{:S(2)}, u32[]{:S(2)}) collective-permute-start(f32[256,512]{1,0:T(8,128)} %copy-done.12), channel_id=1, source_target_pairs={{4,6},{5,7},{6,4},{7,5}} | collective-permute-start | bytes 1572872 | tf_op jit(solution)/shard_map/ppermute | solution.py:106
  42.2 0.0 collective-permute-done.4.got
  42.2 0.0 copy-start.9
  42.2 0.8 copy-done.9
  43.0 1.0 %copy-done.8 = f32[512,256]{1,0:T(8,128)S(1)} copy-done((f32[512,256]{1,0:T(8,128)S(1)}, f32[512,256]{1,0:T(8,128)}, u32[]{:S(2)}) %copy-start.8) | copy-done | bytes 524312
  44.0 1.0 %copy-done.10 = f32[512,256]{1,0:T(8,128)S(1)} copy-done((f32[512,256]{1,0:T(8,128)S(1)}, f32[512,256]{1,0:T(8,128)}, u32[]{:S(2)}) %copy-start.10) | copy-done | bytes 524312
  45.1 1.4 %shard_map.38 = (f32[256,256]{1,0:T(8,128)S(1)}, f32[256,256]{1,0:T(8,128)S(1)}) custom-call(s32[1]{0:T(128)} %bitcast.4.beside, f32[128,1536]{1,0:T(8,128)S(1)} %pad_maximum_fusion.lead.inverse, f32[128,1536]{1,0:T(8,128)S(1)} %collective-permute-done.lead_other.inverse_other, f32[512,256]{1,0:T(8,128)S(1)} %copy-done.8, f32[512,256]{1,0:T(8,128)S(1)} %copy-done.10, ...), custom_call_target="tpu_custom_call" | custom-call | flops 201326592 | tf_op jit(solution)/shard_map/pallas_call | solution.py:41
  46.5 6.5 %collective-permute-start.6 = (f32[256,256]{1,0:T(8,128)S(1)}, f32[256,256]{1,0:T(8,128)S(1)}, u32[]{:S(2)}, u32[]{:S(2)}) collective-permute-start(f32[256,256]{1,0:T(8,128)S(1)} %get-tuple-element.31), channel_id=1, source_target_pairs={{0,24},{1,25},{2,26},{3,27},{4,28},{5,29},{6,30},{7,31}} | collective-permute-start | bytes 786440 | tf_op jit(solution)/shard_map/ppermute | solution.py:112
  53.0 1.3 %collective-permute-start.7 = (f32[256,256]{1,0:T(8,128)S(1)}, f32[256,256]{1,0:T(8,128)S(1)}, u32[]{:S(2)}, u32[]{:S(2)}) collective-permute-start(f32[256,256]{1,0:T(8,128)S(1)} %get-tuple-element.31), channel_id=1, source_target_pairs={{0,16},{1,17},{2,18},{3,19},{4,20},{5,21},{6,22},{7,23}} | collective-permute-start | bytes 786440 | tf_op jit(solution)/shard_map/ppermute | solution.py:112
  54.3 1.3 %collective-permute-start.8 = (f32[256,256]{1,0:T(8,128)S(1)}, f32[256,256]{1,0:T(8,128)S(1)}, u32[]{:S(2)}, u32[]{:S(2)}) collective-permute-start(f32[256,256]{1,0:T(8,128)S(1)} %get-tuple-element.31), channel_id=1, source_target_pairs={{0,8},{1,9},{2,10},{3,11},{4,12},{5,13},{6,14},{7,15}} | collective-permute-start | bytes 786440 | tf_op jit(solution)/shard_map/ppermute | solution.py:112
  55.6 1.9 %collective-permute-start.11 = (f32[256,512]{1,0:T(8,128)}, f32[256,512]{1,0:T(8,128)}, u32[]{:S(2)}, u32[]{:S(2)}) collective-permute-start(f32[256,512]{1,0:T(8,128)} %get-tuple-element.39), channel_id=1, source_target_pairs={{4,6},{5,7},{6,4},{7,5},{8,10},{9,11},{10,8},{11,9},{16,18},{17,19... | collective-permute-start | bytes 1572872 | tf_op jit(solution)/shard_map/ppermute | solution.py:106
  57.5 1.6 %collective-permute-done.6 = f32[256,256]{1,0:T(8,128)S(1)} collective-permute-done((f32[256,256]{1,0:T(8,128)S(1)}, f32[256,256]{1,0:T(8,128)S(1)}, u32[]{:S(2)}, u32[]{:S(2)}) %collective-permute-start.6) | collective-permute-done | bytes 262176 | tf_op jit(solution)/shard_map/ppermute | solution.py:112
  59.1 0.0 collective-permute-done.7
  59.1 3.1 %collective-permute-done.8 = f32[256,256]{1,0:T(8,128)S(1)} collective-permute-done((f32[256,256]{1,0:T(8,128)S(1)}, f32[256,256]{1,0:T(8,128)S(1)}, u32[]{:S(2)}, u32[]{:S(2)}) %collective-permute-start.8) | collective-permute-done | bytes 262176 | tf_op jit(solution)/shard_map/ppermute | solution.py:112
  62.2 0.1 select_select_fusion.held
  62.2 0.0 copy-start.2
  62.3 0.0 collective-permute-done.9.beside
  62.3 0.1 collective-permute-start.12
  62.3 0.7 pad_maximum_fusion.1
  63.1 0.7 collective-permute-start.10
  63.8 8.7 %collective-permute-done.11.tail = f32[256,512]{1,0:T(8,128)} collective-permute-done((f32[256,512]{1,0:T(8,128)}, f32[256,512]{1,0:T(8,128)}, u32[]{:S(2)}, u32[]{:S(2)}) %collective-permute-start.11) | collective-permute-done | bytes 524320 | tf_op jit(solution)/shard_map/ppermute | solution.py:106
  72.5 0.0 collective-permute-done.12.got
  72.5 1.2 %copy-done.4 = f32[256,1024]{1,0:T(8,128)S(1)} copy-done((f32[256,1024]{1,0:T(8,128)S(1)}, f32[256,1024]{1,0:T(8,128)}, u32[]{:S(2)}) %copy-start.4) | copy-done | bytes 1048600
  73.7 2.5 %shard_map.39 = (f32[1024,128]{1,0:T(8,128)S(1)}, f32[1024,128]{1,0:T(8,128)S(1)}) custom-call(s32[1]{0:T(128)} %bitcast.5.odd, f32[256,1024]{1,0:T(8,128)S(1)} %bitcast.11, f32[256,1024]{1,0:T(8,128)S(1)} %copy-done.4, f32[256,512]{1,0:T(8,128)S(1)} %copy-done.6, f32[256,512]{1,0:T(8,128)} %collective-permute-done.9.beside, ...), custom_call_target="tpu_custom_call" | custom-call | flops 805306368 | tf_op jit(solution)/shard_map/pallas_call | solution.py:41
  76.3 1.9 %collective-permute-start.13 = (f32[1024,128]{1,0:T(8,128)S(1)}, f32[1024,128]{1,0:T(8,128)S(1)}, u32[]{:S(2)}, u32[]{:S(2)}) collective-permute-start(f32[1024,128]{1,0:T(8,128)S(1)} %get-tuple-element.42), channel_id=1, source_target_pairs={{4,5},{5,4},{6,7},{7,6},{8,9},{9,8},{10,11},{11,10},{12,13},{13,12... | collective-permute-start | bytes 1572872 | tf_op jit(solution)/shard_map/ppermute | solution.py:106
  78.4 7.8 %collective-permute-done.13 = f32[1024,128]{1,0:T(8,128)S(1)} collective-permute-done((f32[1024,128]{1,0:T(8,128)S(1)}, f32[1024,128]{1,0:T(8,128)S(1)}, u32[]{:S(2)}, u32[]{:S(2)}) %collective-permute-start.13) | collective-permute-done | bytes 524320 | tf_op jit(solution)/shard_map/ppermute | solution.py:106
  86.2 0.9 %subtract_select_fusion = f32[1024,128]{1,0:T(8,128)} fusion(f32[1024,128]{1,0:T(8,128)S(1)} %select_dynamic-update-slice_fusion, f32[1024,128]{1,0:T(8,128)S(1)} %get-tuple-element.41, f32[1024,128]{1,0:T(8,128)S(1)} %collective-permute-done.13, pred[]{:T(512)S(6)} %eq.21), kind=kLoop, calls=%fused_computation.1 | loop fusion | flops 262144 | bytes 2097153 | tf_op jit(solution)/shard_map/jit(_where)/select_n | solution.py:228
  (25 shorter events, 0.2 us)
Async XLA Ops:
  0.0 1.8 %copy-start.11 = (f32[2,128,512]{2,1,0:T(8,128)S(1)}, f32[2,128,512]{2,1,0:T(8,128)}, u32[]{:S(2)}) copy-start(f32[2,128,512]{2,1,0:T(8,128)} %param.5) | copy-start | bytes 1572868
  0.0 9.5 %collective-permute-start.3 = (f32[256,1024]{1,0:T(8,128)}, f32[256,1024]{1,0:T(8,128)S(1)}, u32[]{:S(2)}, u32[]{:S(2)}) collective-permute-start(f32[256,1024]{1,0:T(8,128)} %bitcast.9), channel_id=1, source_target_pairs={{12,14},{13,15},{14,12},{15,13},{20,22},{21,23},{22,20},{23,21},{2... | collective-permute-start | bytes 3145736 | tf_op jit(solution)/shard_map/ppermute | solution.py:106
  1.9 1.0 %copy-start.1 = (f32[1024,128]{1,0:T(8,128)S(1)}, f32[1024,128]{1,0:T(8,128)}, u32[]{:S(2)}) copy-start(f32[1024,128]{1,0:T(8,128)} %base.1) | copy-start | bytes 1572868
  1.9 1.8 %copy-start = (f32[2,128,1024]{2,1,0:T(8,128)S(1)}, f32[2,128,1024]{2,1,0:T(8,128)}, u32[]{:S(2)}) copy-start(f32[2,128,1024]{2,1,0:T(8,128)} %param.4) | copy-start | bytes 3145732
  3.0 3.0 %collective-permute-start = (f32[128,1536]{1,0:T(8,128)S(1)}, f32[128,1536]{1,0:T(8,128)S(1)}, u32[]{:S(2)}, u32[]{:S(2)}) collective-permute-start(f32[128,1536]{1,0:T(8,128)S(1)} %pad_maximum_fusion.lead.inverse), channel_id=1, source_target_pairs={{0,2},{1,3},{2,0},{3,1}} | collective-permute-start | bytes 2359304 | tf_op jit(solution)/shard_map/ppermute | solution.py:106
  4.6 6.6 %copy-start.12 = (f32[256,512]{1,0:T(8,128)}, f32[256,512]{1,0:T(8,128)S(1)}, u32[]{:S(2)}) copy-start(f32[256,512]{1,0:T(8,128)S(1)} %get-tuple-element.34) | copy-start | bytes 1572868
  4.6 4.1 %collective-permute-start.2 = (f32[256,512]{1,0:T(8,128)S(1)}, f32[256,512]{1,0:T(8,128)S(1)}, u32[]{:S(2)}, u32[]{:S(2)}) collective-permute-start(f32[256,512]{1,0:T(8,128)S(1)} %get-tuple-element.34), channel_id=1, source_target_pairs={{8,10},{9,11},{10,8},{11,9},{16,18},{17,19},{18,16},{19,17},{24,26... | collective-permute-start | bytes 1572872 | tf_op jit(solution)/shard_map/ppermute | solution.py:106
  5.3 0.7 collective-permute-start.1
  7.9 0.8 copy-start.7
  8.7 0.8 copy-start.5
  9.5 1.0 %copy-start.3 = (f32[256,1024]{1,0:T(8,128)}, f32[256,1024]{1,0:T(8,128)S(1)}, u32[]{:S(2)}) copy-start(f32[256,1024]{1,0:T(8,128)S(1)} %collective-permute-done.3.whole) | copy-start | bytes 3145732
  10.5 31.7 %collective-permute-start.4 = (f32[512,256]{1,0:T(8,128)}, f32[512,256]{1,0:T(8,128)S(1)}, u32[]{:S(2)}, u32[]{:S(2)}) collective-permute-start(f32[512,256]{1,0:T(8,128)} %get-tuple-element.30), channel_id=1, source_target_pairs={{0,1},{1,0},{2,3},{3,2}} | collective-permute-start | bytes 1572872 | tf_op jit(solution)/shard_map/ppermute | solution.py:106
  11.2 26.0 %collective-permute-start.5 = (f32[256,256]{1,0:T(8,128)S(1)}, f32[256,256]{1,0:T(8,128)}, u32[]{:S(2)}, u32[]{:S(2)}) collective-permute-start(f32[256,256]{1,0:T(8,128)S(1)} %get-tuple-element.27), channel_id=1, source_target_pairs={{0,4},{1,5},{2,6},{3,7}} | collective-permute-start | bytes 786440 | tf_op jit(solution)/shard_map/ppermute | solution.py:112
  37.2 25.1 %collective-permute-start.9 = (f32[256,512]{1,0:T(8,128)}, f32[256,512]{1,0:T(8,128)}, u32[]{:S(2)}, u32[]{:S(2)}) collective-permute-start(f32[256,512]{1,0:T(8,128)} %copy-done.12), channel_id=1, source_target_pairs={{4,6},{5,7},{6,4},{7,5}} | collective-permute-start | bytes 1572872 | tf_op jit(solution)/shard_map/ppermute | solution.py:106
  42.2 0.8 copy-start.9
  43.0 1.0 %copy-start.8 = (f32[512,256]{1,0:T(8,128)S(1)}, f32[512,256]{1,0:T(8,128)}, u32[]{:S(2)}) copy-start(f32[512,256]{1,0:T(8,128)} %copy-done.7) | copy-start | bytes 1572868
  44.0 1.0 %copy-start.10 = (f32[512,256]{1,0:T(8,128)S(1)}, f32[512,256]{1,0:T(8,128)}, u32[]{:S(2)}) copy-start(f32[512,256]{1,0:T(8,128)} %copy-done.9) | copy-start | bytes 1572868
  46.5 12.6 %collective-permute-start.6 = (f32[256,256]{1,0:T(8,128)S(1)}, f32[256,256]{1,0:T(8,128)S(1)}, u32[]{:S(2)}, u32[]{:S(2)}) collective-permute-start(f32[256,256]{1,0:T(8,128)S(1)} %get-tuple-element.31), channel_id=1, source_target_pairs={{0,24},{1,25},{2,26},{3,27},{4,28},{5,29},{6,30},{7,31}} | collective-permute-start | bytes 786440 | tf_op jit(solution)/shard_map/ppermute | solution.py:112
  53.0 6.2 %collective-permute-start.7 = (f32[256,256]{1,0:T(8,128)S(1)}, f32[256,256]{1,0:T(8,128)S(1)}, u32[]{:S(2)}, u32[]{:S(2)}) collective-permute-start(f32[256,256]{1,0:T(8,128)S(1)} %get-tuple-element.31), channel_id=1, source_target_pairs={{0,16},{1,17},{2,18},{3,19},{4,20},{5,21},{6,22},{7,23}} | collective-permute-start | bytes 786440 | tf_op jit(solution)/shard_map/ppermute | solution.py:112
  54.3 7.9 %collective-permute-start.8 = (f32[256,256]{1,0:T(8,128)S(1)}, f32[256,256]{1,0:T(8,128)S(1)}, u32[]{:S(2)}, u32[]{:S(2)}) collective-permute-start(f32[256,256]{1,0:T(8,128)S(1)} %get-tuple-element.31), channel_id=1, source_target_pairs={{0,8},{1,9},{2,10},{3,11},{4,12},{5,13},{6,14},{7,15}} | collective-permute-start | bytes 786440 | tf_op jit(solution)/shard_map/ppermute | solution.py:112
  55.6 16.9 %collective-permute-start.11 = (f32[256,512]{1,0:T(8,128)}, f32[256,512]{1,0:T(8,128)}, u32[]{:S(2)}, u32[]{:S(2)}) collective-permute-start(f32[256,512]{1,0:T(8,128)} %get-tuple-element.39), channel_id=1, source_target_pairs={{4,6},{5,7},{6,4},{7,5},{8,10},{9,11},{10,8},{11,9},{16,18},{17,19... | collective-permute-start | bytes 1572872 | tf_op jit(solution)/shard_map/ppermute | solution.py:106
  62.2 10.3 %copy-start.6 = (f32[256,512]{1,0:T(8,128)S(1)}, f32[256,512]{1,0:T(8,128)}, u32[]{:S(2)}) copy-start(f32[256,512]{1,0:T(8,128)} %copy-done.5) | copy-start | bytes 1572868
  62.2 10.2 %copy-start.2 = (f32[1024,128]{1,0:T(8,128)S(1)}, f32[1024,128]{1,0:T(8,128)}, u32[]{:S(2)}) copy-start(f32[1024,128]{1,0:T(8,128)} %base.1) | copy-start | bytes 1572868
  62.3 10.2 %collective-permute-start.12 = (f32[256,256]{1,0:T(8,128)S(1)}, f32[256,256]{1,0:T(8,128)S(1)}, u32[]{:S(2)}, u32[]{:S(2)}) collective-permute-start(f32[256,256]{1,0:T(8,128)S(1)} %select_select_fusion.held), channel_id=1, source_target_pairs={{0,4},{1,5},{2,6},{3,7},{4,0},{5,1},{6,2},{7,3},{8,12},{9,13},{10,... | collective-permute-start | bytes 786440 | tf_op jit(solution)/shard_map/ppermute | solution.py:136
  63.1 15.1 %collective-permute-start.10 = (f32[512,128]{1,0:T(8,128)}, f32[512,128]{1,0:T(8,128)S(1)}, u32[]{:S(2)}, u32[]{:S(2)}) collective-permute-start(f32[512,128]{1,0:T(8,128)} %pad_maximum_fusion.1), channel_id=1, source_target_pairs={{0,1},{1,0},{2,3},{3,2}} | collective-permute-start | bytes 786440 | tf_op jit(solution)/shard_map/ppermute | solution.py:106
  72.5 1.2 %copy-start.4 = (f32[256,1024]{1,0:T(8,128)S(1)}, f32[256,1024]{1,0:T(8,128)}, u32[]{:S(2)}) copy-start(f32[256,1024]{1,0:T(8,128)} %copy-done.3) | copy-start | bytes 3145732
  76.3 9.9 %collective-permute-start.13 = (f32[1024,128]{1,0:T(8,128)S(1)}, f32[1024,128]{1,0:T(8,128)S(1)}, u32[]{:S(2)}, u32[]{:S(2)}) collective-permute-start(f32[1024,128]{1,0:T(8,128)S(1)} %get-tuple-element.42), channel_id=1, source_target_pairs={{4,5},{5,4},{6,7},{7,6},{8,9},{9,8},{10,11},{11,10},{12,13},{13,12... | collective-permute-start | bytes 1572872 | tf_op jit(solution)/shard_map/ppermute | solution.py:106

commit v10 on v9

--- a/solution.py
+++ b/solution.py
@@ -26,72 +26,112 @@
     return one(left_high, right_high) + (one(left_high, right_low) + one(left_low, right_high))
 
 
-def call(kernel, shapes, flops, operands, flag=None):
-    def spec(shape, place):
-        return pl.BlockSpec(shape, lambda step: place)
-
-    arrays, specs = [], []
-    for operand in operands:
-        array, shape, place = operand if isinstance(operand, tuple) else (operand, None, (0, 0))
-        arrays.append(array)
-        specs.append(spec(shape or array.shape, place))
-    if flag is not None:
-        arrays.insert(0, flag.astype(jnp.int32).reshape(1))
-        specs.insert(0, pl.BlockSpec(memory_space=pltpu.SMEM))
+def call(kernel, shapes, flops, near, far=(), flag=None, scratch=()):
+    flags = [] if flag is None else [flag.astype(jnp.int32).reshape(1)]
+    spaces = [pltpu.SMEM] * len(flags) + [pltpu.VMEM] * len(near) + [pltpu.HBM] * len(far)
     return pl.pallas_call(
         kernel,
-        grid=(1,),
         out_shape=[jax.ShapeDtypeStruct(shape, jnp.float32) for shape in shapes],
-        in_specs=specs,
-        out_specs=[spec(shape, (0, 0)) for shape in shapes],
+        in_specs=[pl.BlockSpec(memory_space=space) for space in spaces],
+        out_specs=[pl.BlockSpec(memory_space=pltpu.VMEM)] * len(shapes),
+        scratch_shapes=[pltpu.VMEM(shape, jnp.float32) for shape in scratch]
+        + [pltpu.SemaphoreType.DMA((6,))] * (1 if far else 0),
         compiler_params=pltpu.CompilerParams(vmem_limit_bytes=LIMIT),
         cost_estimate=pl.CostEstimate(flops=flops, bytes_accessed=0, transcendentals=0),
-    )(*arrays)
-
-
-def first_kernel(places, width, lead, lead_other, rhs, *refs):
-    others, (low, solved, update, shuffled) = refs[:-4], refs[-4:]
+    )(*flags, *near, *far)
+
+
+def first_kernel(places, width, row, lead, lead_other, rhs, *refs):
+    others, (low, solved, shuffled) = refs[:-3], refs[-3:]
     cands = rhs.shape[1]
-    blocks = [rhs[...]] + [other[...] for other in others]
-    blocks = jnp.concatenate(blocks, axis=1)
-    inverse = jnp.concatenate([lead[:, :width], lead_other[:, :width]], axis=0)
-    first = dot(inverse, blocks, 1)
-    solved[...] = first
-    corner = jnp.concatenate([lead[:, width : 2 * width], lead_other[:, width : 2 * width]], axis=0)
-    total = dot(corner, first, 0)
-    pieces = [total[:, at * cands : (at + 1) * cands] for at in range(len(places))]
-    pieces[0] = pieces[0] - low[...]
-    for at, place in enumerate(places):
-        update[:, at * cands : (at + 1) * cands] = pieces[at]
-        shuffled[:, at * cands : (at + 1) * cands] = pieces[place]
-
-
-def second_kernel(beside, inverse, inverse_other, update, got, first, solved, bundle):
-    both = jnp.concatenate([inverse[...], inverse_other[...]], axis=0)
-    second = dot(both, -(update[...] + got[...]), 1)
-    solved[...] = second
-    bundle[...] = jnp.where(beside[0] == 1, first[...], second)
-
-
-def rows_kernel(odd, mine, whole, early, beside, tail, base, held, got, own, send):
+
+    @pl.when(row[0] == 0)
+    def _():
+        blocks = [rhs[...]] + [other[...] for other in others]
+        blocks = jnp.concatenate(blocks, axis=1)
+        inverse = jnp.concatenate([lead[:, :width], lead_other[:, :width]], axis=0)
+        first = dot(inverse, blocks, 1)
+        solved[...] = first
+        middle = slice(width, 2 * width)
+        corner = jnp.concatenate([lead[:, middle], lead_other[:, middle]], axis=0)
+        total = dot(corner, first, 0)
+        pieces = [total[:, at * cands : (at + 1) * cands] for at in range(len(places))]
+        pieces[0] = pieces[0] - low[...]
+        for at, place in enumerate(places):
+            shuffled[:, at * cands : (at + 1) * cands] = pieces[place]
+
+
+def second_kernel(places, row, lead, lead_other, sent, got, first, solved, bundle, *refs):
+    sums, more, sems = refs
+    width = sums.shape[0]
+    cands = sums.shape[1] // len(places)
+
+    @pl.when(row[0] == 0)
+    def _():
+        copies = [
+            pltpu.make_async_copy(sent, sums, sems.at[0]),
+            pltpu.make_async_copy(got, more, sems.at[1]),
+        ]
+        for copy in copies:
+            copy.start()
+        last = slice(2 * width, 3 * width)
+        both = jnp.concatenate([lead[:, last], lead_other[:, last]], axis=0)
+        for copy in copies:
+            copy.wait()
+        rest = [sums[:, place * cands : (place + 1) * cands] for place in places]
+        second = dot(both, -(jnp.concatenate(rest, axis=1) + more[...]), 1)
+        solved[...] = second
+        bundle[...] = second
+
+    @pl.when(row[0] == 1)
+    def _():
+        copy = pltpu.make_async_copy(first, bundle, sems.at[2])
+        copy.start()
+        copy.wait()
+
+
+def rows_kernel(row, held, got, flat, whole, early, beside, tail, cross, own, send, *refs):
+    mine, other, base, sems = refs
     n_design, cands = base.shape
     depth = held.shape[0] // 2
-    is_odd = odd[0] == 1
-    first = jnp.where(is_odd, held[...], got[...])
-    second = jnp.where(is_odd, got[...], held[...])
-    solved = jnp.concatenate(
-        [first[:depth], second[:depth], first[depth:], second[depth:]], axis=0
-    )
     count = n_design // 2
-    for at, parts in enumerate(([early, beside], [tail])):
-        part = slice(at * count, (at + 1) * count)
-        other = whole[:, part]
-        for array in parts:
-            other = other + array[...]
-        factors = jnp.concatenate([mine[:, part], other], axis=0)
-        partial = dot(factors, solved, 0)
-        own[part] = base[part] - partial[:, :cands]
-        send[part] = partial[:, cands:]
+    parts = [slice(0, count), slice(count, n_design)]
+    is_odd = row[0] % 2 == 1
+
+    def fetch(at, source):
+        return pltpu.make_async_copy(source, other.at[:, parts[at]], sems.at[at])
+
+    @pl.when(row[0] > 0)
+    def _():
+        copies = []
+        for at, part in enumerate(parts):
+            copies += [
+                pltpu.make_async_copy(flat.at[:, part], mine.at[:, part], sems.at[2 + at]),
+                pltpu.make_async_copy(cross.at[part], base.at[part], sems.at[4 + at]),
+            ]
+        sources = [
+            (row[0] == 1, [beside, tail]),
+            ((row[0] > 1) & ~is_odd, [early, tail]),
+            ((row[0] > 1) & is_odd, [whole.at[:, part] for part in parts]),
+        ]
+        for at in range(2):
+            for chosen, pair in sources:
+                pl.when(chosen)(lambda at=at, pair=pair: fetch(at, pair[at]).start())
+            for copy in copies[2 * at : 2 * at + 2]:
+                copy.start()
+        first = jnp.where(is_odd, held[...], got[...])
+        second = jnp.where(is_odd, got[...], held[...])
+        solved = jnp.concatenate(
+            [first[:depth], second[:depth], first[depth:], second[depth:]], axis=0
+        )
+        for at, part in enumerate(parts):
+            fetch(at, tail).wait()
+            for copy in copies[2 * at : 2 * at + 2]:
+                copy.wait()
+            factors = jnp.concatenate([mine[:, part], other[:, part]], axis=0)
+            partial = dot(factors, solved, 0)
+            own[part] = base[part] - partial[:, :cands]
+            send[part] = partial[:, cands:]
 
 
 def make_on_device(n_rows, n_cols):
@@ -176,27 +216,31 @@
         arrived = swap(head, half, evens)
         lead_other, head, tail = lax.optimization_barrier((lead_other, head, flat[:, count:]))
 
-        first, update, shuffled = call(
-            functools.partial(first_kernel, [at ^ 1 for at in range(half)], width),
-            [(2 * depth, half * cands)] + [(width, half * cands)] * 2,
+        places = [at ^ 1 for at in range(half)]
+        first, shuffled = call(
+            functools.partial(first_kernel, places, width),
+            [(2 * depth, half * cands), (width, half * cands)],
             6 * width * half * cands * (2 * depth + 2 * depth),
             [lead, lead_other, rhs, *rhs_others, cross_kernel[width : 2 * width]],
+            flag=row_id,
         )
         shuffled, arrived, whole = lax.optimization_barrier((shuffled, arrived, whole))
-        got = swap(shuffled, 1, top)
+        sums = got = swap(shuffled, 1, top)
         bit = 2
         while bit < half:
-            update = update + got
+            update = shuffle(shuffled, 1, cands) + sums
             got = swap(shuffle(update, bit, cands), bit, top)
+            sums = sums + got
             bit *= 2
         first_beside = send_down(first, 1, top)
-        inverse = ((depth, width), (0, 2))
         second, bundle = call(
-            second_kernel,
+            functools.partial(second_kernel, places),
             [(2 * depth, half * cands)] * 2,
             6 * 2 * depth * width * half * cands,
-            [(lead, *inverse), (lead_other, *inverse), update, got, first_beside],
-            row_id == 1,
+            [lead, lead_other],
+            [shuffled, sums, first_beside],
+            row_id,
+            [(width, half * cands)] * 2,
         )
         first_beside, head = lax.optimization_barrier((first_beside, head))
         late = swap(head, half, beside)
@@ -220,13 +264,14 @@
             rows_kernel,
             [(n_design, cands), (n_design, (half - 1) * cands)],
             6 * n_design * 4 * depth * half * cands,
-            [flat, whole, arrived, late, tail, cross_kernel, *solved],
-            row_id % 2 == 1,
+            solved,
+            [flat, whole, arrived, late, tail, cross_kernel],
+            row_id,
+            [(2 * depth, n_design)] * 2 + [(n_design, cands)],
         )
         for step in range(1, half):
             fresh = fresh - swap(block(send, step - 1, cands), step, range(1, n_rows))
-        head = jnp.where(row_id == 0, top_rows, fresh[: 2 * width])
-        return jnp.concatenate([head, fresh[2 * width :]], axis=0)
+        return jnp.where(row_id == 0, top_rows, fresh)
 
     return on_device
 

time: 87.7 us -> 80.9 us (0.922)
  local copies, waits for them, and re-layouts: 9.59 us -> 4.71 us
  Pallas kernels: 5.82 us -> 3.17 us
  starting transfers between devices: 23.5 us -> 24.6 us
    unnamed x26 -> x12, local copies, waits for them, and re-layouts: 7.66 us -> 2.62 us
    pallas_call x3, Pallas kernels: 5.82 us -> 3.17 us  [call(): pl.pallas_call(kernel, out_shape=[jax.ShapeDtypeStruct(shape, jnp.float32...]
    ppermute x9, starting transfers between devices: 13.1 us -> 14.8 us  [swap(): return lax.ppermute(array, AXES, pairs)]
  transfers between devices with their start and end apart: 14 -> 14, of which waited for: 5 -> 5; matrix products, arithmetic and copies ran while one was open for 3% -> 4% of each run, Pallas kernels for 7% -> 4%
where the time goes in v10:
time: 80.9 us; the launch traced here: 80.5 us
  waiting for transfers between devices  45.8 us (57%)
  starting transfers between devices  24.6 us (30%)
  local copies, waits for them, and re-layouts  4.71 us (6%)
  Pallas kernels  3.17 us (4%)
  other arithmetic  1.85 us (2%)
    ppermute x4, waiting for transfers between devices, send_down(): return lax.ppermute(array, AXES, pairs)  28.9 us
    ppermute x9, waiting for transfers between devices, swap(): return lax.ppermute(array, AXES, pairs)  16.9 us
    ppermute x9, starting transfers between devices, swap(): return lax.ppermute(array, AXES, pairs)  14.8 us
    ppermute x4, starting transfers between devices, send_down(): return lax.ppermute(array, AXES, pairs)  9.71 us
    pallas_call x3, Pallas kernels, call(): pl.pallas_call(kernel, out_shape=[jax.ShapeDtypeStruct(shape, jnp.float32...  3.17 us
    unnamed x12, local copies, waits for them, and re-layouts  2.62 us
  transfers between devices with their start and end apart: 14, of which 5 were waited for; matrix products, arithmetic and copies ran while one was open for 4% of the time, Pallas kernels for 4%

profile of v10, /device:TPU:1, one launch (start us, length us, event | category | flops | bytes accessed | tf_op | source)
XLA Modules:
  0.0 80.5 jit_solution(4365218096168130826)
XLA Ops:
  0.0 0.0 copy-start.5
  0.0 1.8 %collective-permute-start.3 = (f32[256,1024]{1,0:T(8,128)}, f32[256,1024]{1,0:T(8,128)}, u32[]{:S(2)}, u32[]{:S(2)}) collective-permute-start(f32[256,1024]{1,0:T(8,128)} %bitcast.8), channel_id=1, source_target_pairs={{12,14},{13,15},{14,12},{15,13},{20,22},{21,23},{22,20},{23,21},{2... | collective-permute-start | bytes 3145736 | tf_op jit(solution)/shard_map/ppermute | solution.py:146
  1.8 1.0 %slice_bitcast_fusion.1 = f32[128,512]{1,0:T(8,128)S(1)} fusion(f32[2,128,1024]{2,1,0:T(8,128)} %param.4), kind=kLoop, calls=%fused_computation.5 | loop fusion | bytes 524288 | tf_op jit(solution)/shard_map/squeeze | solution.py:209
  2.8 0.0 copy-done.5
  2.8 0.0 copy-start.1
  2.8 0.0 copy-start
  2.8 0.1 pad_maximum_fusion.lead
  2.9 1.0 %copy-done.1 = f32[1024,128]{1,0:T(8,128)S(1)} copy-done((f32[1024,128]{1,0:T(8,128)S(1)}, f32[1024,128]{1,0:T(8,128)}, u32[]{:S(2)}) %copy-start.1) | copy-done | bytes 524312
  3.9 0.7 collective-permute-start
  4.6 0.0 copy-done
  4.6 1.1 %fusion = (f32[256,512]{1,0:T(8,128)}, f32[256,512]{1,0:T(8,128)}) fusion(f32[256,1024]{1,0:T(8,128)S(1)} %bitcast.9), kind=kLoop, calls=%fused_computation.23 | loop fusion | bytes 2097152 | tf_op jit(solution)/shard_map/slice | solution.py:217
  5.7 1.5 %collective-permute-start.2 = (f32[256,512]{1,0:T(8,128)}, f32[256,512]{1,0:T(8,128)}, u32[]{:S(2)}, u32[]{:S(2)}) collective-permute-start(f32[256,512]{1,0:T(8,128)} %get-tuple-element.32), channel_id=1, source_target_pairs={{8,10},{9,11},{10,8},{11,9},{16,18},{17,19},{18,16},{19,17},{24,26... | collective-permute-start | bytes 1572872 | tf_op jit(solution)/shard_map/ppermute | solution.py:146
  7.1 0.7 collective-permute-start.1
  7.8 0.0 collective-permute-done.lead_other
  7.8 0.0 collective-permute-done.1.refs_0_
  7.8 0.0 copy-start.3
  7.9 0.7 copy-done.3
  8.5 0.0 copy-start.4
  8.5 0.9 %copy-done.4 = f32[512,128]{1,0:T(8,128)S(1)} copy-done((f32[512,128]{1,0:T(8,128)S(1)}, f32[512,128]{1,0:T(8,128)}, u32[]{:S(2)}) %copy-start.4) | copy-done | bytes 262168
  9.5 0.0 collective-permute-done.2.early
  9.5 0.0 collective-permute-done.3.whole
  9.5 0.7 collective-permute-start.4
  10.2 1.3 %collective-permute-start.5 = (f32[256,256]{1,0:T(8,128)S(1)}, f32[256,256]{1,0:T(8,128)S(1)}, u32[]{:S(2)}, u32[]{:S(2)}) collective-permute-start(f32[256,256]{1,0:T(8,128)S(1)} %get-tuple-element.26), channel_id=1, source_target_pairs={{0,4},{1,5},{2,6},{3,7}} | collective-permute-start | bytes 786440 | tf_op jit(solution)/shard_map/ppermute | solution.py:152
  11.5 24.8 %collective-permute-done.5.first = f32[256,256]{1,0:T(8,128)S(1)} collective-permute-done((f32[256,256]{1,0:T(8,128)S(1)}, f32[256,256]{1,0:T(8,128)S(1)}, u32[]{:S(2)}, u32[]{:S(2)}) %collective-permute-start.5) | collective-permute-done | bytes 262176 | tf_op jit(solution)/shard_map/ppermute | solution.py:152
  36.3 5.0 %collective-permute-start.9 = (f32[256,512]{1,0:T(8,128)}, f32[256,512]{1,0:T(8,128)}, u32[]{:S(2)}, u32[]{:S(2)}) collective-permute-start(f32[256,512]{1,0:T(8,128)} %get-tuple-element.32), channel_id=1, source_target_pairs={{4,6},{5,7},{6,4},{7,5}} | collective-permute-start | bytes 1572872 | tf_op jit(solution)/shard_map/ppermute | solution.py:146
  41.3 0.0 collective-permute-done.4.got
  41.3 0.1 shard_map.38
  41.4 5.8 %collective-permute-start.6 = (f32[256,256]{1,0:T(8,128)S(1)}, f32[256,256]{1,0:T(8,128)S(1)}, u32[]{:S(2)}, u32[]{:S(2)}) collective-permute-start(f32[256,256]{1,0:T(8,128)S(1)} %get-tuple-element.29), channel_id=1, source_target_pairs={{0,24},{1,25},{2,26},{3,27},{4,28},{5,29},{6,30},{7,31}} | collective-permute-start | bytes 786440 | tf_op jit(solution)/shard_map/ppermute | solution.py:152
  47.2 1.3 %collective-permute-start.7 = (f32[256,256]{1,0:T(8,128)S(1)}, f32[256,256]{1,0:T(8,128)S(1)}, u32[]{:S(2)}, u32[]{:S(2)}) collective-permute-start(f32[256,256]{1,0:T(8,128)S(1)} %get-tuple-element.29), channel_id=1, source_target_pairs={{0,16},{1,17},{2,18},{3,19},{4,20},{5,21},{6,22},{7,23}} | collective-permute-start | bytes 786440 | tf_op jit(solution)/shard_map/ppermute | solution.py:152
  48.5 1.3 %collective-permute-start.8 = (f32[256,256]{1,0:T(8,128)S(1)}, f32[256,256]{1,0:T(8,128)S(1)}, u32[]{:S(2)}, u32[]{:S(2)}) collective-permute-start(f32[256,256]{1,0:T(8,128)S(1)} %get-tuple-element.29), channel_id=1, source_target_pairs={{0,8},{1,9},{2,10},{3,11},{4,12},{5,13},{6,14},{7,15}} | collective-permute-start | bytes 786440 | tf_op jit(solution)/shard_map/ppermute | solution.py:152
  49.9 1.9 %collective-permute-start.12 = (f32[256,512]{1,0:T(8,128)}, f32[256,512]{1,0:T(8,128)S(1)}, u32[]{:S(2)}, u32[]{:S(2)}) collective-permute-start(f32[256,512]{1,0:T(8,128)} %get-tuple-element.38), channel_id=1, source_target_pairs={{4,6},{5,7},{6,4},{7,5},{8,10},{9,11},{10,8},{11,9},{16,18},{17,19... | collective-permute-start | bytes 1572872 | tf_op jit(solution)/shard_map/ppermute | solution.py:146
  51.8 1.3 %collective-permute-done.6 = f32[256,256]{1,0:T(8,128)S(1)} collective-permute-done((f32[256,256]{1,0:T(8,128)S(1)}, f32[256,256]{1,0:T(8,128)S(1)}, u32[]{:S(2)}, u32[]{:S(2)}) %collective-permute-start.6) | collective-permute-done | bytes 262176 | tf_op jit(solution)/shard_map/ppermute | solution.py:152
  53.1 0.0 collective-permute-done.7
  53.1 2.8 %collective-permute-done.8 = f32[256,256]{1,0:T(8,128)S(1)} collective-permute-done((f32[256,256]{1,0:T(8,128)S(1)}, f32[256,256]{1,0:T(8,128)S(1)}, u32[]{:S(2)}, u32[]{:S(2)}) %collective-permute-start.8) | collective-permute-done | bytes 262176 | tf_op jit(solution)/shard_map/ppermute | solution.py:152
  55.9 0.1 select_select_fusion.held
  56.0 0.0 copy-start.2
  56.0 0.0 collective-permute-done.9.beside
  56.0 0.1 collective-permute-start.11
  56.1 0.7 pad_maximum_fusion.1
  56.8 0.7 collective-permute-start.10
  57.5 9.1 %collective-permute-done.12.tail = f32[256,512]{1,0:T(8,128)S(1)} collective-permute-done((f32[256,512]{1,0:T(8,128)}, f32[256,512]{1,0:T(8,128)S(1)}, u32[]{:S(2)}, u32[]{:S(2)}) %collective-permute-start.12) | collective-permute-done | bytes 524320 | tf_op jit(solution)/shard_map/ppermute | solution.py:146
  66.6 0.0 collective-permute-done.11.got
  66.6 0.0 copy-done.2
  66.6 3.1 %shard_map.39 = (f32[1024,128]{1,0:T(8,128)S(1)}, f32[1024,128]{1,0:T(8,128)S(1)}) custom-call(s32[1]{0:T(128)} %bitcast.row, f32[256,256]{1,0:T(8,128)S(1)} %select_select_fusion.held, f32[256,256]{1,0:T(8,128)S(1)} %collective-permute-done.11.got, f32[256,1024]{1,0:T(8,128)S(1)} %bitcast.10, f32[256,1024]{1,0:T(8,128)} %collective-permute-done.3.whole, ...), custom_call_target="tpu_custom_call" | custom-call | flops 805306368 | tf_op jit(solution)/shard_map/pallas_call | solution.py:32
  69.7 1.9 %collective-permute-start.13 = (f32[1024,128]{1,0:T(8,128)S(1)}, f32[1024,128]{1,0:T(8,128)S(1)}, u32[]{:S(2)}, u32[]{:S(2)}) collective-permute-start(f32[1024,128]{1,0:T(8,128)S(1)} %get-tuple-element.40), channel_id=1, source_target_pairs={{4,5},{5,4},{6,7},{7,6},{8,9},{9,8},{10,11},{11,10},{12,13},{13,12... | collective-permute-start | bytes 1572872 | tf_op jit(solution)/shard_map/ppermute | solution.py:146
  71.6 0.0 collective-permute-done.10
  71.8 7.8 %collective-permute-done.13 = f32[1024,128]{1,0:T(8,128)S(1)} collective-permute-done((f32[1024,128]{1,0:T(8,128)S(1)}, f32[1024,128]{1,0:T(8,128)S(1)}, u32[]{:S(2)}, u32[]{:S(2)}) %collective-permute-start.13) | collective-permute-done | bytes 524320 | tf_op jit(solution)/shard_map/ppermute | solution.py:146
  79.6 0.9 %subtract_select_fusion = f32[1024,128]{1,0:T(8,128)} fusion(f32[1024,128]{1,0:T(8,128)S(1)} %select_dynamic-update-slice_fusion, f32[1024,128]{1,0:T(8,128)S(1)} %get-tuple-element.39, f32[1024,128]{1,0:T(8,128)S(1)} %collective-permute-done.13, pred[]{:T(512)S(6)} %eq.14), kind=kLoop, calls=%fused_computation.1 | loop fusion | flops 262144 | bytes 2097153 | tf_op jit(solution)/shard_map/jit(_where)/select_n | solution.py:274
  (11 shorter events, 0.2 us)
Async XLA Ops:
  0.0 2.8 %copy-start.5 = (f32[2,128,512]{2,1,0:T(8,128)S(1)}, f32[2,128,512]{2,1,0:T(8,128)}, u32[]{:S(2)}) copy-start(f32[2,128,512]{2,1,0:T(8,128)} %param.5) | copy-start | bytes 1572868
  0.0 9.5 %collective-permute-start.3 = (f32[256,1024]{1,0:T(8,128)}, f32[256,1024]{1,0:T(8,128)}, u32[]{:S(2)}, u32[]{:S(2)}) collective-permute-start(f32[256,1024]{1,0:T(8,128)} %bitcast.8), channel_id=1, source_target_pairs={{12,14},{13,15},{14,12},{15,13},{20,22},{21,23},{22,20},{23,21},{2... | collective-permute-start | bytes 3145736 | tf_op jit(solution)/shard_map/ppermute | solution.py:146
  2.8 1.0 %copy-start.1 = (f32[1024,128]{1,0:T(8,128)S(1)}, f32[1024,128]{1,0:T(8,128)}, u32[]{:S(2)}) copy-start(f32[1024,128]{1,0:T(8,128)} %cross.1) | copy-start | bytes 1572868
  2.8 1.8 %copy-start = (f32[2,128,1024]{2,1,0:T(8,128)S(1)}, f32[2,128,1024]{2,1,0:T(8,128)}, u32[]{:S(2)}) copy-start(f32[2,128,1024]{2,1,0:T(8,128)} %param.4) | copy-start | bytes 3145732
  3.9 3.9 %collective-permute-start = (f32[128,1536]{1,0:T(8,128)S(1)}, f32[128,1536]{1,0:T(8,128)S(1)}, u32[]{:S(2)}, u32[]{:S(2)}) collective-permute-start(f32[128,1536]{1,0:T(8,128)S(1)} %pad_maximum_fusion.lead), channel_id=1, source_target_pairs={{0,2},{1,3},{2,0},{3,1}} | collective-permute-start | bytes 2359304 | tf_op jit(solution)/shard_map/ppermute | solution.py:146
  5.7 3.8 %collective-permute-start.2 = (f32[256,512]{1,0:T(8,128)}, f32[256,512]{1,0:T(8,128)}, u32[]{:S(2)}, u32[]{:S(2)}) collective-permute-start(f32[256,512]{1,0:T(8,128)} %get-tuple-element.32), channel_id=1, source_target_pairs={{8,10},{9,11},{10,8},{11,9},{16,18},{17,19},{18,16},{19,17},{24,26... | collective-permute-start | bytes 1572872 | tf_op jit(solution)/shard_map/ppermute | solution.py:146
  7.1 0.7 collective-permute-start.1
  7.8 0.7 copy-start.3
  8.5 0.9 %copy-start.4 = (f32[512,128]{1,0:T(8,128)S(1)}, f32[512,128]{1,0:T(8,128)}, u32[]{:S(2)}) copy-start(f32[512,128]{1,0:T(8,128)} %copy-done.3) | copy-start | bytes 786436
  9.5 31.8 %collective-permute-start.4 = (f32[512,256]{1,0:T(8,128)S(1)}, f32[512,256]{1,0:T(8,128)S(1)}, u32[]{:S(2)}, u32[]{:S(2)}) collective-permute-start(f32[512,256]{1,0:T(8,128)S(1)} %get-tuple-element.28.sent), channel_id=1, source_target_pairs={{0,1},{1,0},{2,3},{3,2}} | collective-permute-start | bytes 1572872 | tf_op jit(solution)/shard_map/ppermute | solution.py:146
  10.2 26.1 %collective-permute-start.5 = (f32[256,256]{1,0:T(8,128)S(1)}, f32[256,256]{1,0:T(8,128)S(1)}, u32[]{:S(2)}, u32[]{:S(2)}) collective-permute-start(f32[256,256]{1,0:T(8,128)S(1)} %get-tuple-element.26), channel_id=1, source_target_pairs={{0,4},{1,5},{2,6},{3,7}} | collective-permute-start | bytes 786440 | tf_op jit(solution)/shard_map/ppermute | solution.py:152
  36.3 19.7 %collective-permute-start.9 = (f32[256,512]{1,0:T(8,128)}, f32[256,512]{1,0:T(8,128)}, u32[]{:S(2)}, u32[]{:S(2)}) collective-permute-start(f32[256,512]{1,0:T(8,128)} %get-tuple-element.32), channel_id=1, source_target_pairs={{4,6},{5,7},{6,4},{7,5}} | collective-permute-start | bytes 1572872 | tf_op jit(solution)/shard_map/ppermute | solution.py:146
  41.4 11.7 %collective-permute-start.6 = (f32[256,256]{1,0:T(8,128)S(1)}, f32[256,256]{1,0:T(8,128)S(1)}, u32[]{:S(2)}, u32[]{:S(2)}) collective-permute-start(f32[256,256]{1,0:T(8,128)S(1)} %get-tuple-element.29), channel_id=1, source_target_pairs={{0,24},{1,25},{2,26},{3,27},{4,28},{5,29},{6,30},{7,31}} | collective-permute-start | bytes 786440 | tf_op jit(solution)/shard_map/ppermute | solution.py:152
  47.2 5.9 %collective-permute-start.7 = (f32[256,256]{1,0:T(8,128)S(1)}, f32[256,256]{1,0:T(8,128)S(1)}, u32[]{:S(2)}, u32[]{:S(2)}) collective-permute-start(f32[256,256]{1,0:T(8,128)S(1)} %get-tuple-element.29), channel_id=1, source_target_pairs={{0,16},{1,17},{2,18},{3,19},{4,20},{5,21},{6,22},{7,23}} | collective-permute-start | bytes 786440 | tf_op jit(solution)/shard_map/ppermute | solution.py:152
  48.5 7.4 %collective-permute-start.8 = (f32[256,256]{1,0:T(8,128)S(1)}, f32[256,256]{1,0:T(8,128)S(1)}, u32[]{:S(2)}, u32[]{:S(2)}) collective-permute-start(f32[256,256]{1,0:T(8,128)S(1)} %get-tuple-element.29), channel_id=1, source_target_pairs={{0,8},{1,9},{2,10},{3,11},{4,12},{5,13},{6,14},{7,15}} | collective-permute-start | bytes 786440 | tf_op jit(solution)/shard_map/ppermute | solution.py:152
  49.9 16.8 %collective-permute-start.12 = (f32[256,512]{1,0:T(8,128)}, f32[256,512]{1,0:T(8,128)S(1)}, u32[]{:S(2)}, u32[]{:S(2)}) collective-permute-start(f32[256,512]{1,0:T(8,128)} %get-tuple-element.38), channel_id=1, source_target_pairs={{4,6},{5,7},{6,4},{7,5},{8,10},{9,11},{10,8},{11,9},{16,18},{17,19... | collective-permute-start | bytes 1572872 | tf_op jit(solution)/shard_map/ppermute | solution.py:146
  56.0 10.6 %copy-start.2 = (f32[1024,128]{1,0:T(8,128)S(1)}, f32[1024,128]{1,0:T(8,128)}, u32[]{:S(2)}) copy-start(f32[1024,128]{1,0:T(8,128)} %cross.1) | copy-start | bytes 1572868
  56.0 10.6 %collective-permute-start.11 = (f32[256,256]{1,0:T(8,128)S(1)}, f32[256,256]{1,0:T(8,128)S(1)}, u32[]{:S(2)}, u32[]{:S(2)}) collective-permute-start(f32[256,256]{1,0:T(8,128)S(1)} %select_select_fusion.held), channel_id=1, source_target_pairs={{0,4},{1,5},{2,6},{3,7},{4,0},{5,1},{6,2},{7,3},{8,12},{9,13},{10,... | collective-permute-start | bytes 786440 | tf_op jit(solution)/shard_map/ppermute | solution.py:176
  56.8 14.8 %collective-permute-start.10 = (f32[512,128]{1,0:T(8,128)}, f32[512,128]{1,0:T(8,128)S(1)}, u32[]{:S(2)}, u32[]{:S(2)}) collective-permute-start(f32[512,128]{1,0:T(8,128)} %pad_maximum_fusion.1), channel_id=1, source_target_pairs={{0,1},{1,0},{2,3},{3,2}} | collective-permute-start | bytes 786440 | tf_op jit(solution)/shard_map/ppermute | solution.py:146
  69.7 9.9 %collective-permute-start.13 = (f32[1024,128]{1,0:T(8,128)S(1)}, f32[1024,128]{1,0:T(8,128)S(1)}, u32[]{:S(2)}, u32[]{:S(2)}) collective-permute-start(f32[1024,128]{1,0:T(8,128)S(1)} %get-tuple-element.40), channel_id=1, source_target_pairs={{4,5},{5,4},{6,7},{7,6},{8,9},{9,8},{10,11},{11,10},{12,13},{13,12... | collective-permute-start | bytes 1572872 | tf_op jit(solution)/shard_map/ppermute | solution.py:146

commit v11 on v10

--- a/solution.py
+++ b/solution.py
@@ -42,13 +42,20 @@
 
 
 def first_kernel(places, width, row, lead, lead_other, rhs, *refs):
-    others, (low, solved, shuffled) = refs[:-3], refs[-3:]
+    others, (solved, shuffled, *held, sems) = refs[: len(places) - 1], refs[len(places) - 1 :]
     cands = rhs.shape[1]
 
     @pl.when(row[0] == 0)
     def _():
-        blocks = [rhs[...]] + [other[...] for other in others]
-        blocks = jnp.concatenate(blocks, axis=1)
+        copies = [
+            pltpu.make_async_copy(other.at[:width], place, sems.at[at])
+            for at, (other, place) in enumerate(zip(others, held))
+        ]
+        for copy in copies:
+            copy.start()
+        for copy in copies:
+            copy.wait()
+        blocks = jnp.concatenate([rhs[:width]] + [place[...] for place in held], axis=1)
         inverse = jnp.concatenate([lead[:, :width], lead_other[:, :width]], axis=0)
         first = dot(inverse, blocks, 1)
         solved[...] = first
@@ -56,12 +63,12 @@
         corner = jnp.concatenate([lead[:, middle], lead_other[:, middle]], axis=0)
         total = dot(corner, first, 0)
         pieces = [total[:, at * cands : (at + 1) * cands] for at in range(len(places))]
-        pieces[0] = pieces[0] - low[...]
+        pieces[0] = pieces[0] - rhs[middle]
         for at, place in enumerate(places):
             shuffled[:, at * cands : (at + 1) * cands] = pieces[place]
 
 
-def second_kernel(places, row, lead, lead_other, sent, got, first, solved, bundle, *refs):
+def second_kernel(places, row, inverse, inverse_other, sent, got, first, solved, bundle, *refs):
     sums, more, sems = refs
     width = sums.shape[0]
     cands = sums.shape[1] // len(places)
@@ -74,8 +81,7 @@
         ]
         for copy in copies:
             copy.start()
-        last = slice(2 * width, 3 * width)
-        both = jnp.concatenate([lead[:, last], lead_other[:, last]], axis=0)
+        both = jnp.concatenate([inverse[...], inverse_other[...]], axis=0)
         for copy in copies:
             copy.wait()
         rest = [sums[:, place * cands : (place + 1) * cands] for place in places]
@@ -94,7 +100,7 @@
     mine, other, base, sems = refs
     n_design, cands = base.shape
     depth = held.shape[0] // 2
-    count = n_design // 2
+    count = early.shape[1]
     parts = [slice(0, count), slice(count, n_design)]
     is_odd = row[0] % 2 == 1
 
@@ -110,7 +116,7 @@
                 pltpu.make_async_copy(cross.at[part], base.at[part], sems.at[4 + at]),
             ]
         sources = [
-            (row[0] == 1, [beside, tail]),
+            (row[0] == 1, [beside.at[:, parts[0]], tail]),
             ((row[0] > 1) & ~is_odd, [early, tail]),
             ((row[0] > 1) & is_odd, [whole.at[:, part] for part in parts]),
         ]
@@ -125,7 +131,7 @@
             [first[:depth], second[:depth], first[depth:], second[depth:]], axis=0
         )
         for at, part in enumerate(parts):
-            fetch(at, tail).wait()
+            fetch(at, whole.at[:, part]).wait()
             for copy in copies[2 * at : 2 * at + 2]:
                 copy.wait()
             factors = jnp.concatenate([mine[:, part], other[:, part]], axis=0)
@@ -199,31 +205,36 @@
         width = block_inverses.shape[2]
         depth = block_inverses.shape[1]
         n_design, cands = cross_kernel.shape
-        count = n_design // 2
+        count = n_design * 3 // 8
         top = [0]
         beside = [1]
         evens, odds = range(2, n_rows, 2), range(3, n_rows, 2)
         flat = factor_panels.reshape(2 * depth, n_design)
 
         lead = jnp.concatenate(
-            [block_inverses[0], factor_panels[0, :, width : 2 * width], block_inverses[1]], axis=1
-        )
-        lead, rhs = lax.optimization_barrier((lead, cross_kernel[:width]))
+            [block_inverses[0], factor_panels[0, :, width : 2 * width]], axis=1
+        )
+        lead, rhs = lax.optimization_barrier((lead, cross_kernel))
         lead_other = swap(lead, half, top)
         rhs_others = [swap(rhs, step, top) for step in range(1, half)]
         whole = swap(flat, half, odds)
-        head = flat[:, :count]
-        arrived = swap(head, half, evens)
-        lead_other, head, tail = lax.optimization_barrier((lead_other, head, flat[:, count:]))
+        arrived = swap(flat[:, :count], half, evens)
+        lead_other, head, tail, inverse = lax.optimization_barrier(
+            (lead_other, flat[:, : n_design // 2], flat[:, count:], block_inverses[1])
+        )
 
         places = [at ^ 1 for at in range(half)]
         first, shuffled = call(
             functools.partial(first_kernel, places, width),
             [(2 * depth, half * cands), (width, half * cands)],
             6 * width * half * cands * (2 * depth + 2 * depth),
-            [lead, lead_other, rhs, *rhs_others, cross_kernel[width : 2 * width]],
-            flag=row_id,
-        )
+            [lead, lead_other, rhs],
+            rhs_others,
+            row_id,
+            [(width, cands)] * len(rhs_others),
+        )
+        first, inverse = lax.optimization_barrier((first, inverse))
+        inverse_other = swap(inverse, half, top)
         shuffled, arrived, whole = lax.optimization_barrier((shuffled, arrived, whole))
         sums = got = swap(shuffled, 1, top)
         bit = 2
@@ -237,7 +248,7 @@
             functools.partial(second_kernel, places),
             [(2 * depth, half * cands)] * 2,
             6 * 2 * depth * width * half * cands,
-            [lead, lead_other],
+            [inverse, inverse_other],
             [shuffled, sums, first_beside],
             row_id,
             [(width, half * cands)] * 2,

time: 80.9 us -> 85.6 us (1.058)
  the two profiles are of different devices: /device:TPU:1 before, /device:TPU:2 now
where the time goes in v11:
time: 85.6 us; the launch traced here: 84.7 us
  waiting for transfers between devices  44.5 us (52%)
  starting transfers between devices  19.8 us (23%)
  other arithmetic  9.77 us (11%)
  local copies, waits for them, and re-layouts  5.67 us (7%)
  Pallas kernels  4.62 us (5%)
    ppermute x10, waiting for transfers between devices, swap(): return lax.ppermute(array, AXES, pairs)  24.2 us
    ppermute x4, waiting for transfers between devices, send_down(): return lax.ppermute(array, AXES, pairs)  20.3 us
    ppermute x10, starting transfers between devices, swap(): return lax.ppermute(array, AXES, pairs)  15.1 us
    unnamed x7, other arithmetic  6.23 us
    ppermute x4, starting transfers between devices, send_down(): return lax.ppermute(array, AXES, pairs)  4.7 us
    pallas_call x3, Pallas kernels, call(): pl.pallas_call(kernel, out_shape=[jax.ShapeDtypeStruct(shape, jnp.float32...  4.62 us
    unnamed x10, local copies, waits for them, and re-layouts  2.08 us
  transfers between devices with their start and end apart: 15, of which 3 were waited for; matrix products, arithmetic and copies ran while one was open for 15% of the time, Pallas kernels for 5%

profile of v11, /device:TPU:2, one launch (start us, length us, event | category | flops | bytes accessed | tf_op | source)
XLA Modules:
  0.0 84.7 jit_solution(351615071447980431)
XLA Ops:
  0.0 1.8 %collective-permute-start.4 = (f32[256,1024]{1,0:T(8,128)}, f32[256,1024]{1,0:T(8,128)}, u32[]{:S(2)}, u32[]{:S(2)}) collective-permute-start(f32[256,1024]{1,0:T(8,128)} %bitcast.8), channel_id=1, source_target_pairs={{12,14},{13,15},{14,12},{15,13},{20,22},{21,23},{22,20},{23,21},{2... | collective-permute-start | bytes 3145736 | tf_op jit(solution)/shard_map/ppermute | solution.py:152
  1.8 1.0 %slice_bitcast_fusion.1 = f32[128,512]{1,0:T(8,128)S(1)} fusion(f32[2,128,1024]{2,1,0:T(8,128)} %param.4), kind=kLoop, calls=%fused_computation.5 | loop fusion | bytes 524288 | tf_op jit(solution)/shard_map/squeeze | solution.py:215
  2.8 0.0 copy-start
  2.8 0.0 copy-start.1
  2.9 0.8 collective-permute-start
  3.7 0.2 copy-done.1
  3.9 0.7 collective-permute-start.1
  4.6 0.8 slice.71
  5.5 4.5 %collective-permute-start.3 = (f32[256,384]{1,0:T(8,128)}, f32[256,384]{1,0:T(8,128)}, u32[]{:S(2)}, u32[]{:S(2)}) collective-permute-start(f32[256,384]{1,0:T(8,128)} %slice.71), channel_id=1, source_target_pairs={{8,10},{9,11},{10,8},{11,9},{16,18},{17,19},{18,16},{19,17},{24,26... | collective-permute-start | bytes 1179656 | tf_op jit(solution)/shard_map/ppermute | solution.py:152
  10.0 0.9 %slice.70 = f32[256,640]{1,0:T(8,128)} slice(f32[256,1024]{1,0:T(8,128)S(1)} %bitcast.10), slice={[0:256], [384:1024]} | slice | bytes 1310720 | tf_op jit(solution)/shard_map/slice | solution.py:223
  10.9 0.8 slice.69
  11.7 0.8 copy-done.2
  12.5 1.0 %copy-done.3 = f32[1024,128]{1,0:T(8,128)S(1)} copy-done((f32[1024,128]{1,0:T(8,128)S(1)}, f32[1024,128]{1,0:T(8,128)}, u32[]{:S(2)}) %copy-start.3) | copy-done | bytes 524312
  13.6 0.1 shard_map.37
  13.6 17.1 %collective-permute-done.3.early = f32[256,384]{1,0:T(8,128)} collective-permute-done((f32[256,384]{1,0:T(8,128)}, f32[256,384]{1,0:T(8,128)}, u32[]{:S(2)}, u32[]{:S(2)}) %collective-permute-start.3) | collective-permute-done | bytes 393248 | tf_op jit(solution)/shard_map/ppermute | solution.py:152
  30.7 0.0 collective-permute-done.4.whole
  30.7 0.7 collective-permute-start.5
  31.4 0.7 collective-permute-start.6
  32.1 0.7 collective-permute-start.2
  32.8 0.0 collective-permute-done.6.first
  32.8 0.7 collective-permute-start.10
  33.5 0.0 collective-permute-done.2.inverse_other
  33.5 0.0 collective-permute-done.5.got
  33.5 0.8 shard_map.38
  34.3 1.4 %collective-permute-start.7 = (f32[256,256]{1,0:T(8,128)}, f32[256,256]{1,0:T(8,128)}, u32[]{:S(2)}, u32[]{:S(2)}) collective-permute-start(f32[256,256]{1,0:T(8,128)} %get-tuple-element.35), channel_id=1, source_target_pairs={{0,24},{1,25},{2,26},{3,27},{4,28},{5,29},{6,30},{7,31}} | collective-permute-start | bytes 786440 | tf_op jit(solution)/shard_map/ppermute | solution.py:158
  35.7 1.4 %collective-permute-start.8 = (f32[256,256]{1,0:T(8,128)}, f32[256,256]{1,0:T(8,128)}, u32[]{:S(2)}, u32[]{:S(2)}) collective-permute-start(f32[256,256]{1,0:T(8,128)} %get-tuple-element.35), channel_id=1, source_target_pairs={{0,16},{1,17},{2,18},{3,19},{4,20},{5,21},{6,22},{7,23}} | collective-permute-start | bytes 786440 | tf_op jit(solution)/shard_map/ppermute | solution.py:158
  37.0 1.3 %collective-permute-start.9 = (f32[256,256]{1,0:T(8,128)}, f32[256,256]{1,0:T(8,128)}, u32[]{:S(2)}, u32[]{:S(2)}) collective-permute-start(f32[256,256]{1,0:T(8,128)} %get-tuple-element.35), channel_id=1, source_target_pairs={{0,8},{1,9},{2,10},{3,11},{4,12},{5,13},{6,14},{7,15}} | collective-permute-start | bytes 786440 | tf_op jit(solution)/shard_map/ppermute | solution.py:158
  38.3 1.9 %collective-permute-start.13 = (f32[256,640]{1,0:T(8,128)}, f32[256,640]{1,0:T(8,128)S(1)}, u32[]{:S(2)}, u32[]{:S(2)}) collective-permute-start(f32[256,640]{1,0:T(8,128)} %slice.70), channel_id=1, source_target_pairs={{4,6},{5,7},{6,4},{7,5},{8,10},{9,11},{10,8},{11,9},{16,18},{17,19... | collective-permute-start | bytes 1966088 | tf_op jit(solution)/shard_map/ppermute | solution.py:152
  40.3 0.0 collective-permute-done.8
  40.3 20.3 %collective-permute-done.9 = f32[256,256]{1,0:T(8,128)} collective-permute-done((f32[256,256]{1,0:T(8,128)}, f32[256,256]{1,0:T(8,128)}, u32[]{:S(2)}, u32[]{:S(2)}) %collective-permute-start.9) | collective-permute-done | bytes 262176 | tf_op jit(solution)/shard_map/ppermute | solution.py:158
  60.6 1.0 %select_select_fusion.held = f32[256,256]{1,0:T(8,128)S(1)} fusion(f32[256,256]{1,0:T(8,128)} %collective-permute-done.7, f32[256,256]{1,0:T(8,128)} %collective-permute-done.8, f32[256,256]{1,0:T(8,128)} %collective-permute-done.9, f32[256,256]{1,0:T(8,128)} %get-tuple-element.35, pred[]{:T(512)S(6)} %eq.17, pred[]{:T(512)S(6)} %eq.16, pred[]{:T(512)S(6)} %eq.15), kind=kLoop, calls=%fused_computation.3 | loop fusion | flops 196608 | bytes 1310723 | tf_op jit(solution)/shard_map/jit(_where)/select_n | solution.py:164
  61.6 0.1 collective-permute-start.12
  61.7 0.7 pad_maximum_fusion.1
  62.4 1.4 %collective-permute-start.11 = (f32[512,128]{1,0:T(8,128)}, f32[512,128]{1,0:T(8,128)}, u32[]{:S(2)}, u32[]{:S(2)}) collective-permute-start(f32[512,128]{1,0:T(8,128)} %pad_maximum_fusion.1), channel_id=1, source_target_pairs={{0,1},{1,0},{2,3},{3,2}} | collective-permute-start | bytes 786440 | tf_op jit(solution)/shard_map/ppermute | solution.py:152
  63.8 0.0 collective-permute-done.13.tail
  63.8 3.8 %shard_map.39 = (f32[1024,128]{1,0:T(8,128)S(1)}, f32[1024,128]{1,0:T(8,128)S(1)}) custom-call(s32[1]{0:T(128)} %bitcast.row, f32[256,256]{1,0:T(8,128)S(1)} %select_select_fusion.held, f32[256,256]{1,0:T(8,128)} %collective-permute-done.12.got, f32[256,1024]{1,0:T(8,128)S(1)} %bitcast.12, f32[256,1024]{1,0:T(8,128)} %collective-permute-done.4.whole, ...), custom_call_target="tpu_custom_call" | custom-call | flops 805306368 | tf_op jit(solution)/shard_map/pallas_call | solution.py:32
  67.6 1.9 %collective-permute-start.14 = (f32[1024,128]{1,0:T(8,128)S(1)}, f32[1024,128]{1,0:T(8,128)S(1)}, u32[]{:S(2)}, u32[]{:S(2)}) collective-permute-start(f32[1024,128]{1,0:T(8,128)S(1)} %get-tuple-element.46), channel_id=1, source_target_pairs={{4,5},{5,4},{6,7},{7,6},{8,9},{9,8},{10,11},{11,10},{12,13},{13,12... | collective-permute-start | bytes 1572872 | tf_op jit(solution)/shard_map/ppermute | solution.py:152
  69.6 0.0 collective-permute-done.11
  69.6 0.9 %select_dynamic-update-slice_fusion.7 = f32[1024,128]{1,0:T(8,128)S(1)} fusion(pred[]{:T(512)S(6)} %ne.22, f32[256,256]{1,0:T(8,128)S(1)} %get-tuple-element.31, f32[512,128]{1,0:T(8,128)} %collective-permute-done.11, pred[]{:T(512)S(6)} %ne.23), kind=kLoop, calls=%fused_computation.14 | loop fusion | flops 49151 | bytes 327682
  70.5 0.9 %select_dynamic-update-slice_fusion.6 = f32[1024,128]{1,0:T(8,128)S(1)} fusion(f32[1024,128]{1,0:T(8,128)S(1)} %select_dynamic-update-slice_fusion.7, pred[]{:T(512)S(6)} %ne.22, f32[512,128]{1,0:T(8,128)} %collective-permute-done.11, f32[256,256]{1,0:T(8,128)S(1)} %get-tuple-element.31, pred[]{:T(512)S(6)} %ne.23), kind=kLoop, calls=%fused_computation.13 | loop fusion | flops 49152 | bytes 327682
  71.4 0.9 %select_dynamic-update-slice_fusion.5 = f32[1024,128]{1,0:T(8,128)S(1)} fusion(f32[1024,128]{1,0:T(8,128)S(1)} %select_dynamic-update-slice_fusion.6, pred[]{:T(512)S(6)} %ne.22, f32[256,256]{1,0:T(8,128)S(1)} %get-tuple-element.31, f32[512,128]{1,0:T(8,128)} %collective-permute-done.11, pred[]{:T(512)S(6)} %ne.23), kind=kLoop, calls=%fused_computation.12 | loop fusion | flops 49152 | bytes 327682
  72.3 0.9 %select_dynamic-update-slice_fusion.4 = f32[1024,128]{1,0:T(8,128)S(1)} fusion(f32[1024,128]{1,0:T(8,128)S(1)} %select_dynamic-update-slice_fusion.5, pred[]{:T(512)S(6)} %ne.22, f32[512,128]{1,0:T(8,128)} %collective-permute-done.11, f32[256,256]{1,0:T(8,128)S(1)} %get-tuple-element.31, pred[]{:T(512)S(6)} %ne.23), kind=kLoop, calls=%fused_computation.11 | loop fusion | flops 49152 | bytes 327682
  73.2 0.9 %select_dynamic-update-slice_fusion.3 = f32[1024,128]{1,0:T(8,128)S(1)} fusion(f32[1024,128]{1,0:T(8,128)S(1)} %select_dynamic-update-slice_fusion.4, pred[]{:T(512)S(6)} %ne.22, f32[256,256]{1,0:T(8,128)S(1)} %get-tuple-element.39, f32[512,128]{1,0:T(8,128)} %collective-permute-done.11, pred[]{:T(512)S(6)} %ne.23), kind=kLoop, calls=%fused_computation.10 | loop fusion | flops 49152 | bytes 327682
  74.0 0.9 %select_dynamic-update-slice_fusion.2 = f32[1024,128]{1,0:T(8,128)S(1)} fusion(f32[1024,128]{1,0:T(8,128)S(1)} %select_dynamic-update-slice_fusion.3, pred[]{:T(512)S(6)} %ne.22, f32[512,128]{1,0:T(8,128)} %collective-permute-done.11, f32[256,256]{1,0:T(8,128)S(1)} %get-tuple-element.39, pred[]{:T(512)S(6)} %ne.23), kind=kLoop, calls=%fused_computation.9 | loop fusion | flops 49152 | bytes 327682
  74.9 0.9 %select_dynamic-update-slice_fusion.1 = f32[1024,128]{1,0:T(8,128)S(1)} fusion(f32[1024,128]{1,0:T(8,128)S(1)} %select_dynamic-update-slice_fusion.2, pred[]{:T(512)S(6)} %ne.22, f32[256,256]{1,0:T(8,128)S(1)} %get-tuple-element.39, f32[512,128]{1,0:T(8,128)} %collective-permute-done.11, pred[]{:T(512)S(6)} %ne.23), kind=kLoop, calls=%fused_computation.8 | loop fusion | flops 49152 | bytes 327682
  75.8 0.9 %select_dynamic-update-slice_fusion = f32[1024,128]{1,0:T(8,128)S(1)} fusion(f32[1024,128]{1,0:T(8,128)S(1)} %select_dynamic-update-slice_fusion.1, pred[]{:T(512)S(6)} %ne.22, f32[512,128]{1,0:T(8,128)} %collective-permute-done.11, f32[256,256]{1,0:T(8,128)S(1)} %get-tuple-element.39, pred[]{:T(512)S(6)} %ne.23), kind=kLoop, calls=%fused_computation.7 | loop fusion | flops 49152 | bytes 327682 | tf_op jit(solution)/shard_map/concatenate | solution.py:270
  76.7 7.1 %collective-permute-done.14 = f32[1024,128]{1,0:T(8,128)S(1)} collective-permute-done((f32[1024,128]{1,0:T(8,128)S(1)}, f32[1024,128]{1,0:T(8,128)S(1)}, u32[]{:S(2)}, u32[]{:S(2)}) %collective-permute-start.14) | collective-permute-done | bytes 524320 | tf_op jit(solution)/shard_map/ppermute | solution.py:152
  83.9 0.9 %subtract_select_fusion = f32[1024,128]{1,0:T(8,128)} fusion(f32[1024,128]{1,0:T(8,128)S(1)} %select_dynamic-update-slice_fusion, f32[1024,128]{1,0:T(8,128)S(1)} %get-tuple-element.45, f32[1024,128]{1,0:T(8,128)S(1)} %collective-permute-done.14, pred[]{:T(512)S(6)} %eq.14), kind=kLoop, calls=%fused_computation.1 | loop fusion | flops 262144 | bytes 2097153 | tf_op jit(solution)/shard_map/jit(_where)/select_n | solution.py:285
  (12 shorter events, 0.1 us)
Async XLA Ops:
  0.0 2.8 %copy-start.4 = (f32[2,128,512]{2,1,0:T(8,128)S(1)}, f32[2,128,512]{2,1,0:T(8,128)}, u32[]{:S(2)}) copy-start(f32[2,128,512]{2,1,0:T(8,128)} %param.5) | copy-start | bytes 1572868
  0.0 30.7 %collective-permute-start.4 = (f32[256,1024]{1,0:T(8,128)}, f32[256,1024]{1,0:T(8,128)}, u32[]{:S(2)}, u32[]{:S(2)}) collective-permute-start(f32[256,1024]{1,0:T(8,128)} %bitcast.8), channel_id=1, source_target_pairs={{12,14},{13,15},{14,12},{15,13},{20,22},{21,23},{22,20},{23,21},{2... | collective-permute-start | bytes 3145736 | tf_op jit(solution)/shard_map/ppermute | solution.py:152
  2.8 1.9 %copy-start = (f32[2,128,1024]{2,1,0:T(8,128)S(1)}, f32[2,128,1024]{2,1,0:T(8,128)}, u32[]{:S(2)}) copy-start(f32[2,128,1024]{2,1,0:T(8,128)} %param.4) | copy-start | bytes 3145732
  2.8 1.1 %copy-start.1 = (f32[1024,128]{1,0:T(8,128)S(1)}, f32[1024,128]{1,0:T(8,128)}, u32[]{:S(2)}) copy-start(f32[1024,128]{1,0:T(8,128)} %cross.1) | copy-start | bytes 1572868
  2.9 8.9 %collective-permute-start = (f32[128,1024]{1,0:T(8,128)S(1)}, f32[128,1024]{1,0:T(8,128)S(1)}, u32[]{:S(2)}, u32[]{:S(2)}) collective-permute-start(f32[128,1024]{1,0:T(8,128)S(1)} %pad_maximum_fusion.lead), channel_id=1, source_target_pairs={{0,2},{1,3},{2,0},{3,1}} | collective-permute-start | bytes 1572872 | tf_op jit(solution)/shard_map/ppermute | solution.py:152
  3.9 7.8 %collective-permute-start.1 = (f32[1024,128]{1,0:T(8,128)S(1)}, f32[1024,128]{1,0:T(8,128)S(1)}, u32[]{:S(2)}, u32[]{:S(2)}) collective-permute-start(f32[1024,128]{1,0:T(8,128)S(1)} %copy-done.1), channel_id=1, source_target_pairs={{0,1},{1,0},{2,3},{3,2}} | collective-permute-start | bytes 1572872 | tf_op jit(solution)/shard_map/ppermute | solution.py:152
  5.5 25.2 %collective-permute-start.3 = (f32[256,384]{1,0:T(8,128)}, f32[256,384]{1,0:T(8,128)}, u32[]{:S(2)}, u32[]{:S(2)}) collective-permute-start(f32[256,384]{1,0:T(8,128)} %slice.71), channel_id=1, source_target_pairs={{8,10},{9,11},{10,8},{11,9},{16,18},{17,19},{18,16},{19,17},{24,26... | collective-permute-start | bytes 1179656 | tf_op jit(solution)/shard_map/ppermute | solution.py:152
  11.7 0.8 copy-start.2
  12.5 1.0 %copy-start.3 = (f32[1024,128]{1,0:T(8,128)S(1)}, f32[1024,128]{1,0:T(8,128)}, u32[]{:S(2)}) copy-start(f32[1024,128]{1,0:T(8,128)} %copy-done.2) | copy-start | bytes 1572868
  30.7 2.8 %collective-permute-start.5 = (f32[512,256]{1,0:T(8,128)S(1)}, f32[512,256]{1,0:T(8,128)S(1)}, u32[]{:S(2)}, u32[]{:S(2)}) collective-permute-start(f32[512,256]{1,0:T(8,128)S(1)} %get-tuple-element.34.sent), channel_id=1, source_target_pairs={{0,1},{1,0},{2,3},{3,2}} | collective-permute-start | bytes 1572872 | tf_op jit(solution)/shard_map/ppermute | solution.py:152
  31.4 1.4 %collective-permute-start.6 = (f32[256,256]{1,0:T(8,128)S(1)}, f32[256,256]{1,0:T(8,128)S(1)}, u32[]{:S(2)}, u32[]{:S(2)}) collective-permute-start(f32[256,256]{1,0:T(8,128)S(1)} %get-tuple-element.31), channel_id=1, source_target_pairs={{0,4},{1,5},{2,6},{3,7}} | collective-permute-start | bytes 786440 | tf_op jit(solution)/shard_map/ppermute | solution.py:158
  32.1 1.4 %collective-permute-start.2 = (f32[128,512]{1,0:T(8,128)S(1)}, f32[128,512]{1,0:T(8,128)S(1)}, u32[]{:S(2)}, u32[]{:S(2)}) collective-permute-start(f32[128,512]{1,0:T(8,128)S(1)} %get-tuple-element.32.inverse), channel_id=1, source_target_pairs={{0,2},{1,3},{2,0},{3,1}} | collective-permute-start | bytes 786440 | tf_op jit(solution)/shard_map/ppermute | solution.py:152
  32.8 28.9 %collective-permute-start.10 = (f32[256,512]{1,0:T(8,128)}, f32[256,512]{1,0:T(8,128)S(1)}, u32[]{:S(2)}, u32[]{:S(2)}) collective-permute-start(f32[256,512]{1,0:T(8,128)} %slice.69), channel_id=1, source_target_pairs={{4,6},{5,7},{6,4},{7,5}} | collective-permute-start | bytes 1572872 | tf_op jit(solution)/shard_map/ppermute | solution.py:152
  34.3 6.0 %collective-permute-start.7 = (f32[256,256]{1,0:T(8,128)}, f32[256,256]{1,0:T(8,128)}, u32[]{:S(2)}, u32[]{:S(2)}) collective-permute-start(f32[256,256]{1,0:T(8,128)} %get-tuple-element.35), channel_id=1, source_target_pairs={{0,24},{1,25},{2,26},{3,27},{4,28},{5,29},{6,30},{7,31}} | collective-permute-start | bytes 786440 | tf_op jit(solution)/shard_map/ppermute | solution.py:158
  35.7 4.6 %collective-permute-start.8 = (f32[256,256]{1,0:T(8,128)}, f32[256,256]{1,0:T(8,128)}, u32[]{:S(2)}, u32[]{:S(2)}) collective-permute-start(f32[256,256]{1,0:T(8,128)} %get-tuple-element.35), channel_id=1, source_target_pairs={{0,16},{1,17},{2,18},{3,19},{4,20},{5,21},{6,22},{7,23}} | collective-permute-start | bytes 786440 | tf_op jit(solution)/shard_map/ppermute | solution.py:158
  37.0 23.6 %collective-permute-start.9 = (f32[256,256]{1,0:T(8,128)}, f32[256,256]{1,0:T(8,128)}, u32[]{:S(2)}, u32[]{:S(2)}) collective-permute-start(f32[256,256]{1,0:T(8,128)} %get-tuple-element.35), channel_id=1, source_target_pairs={{0,8},{1,9},{2,10},{3,11},{4,12},{5,13},{6,14},{7,15}} | collective-permute-start | bytes 786440 | tf_op jit(solution)/shard_map/ppermute | solution.py:158
  38.3 25.5 %collective-permute-start.13 = (f32[256,640]{1,0:T(8,128)}, f32[256,640]{1,0:T(8,128)S(1)}, u32[]{:S(2)}, u32[]{:S(2)}) collective-permute-start(f32[256,640]{1,0:T(8,128)} %slice.70), channel_id=1, source_target_pairs={{4,6},{5,7},{6,4},{7,5},{8,10},{9,11},{10,8},{11,9},{16,18},{17,19... | collective-permute-start | bytes 1966088 | tf_op jit(solution)/shard_map/ppermute | solution.py:152
  61.6 2.2 %collective-permute-start.12 = (f32[256,256]{1,0:T(8,128)S(1)}, f32[256,256]{1,0:T(8,128)}, u32[]{:S(2)}, u32[]{:S(2)}) collective-permute-start(f32[256,256]{1,0:T(8,128)S(1)} %select_select_fusion.held), channel_id=1, source_target_pairs={{0,4},{1,5},{2,6},{3,7},{4,0},{5,1},{6,2},{7,3},{8,12},{9,13},{10,... | collective-permute-start | bytes 786440 | tf_op jit(solution)/shard_map/ppermute | solution.py:182
  62.4 7.1 %collective-permute-start.11 = (f32[512,128]{1,0:T(8,128)}, f32[512,128]{1,0:T(8,128)}, u32[]{:S(2)}, u32[]{:S(2)}) collective-permute-start(f32[512,128]{1,0:T(8,128)} %pad_maximum_fusion.1), channel_id=1, source_target_pairs={{0,1},{1,0},{2,3},{3,2}} | collective-permute-start | bytes 786440 | tf_op jit(solution)/shard_map/ppermute | solution.py:152
  67.6 16.2 %collective-permute-start.14 = (f32[1024,128]{1,0:T(8,128)S(1)}, f32[1024,128]{1,0:T(8,128)S(1)}, u32[]{:S(2)}, u32[]{:S(2)}) collective-permute-start(f32[1024,128]{1,0:T(8,128)S(1)} %get-tuple-element.46), channel_id=1, source_target_pairs={{4,5},{5,4},{6,7},{7,6},{8,9},{9,8},{10,11},{11,10},{12,13},{13,12... | collective-permute-start | bytes 1572872 | tf_op jit(solution)/shard_map/ppermute | solution.py:152

commit v12 on v11

--- a/solution.py
+++ b/solution.py
@@ -22,7 +22,7 @@
         )
 
     left_high, left_low = split(left)
-    right_high, right_low = split(right)
+    right_high, right_low = right if isinstance(right, tuple) else split(right)
     return one(left_high, right_high) + (one(left_high, right_low) + one(left_low, right_high))
 
 
@@ -41,8 +41,11 @@
     )(*flags, *near, *far)
 
 
-def first_kernel(places, width, row, lead, lead_other, rhs, *refs):
-    others, (solved, shuffled, *held, sems) = refs[: len(places) - 1], refs[len(places) - 1 :]
+def first_kernel(places, width, row, lead, rhs, far_lead, *refs):
+    others, (solved, shuffled, lead_other, *held, sems) = (
+        refs[: len(places) - 1],
+        refs[len(places) - 1 :],
+    )
     cands = rhs.shape[1]
 
     @pl.when(row[0] == 0)
@@ -51,6 +54,11 @@
             pltpu.make_async_copy(other.at[:width], place, sems.at[at])
             for at, (other, place) in enumerate(zip(others, held))
         ]
+        copies.append(
+            pltpu.make_async_copy(
+                far_lead.at[:, : 2 * width], lead_other, sems.at[len(copies)]
+            )
+        )
         for copy in copies:
             copy.start()
         for copy in copies:
@@ -68,22 +76,25 @@
             shuffled[:, at * cands : (at + 1) * cands] = pieces[place]
 
 
-def second_kernel(places, row, inverse, inverse_other, sent, got, first, solved, bundle, *refs):
-    sums, more, sems = refs
+def second_kernel(places, row, lead, far_lead, sent, got, first, solved, bundle, *refs):
+    inverse_other, sums, more, sems = refs
     width = sums.shape[0]
     cands = sums.shape[1] // len(places)
+
+    last = slice(2 * width, 3 * width)
 
     @pl.when(row[0] == 0)
     def _():
         copies = [
             pltpu.make_async_copy(sent, sums, sems.at[0]),
             pltpu.make_async_copy(got, more, sems.at[1]),
+            pltpu.make_async_copy(far_lead.at[:, last], inverse_other, sems.at[2]),
         ]
         for copy in copies:
             copy.start()
-        both = jnp.concatenate([inverse[...], inverse_other[...]], axis=0)
         for copy in copies:
             copy.wait()
+        both = jnp.concatenate([lead[:, last], inverse_other[...]], axis=0)
         rest = [sums[:, place * cands : (place + 1) * cands] for place in places]
         second = dot(both, -(jnp.concatenate(rest, axis=1) + more[...]), 1)
         solved[...] = second
@@ -91,7 +102,7 @@
 
     @pl.when(row[0] == 1)
     def _():
-        copy = pltpu.make_async_copy(first, bundle, sems.at[2])
+        copy = pltpu.make_async_copy(first, bundle, sems.at[3])
         copy.start()
         copy.wait()
 
@@ -125,11 +136,13 @@
                 pl.when(chosen)(lambda at=at, pair=pair: fetch(at, pair[at]).start())
             for copy in copies[2 * at : 2 * at + 2]:
                 copy.start()
-        first = jnp.where(is_odd, held[...], got[...])
-        second = jnp.where(is_odd, got[...], held[...])
+        has_first = (row[0] == 1) | ((row[0] > 1) & ~is_odd)
+        first = jnp.where(has_first, held[...], got[...])
+        second = jnp.where(has_first, got[...], held[...])
         solved = jnp.concatenate(
             [first[:depth], second[:depth], first[depth:], second[depth:]], axis=0
         )
+        solved = split(solved)
         for at, part in enumerate(parts):
             fetch(at, whole.at[:, part]).wait()
             for copy in copies[2 * at : 2 * at + 2]:
@@ -140,6 +153,28 @@
             send[part] = partial[:, cands:]
 
 
+def top_kernel(offsets, col, pair, *refs):
+    others, out = refs[:-1], refs[-1]
+    cands = out.shape[1]
+    depth = pair.shape[0] // 4
+    n_cols = len(offsets)
+    sources = [pair[:, :cands]] + [other[...] for other in others]
+    for panel in range(2):
+        pieces = []
+        for source in sources:
+            for at in (2 * panel, 2 * panel + 1):
+                pieces.append(source[at * depth : (at + 1) * depth])
+        pieces = [pieces[offsets.index(at)] for at in range(n_cols)]
+        bit = 1
+        while bit < n_cols:
+            flipped = (col[0] & bit) != 0
+            pieces = [jnp.where(flipped, pieces[at ^ bit], pieces[at]) for at in range(n_cols)]
+            bit *= 2
+        for at, piece in enumerate(pieces):
+            place = (panel * n_cols + at) * depth
+            out[place : place + depth] = piece
+
+
 def make_on_device(n_rows, n_cols):
     half = n_cols // 2
 
@@ -153,16 +188,21 @@
 
     def send_down(array, offset, have):
         pairs = [
-            (row * n_cols + col, (row + offset) * n_cols + col) for row in have for col in range(n_cols)
+            (row * n_cols + col, target(row, offset) * n_cols + col)
+            for row in have
+            for col in range(n_cols)
         ]
         return lax.ppermute(array, AXES, pairs)
+
+    def target(row, offset):
+        return (row + offset) ^ (1 if row < 2 and offset > 1 else 0)
 
     def spread(array, row_id, low, radix, have):
         digit = (row_id // low) % radix
         result = array
-        for step in range(1, radix):
+        for step in (2, 1, 3) if radix == 4 else range(1, radix):
             result = jnp.where(digit == step, send_down(array, step * low, have), result)
-        return result, [row + step * low for row in have for step in range(radix)]
+        return result, [target(row, step * low) for row in have for step in range(radix)]
 
     def broadcast_outer(array, row_id):
         low = n_rows
@@ -186,18 +226,6 @@
 
     def shuffle(array, flip, cands):
         return jnp.concatenate([block(array, at ^ flip, cands) for at in range(half)], axis=1)
-
-    def in_order(pieces, col_id):
-        offsets = [at for step in range(half) for at in (step, step ^ half)]
-        pieces = [pieces[offsets.index(at)] for at in range(n_cols)]
-        bit = 1
-        while bit < n_cols:
-            flipped = (col_id & bit) != 0
-            pieces = [
-                jnp.where(flipped, pieces[at ^ bit], pieces[at]) for at in range(n_cols)
-            ]
-            bit *= 2
-        return pieces
 
     def on_device(cross_kernel, factor_panels, block_inverses):
         row_id = lax.axis_index("rows")
@@ -212,15 +240,15 @@
         flat = factor_panels.reshape(2 * depth, n_design)
 
         lead = jnp.concatenate(
-            [block_inverses[0], factor_panels[0, :, width : 2 * width]], axis=1
+            [block_inverses[0], factor_panels[0, :, width : 2 * width], block_inverses[1]], axis=1
         )
         lead, rhs = lax.optimization_barrier((lead, cross_kernel))
         lead_other = swap(lead, half, top)
         rhs_others = [swap(rhs, step, top) for step in range(1, half)]
         whole = swap(flat, half, odds)
         arrived = swap(flat[:, :count], half, evens)
-        lead_other, head, tail, inverse = lax.optimization_barrier(
-            (lead_other, flat[:, : n_design // 2], flat[:, count:], block_inverses[1])
+        lead_other, head, tail = lax.optimization_barrier(
+            (lead_other, flat[:, : n_design // 2], flat[:, count:])
         )
 
         places = [at ^ 1 for at in range(half)]
@@ -228,13 +256,11 @@
             functools.partial(first_kernel, places, width),
             [(2 * depth, half * cands), (width, half * cands)],
             6 * width * half * cands * (2 * depth + 2 * depth),
-            [lead, lead_other, rhs],
-            rhs_others,
+            [lead, rhs],
+            [lead_other, *rhs_others],
             row_id,
-            [(width, cands)] * len(rhs_others),
-        )
-        first, inverse = lax.optimization_barrier((first, inverse))
-        inverse_other = swap(inverse, half, top)
+            [(depth, 2 * width)] + [(width, cands)] * len(rhs_others),
+        )
         shuffled, arrived, whole = lax.optimization_barrier((shuffled, arrived, whole))
         sums = got = swap(shuffled, 1, top)
         bit = 2
@@ -248,10 +274,10 @@
             functools.partial(second_kernel, places),
             [(2 * depth, half * cands)] * 2,
             6 * 2 * depth * width * half * cands,
-            [inverse, inverse_other],
-            [shuffled, sums, first_beside],
+            [lead],
+            [lead_other, shuffled, sums, first_beside],
             row_id,
-            [(width, half * cands)] * 2,
+            [(depth, width)] + [(width, half * cands)] * 2,
         )
         first_beside, head = lax.optimization_barrier((first_beside, head))
         late = swap(head, half, beside)
@@ -261,14 +287,14 @@
         solved = [held, swap_cores(held)]
 
         pair = jnp.concatenate([first, second], axis=0)
-        others = [block(pair, 0, cands)]
-        others += [swap(block(pair, step, cands), step, top) for step in range(1, half)]
-        pieces = [[], []]
-        for got in others:
-            for at in range(4):
-                pieces[at // 2].append(got[at * depth : (at + 1) * depth])
-        top_rows = jnp.concatenate(
-            in_order(pieces[0], col_id) + in_order(pieces[1], col_id), axis=0
+        others = [swap(block(pair, step, cands), step, top) for step in range(1, half)]
+        offsets = [at for step in range(half) for at in (step, step ^ half)]
+        (top_rows,) = call(
+            functools.partial(top_kernel, offsets),
+            [(2 * width, cands)],
+            0,
+            [pair, *others],
+            flag=col_id,
         )
 
         fresh, send = call(

time: 85.6 us -> 81.3 us (0.950)
  the two profiles are of different devices: /device:TPU:2 before, /device:TPU:1 now
where the time goes in v12:
time: 81.3 us; the launch traced here: 80.9 us
  waiting for transfers between devices  49.2 us (61%)
  starting transfers between devices  20.3 us (25%)
  local copies, waits for them, and re-layouts  4.55 us (6%)
  Pallas kernels  4.54 us (6%)
  other arithmetic  1.94 us (2%)
    ppermute x4, waiting for transfers between devices, send_down(): return lax.ppermute(array, AXES, pairs)  27.6 us
    ppermute x9, waiting for transfers between devices, swap(): return lax.ppermute(array, AXES, pairs)  21.6 us
    ppermute x9, starting transfers between devices, swap(): return lax.ppermute(array, AXES, pairs)  15.1 us
    ppermute x4, starting transfers between devices, send_down(): return lax.ppermute(array, AXES, pairs)  5.2 us
    pallas_call x4, Pallas kernels, call(): pl.pallas_call(kernel, out_shape=[jax.ShapeDtypeStruct(shape, jnp.float32...  4.54 us
  transfers between devices with their start and end apart: 14, of which 5 were waited for; matrix products, arithmetic and copies ran while one was open for 6% of the time, Pallas kernels for 1%

profile of v12, /device:TPU:1, one launch (start us, length us, event | category | flops | bytes accessed | tf_op | source)
XLA Modules:
  0.0 80.9 jit_solution(6502092250736109236)
XLA Ops:
  0.0 1.8 %collective-permute-start.3 = (f32[256,1024]{1,0:T(8,128)}, f32[256,1024]{1,0:T(8,128)}, u32[]{:S(2)}, u32[]{:S(2)}) collective-permute-start(f32[256,1024]{1,0:T(8,128)} %bitcast.9), channel_id=1, source_target_pairs={{12,14},{13,15},{14,12},{15,13},{20,22},{21,23},{22,20},{23,21},{2... | collective-permute-start | bytes 3145736 | tf_op jit(solution)/shard_map/ppermute | solution.py:187
  1.8 1.0 %slice_bitcast_fusion.1 = f32[128,512]{1,0:T(8,128)S(1)} fusion(f32[2,128,1024]{2,1,0:T(8,128)} %param.4), kind=kLoop, calls=%fused_computation.4 | loop fusion | bytes 524288 | tf_op jit(solution)/shard_map/squeeze | solution.py:243
  2.8 0.0 copy-done.6
  2.8 0.0 copy-start
  2.8 0.0 copy-start.1
  2.8 0.1 pad_maximum_fusion.lead
  2.9 0.8 %collective-permute-start = (f32[128,1536]{1,0:T(8,128)S(1)}, f32[128,1536]{1,0:T(8,128)S(1)}, u32[]{:S(2)}, u32[]{:S(2)}) collective-permute-start(f32[128,1536]{1,0:T(8,128)S(1)} %pad_maximum_fusion.lead), channel_id=1, source_target_pairs={{0,2},{1,3},{2,0},{3,1}} | collective-permute-start | bytes 2359304 | tf_op jit(solution)/shard_map/ppermute | solution.py:187
  3.7 0.2 copy-done.1
  4.0 1.5 %collective-permute-start.1 = (f32[1024,128]{1,0:T(8,128)S(1)}, f32[1024,128]{1,0:T(8,128)}, u32[]{:S(2)}, u32[]{:S(2)}) collective-permute-start(f32[1024,128]{1,0:T(8,128)S(1)} %copy-done.1), channel_id=1, source_target_pairs={{0,1},{1,0},{2,3},{3,2}} | collective-permute-start | bytes 1572872 | tf_op jit(solution)/shard_map/ppermute | solution.py:187
  5.4 0.0 copy-done
  5.4 0.8 slice.30
  6.2 0.7 collective-permute-start.2
  6.9 0.9 %slice.29 = f32[256,640]{1,0:T(8,128)} slice(f32[256,1024]{1,0:T(8,128)S(1)} %bitcast.11), slice={[0:256], [384:1024]} | slice | bytes 1310720 | tf_op jit(solution)/shard_map/slice | solution.py:251
  7.8 0.8 %slice.28 = f32[256,512]{1,0:T(8,128)} slice(f32[256,1024]{1,0:T(8,128)S(1)} %bitcast.12), slice={[0:256], [0:512]} | slice | bytes 1048576 | tf_op jit(solution)/shard_map/slice | solution.py:251
  8.6 0.0 collective-permute-done.far_lead
  8.6 0.0 collective-permute-done.1.refs_0_
  8.6 0.1 shard_map.37
  8.7 0.0 copy-start.2
  8.7 0.0 collective-permute-done.2.early
  8.7 0.0 collective-permute-done.3.whole
  8.7 0.7 collective-permute-start.4
  9.4 1.3 %collective-permute-start.5 = (f32[256,256]{1,0:T(8,128)S(1)}, f32[256,256]{1,0:T(8,128)S(1)}, u32[]{:S(2)}, u32[]{:S(2)}) collective-permute-start(f32[256,256]{1,0:T(8,128)S(1)} %get-tuple-element.26), channel_id=1, source_target_pairs={{0,4},{1,5},{2,6},{3,7}} | collective-permute-start | bytes 786440 | tf_op jit(solution)/shard_map/ppermute | solution.py:195
  10.7 24.0 %collective-permute-done.5.first = f32[256,256]{1,0:T(8,128)S(1)} collective-permute-done((f32[256,256]{1,0:T(8,128)S(1)}, f32[256,256]{1,0:T(8,128)S(1)}, u32[]{:S(2)}, u32[]{:S(2)}) %collective-permute-start.5) | collective-permute-done | bytes 262176 | tf_op jit(solution)/shard_map/ppermute | solution.py:195
  34.8 5.0 %collective-permute-start.9 = (f32[256,512]{1,0:T(8,128)}, f32[256,512]{1,0:T(8,128)}, u32[]{:S(2)}, u32[]{:S(2)}) collective-permute-start(f32[256,512]{1,0:T(8,128)} %slice.28), channel_id=1, source_target_pairs={{4,6},{5,7},{6,4},{7,5}} | collective-permute-start | bytes 1572872 | tf_op jit(solution)/shard_map/ppermute | solution.py:187
  39.8 0.0 collective-permute-done.4.got
  39.8 0.8 shard_map.38
  40.6 0.0 copy-done.2
  40.6 0.0 copy-start.4
  40.6 0.7 copy-done.4
  41.3 1.3 %collective-permute-start.6 = (f32[256,256]{1,0:T(8,128)}, f32[256,256]{1,0:T(8,128)S(1)}, u32[]{:S(2)}, u32[]{:S(2)}) collective-permute-start(f32[256,256]{1,0:T(8,128)} %get-tuple-element.29), channel_id=1, source_target_pairs={{0,28},{1,29},{2,30},{3,31},{4,24},{5,25},{6,26},{7,27}} | collective-permute-start | bytes 786440 | tf_op jit(solution)/shard_map/ppermute | solution.py:195
  42.6 1.3 %collective-permute-start.7 = (f32[256,256]{1,0:T(8,128)}, f32[256,256]{1,0:T(8,128)S(1)}, u32[]{:S(2)}, u32[]{:S(2)}) collective-permute-start(f32[256,256]{1,0:T(8,128)} %get-tuple-element.29), channel_id=1, source_target_pairs={{0,12},{1,13},{2,14},{3,15},{4,8},{5,9},{6,10},{7,11}} | collective-permute-start | bytes 786440 | tf_op jit(solution)/shard_map/ppermute | solution.py:195
  43.9 1.3 %collective-permute-start.8 = (f32[256,256]{1,0:T(8,128)}, f32[256,256]{1,0:T(8,128)S(1)}, u32[]{:S(2)}, u32[]{:S(2)}) collective-permute-start(f32[256,256]{1,0:T(8,128)} %get-tuple-element.29), channel_id=1, source_target_pairs={{0,20},{1,21},{2,22},{3,23},{4,16},{5,17},{6,18},{7,19}} | collective-permute-start | bytes 786440 | tf_op jit(solution)/shard_map/ppermute | solution.py:195
  45.2 1.9 %collective-permute-start.12 = (f32[256,640]{1,0:T(8,128)}, f32[256,640]{1,0:T(8,128)S(1)}, u32[]{:S(2)}, u32[]{:S(2)}) collective-permute-start(f32[256,640]{1,0:T(8,128)} %slice.29), channel_id=1, source_target_pairs={{4,6},{5,7},{6,4},{7,5},{8,10},{9,11},{10,8},{11,9},{16,18},{17,19... | collective-permute-start | bytes 1966088 | tf_op jit(solution)/shard_map/ppermute | solution.py:187
  47.2 0.0 collective-permute-done.6
  47.2 3.6 %collective-permute-done.7 = f32[256,256]{1,0:T(8,128)S(1)} collective-permute-done((f32[256,256]{1,0:T(8,128)}, f32[256,256]{1,0:T(8,128)S(1)}, u32[]{:S(2)}, u32[]{:S(2)}) %collective-permute-start.7) | collective-permute-done | bytes 262176 | tf_op jit(solution)/shard_map/ppermute | solution.py:195
  50.8 0.0 collective-permute-done.8
  50.8 1.0 %select_select_fusion.held = f32[256,256]{1,0:T(8,128)S(1)} fusion(f32[256,256]{1,0:T(8,128)S(1)} %collective-permute-done.6, f32[256,256]{1,0:T(8,128)S(1)} %collective-permute-done.7, f32[256,256]{1,0:T(8,128)S(1)} %collective-permute-done.8, f32[256,256]{1,0:T(8,128)} %get-tuple-element.29, pred[]{:T(512)S(6)} %eq.17, pred[]{:T(512)S(6)} %eq.16, pred[]{:T(512)S(6)} %eq.15), kind=kLoop, calls=%fused_computation.2 | loop fusion | flops 196608 | bytes 1310723 | tf_op jit(solution)/shard_map/jit(_where)/select_n | solution.py:204
  51.8 7.4 %collective-permute-done.9.beside = f32[256,512]{1,0:T(8,128)} collective-permute-done((f32[256,512]{1,0:T(8,128)}, f32[256,512]{1,0:T(8,128)}, u32[]{:S(2)}, u32[]{:S(2)}) %collective-permute-start.9) | collective-permute-done | bytes 524320 | tf_op jit(solution)/shard_map/ppermute | solution.py:187
  59.2 0.0 collective-permute-start.11
  59.2 6.9 %collective-permute-done.12.tail = f32[256,640]{1,0:T(8,128)S(1)} collective-permute-done((f32[256,640]{1,0:T(8,128)}, f32[256,640]{1,0:T(8,128)S(1)}, u32[]{:S(2)}, u32[]{:S(2)}) %collective-permute-start.12) | collective-permute-done | bytes 655392 | tf_op jit(solution)/shard_map/ppermute | solution.py:187
  66.1 0.0 collective-permute-done.11.got
  66.1 3.6 %shard_map.40 = (f32[1024,128]{1,0:T(8,128)S(1)}, f32[1024,128]{1,0:T(8,128)}) custom-call(s32[1]{0:T(128)} %bitcast.1.row, f32[256,256]{1,0:T(8,128)S(1)} %select_select_fusion.held, f32[256,256]{1,0:T(8,128)S(1)} %collective-permute-done.11.got, f32[256,1024]{1,0:T(8,128)S(1)} %bitcast.13, f32[256,1024]{1,0:T(8,128)} %collective-permute-done.3.whole, ...), custom_call_target="tpu_custom_call" | custom-call | flops 805306368 | tf_op jit(solution)/shard_map/pallas_call | solution.py:32
  69.7 2.1 %collective-permute-start.13 = (f32[1024,128]{1,0:T(8,128)}, f32[1024,128]{1,0:T(8,128)S(1)}, u32[]{:S(2)}, u32[]{:S(2)}) collective-permute-start(f32[1024,128]{1,0:T(8,128)} %get-tuple-element.40), channel_id=1, source_target_pairs={{4,5},{5,4},{6,7},{7,6},{8,9},{9,8},{10,11},{11,10},{12,13},{13,12... | collective-permute-start | bytes 1572872 | tf_op jit(solution)/shard_map/ppermute | solution.py:187
  71.9 0.7 collective-permute-start.10
  72.6 0.0 collective-permute-done.10.refs_0_
  72.6 0.1 shard_map.39
  72.7 7.3 %collective-permute-done.13 = f32[1024,128]{1,0:T(8,128)S(1)} collective-permute-done((f32[1024,128]{1,0:T(8,128)}, f32[1024,128]{1,0:T(8,128)S(1)}, u32[]{:S(2)}, u32[]{:S(2)}) %collective-permute-start.13) | collective-permute-done | bytes 524320 | tf_op jit(solution)/shard_map/ppermute | solution.py:187
  80.0 0.9 %subtract_select_fusion = f32[1024,128]{1,0:T(8,128)} fusion(f32[1024,128]{1,0:T(8,128)S(1)} %shard_map.39, f32[1024,128]{1,0:T(8,128)S(1)} %get-tuple-element.39, f32[1024,128]{1,0:T(8,128)S(1)} %collective-permute-done.13, pred[]{:T(512)S(6)} %eq.14), kind=kLoop, calls=%fused_computation.1 | loop fusion | flops 262144 | bytes 2097153 | tf_op jit(solution)/shard_map/jit(_where)/select_n | solution.py:311
  (9 shorter events, 0.1 us)
Async XLA Ops:
  0.0 2.8 %copy-start.6 = (f32[2,128,512]{2,1,0:T(8,128)S(1)}, f32[2,128,512]{2,1,0:T(8,128)}, u32[]{:S(2)}) copy-start(f32[2,128,512]{2,1,0:T(8,128)} %param.5) | copy-start | bytes 1572868
  0.0 8.7 %collective-permute-start.3 = (f32[256,1024]{1,0:T(8,128)}, f32[256,1024]{1,0:T(8,128)}, u32[]{:S(2)}, u32[]{:S(2)}) collective-permute-start(f32[256,1024]{1,0:T(8,128)} %bitcast.9), channel_id=1, source_target_pairs={{12,14},{13,15},{14,12},{15,13},{20,22},{21,23},{22,20},{23,21},{2... | collective-permute-start | bytes 3145736 | tf_op jit(solution)/shard_map/ppermute | solution.py:187
  2.8 2.6 %copy-start = (f32[2,128,1024]{2,1,0:T(8,128)S(1)}, f32[2,128,1024]{2,1,0:T(8,128)}, u32[]{:S(2)}) copy-start(f32[2,128,1024]{2,1,0:T(8,128)} %param.4) | copy-start | bytes 3145732
  2.8 1.1 %copy-start.1 = (f32[1024,128]{1,0:T(8,128)S(1)}, f32[1024,128]{1,0:T(8,128)}, u32[]{:S(2)}) copy-start(f32[1024,128]{1,0:T(8,128)} %cross.1) | copy-start | bytes 1572868
  2.9 5.7 %collective-permute-start = (f32[128,1536]{1,0:T(8,128)S(1)}, f32[128,1536]{1,0:T(8,128)S(1)}, u32[]{:S(2)}, u32[]{:S(2)}) collective-permute-start(f32[128,1536]{1,0:T(8,128)S(1)} %pad_maximum_fusion.lead), channel_id=1, source_target_pairs={{0,2},{1,3},{2,0},{3,1}} | collective-permute-start | bytes 2359304 | tf_op jit(solution)/shard_map/ppermute | solution.py:187
  4.0 4.7 %collective-permute-start.1 = (f32[1024,128]{1,0:T(8,128)S(1)}, f32[1024,128]{1,0:T(8,128)}, u32[]{:S(2)}, u32[]{:S(2)}) collective-permute-start(f32[1024,128]{1,0:T(8,128)S(1)} %copy-done.1), channel_id=1, source_target_pairs={{0,1},{1,0},{2,3},{3,2}} | collective-permute-start | bytes 1572872 | tf_op jit(solution)/shard_map/ppermute | solution.py:187
  6.2 2.5 %collective-permute-start.2 = (f32[256,384]{1,0:T(8,128)}, f32[256,384]{1,0:T(8,128)S(1)}, u32[]{:S(2)}, u32[]{:S(2)}) collective-permute-start(f32[256,384]{1,0:T(8,128)} %slice.30), channel_id=1, source_target_pairs={{8,10},{9,11},{10,8},{11,9},{16,18},{17,19},{18,16},{19,17},{24,26... | collective-permute-start | bytes 1179656 | tf_op jit(solution)/shard_map/ppermute | solution.py:187
  8.7 31.9 %copy-start.2 = (f32[256,256]{1,0:T(8,128)}, f32[256,256]{1,0:T(8,128)S(1)}, u32[]{:S(2)}) copy-start(f32[256,256]{1,0:T(8,128)S(1)} %get-tuple-element.26) | copy-start | bytes 786436
  8.7 31.0 %collective-permute-start.4 = (f32[512,256]{1,0:T(8,128)S(1)}, f32[512,256]{1,0:T(8,128)S(1)}, u32[]{:S(2)}, u32[]{:S(2)}) collective-permute-start(f32[512,256]{1,0:T(8,128)S(1)} %get-tuple-element.28.sent), channel_id=1, source_target_pairs={{0,1},{1,0},{2,3},{3,2}} | collective-permute-start | bytes 1572872 | tf_op jit(solution)/shard_map/ppermute | solution.py:187
  9.4 25.3 %collective-permute-start.5 = (f32[256,256]{1,0:T(8,128)S(1)}, f32[256,256]{1,0:T(8,128)S(1)}, u32[]{:S(2)}, u32[]{:S(2)}) collective-permute-start(f32[256,256]{1,0:T(8,128)S(1)} %get-tuple-element.26), channel_id=1, source_target_pairs={{0,4},{1,5},{2,6},{3,7}} | collective-permute-start | bytes 786440 | tf_op jit(solution)/shard_map/ppermute | solution.py:195
  34.8 24.4 %collective-permute-start.9 = (f32[256,512]{1,0:T(8,128)}, f32[256,512]{1,0:T(8,128)}, u32[]{:S(2)}, u32[]{:S(2)}) collective-permute-start(f32[256,512]{1,0:T(8,128)} %slice.28), channel_id=1, source_target_pairs={{4,6},{5,7},{6,4},{7,5}} | collective-permute-start | bytes 1572872 | tf_op jit(solution)/shard_map/ppermute | solution.py:187
  40.6 0.7 copy-start.4
  41.3 5.9 %collective-permute-start.6 = (f32[256,256]{1,0:T(8,128)}, f32[256,256]{1,0:T(8,128)S(1)}, u32[]{:S(2)}, u32[]{:S(2)}) collective-permute-start(f32[256,256]{1,0:T(8,128)} %get-tuple-element.29), channel_id=1, source_target_pairs={{0,28},{1,29},{2,30},{3,31},{4,24},{5,25},{6,26},{7,27}} | collective-permute-start | bytes 786440 | tf_op jit(solution)/shard_map/ppermute | solution.py:195
  42.6 8.2 %collective-permute-start.7 = (f32[256,256]{1,0:T(8,128)}, f32[256,256]{1,0:T(8,128)S(1)}, u32[]{:S(2)}, u32[]{:S(2)}) collective-permute-start(f32[256,256]{1,0:T(8,128)} %get-tuple-element.29), channel_id=1, source_target_pairs={{0,12},{1,13},{2,14},{3,15},{4,8},{5,9},{6,10},{7,11}} | collective-permute-start | bytes 786440 | tf_op jit(solution)/shard_map/ppermute | solution.py:195
  43.9 6.9 %collective-permute-start.8 = (f32[256,256]{1,0:T(8,128)}, f32[256,256]{1,0:T(8,128)S(1)}, u32[]{:S(2)}, u32[]{:S(2)}) collective-permute-start(f32[256,256]{1,0:T(8,128)} %get-tuple-element.29), channel_id=1, source_target_pairs={{0,20},{1,21},{2,22},{3,23},{4,16},{5,17},{6,18},{7,19}} | collective-permute-start | bytes 786440 | tf_op jit(solution)/shard_map/ppermute | solution.py:195
  45.2 20.9 %collective-permute-start.12 = (f32[256,640]{1,0:T(8,128)}, f32[256,640]{1,0:T(8,128)S(1)}, u32[]{:S(2)}, u32[]{:S(2)}) collective-permute-start(f32[256,640]{1,0:T(8,128)} %slice.29), channel_id=1, source_target_pairs={{4,6},{5,7},{6,4},{7,5},{8,10},{9,11},{10,8},{11,9},{16,18},{17,19... | collective-permute-start | bytes 1966088 | tf_op jit(solution)/shard_map/ppermute | solution.py:187
  59.2 12.6 %copy-start.3 = (f32[256,256]{1,0:T(8,128)S(1)}, f32[256,256]{1,0:T(8,128)}, u32[]{:S(2)}) copy-start(f32[256,256]{1,0:T(8,128)} %copy-done.2) | copy-start | bytes 786436
  59.2 6.9 %collective-permute-start.11 = (f32[256,256]{1,0:T(8,128)S(1)}, f32[256,256]{1,0:T(8,128)S(1)}, u32[]{:S(2)}, u32[]{:S(2)}) collective-permute-start(f32[256,256]{1,0:T(8,128)S(1)} %select_select_fusion.held), channel_id=1, source_target_pairs={{0,4},{1,5},{2,6},{3,7},{4,0},{5,1},{6,2},{7,3},{8,12},{9,13},{10,... | collective-permute-start | bytes 786440 | tf_op jit(solution)/shard_map/ppermute | solution.py:222
  69.7 2.1 %copy-start.5 = (f32[256,256]{1,0:T(8,128)S(1)}, f32[256,256]{1,0:T(8,128)}, u32[]{:S(2)}) copy-start(f32[256,256]{1,0:T(8,128)} %copy-done.4) | copy-start | bytes 786436
  69.7 10.3 %collective-permute-start.13 = (f32[1024,128]{1,0:T(8,128)}, f32[1024,128]{1,0:T(8,128)S(1)}, u32[]{:S(2)}, u32[]{:S(2)}) collective-permute-start(f32[1024,128]{1,0:T(8,128)} %get-tuple-element.40), channel_id=1, source_target_pairs={{4,5},{5,4},{6,7},{7,6},{8,9},{9,8},{10,11},{11,10},{12,13},{13,12... | collective-permute-start | bytes 1572872 | tf_op jit(solution)/shard_map/ppermute | solution.py:187
  71.9 0.7 collective-permute-start.10

commit v13 on v12

--- a/solution.py
+++ b/solution.py
@@ -35,7 +35,7 @@
         in_specs=[pl.BlockSpec(memory_space=space) for space in spaces],
         out_specs=[pl.BlockSpec(memory_space=pltpu.VMEM)] * len(shapes),
         scratch_shapes=[pltpu.VMEM(shape, jnp.float32) for shape in scratch]
-        + [pltpu.SemaphoreType.DMA((6,))] * (1 if far else 0),
+        + [pltpu.SemaphoreType.DMA((12,))] * (1 if far else 0),
         compiler_params=pltpu.CompilerParams(vmem_limit_bytes=LIMIT),
         cost_estimate=pl.CostEstimate(flops=flops, bytes_accessed=0, transcendentals=0),
     )(*flags, *near, *far)
@@ -76,7 +76,7 @@
             shuffled[:, at * cands : (at + 1) * cands] = pieces[place]
 
 
-def second_kernel(places, row, lead, far_lead, sent, got, first, solved, bundle, *refs):
+def second_kernel(places, row, lead, far_lead, sent, got, first, bundle, *refs):
     inverse_other, sums, more, sems = refs
     width = sums.shape[0]
     cands = sums.shape[1] // len(places)
@@ -97,7 +97,6 @@
         both = jnp.concatenate([lead[:, last], inverse_other[...]], axis=0)
         rest = [sums[:, place * cands : (place + 1) * cands] for place in places]
         second = dot(both, -(jnp.concatenate(rest, axis=1) + more[...]), 1)
-        solved[...] = second
         bundle[...] = second
 
     @pl.when(row[0] == 1)
@@ -111,8 +110,7 @@
     mine, other, base, sems = refs
     n_design, cands = base.shape
     depth = held.shape[0] // 2
-    count = early.shape[1]
-    parts = [slice(0, count), slice(count, n_design)]
+    parts = [slice(at * n_design // 4, (at + 1) * n_design // 4) for at in range(4)]
     is_odd = row[0] % 2 == 1
 
     def fetch(at, source):
@@ -122,19 +120,24 @@
     def _():
         copies = []
         for at, part in enumerate(parts):
-            copies += [
-                pltpu.make_async_copy(flat.at[:, part], mine.at[:, part], sems.at[2 + at]),
-                pltpu.make_async_copy(cross.at[part], base.at[part], sems.at[4 + at]),
-            ]
+            copies.append(
+                [
+                    pltpu.make_async_copy(flat.at[:, part], mine.at[:, part], sems.at[4 + at]),
+                    pltpu.make_async_copy(cross.at[part], base.at[part], sems.at[8 + at]),
+                ]
+            )
         sources = [
-            (row[0] == 1, [beside.at[:, parts[0]], tail]),
-            ((row[0] > 1) & ~is_odd, [early, tail]),
+            (row[0] == 1, [array.at[:, part] for array in (beside, tail) for part in parts[:2]]),
+            (
+                (row[0] > 1) & ~is_odd,
+                [array.at[:, part] for array in (early, tail) for part in parts[:2]],
+            ),
             ((row[0] > 1) & is_odd, [whole.at[:, part] for part in parts]),
         ]
-        for at in range(2):
-            for chosen, pair in sources:
-                pl.when(chosen)(lambda at=at, pair=pair: fetch(at, pair[at]).start())
-            for copy in copies[2 * at : 2 * at + 2]:
+        for at in range(4):
+            for chosen, pieces in sources:
+                pl.when(chosen)(lambda at=at, pieces=pieces: fetch(at, pieces[at]).start())
+            for copy in copies[at]:
                 copy.start()
         has_first = (row[0] == 1) | ((row[0] > 1) & ~is_odd)
         first = jnp.where(has_first, held[...], got[...])
@@ -145,7 +148,7 @@
         solved = split(solved)
         for at, part in enumerate(parts):
             fetch(at, whole.at[:, part]).wait()
-            for copy in copies[2 * at : 2 * at + 2]:
+            for copy in copies[at]:
                 copy.wait()
             factors = jnp.concatenate([mine[:, part], other[:, part]], axis=0)
             partial = dot(factors, solved, 0)
@@ -233,7 +236,7 @@
         width = block_inverses.shape[2]
         depth = block_inverses.shape[1]
         n_design, cands = cross_kernel.shape
-        count = n_design * 3 // 8
+        count = n_design // 2
         top = [0]
         beside = [1]
         evens, odds = range(2, n_rows, 2), range(3, n_rows, 2)
@@ -270,9 +273,9 @@
             sums = sums + got
             bit *= 2
         first_beside = send_down(first, 1, top)
-        second, bundle = call(
+        (bundle,) = call(
             functools.partial(second_kernel, places),
-            [(2 * depth, half * cands)] * 2,
+            [(2 * depth, half * cands)],
             6 * 2 * depth * width * half * cands,
             [lead],
             [lead_other, shuffled, sums, first_beside],
@@ -282,11 +285,11 @@
         first_beside, head = lax.optimization_barrier((first_beside, head))
         late = swap(head, half, beside)
         held = broadcast_outer(bundle, row_id)
-        held, second, late = lax.optimization_barrier((held, second, late))
+        held, late = lax.optimization_barrier((held, late))
         tail = swap(tail, half, [*beside, *evens])
         solved = [held, swap_cores(held)]
 
-        pair = jnp.concatenate([first, second], axis=0)
+        pair = jnp.concatenate([first, held], axis=0)
         others = [swap(block(pair, step, cands), step, top) for step in range(1, half)]
         offsets = [at for step in range(half) for at in (step, step ^ half)]
         (top_rows,) = call(

time: 81.3 us -> 79 us (0.972)
  the two profiles are of different devices: /device:TPU:1 before, /device:TPU:2 now
where the time goes in v13:
time: 79 us; the launch traced here: 77.8 us
  waiting for transfers between devices  46.4 us (59%)
  starting transfers between devices  23.2 us (29%)
  Pallas kernels  4.48 us (6%)
  local copies, waits for them, and re-layouts  2.36 us (3%)
  other arithmetic  0.99 us (1%)
    ppermute x9, waiting for transfers between devices, swap(): return lax.ppermute(array, AXES, pairs)  38.5 us
    ppermute x9, starting transfers between devices, swap(): return lax.ppermute(array, AXES, pairs)  15.2 us
    ppermute x4, waiting for transfers between devices, send_down(): return lax.ppermute(array, AXES, pairs)  7.93 us
    ppermute x1, starting transfers between devices, swap_cores(): return lax.ppermute(array, AXES, pairs)  4.69 us
    pallas_call x4, Pallas kernels, call(): pl.pallas_call(kernel, out_shape=[jax.ShapeDtypeStruct(shape, jnp.float32...  4.48 us
    ppermute x4, starting transfers between devices, send_down(): return lax.ppermute(array, AXES, pairs)  3.32 us
  transfers between devices with their start and end apart: 14, of which 4 were waited for; matrix products, arithmetic and copies ran while one was open for 3% of the time, Pallas kernels for 0%

profile of v13, /device:TPU:2, one launch (start us, length us, event | category | flops | bytes accessed | tf_op | source)
XLA Modules:
  0.0 77.8 jit_solution(14686880739154317476)
XLA Ops:
  0.0 0.0 copy-start.4
  0.0 1.8 %collective-permute-start.3 = (f32[256,1024]{1,0:T(8,128)}, f32[256,1024]{1,0:T(8,128)}, u32[]{:S(2)}, u32[]{:S(2)}) collective-permute-start(f32[256,1024]{1,0:T(8,128)} %bitcast.9), channel_id=1, source_target_pairs={{12,14},{13,15},{14,12},{15,13},{20,22},{21,23},{22,20},{23,21},{2... | collective-permute-start | bytes 3145736 | tf_op jit(solution)/shard_map/ppermute | solution.py:190
  1.8 1.0 %slice_bitcast_fusion.1 = f32[128,512]{1,0:T(8,128)S(1)} fusion(f32[2,128,1024]{2,1,0:T(8,128)} %param.4), kind=kLoop, calls=%fused_computation.4 | loop fusion | bytes 524288 | tf_op jit(solution)/shard_map/squeeze | solution.py:246
  2.8 0.0 copy-done.4
  2.8 0.0 copy-start
  2.8 0.0 copy-start.1
  2.8 0.1 pad_maximum_fusion.lead
  2.9 0.8 %collective-permute-start = (f32[128,1536]{1,0:T(8,128)S(1)}, f32[128,1536]{1,0:T(8,128)S(1)}, u32[]{:S(2)}, u32[]{:S(2)}) collective-permute-start(f32[128,1536]{1,0:T(8,128)S(1)} %pad_maximum_fusion.lead), channel_id=1, source_target_pairs={{0,2},{1,3},{2,0},{3,1}} | collective-permute-start | bytes 2359304 | tf_op jit(solution)/shard_map/ppermute | solution.py:190
  3.8 0.2 copy-done.1
  4.0 1.4 %collective-permute-start.1 = (f32[1024,128]{1,0:T(8,128)S(1)}, f32[1024,128]{1,0:T(8,128)}, u32[]{:S(2)}, u32[]{:S(2)}) collective-permute-start(f32[1024,128]{1,0:T(8,128)S(1)} %copy-done.1), channel_id=1, source_target_pairs={{0,1},{1,0},{2,3},{3,2}} | collective-permute-start | bytes 1572872 | tf_op jit(solution)/shard_map/ppermute | solution.py:190
  5.4 0.0 copy-done
  5.4 1.1 %fusion = (f32[256,512]{1,0:T(8,128)}, f32[256,512]{1,0:T(8,128)}) fusion(f32[256,1024]{1,0:T(8,128)S(1)} %bitcast.10), kind=kLoop, calls=%fused_computation.8 | loop fusion | bytes 2097152 | tf_op jit(solution)/shard_map/slice | solution.py:254
  6.5 4.5 %collective-permute-start.2 = (f32[256,512]{1,0:T(8,128)}, f32[256,512]{1,0:T(8,128)}, u32[]{:S(2)}, u32[]{:S(2)}) collective-permute-start(f32[256,512]{1,0:T(8,128)} %get-tuple-element.27), channel_id=1, source_target_pairs={{8,10},{9,11},{10,8},{11,9},{16,18},{17,19},{18,16},{19,17},{24,26... | collective-permute-start | bytes 1572872 | tf_op jit(solution)/shard_map/ppermute | solution.py:190
  11.0 0.0 collective-permute-done.far_lead
  11.0 0.0 collective-permute-done.1.refs_0_
  11.0 0.1 shard_map.37
  11.1 0.0 copy-start.2
  11.1 23.8 %collective-permute-done.2.early = f32[256,512]{1,0:T(8,128)} collective-permute-done((f32[256,512]{1,0:T(8,128)}, f32[256,512]{1,0:T(8,128)}, u32[]{:S(2)}, u32[]{:S(2)}) %collective-permute-start.2) | collective-permute-done | bytes 524320 | tf_op jit(solution)/shard_map/ppermute | solution.py:190
  34.9 0.0 collective-permute-done.3.whole
  34.9 0.7 collective-permute-start.4
  35.6 0.7 collective-permute-start.5
  36.3 0.0 collective-permute-done.5.first
  36.3 1.5 %collective-permute-start.9 = (f32[256,512]{1,0:T(8,128)}, f32[256,512]{1,0:T(8,128)}, u32[]{:S(2)}, u32[]{:S(2)}) collective-permute-start(f32[256,512]{1,0:T(8,128)} %get-tuple-element.27), channel_id=1, source_target_pairs={{4,6},{5,7},{6,4},{7,5}} | collective-permute-start | bytes 1572872 | tf_op jit(solution)/shard_map/ppermute | solution.py:190
  37.8 0.0 collective-permute-done.4.got
  37.8 0.1 shard_map.38
  37.9 0.0 copy-done.2
  37.9 0.7 collective-permute-start.6
  38.6 1.3 %collective-permute-start.7 = (f32[256,256]{1,0:T(8,128)S(1)}, f32[256,256]{1,0:T(8,128)S(1)}, u32[]{:S(2)}, u32[]{:S(2)}) collective-permute-start(f32[256,256]{1,0:T(8,128)S(1)} %shard_map.38), channel_id=1, source_target_pairs={{0,12},{1,13},{2,14},{3,15},{4,8},{5,9},{6,10},{7,11}} | collective-permute-start | bytes 786440 | tf_op jit(solution)/shard_map/ppermute | solution.py:198
  39.9 0.7 collective-permute-start.8
  40.6 1.9 %collective-permute-start.12 = (f32[256,512]{1,0:T(8,128)}, f32[256,512]{1,0:T(8,128)S(1)}, u32[]{:S(2)}, u32[]{:S(2)}) collective-permute-start(f32[256,512]{1,0:T(8,128)} %get-tuple-element.32), channel_id=1, source_target_pairs={{4,6},{5,7},{6,4},{7,5},{8,10},{9,11},{10,8},{11,9},{16,18},{17,19... | collective-permute-start | bytes 1572872 | tf_op jit(solution)/shard_map/ppermute | solution.py:190
  42.5 0.0 collective-permute-done.6
  42.5 7.9 %collective-permute-done.7 = f32[256,256]{1,0:T(8,128)S(1)} collective-permute-done((f32[256,256]{1,0:T(8,128)S(1)}, f32[256,256]{1,0:T(8,128)S(1)}, u32[]{:S(2)}, u32[]{:S(2)}) %collective-permute-start.7) | collective-permute-done | bytes 262176 | tf_op jit(solution)/shard_map/ppermute | solution.py:198
  50.5 0.0 collective-permute-done.8
  50.5 0.1 select_select_fusion.held
  50.5 0.0 copy-start.3
  50.5 0.0 collective-permute-done.9.beside
  50.6 4.7 %collective-permute-start.11 = (f32[256,256]{1,0:T(8,128)S(1)}, f32[256,256]{1,0:T(8,128)S(1)}, u32[]{:S(2)}, u32[]{:S(2)}) collective-permute-start(f32[256,256]{1,0:T(8,128)S(1)} %select_select_fusion.held), channel_id=1, source_target_pairs={{0,4},{1,5},{2,6},{3,7},{4,0},{5,1},{6,2},{7,3},{8,12},{9,13},{10,... | collective-permute-start | bytes 786440 | tf_op jit(solution)/shard_map/ppermute | solution.py:225
  55.3 2.6 %collective-permute-done.12.tail = f32[256,512]{1,0:T(8,128)S(1)} collective-permute-done((f32[256,512]{1,0:T(8,128)}, f32[256,512]{1,0:T(8,128)S(1)}, u32[]{:S(2)}, u32[]{:S(2)}) %collective-permute-start.12) | collective-permute-done | bytes 524320 | tf_op jit(solution)/shard_map/ppermute | solution.py:190
  57.9 0.0 collective-permute-done.11.got
  57.9 4.2 %shard_map.40 = (f32[1024,128]{1,0:T(8,128)S(1)}, f32[1024,128]{1,0:T(8,128)}) custom-call(s32[1]{0:T(128)} %bitcast.1.row, f32[256,256]{1,0:T(8,128)S(1)} %select_select_fusion.held, f32[256,256]{1,0:T(8,128)S(1)} %collective-permute-done.11.got, f32[256,1024]{1,0:T(8,128)S(1)} %bitcast.11, f32[256,1024]{1,0:T(8,128)} %collective-permute-done.3.whole, ...), custom_call_target="tpu_custom_call" | custom-call | flops 805306368 | tf_op jit(solution)/shard_map/pallas_call | solution.py:32
  62.1 1.9 %collective-permute-start.13 = (f32[1024,128]{1,0:T(8,128)}, f32[1024,128]{1,0:T(8,128)S(1)}, u32[]{:S(2)}, u32[]{:S(2)}) collective-permute-start(f32[1024,128]{1,0:T(8,128)} %get-tuple-element.34), channel_id=1, source_target_pairs={{4,5},{5,4},{6,7},{7,6},{8,9},{9,8},{10,11},{11,10},{12,13},{13,12... | collective-permute-start | bytes 1572872 | tf_op jit(solution)/shard_map/ppermute | solution.py:190
  64.0 0.0 copy-done.3
  64.1 0.7 collective-permute-start.10
  64.8 0.0 collective-permute-done.10.refs_0_
  64.8 0.1 shard_map.39
  64.9 12.1 %collective-permute-done.13 = f32[1024,128]{1,0:T(8,128)S(1)} collective-permute-done((f32[1024,128]{1,0:T(8,128)}, f32[1024,128]{1,0:T(8,128)S(1)}, u32[]{:S(2)}, u32[]{:S(2)}) %collective-permute-start.13) | collective-permute-done | bytes 524320 | tf_op jit(solution)/shard_map/ppermute | solution.py:190
  76.9 0.9 %subtract_select_fusion = f32[1024,128]{1,0:T(8,128)} fusion(f32[1024,128]{1,0:T(8,128)S(1)} %shard_map.39, f32[1024,128]{1,0:T(8,128)S(1)} %get-tuple-element.33, f32[1024,128]{1,0:T(8,128)S(1)} %collective-permute-done.13, pred[]{:T(512)S(6)} %eq.14), kind=kLoop, calls=%fused_computation.1 | loop fusion | flops 262144 | bytes 2097153 | tf_op jit(solution)/shard_map/jit(_where)/select_n | solution.py:314
  (4 shorter events, 0.1 us)
Async XLA Ops:
  0.0 2.8 %copy-start.4 = (f32[2,128,512]{2,1,0:T(8,128)S(1)}, f32[2,128,512]{2,1,0:T(8,128)}, u32[]{:S(2)}) copy-start(f32[2,128,512]{2,1,0:T(8,128)} %param.5) | copy-start | bytes 1572868
  0.0 34.9 %collective-permute-start.3 = (f32[256,1024]{1,0:T(8,128)}, f32[256,1024]{1,0:T(8,128)}, u32[]{:S(2)}, u32[]{:S(2)}) collective-permute-start(f32[256,1024]{1,0:T(8,128)} %bitcast.9), channel_id=1, source_target_pairs={{12,14},{13,15},{14,12},{15,13},{20,22},{21,23},{22,20},{23,21},{2... | collective-permute-start | bytes 3145736 | tf_op jit(solution)/shard_map/ppermute | solution.py:190
  2.8 2.6 %copy-start = (f32[2,128,1024]{2,1,0:T(8,128)S(1)}, f32[2,128,1024]{2,1,0:T(8,128)}, u32[]{:S(2)}) copy-start(f32[2,128,1024]{2,1,0:T(8,128)} %param.4) | copy-start | bytes 3145732
  2.8 1.1 %copy-start.1 = (f32[1024,128]{1,0:T(8,128)S(1)}, f32[1024,128]{1,0:T(8,128)}, u32[]{:S(2)}) copy-start(f32[1024,128]{1,0:T(8,128)} %cross.1) | copy-start | bytes 1572868
  2.9 8.1 %collective-permute-start = (f32[128,1536]{1,0:T(8,128)S(1)}, f32[128,1536]{1,0:T(8,128)S(1)}, u32[]{:S(2)}, u32[]{:S(2)}) collective-permute-start(f32[128,1536]{1,0:T(8,128)S(1)} %pad_maximum_fusion.lead), channel_id=1, source_target_pairs={{0,2},{1,3},{2,0},{3,1}} | collective-permute-start | bytes 2359304 | tf_op jit(solution)/shard_map/ppermute | solution.py:190
  4.0 7.0 %collective-permute-start.1 = (f32[1024,128]{1,0:T(8,128)S(1)}, f32[1024,128]{1,0:T(8,128)}, u32[]{:S(2)}, u32[]{:S(2)}) collective-permute-start(f32[1024,128]{1,0:T(8,128)S(1)} %copy-done.1), channel_id=1, source_target_pairs={{0,1},{1,0},{2,3},{3,2}} | collective-permute-start | bytes 1572872 | tf_op jit(solution)/shard_map/ppermute | solution.py:190
  6.5 28.4 %collective-permute-start.2 = (f32[256,512]{1,0:T(8,128)}, f32[256,512]{1,0:T(8,128)}, u32[]{:S(2)}, u32[]{:S(2)}) collective-permute-start(f32[256,512]{1,0:T(8,128)} %get-tuple-element.27), channel_id=1, source_target_pairs={{8,10},{9,11},{10,8},{11,9},{16,18},{17,19},{18,16},{19,17},{24,26... | collective-permute-start | bytes 1572872 | tf_op jit(solution)/shard_map/ppermute | solution.py:190
  11.1 26.8 %copy-start.2 = (f32[256,256]{1,0:T(8,128)}, f32[256,256]{1,0:T(8,128)S(1)}, u32[]{:S(2)}) copy-start(f32[256,256]{1,0:T(8,128)S(1)} %get-tuple-element.23) | copy-start | bytes 786436
  34.9 2.8 %collective-permute-start.4 = (f32[512,256]{1,0:T(8,128)S(1)}, f32[512,256]{1,0:T(8,128)S(1)}, u32[]{:S(2)}, u32[]{:S(2)}) collective-permute-start(f32[512,256]{1,0:T(8,128)S(1)} %get-tuple-element.25.sent), channel_id=1, source_target_pairs={{0,1},{1,0},{2,3},{3,2}} | collective-permute-start | bytes 1572872 | tf_op jit(solution)/shard_map/ppermute | solution.py:190
  35.6 0.7 collective-permute-start.5
  36.3 14.2 %collective-permute-start.9 = (f32[256,512]{1,0:T(8,128)}, f32[256,512]{1,0:T(8,128)}, u32[]{:S(2)}, u32[]{:S(2)}) collective-permute-start(f32[256,512]{1,0:T(8,128)} %get-tuple-element.27), channel_id=1, source_target_pairs={{4,6},{5,7},{6,4},{7,5}} | collective-permute-start | bytes 1572872 | tf_op jit(solution)/shard_map/ppermute | solution.py:190
  37.9 4.6 %collective-permute-start.6 = (f32[256,256]{1,0:T(8,128)S(1)}, f32[256,256]{1,0:T(8,128)S(1)}, u32[]{:S(2)}, u32[]{:S(2)}) collective-permute-start(f32[256,256]{1,0:T(8,128)S(1)} %shard_map.38), channel_id=1, source_target_pairs={{0,28},{1,29},{2,30},{3,31},{4,24},{5,25},{6,26},{7,27}} | collective-permute-start | bytes 786440 | tf_op jit(solution)/shard_map/ppermute | solution.py:198
  38.6 11.9 %collective-permute-start.7 = (f32[256,256]{1,0:T(8,128)S(1)}, f32[256,256]{1,0:T(8,128)S(1)}, u32[]{:S(2)}, u32[]{:S(2)}) collective-permute-start(f32[256,256]{1,0:T(8,128)S(1)} %shard_map.38), channel_id=1, source_target_pairs={{0,12},{1,13},{2,14},{3,15},{4,8},{5,9},{6,10},{7,11}} | collective-permute-start | bytes 786440 | tf_op jit(solution)/shard_map/ppermute | solution.py:198
  39.9 10.6 %collective-permute-start.8 = (f32[256,256]{1,0:T(8,128)S(1)}, f32[256,256]{1,0:T(8,128)S(1)}, u32[]{:S(2)}, u32[]{:S(2)}) collective-permute-start(f32[256,256]{1,0:T(8,128)S(1)} %shard_map.38), channel_id=1, source_target_pairs={{0,20},{1,21},{2,22},{3,23},{4,16},{5,17},{6,18},{7,19}} | collective-permute-start | bytes 786440 | tf_op jit(solution)/shard_map/ppermute | solution.py:198
  40.6 17.3 %collective-permute-start.12 = (f32[256,512]{1,0:T(8,128)}, f32[256,512]{1,0:T(8,128)S(1)}, u32[]{:S(2)}, u32[]{:S(2)}) collective-permute-start(f32[256,512]{1,0:T(8,128)} %get-tuple-element.32), channel_id=1, source_target_pairs={{4,6},{5,7},{6,4},{7,5},{8,10},{9,11},{10,8},{11,9},{16,18},{17,19... | collective-permute-start | bytes 1572872 | tf_op jit(solution)/shard_map/ppermute | solution.py:190
  50.5 13.5 %copy-start.3 = (f32[256,256]{1,0:T(8,128)S(1)}, f32[256,256]{1,0:T(8,128)}, u32[]{:S(2)}) copy-start(f32[256,256]{1,0:T(8,128)} %copy-done.2) | copy-start | bytes 786436
  50.6 7.3 %collective-permute-start.11 = (f32[256,256]{1,0:T(8,128)S(1)}, f32[256,256]{1,0:T(8,128)S(1)}, u32[]{:S(2)}, u32[]{:S(2)}) collective-permute-start(f32[256,256]{1,0:T(8,128)S(1)} %select_select_fusion.held), channel_id=1, source_target_pairs={{0,4},{1,5},{2,6},{3,7},{4,0},{5,1},{6,2},{7,3},{8,12},{9,13},{10,... | collective-permute-start | bytes 786440 | tf_op jit(solution)/shard_map/ppermute | solution.py:225
  62.1 14.8 %collective-permute-start.13 = (f32[1024,128]{1,0:T(8,128)}, f32[1024,128]{1,0:T(8,128)S(1)}, u32[]{:S(2)}, u32[]{:S(2)}) collective-permute-start(f32[1024,128]{1,0:T(8,128)} %get-tuple-element.34), channel_id=1, source_target_pairs={{4,5},{5,4},{6,7},{7,6},{8,9},{9,8},{10,11},{11,10},{12,13},{13,12... | collective-permute-start | bytes 1572872 | tf_op jit(solution)/shard_map/ppermute | solution.py:190
  64.1 0.7 collective-permute-start.10

commit v14 on v13

--- a/solution.py
+++ b/solution.py
@@ -127,7 +127,7 @@
                 ]
             )
         sources = [
-            (row[0] == 1, [array.at[:, part] for array in (beside, tail) for part in parts[:2]]),
+            (row[0] == 1, [beside.at[:, part] for part in parts]),
             (
                 (row[0] > 1) & ~is_odd,
                 [array.at[:, part] for array in (early, tail) for part in parts[:2]],
@@ -250,9 +250,7 @@
         rhs_others = [swap(rhs, step, top) for step in range(1, half)]
         whole = swap(flat, half, odds)
         arrived = swap(flat[:, :count], half, evens)
-        lead_other, head, tail = lax.optimization_barrier(
-            (lead_other, flat[:, : n_design // 2], flat[:, count:])
-        )
+        lead_other, tail = lax.optimization_barrier((lead_other, flat[:, count:]))
 
         places = [at ^ 1 for at in range(half)]
         first, shuffled = call(
@@ -282,11 +280,11 @@
             row_id,
             [(depth, width)] + [(width, half * cands)] * 2,
         )
-        first_beside, head = lax.optimization_barrier((first_beside, head))
-        late = swap(head, half, beside)
+        first_beside, late = lax.optimization_barrier((first_beside, flat))
+        late = swap(late, half, beside)
         held = broadcast_outer(bundle, row_id)
-        held, late = lax.optimization_barrier((held, late))
-        tail = swap(tail, half, [*beside, *evens])
+        tail = swap(tail, half, evens)
+        held, late, tail = lax.optimization_barrier((held, late, tail))
         solved = [held, swap_cores(held)]
 
         pair = jnp.concatenate([first, held], axis=0)

time: 79 us -> 82.7 us (1.047)
  waiting for transfers between devices: 46.4 us -> 50.6 us
    ppermute x9, starting transfers between devices: 15.2 us -> 18.2 us  [swap(): return lax.ppermute(array, AXES, pairs)]
    ppermute x1, starting transfers between devices: 4.69 us -> 1.74 us  [swap_cores(): return lax.ppermute(array, AXES, pairs)]
    ppermute x4, waiting for transfers between devices: 7.93 us -> 10.4 us  [send_down(): return lax.ppermute(array, AXES, pairs)]
    ppermute x1, waiting for transfers between devices: 0.01 us -> 1.16 us  [swap_cores(): return lax.ppermute(array, AXES, pairs)]
    squeeze x1, local copies, waits for them, and re-layouts: 0.04 us -> 1.15 us  [on_device(): block_inverses[0]]
    squeeze x1, local copies, waits for them, and re-layouts: 0.97 us -> 0.02 us  [on_device(): factor_panels[0, :, width:2 * width]]
  transfers between devices with their start and end apart: 14 -> 14, of which waited for: 4 -> 5; matrix products, arithmetic and copies ran while one was open for 3% -> 1% of each run, Pallas kernels for 0% -> 0%
where the time goes in v14:
time: 82.7 us; the launch traced here: 82.2 us
  waiting for transfers between devices  50.6 us (61%)
  starting transfers between devices  23.3 us (28%)
  Pallas kernels  4.5 us (5%)
  local copies, waits for them, and re-layouts  2.52 us (3%)
  other arithmetic  0.99 us (1%)
    ppermute x9, waiting for transfers between devices, swap(): return lax.ppermute(array, AXES, pairs)  39.1 us
    ppermute x9, starting transfers between devices, swap(): return lax.ppermute(array, AXES, pairs)  18.2 us
    ppermute x4, waiting for transfers between devices, send_down(): return lax.ppermute(array, AXES, pairs)  10.4 us
    pallas_call x4, Pallas kernels, call(): pl.pallas_call(kernel, out_shape=[jax.ShapeDtypeStruct(shape, jnp.float32...  4.5 us
    ppermute x4, starting transfers between devices, send_down(): return lax.ppermute(array, AXES, pairs)  3.32 us
    ppermute x1, starting transfers between devices, swap_cores(): return lax.ppermute(array, AXES, pairs)  1.74 us
  transfers between devices with their start and end apart: 14, of which 5 were waited for; matrix products, arithmetic and copies ran while one was open for 1% of the time, Pallas kernels for 0%

profile of v14, /device:TPU:2, one launch (start us, length us, event | category | flops | bytes accessed | tf_op | source)
XLA Modules:
  0.0 82.2 jit_solution(7447550588004196938)
XLA Ops:
  0.0 0.0 copy-start
  0.0 1.2 %slice_bitcast_fusion.2 = (f32[128,512]{1,0:T(8,128)S(1)}, f32[128,512]{1,0:T(8,128)S(1)}) fusion(f32[2,128,512]{2,1,0:T(8,128)} %param.5), kind=kLoop, calls=%fused_computation.5 | loop fusion | bytes 1048576 | tf_op jit(solution)/shard_map/squeeze | solution.py:246
  1.2 0.2 copy-done
  1.4 0.0 copy-start.1
  1.4 0.1 pad_maximum_fusion.lead
  1.5 0.8 %collective-permute-start = (f32[128,1536]{1,0:T(8,128)S(1)}, f32[128,1536]{1,0:T(8,128)S(1)}, u32[]{:S(2)}, u32[]{:S(2)}) collective-permute-start(f32[128,1536]{1,0:T(8,128)S(1)} %pad_maximum_fusion.lead), channel_id=1, source_target_pairs={{0,2},{1,3},{2,0},{3,1}} | collective-permute-start | bytes 2359304 | tf_op jit(solution)/shard_map/ppermute | solution.py:190
  2.3 1.7 %collective-permute-start.3 = (f32[256,1024]{1,0:T(8,128)S(1)}, f32[256,1024]{1,0:T(8,128)}, u32[]{:S(2)}, u32[]{:S(2)}) collective-permute-start(f32[256,1024]{1,0:T(8,128)S(1)} %bitcast.9), channel_id=1, source_target_pairs={{12,14},{13,15},{14,12},{15,13},{20,22},{21,23},{22,20},{23,21},{2... | collective-permute-start | bytes 3145736 | tf_op jit(solution)/shard_map/ppermute | solution.py:190
  4.0 0.0 copy-done.1
  4.0 1.5 %collective-permute-start.1 = (f32[1024,128]{1,0:T(8,128)S(1)}, f32[1024,128]{1,0:T(8,128)}, u32[]{:S(2)}, u32[]{:S(2)}) collective-permute-start(f32[1024,128]{1,0:T(8,128)S(1)} %copy-done.1), channel_id=1, source_target_pairs={{0,1},{1,0},{2,3},{3,2}} | collective-permute-start | bytes 1572872 | tf_op jit(solution)/shard_map/ppermute | solution.py:190
  5.4 1.0 %fusion = (f32[256,512]{1,0:T(8,128)}, f32[256,512]{1,0:T(8,128)}) fusion(f32[256,1024]{1,0:T(8,128)S(1)} %bitcast.10), kind=kLoop, calls=%fused_computation.8 | loop fusion | bytes 2097152 | tf_op jit(solution)/shard_map/slice | solution.py:252
  6.5 4.5 %collective-permute-start.2 = (f32[256,512]{1,0:T(8,128)}, f32[256,512]{1,0:T(8,128)}, u32[]{:S(2)}, u32[]{:S(2)}) collective-permute-start(f32[256,512]{1,0:T(8,128)} %get-tuple-element.35), channel_id=1, source_target_pairs={{8,10},{9,11},{10,8},{11,9},{16,18},{17,19},{18,16},{19,17},{24,26... | collective-permute-start | bytes 1572872 | tf_op jit(solution)/shard_map/ppermute | solution.py:190
  11.0 0.0 collective-permute-done.far_lead
  11.0 0.0 collective-permute-done.1.refs_0_
  11.0 0.1 shard_map.37
  11.1 0.0 copy-start.2
  11.1 0.7 collective-permute-start.5
  11.8 25.1 %collective-permute-done.2.early = f32[256,512]{1,0:T(8,128)} collective-permute-done((f32[256,512]{1,0:T(8,128)}, f32[256,512]{1,0:T(8,128)}, u32[]{:S(2)}, u32[]{:S(2)}) %collective-permute-start.2) | collective-permute-done | bytes 524320 | tf_op jit(solution)/shard_map/ppermute | solution.py:190
  36.9 0.0 collective-permute-done.3.whole
  36.9 0.7 collective-permute-start.4
  37.6 0.0 collective-permute-done.5.first
  37.6 1.6 %collective-permute-start.9 = (f32[256,1024]{1,0:T(8,128)S(1)}, f32[256,1024]{1,0:T(8,128)}, u32[]{:S(2)}, u32[]{:S(2)}) collective-permute-start(f32[256,1024]{1,0:T(8,128)S(1)} %bitcast.11), channel_id=1, source_target_pairs={{4,6},{5,7},{6,4},{7,5}} | collective-permute-start | bytes 3145736 | tf_op jit(solution)/shard_map/ppermute | solution.py:190
  39.3 1.9 %collective-permute-start.10 = (f32[256,512]{1,0:T(8,128)}, f32[256,512]{1,0:T(8,128)}, u32[]{:S(2)}, u32[]{:S(2)}) collective-permute-start(f32[256,512]{1,0:T(8,128)} %get-tuple-element.27), channel_id=1, source_target_pairs={{8,10},{9,11},{10,8},{11,9},{16,18},{17,19},{18,16},{19,17},{24,26... | collective-permute-start | bytes 1572872 | tf_op jit(solution)/shard_map/ppermute | solution.py:190
  41.2 0.0 collective-permute-done.4.got
  41.2 0.1 shard_map.38
  41.3 0.0 copy-done.2
  41.3 0.7 collective-permute-start.6
  42.0 1.3 %collective-permute-start.7 = (f32[256,256]{1,0:T(8,128)S(1)}, f32[256,256]{1,0:T(8,128)S(1)}, u32[]{:S(2)}, u32[]{:S(2)}) collective-permute-start(f32[256,256]{1,0:T(8,128)S(1)} %shard_map.38), channel_id=1, source_target_pairs={{0,12},{1,13},{2,14},{3,15},{4,8},{5,9},{6,10},{7,11}} | collective-permute-start | bytes 786440 | tf_op jit(solution)/shard_map/ppermute | solution.py:198
  43.3 0.7 collective-permute-start.8
  44.0 0.0 collective-permute-done.6
  44.1 10.4 %collective-permute-done.7 = f32[256,256]{1,0:T(8,128)S(1)} collective-permute-done((f32[256,256]{1,0:T(8,128)S(1)}, f32[256,256]{1,0:T(8,128)S(1)}, u32[]{:S(2)}, u32[]{:S(2)}) %collective-permute-start.7) | collective-permute-done | bytes 262176 | tf_op jit(solution)/shard_map/ppermute | solution.py:198
  54.4 0.0 collective-permute-done.8
  54.4 0.1 select_select_fusion.held
  54.5 0.0 copy-start.3
  54.5 2.2 %collective-permute-done.10.tail = f32[256,512]{1,0:T(8,128)} collective-permute-done((f32[256,512]{1,0:T(8,128)}, f32[256,512]{1,0:T(8,128)}, u32[]{:S(2)}, u32[]{:S(2)}) %collective-permute-start.10) | collective-permute-done | bytes 524320 | tf_op jit(solution)/shard_map/ppermute | solution.py:190
  56.7 0.0 collective-permute-done.9.beside
  56.7 1.7 %collective-permute-start.12 = (f32[256,256]{1,0:T(8,128)S(1)}, f32[256,256]{1,0:T(8,128)S(1)}, u32[]{:S(2)}, u32[]{:S(2)}) collective-permute-start(f32[256,256]{1,0:T(8,128)S(1)} %select_select_fusion.held), channel_id=1, source_target_pairs={{0,4},{1,5},{2,6},{3,7},{4,0},{5,1},{6,2},{7,3},{8,12},{9,13},{10,... | collective-permute-start | bytes 786440 | tf_op jit(solution)/shard_map/ppermute | solution.py:225
  58.4 1.2 %collective-permute-done.12.got = f32[256,256]{1,0:T(8,128)S(1)} collective-permute-done((f32[256,256]{1,0:T(8,128)S(1)}, f32[256,256]{1,0:T(8,128)S(1)}, u32[]{:S(2)}, u32[]{:S(2)}) %collective-permute-start.12) | collective-permute-done | bytes 262176 | tf_op jit(solution)/shard_map/ppermute | solution.py:225
  59.6 4.2 %shard_map.40 = (f32[1024,128]{1,0:T(8,128)S(1)}, f32[1024,128]{1,0:T(8,128)}) custom-call(s32[1]{0:T(128)} %bitcast.1.row, f32[256,256]{1,0:T(8,128)S(1)} %select_select_fusion.held, f32[256,256]{1,0:T(8,128)S(1)} %collective-permute-done.12.got, f32[256,1024]{1,0:T(8,128)S(1)} %bitcast.12, f32[256,1024]{1,0:T(8,128)} %collective-permute-done.3.whole, ...), custom_call_target="tpu_custom_call" | custom-call | flops 805306368 | tf_op jit(solution)/shard_map/pallas_call | solution.py:32
  63.8 4.9 %collective-permute-start.13 = (f32[1024,128]{1,0:T(8,128)}, f32[1024,128]{1,0:T(8,128)S(1)}, u32[]{:S(2)}, u32[]{:S(2)}) collective-permute-start(f32[1024,128]{1,0:T(8,128)} %get-tuple-element.34), channel_id=1, source_target_pairs={{4,5},{5,4},{6,7},{7,6},{8,9},{9,8},{10,11},{11,10},{12,13},{13,12... | collective-permute-start | bytes 1572872 | tf_op jit(solution)/shard_map/ppermute | solution.py:190
  68.7 0.0 copy-done.3
  68.8 0.7 collective-permute-start.11
  69.4 0.0 collective-permute-done.11.refs_0_
  69.5 0.1 shard_map.39
  69.5 11.8 %collective-permute-done.13 = f32[1024,128]{1,0:T(8,128)S(1)} collective-permute-done((f32[1024,128]{1,0:T(8,128)}, f32[1024,128]{1,0:T(8,128)S(1)}, u32[]{:S(2)}, u32[]{:S(2)}) %collective-permute-start.13) | collective-permute-done | bytes 524320 | tf_op jit(solution)/shard_map/ppermute | solution.py:190
  81.3 0.9 %subtract_select_fusion = f32[1024,128]{1,0:T(8,128)} fusion(f32[1024,128]{1,0:T(8,128)S(1)} %shard_map.39, f32[1024,128]{1,0:T(8,128)S(1)} %get-tuple-element.33, f32[1024,128]{1,0:T(8,128)S(1)} %collective-permute-done.13, pred[]{:T(512)S(6)} %eq.14), kind=kLoop, calls=%fused_computation.1 | loop fusion | flops 262144 | bytes 2097153 | tf_op jit(solution)/shard_map/jit(_where)/select_n | solution.py:312
  (4 shorter events, 0.1 us)
Async XLA Ops:
  0.0 1.4 %copy-start = (f32[2,128,1024]{2,1,0:T(8,128)S(1)}, f32[2,128,1024]{2,1,0:T(8,128)}, u32[]{:S(2)}) copy-start(f32[2,128,1024]{2,1,0:T(8,128)} %param.4) | copy-start | bytes 3145732
  1.4 2.6 %copy-start.1 = (f32[1024,128]{1,0:T(8,128)S(1)}, f32[1024,128]{1,0:T(8,128)}, u32[]{:S(2)}) copy-start(f32[1024,128]{1,0:T(8,128)} %cross.1) | copy-start | bytes 1572868
  1.5 9.5 %collective-permute-start = (f32[128,1536]{1,0:T(8,128)S(1)}, f32[128,1536]{1,0:T(8,128)S(1)}, u32[]{:S(2)}, u32[]{:S(2)}) collective-permute-start(f32[128,1536]{1,0:T(8,128)S(1)} %pad_maximum_fusion.lead), channel_id=1, source_target_pairs={{0,2},{1,3},{2,0},{3,1}} | collective-permute-start | bytes 2359304 | tf_op jit(solution)/shard_map/ppermute | solution.py:190
  2.3 34.6 %collective-permute-start.3 = (f32[256,1024]{1,0:T(8,128)S(1)}, f32[256,1024]{1,0:T(8,128)}, u32[]{:S(2)}, u32[]{:S(2)}) collective-permute-start(f32[256,1024]{1,0:T(8,128)S(1)} %bitcast.9), channel_id=1, source_target_pairs={{12,14},{13,15},{14,12},{15,13},{20,22},{21,23},{22,20},{23,21},{2... | collective-permute-start | bytes 3145736 | tf_op jit(solution)/shard_map/ppermute | solution.py:190
  4.0 7.0 %collective-permute-start.1 = (f32[1024,128]{1,0:T(8,128)S(1)}, f32[1024,128]{1,0:T(8,128)}, u32[]{:S(2)}, u32[]{:S(2)}) collective-permute-start(f32[1024,128]{1,0:T(8,128)S(1)} %copy-done.1), channel_id=1, source_target_pairs={{0,1},{1,0},{2,3},{3,2}} | collective-permute-start | bytes 1572872 | tf_op jit(solution)/shard_map/ppermute | solution.py:190
  6.5 30.4 %collective-permute-start.2 = (f32[256,512]{1,0:T(8,128)}, f32[256,512]{1,0:T(8,128)}, u32[]{:S(2)}, u32[]{:S(2)}) collective-permute-start(f32[256,512]{1,0:T(8,128)} %get-tuple-element.35), channel_id=1, source_target_pairs={{8,10},{9,11},{10,8},{11,9},{16,18},{17,19},{18,16},{19,17},{24,26... | collective-permute-start | bytes 1572872 | tf_op jit(solution)/shard_map/ppermute | solution.py:190
  11.1 30.2 %copy-start.2 = (f32[256,256]{1,0:T(8,128)}, f32[256,256]{1,0:T(8,128)S(1)}, u32[]{:S(2)}) copy-start(f32[256,256]{1,0:T(8,128)S(1)} %get-tuple-element.23) | copy-start | bytes 786436
  11.1 26.5 %collective-permute-start.5 = (f32[256,256]{1,0:T(8,128)S(1)}, f32[256,256]{1,0:T(8,128)S(1)}, u32[]{:S(2)}, u32[]{:S(2)}) collective-permute-start(f32[256,256]{1,0:T(8,128)S(1)} %get-tuple-element.23), channel_id=1, source_target_pairs={{0,4},{1,5},{2,6},{3,7}} | collective-permute-start | bytes 786440 | tf_op jit(solution)/shard_map/ppermute | solution.py:198
  36.9 4.3 %collective-permute-start.4 = (f32[512,256]{1,0:T(8,128)S(1)}, f32[512,256]{1,0:T(8,128)S(1)}, u32[]{:S(2)}, u32[]{:S(2)}) collective-permute-start(f32[512,256]{1,0:T(8,128)S(1)} %get-tuple-element.25.sent), channel_id=1, source_target_pairs={{0,1},{1,0},{2,3},{3,2}} | collective-permute-start | bytes 1572872 | tf_op jit(solution)/shard_map/ppermute | solution.py:190
  37.6 19.0 %collective-permute-start.9 = (f32[256,1024]{1,0:T(8,128)S(1)}, f32[256,1024]{1,0:T(8,128)}, u32[]{:S(2)}, u32[]{:S(2)}) collective-permute-start(f32[256,1024]{1,0:T(8,128)S(1)} %bitcast.11), channel_id=1, source_target_pairs={{4,6},{5,7},{6,4},{7,5}} | collective-permute-start | bytes 3145736 | tf_op jit(solution)/shard_map/ppermute | solution.py:190
  39.3 17.4 %collective-permute-start.10 = (f32[256,512]{1,0:T(8,128)}, f32[256,512]{1,0:T(8,128)}, u32[]{:S(2)}, u32[]{:S(2)}) collective-permute-start(f32[256,512]{1,0:T(8,128)} %get-tuple-element.27), channel_id=1, source_target_pairs={{8,10},{9,11},{10,8},{11,9},{16,18},{17,19},{18,16},{19,17},{24,26... | collective-permute-start | bytes 1572872 | tf_op jit(solution)/shard_map/ppermute | solution.py:190
  41.3 2.7 %collective-permute-start.6 = (f32[256,256]{1,0:T(8,128)S(1)}, f32[256,256]{1,0:T(8,128)S(1)}, u32[]{:S(2)}, u32[]{:S(2)}) collective-permute-start(f32[256,256]{1,0:T(8,128)S(1)} %shard_map.38), channel_id=1, source_target_pairs={{0,28},{1,29},{2,30},{3,31},{4,24},{5,25},{6,26},{7,27}} | collective-permute-start | bytes 786440 | tf_op jit(solution)/shard_map/ppermute | solution.py:198
  42.0 12.4 %collective-permute-start.7 = (f32[256,256]{1,0:T(8,128)S(1)}, f32[256,256]{1,0:T(8,128)S(1)}, u32[]{:S(2)}, u32[]{:S(2)}) collective-permute-start(f32[256,256]{1,0:T(8,128)S(1)} %shard_map.38), channel_id=1, source_target_pairs={{0,12},{1,13},{2,14},{3,15},{4,8},{5,9},{6,10},{7,11}} | collective-permute-start | bytes 786440 | tf_op jit(solution)/shard_map/ppermute | solution.py:198
  43.3 11.1 %collective-permute-start.8 = (f32[256,256]{1,0:T(8,128)S(1)}, f32[256,256]{1,0:T(8,128)S(1)}, u32[]{:S(2)}, u32[]{:S(2)}) collective-permute-start(f32[256,256]{1,0:T(8,128)S(1)} %shard_map.38), channel_id=1, source_target_pairs={{0,20},{1,21},{2,22},{3,23},{4,16},{5,17},{6,18},{7,19}} | collective-permute-start | bytes 786440 | tf_op jit(solution)/shard_map/ppermute | solution.py:198
  54.5 14.2 %copy-start.3 = (f32[256,256]{1,0:T(8,128)S(1)}, f32[256,256]{1,0:T(8,128)}, u32[]{:S(2)}) copy-start(f32[256,256]{1,0:T(8,128)} %copy-done.2) | copy-start | bytes 786436
  56.7 2.9 %collective-permute-start.12 = (f32[256,256]{1,0:T(8,128)S(1)}, f32[256,256]{1,0:T(8,128)S(1)}, u32[]{:S(2)}, u32[]{:S(2)}) collective-permute-start(f32[256,256]{1,0:T(8,128)S(1)} %select_select_fusion.held), channel_id=1, source_target_pairs={{0,4},{1,5},{2,6},{3,7},{4,0},{5,1},{6,2},{7,3},{8,12},{9,13},{10,... | collective-permute-start | bytes 786440 | tf_op jit(solution)/shard_map/ppermute | solution.py:225
  63.8 17.5 %collective-permute-start.13 = (f32[1024,128]{1,0:T(8,128)}, f32[1024,128]{1,0:T(8,128)S(1)}, u32[]{:S(2)}, u32[]{:S(2)}) collective-permute-start(f32[1024,128]{1,0:T(8,128)} %get-tuple-element.34), channel_id=1, source_target_pairs={{4,5},{5,4},{6,7},{7,6},{8,9},{9,8},{10,11},{11,10},{12,13},{13,12... | collective-permute-start | bytes 1572872 | tf_op jit(solution)/shard_map/ppermute | solution.py:190
  68.8 0.7 collective-permute-start.11

commit v15 on v14

--- a/solution.py
+++ b/solution.py
@@ -22,7 +22,7 @@
         )
 
     left_high, left_low = split(left)
-    right_high, right_low = right if isinstance(right, tuple) else split(right)
+    right_high, right_low = split(right)
     return one(left_high, right_high) + (one(left_high, right_low) + one(left_low, right_high))
 
 
@@ -35,7 +35,7 @@
         in_specs=[pl.BlockSpec(memory_space=space) for space in spaces],
         out_specs=[pl.BlockSpec(memory_space=pltpu.VMEM)] * len(shapes),
         scratch_shapes=[pltpu.VMEM(shape, jnp.float32) for shape in scratch]
-        + [pltpu.SemaphoreType.DMA((12,))] * (1 if far else 0),
+        + [pltpu.SemaphoreType.DMA((6,))] * (1 if far else 0),
         compiler_params=pltpu.CompilerParams(vmem_limit_bytes=LIMIT),
         cost_estimate=pl.CostEstimate(flops=flops, bytes_accessed=0, transcendentals=0),
     )(*flags, *near, *far)
@@ -110,7 +110,7 @@
     mine, other, base, sems = refs
     n_design, cands = base.shape
     depth = held.shape[0] // 2
-    parts = [slice(at * n_design // 4, (at + 1) * n_design // 4) for at in range(4)]
+    parts = [slice(at * n_design // 2, (at + 1) * n_design // 2) for at in range(2)]
     is_odd = row[0] % 2 == 1
 
     def fetch(at, source):
@@ -122,19 +122,16 @@
         for at, part in enumerate(parts):
             copies.append(
                 [
-                    pltpu.make_async_copy(flat.at[:, part], mine.at[:, part], sems.at[4 + at]),
-                    pltpu.make_async_copy(cross.at[part], base.at[part], sems.at[8 + at]),
+                    pltpu.make_async_copy(flat.at[:, part], mine.at[:, part], sems.at[2 + at]),
+                    pltpu.make_async_copy(cross.at[part], base.at[part], sems.at[4 + at]),
                 ]
             )
         sources = [
             (row[0] == 1, [beside.at[:, part] for part in parts]),
-            (
-                (row[0] > 1) & ~is_odd,
-                [array.at[:, part] for array in (early, tail) for part in parts[:2]],
-            ),
+            ((row[0] > 1) & ~is_odd, [early, tail]),
             ((row[0] > 1) & is_odd, [whole.at[:, part] for part in parts]),
         ]
-        for at in range(4):
+        for at in range(2):
             for chosen, pieces in sources:
                 pl.when(chosen)(lambda at=at, pieces=pieces: fetch(at, pieces[at]).start())
             for copy in copies[at]:
@@ -145,15 +142,14 @@
         solved = jnp.concatenate(
             [first[:depth], second[:depth], first[depth:], second[depth:]], axis=0
         )
-        solved = split(solved)
         for at, part in enumerate(parts):
             fetch(at, whole.at[:, part]).wait()
             for copy in copies[at]:
                 copy.wait()
             factors = jnp.concatenate([mine[:, part], other[:, part]], axis=0)
-            partial = dot(factors, solved, 0)
-            own[part] = base[part] - partial[:, :cands]
-            send[part] = partial[:, cands:]
+            partial = dot(solved, factors, 0)
+            own[part] = base[part] - partial[:cands].T
+            send[part] = partial[cands:].T
 
 
 def top_kernel(offsets, col, pair, *refs):
@@ -284,7 +280,7 @@
         late = swap(late, half, beside)
         held = broadcast_outer(bundle, row_id)
         tail = swap(tail, half, evens)
-        held, late, tail = lax.optimization_barrier((held, late, tail))
+        held, tail = lax.optimization_barrier((held, tail))
         solved = [held, swap_cores(held)]
 
         pair = jnp.concatenate([first, held], axis=0)

time: 82.7 us -> 80.5 us (0.973)
  waiting for transfers between devices: 50.6 us -> 49.4 us
  Pallas kernels: 4.5 us -> 3.56 us
    ppermute x9, waiting for transfers between devices: 39.1 us -> 37.9 us  [swap(): return lax.ppermute(array, AXES, pairs)]
    squeeze x1, local copies, waits for them, and re-layouts: 1.15 us -> 0.04 us  [on_device(): block_inverses[0]]
    squeeze x1, local copies, waits for them, and re-layouts: 0.02 us -> 0.97 us  [on_device(): factor_panels[0, :, width:2 * width]]
    pallas_call x4, Pallas kernels: 4.5 us -> 3.56 us  [call(): pl.pallas_call(kernel, out_shape=[jax.ShapeDtypeStruct(shape, jnp.float32...]
  transfers between devices with their start and end apart: 14 -> 14, of which waited for: 5 -> 5; matrix products, arithmetic and copies ran while one was open for 1% -> 3% of each run, Pallas kernels for 0% -> 0%
where the time goes in v15:
time: 80.5 us; the launch traced here: 80 us
  waiting for transfers between devices  49.4 us (61%)
  starting transfers between devices  23.4 us (29%)
  Pallas kernels  3.56 us (4%)
  local copies, waits for them, and re-layouts  2.34 us (3%)
  other arithmetic  0.99 us (1%)
    ppermute x9, waiting for transfers between devices, swap(): return lax.ppermute(array, AXES, pairs)  37.9 us
    ppermute x9, starting transfers between devices, swap(): return lax.ppermute(array, AXES, pairs)  18.4 us
    ppermute x4, waiting for transfers between devices, send_down(): return lax.ppermute(array, AXES, pairs)  10.4 us
    pallas_call x4, Pallas kernels, call(): pl.pallas_call(kernel, out_shape=[jax.ShapeDtypeStruct(shape, jnp.float32...  3.56 us
    ppermute x4, starting transfers between devices, send_down(): return lax.ppermute(array, AXES, pairs)  3.32 us
    ppermute x1, starting transfers between devices, swap_cores(): return lax.ppermute(array, AXES, pairs)  1.68 us
  transfers between devices with their start and end apart: 14, of which 5 were waited for; matrix products, arithmetic and copies ran while one was open for 3% of the time, Pallas kernels for 0%

profile of v15, /device:TPU:2, one launch (start us, length us, event | category | flops | bytes accessed | tf_op | source)
XLA Modules:
  0.0 80.0 jit_solution(2470234064180727251)
XLA Ops:
  0.0 0.0 copy-start.4
  0.0 1.8 %collective-permute-start.3 = (f32[256,1024]{1,0:T(8,128)}, f32[256,1024]{1,0:T(8,128)}, u32[]{:S(2)}, u32[]{:S(2)}) collective-permute-start(f32[256,1024]{1,0:T(8,128)} %bitcast.9), channel_id=1, source_target_pairs={{12,14},{13,15},{14,12},{15,13},{20,22},{21,23},{22,20},{23,21},{2... | collective-permute-start | bytes 3145736 | tf_op jit(solution)/shard_map/ppermute | solution.py:186
  1.8 1.0 %slice_bitcast_fusion.1 = f32[128,512]{1,0:T(8,128)S(1)} fusion(f32[2,128,1024]{2,1,0:T(8,128)} %param.4), kind=kLoop, calls=%fused_computation.4 | loop fusion | bytes 524288 | tf_op jit(solution)/shard_map/squeeze | solution.py:242
  2.8 0.0 copy-done.4
  2.8 0.0 copy-start
  2.8 0.0 copy-start.1
  2.8 0.1 pad_maximum_fusion.lead
  2.9 0.8 %collective-permute-start = (f32[128,1536]{1,0:T(8,128)S(1)}, f32[128,1536]{1,0:T(8,128)S(1)}, u32[]{:S(2)}, u32[]{:S(2)}) collective-permute-start(f32[128,1536]{1,0:T(8,128)S(1)} %pad_maximum_fusion.lead), channel_id=1, source_target_pairs={{0,2},{1,3},{2,0},{3,1}} | collective-permute-start | bytes 2359304 | tf_op jit(solution)/shard_map/ppermute | solution.py:186
  3.8 0.2 copy-done.1
  4.0 1.4 %collective-permute-start.1 = (f32[1024,128]{1,0:T(8,128)S(1)}, f32[1024,128]{1,0:T(8,128)}, u32[]{:S(2)}, u32[]{:S(2)}) collective-permute-start(f32[1024,128]{1,0:T(8,128)S(1)} %copy-done.1), channel_id=1, source_target_pairs={{0,1},{1,0},{2,3},{3,2}} | collective-permute-start | bytes 1572872 | tf_op jit(solution)/shard_map/ppermute | solution.py:186
  5.4 0.0 copy-done
  5.4 1.1 %fusion = (f32[256,512]{1,0:T(8,128)}, f32[256,512]{1,0:T(8,128)}) fusion(f32[256,1024]{1,0:T(8,128)S(1)} %bitcast.10), kind=kLoop, calls=%fused_computation.8 | loop fusion | bytes 2097152 | tf_op jit(solution)/shard_map/slice | solution.py:248
  6.5 4.5 %collective-permute-start.2 = (f32[256,512]{1,0:T(8,128)}, f32[256,512]{1,0:T(8,128)}, u32[]{:S(2)}, u32[]{:S(2)}) collective-permute-start(f32[256,512]{1,0:T(8,128)} %get-tuple-element.33), channel_id=1, source_target_pairs={{8,10},{9,11},{10,8},{11,9},{16,18},{17,19},{18,16},{19,17},{24,26... | collective-permute-start | bytes 1572872 | tf_op jit(solution)/shard_map/ppermute | solution.py:186
  11.0 0.0 collective-permute-done.far_lead
  11.0 0.0 collective-permute-done.1.refs_0_
  11.0 0.1 shard_map.37
  11.1 0.0 copy-start.2
  11.1 23.9 %collective-permute-done.2.early = f32[256,512]{1,0:T(8,128)} collective-permute-done((f32[256,512]{1,0:T(8,128)}, f32[256,512]{1,0:T(8,128)}, u32[]{:S(2)}, u32[]{:S(2)}) %collective-permute-start.2) | collective-permute-done | bytes 524320 | tf_op jit(solution)/shard_map/ppermute | solution.py:186
  34.9 0.0 collective-permute-done.3.whole
  34.9 0.7 collective-permute-start.4
  35.6 0.7 collective-permute-start.5
  36.3 0.0 collective-permute-done.5.first
  36.3 1.6 %collective-permute-start.12 = (f32[256,1024]{1,0:T(8,128)S(1)}, f32[256,1024]{1,0:T(8,128)}, u32[]{:S(2)}, u32[]{:S(2)}) collective-permute-start(f32[256,1024]{1,0:T(8,128)S(1)} %bitcast.11), channel_id=1, source_target_pairs={{4,6},{5,7},{6,4},{7,5}} | collective-permute-start | bytes 3145736 | tf_op jit(solution)/shard_map/ppermute | solution.py:186
  38.0 1.9 %collective-permute-start.9 = (f32[256,512]{1,0:T(8,128)}, f32[256,512]{1,0:T(8,128)}, u32[]{:S(2)}, u32[]{:S(2)}) collective-permute-start(f32[256,512]{1,0:T(8,128)} %get-tuple-element.25), channel_id=1, source_target_pairs={{8,10},{9,11},{10,8},{11,9},{16,18},{17,19},{18,16},{19,17},{24,26... | collective-permute-start | bytes 1572872 | tf_op jit(solution)/shard_map/ppermute | solution.py:186
  39.9 0.0 collective-permute-done.4.got
  39.9 0.1 shard_map.38
  40.0 0.0 copy-done.2
  40.0 0.7 collective-permute-start.6
  40.7 1.3 %collective-permute-start.7 = (f32[256,256]{1,0:T(8,128)S(1)}, f32[256,256]{1,0:T(8,128)S(1)}, u32[]{:S(2)}, u32[]{:S(2)}) collective-permute-start(f32[256,256]{1,0:T(8,128)S(1)} %shard_map.38), channel_id=1, source_target_pairs={{0,12},{1,13},{2,14},{3,15},{4,8},{5,9},{6,10},{7,11}} | collective-permute-start | bytes 786440 | tf_op jit(solution)/shard_map/ppermute | solution.py:194
  42.0 0.7 collective-permute-start.8
  42.7 0.0 collective-permute-done.6
  42.7 10.3 %collective-permute-done.7 = f32[256,256]{1,0:T(8,128)S(1)} collective-permute-done((f32[256,256]{1,0:T(8,128)S(1)}, f32[256,256]{1,0:T(8,128)S(1)}, u32[]{:S(2)}, u32[]{:S(2)}) %collective-permute-start.7) | collective-permute-done | bytes 262176 | tf_op jit(solution)/shard_map/ppermute | solution.py:194
  53.0 0.0 collective-permute-done.8
  53.0 0.1 select_select_fusion.held
  53.1 0.0 copy-start.3
  53.1 2.2 %collective-permute-done.9.tail = f32[256,512]{1,0:T(8,128)} collective-permute-done((f32[256,512]{1,0:T(8,128)}, f32[256,512]{1,0:T(8,128)}, u32[]{:S(2)}, u32[]{:S(2)}) %collective-permute-start.9) | collective-permute-done | bytes 524320 | tf_op jit(solution)/shard_map/ppermute | solution.py:186
  55.3 1.7 %collective-permute-start.11 = (f32[256,256]{1,0:T(8,128)S(1)}, f32[256,256]{1,0:T(8,128)S(1)}, u32[]{:S(2)}, u32[]{:S(2)}) collective-permute-start(f32[256,256]{1,0:T(8,128)S(1)} %select_select_fusion.held), channel_id=1, source_target_pairs={{0,4},{1,5},{2,6},{3,7},{4,0},{5,1},{6,2},{7,3},{8,12},{9,13},{10,... | collective-permute-start | bytes 786440 | tf_op jit(solution)/shard_map/ppermute | solution.py:221
  57.0 1.2 %collective-permute-done.11.got = f32[256,256]{1,0:T(8,128)S(1)} collective-permute-done((f32[256,256]{1,0:T(8,128)S(1)}, f32[256,256]{1,0:T(8,128)S(1)}, u32[]{:S(2)}, u32[]{:S(2)}) %collective-permute-start.11) | collective-permute-done | bytes 262176 | tf_op jit(solution)/shard_map/ppermute | solution.py:221
  58.2 0.0 collective-permute-done.12.beside
  58.2 3.4 %shard_map.40 = (f32[1024,128]{1,0:T(8,128)S(1)}, f32[1024,128]{1,0:T(8,128)}) custom-call(s32[1]{0:T(128)} %bitcast.1.row, f32[256,256]{1,0:T(8,128)S(1)} %select_select_fusion.held, f32[256,256]{1,0:T(8,128)S(1)} %collective-permute-done.11.got, f32[256,1024]{1,0:T(8,128)S(1)} %bitcast.12, f32[256,1024]{1,0:T(8,128)} %collective-permute-done.3.whole, ...), custom_call_target="tpu_custom_call" | custom-call | flops 805306368 | tf_op jit(solution)/shard_map/pallas_call | solution.py:32
  61.6 4.9 %collective-permute-start.13 = (f32[1024,128]{1,0:T(8,128)}, f32[1024,128]{1,0:T(8,128)S(1)}, u32[]{:S(2)}, u32[]{:S(2)}) collective-permute-start(f32[1024,128]{1,0:T(8,128)} %get-tuple-element.32), channel_id=1, source_target_pairs={{4,5},{5,4},{6,7},{7,6},{8,9},{9,8},{10,11},{11,10},{12,13},{13,12... | collective-permute-start | bytes 1572872 | tf_op jit(solution)/shard_map/ppermute | solution.py:186
  66.5 0.0 copy-done.3
  66.5 0.7 collective-permute-start.10
  67.2 0.0 collective-permute-done.10.refs_0_
  67.2 0.1 shard_map.39
  67.3 11.8 %collective-permute-done.13 = f32[1024,128]{1,0:T(8,128)S(1)} collective-permute-done((f32[1024,128]{1,0:T(8,128)}, f32[1024,128]{1,0:T(8,128)S(1)}, u32[]{:S(2)}, u32[]{:S(2)}) %collective-permute-start.13) | collective-permute-done | bytes 524320 | tf_op jit(solution)/shard_map/ppermute | solution.py:186
  79.1 0.9 %subtract_select_fusion = f32[1024,128]{1,0:T(8,128)} fusion(f32[1024,128]{1,0:T(8,128)S(1)} %shard_map.39, f32[1024,128]{1,0:T(8,128)S(1)} %get-tuple-element.31, f32[1024,128]{1,0:T(8,128)S(1)} %collective-permute-done.13, pred[]{:T(512)S(6)} %eq.14), kind=kLoop, calls=%fused_computation.1 | loop fusion | flops 262144 | bytes 2097153 | tf_op jit(solution)/shard_map/jit(_where)/select_n | solution.py:308
  (4 shorter events, 0.1 us)
Async XLA Ops:
  0.0 2.8 %copy-start.4 = (f32[2,128,512]{2,1,0:T(8,128)S(1)}, f32[2,128,512]{2,1,0:T(8,128)}, u32[]{:S(2)}) copy-start(f32[2,128,512]{2,1,0:T(8,128)} %param.5) | copy-start | bytes 1572868
  0.0 34.9 %collective-permute-start.3 = (f32[256,1024]{1,0:T(8,128)}, f32[256,1024]{1,0:T(8,128)}, u32[]{:S(2)}, u32[]{:S(2)}) collective-permute-start(f32[256,1024]{1,0:T(8,128)} %bitcast.9), channel_id=1, source_target_pairs={{12,14},{13,15},{14,12},{15,13},{20,22},{21,23},{22,20},{23,21},{2... | collective-permute-start | bytes 3145736 | tf_op jit(solution)/shard_map/ppermute | solution.py:186
  2.8 2.6 %copy-start = (f32[2,128,1024]{2,1,0:T(8,128)S(1)}, f32[2,128,1024]{2,1,0:T(8,128)}, u32[]{:S(2)}) copy-start(f32[2,128,1024]{2,1,0:T(8,128)} %param.4) | copy-start | bytes 3145732
  2.8 1.1 %copy-start.1 = (f32[1024,128]{1,0:T(8,128)S(1)}, f32[1024,128]{1,0:T(8,128)}, u32[]{:S(2)}) copy-start(f32[1024,128]{1,0:T(8,128)} %cross.1) | copy-start | bytes 1572868
  2.9 8.1 %collective-permute-start = (f32[128,1536]{1,0:T(8,128)S(1)}, f32[128,1536]{1,0:T(8,128)S(1)}, u32[]{:S(2)}, u32[]{:S(2)}) collective-permute-start(f32[128,1536]{1,0:T(8,128)S(1)} %pad_maximum_fusion.lead), channel_id=1, source_target_pairs={{0,2},{1,3},{2,0},{3,1}} | collective-permute-start | bytes 2359304 | tf_op jit(solution)/shard_map/ppermute | solution.py:186
  4.0 7.0 %collective-permute-start.1 = (f32[1024,128]{1,0:T(8,128)S(1)}, f32[1024,128]{1,0:T(8,128)}, u32[]{:S(2)}, u32[]{:S(2)}) collective-permute-start(f32[1024,128]{1,0:T(8,128)S(1)} %copy-done.1), channel_id=1, source_target_pairs={{0,1},{1,0},{2,3},{3,2}} | collective-permute-start | bytes 1572872 | tf_op jit(solution)/shard_map/ppermute | solution.py:186
  6.5 28.5 %collective-permute-start.2 = (f32[256,512]{1,0:T(8,128)}, f32[256,512]{1,0:T(8,128)}, u32[]{:S(2)}, u32[]{:S(2)}) collective-permute-start(f32[256,512]{1,0:T(8,128)} %get-tuple-element.33), channel_id=1, source_target_pairs={{8,10},{9,11},{10,8},{11,9},{16,18},{17,19},{18,16},{19,17},{24,26... | collective-permute-start | bytes 1572872 | tf_op jit(solution)/shard_map/ppermute | solution.py:186
  11.1 28.9 %copy-start.2 = (f32[256,256]{1,0:T(8,128)}, f32[256,256]{1,0:T(8,128)S(1)}, u32[]{:S(2)}) copy-start(f32[256,256]{1,0:T(8,128)S(1)} %get-tuple-element.22) | copy-start | bytes 786436
  34.9 4.9 %collective-permute-start.4 = (f32[512,256]{1,0:T(8,128)S(1)}, f32[512,256]{1,0:T(8,128)S(1)}, u32[]{:S(2)}, u32[]{:S(2)}) collective-permute-start(f32[512,256]{1,0:T(8,128)S(1)} %get-tuple-element.24.sent), channel_id=1, source_target_pairs={{0,1},{1,0},{2,3},{3,2}} | collective-permute-start | bytes 1572872 | tf_op jit(solution)/shard_map/ppermute | solution.py:186
  35.6 0.7 collective-permute-start.5
  36.3 21.9 %collective-permute-start.12 = (f32[256,1024]{1,0:T(8,128)S(1)}, f32[256,1024]{1,0:T(8,128)}, u32[]{:S(2)}, u32[]{:S(2)}) collective-permute-start(f32[256,1024]{1,0:T(8,128)S(1)} %bitcast.11), channel_id=1, source_target_pairs={{4,6},{5,7},{6,4},{7,5}} | collective-permute-start | bytes 3145736 | tf_op jit(solution)/shard_map/ppermute | solution.py:186
  38.0 17.4 %collective-permute-start.9 = (f32[256,512]{1,0:T(8,128)}, f32[256,512]{1,0:T(8,128)}, u32[]{:S(2)}, u32[]{:S(2)}) collective-permute-start(f32[256,512]{1,0:T(8,128)} %get-tuple-element.25), channel_id=1, source_target_pairs={{8,10},{9,11},{10,8},{11,9},{16,18},{17,19},{18,16},{19,17},{24,26... | collective-permute-start | bytes 1572872 | tf_op jit(solution)/shard_map/ppermute | solution.py:186
  40.0 2.7 %collective-permute-start.6 = (f32[256,256]{1,0:T(8,128)S(1)}, f32[256,256]{1,0:T(8,128)S(1)}, u32[]{:S(2)}, u32[]{:S(2)}) collective-permute-start(f32[256,256]{1,0:T(8,128)S(1)} %shard_map.38), channel_id=1, source_target_pairs={{0,28},{1,29},{2,30},{3,31},{4,24},{5,25},{6,26},{7,27}} | collective-permute-start | bytes 786440 | tf_op jit(solution)/shard_map/ppermute | solution.py:194
  40.7 12.4 %collective-permute-start.7 = (f32[256,256]{1,0:T(8,128)S(1)}, f32[256,256]{1,0:T(8,128)S(1)}, u32[]{:S(2)}, u32[]{:S(2)}) collective-permute-start(f32[256,256]{1,0:T(8,128)S(1)} %shard_map.38), channel_id=1, source_target_pairs={{0,12},{1,13},{2,14},{3,15},{4,8},{5,9},{6,10},{7,11}} | collective-permute-start | bytes 786440 | tf_op jit(solution)/shard_map/ppermute | solution.py:194
  42.0 11.1 %collective-permute-start.8 = (f32[256,256]{1,0:T(8,128)S(1)}, f32[256,256]{1,0:T(8,128)S(1)}, u32[]{:S(2)}, u32[]{:S(2)}) collective-permute-start(f32[256,256]{1,0:T(8,128)S(1)} %shard_map.38), channel_id=1, source_target_pairs={{0,20},{1,21},{2,22},{3,23},{4,16},{5,17},{6,18},{7,19}} | collective-permute-start | bytes 786440 | tf_op jit(solution)/shard_map/ppermute | solution.py:194
  53.1 13.4 %copy-start.3 = (f32[256,256]{1,0:T(8,128)S(1)}, f32[256,256]{1,0:T(8,128)}, u32[]{:S(2)}) copy-start(f32[256,256]{1,0:T(8,128)} %copy-done.2) | copy-start | bytes 786436
  55.3 2.8 %collective-permute-start.11 = (f32[256,256]{1,0:T(8,128)S(1)}, f32[256,256]{1,0:T(8,128)S(1)}, u32[]{:S(2)}, u32[]{:S(2)}) collective-permute-start(f32[256,256]{1,0:T(8,128)S(1)} %select_select_fusion.held), channel_id=1, source_target_pairs={{0,4},{1,5},{2,6},{3,7},{4,0},{5,1},{6,2},{7,3},{8,12},{9,13},{10,... | collective-permute-start | bytes 786440 | tf_op jit(solution)/shard_map/ppermute | solution.py:221
  61.6 17.5 %collective-permute-start.13 = (f32[1024,128]{1,0:T(8,128)}, f32[1024,128]{1,0:T(8,128)S(1)}, u32[]{:S(2)}, u32[]{:S(2)}) collective-permute-start(f32[1024,128]{1,0:T(8,128)} %get-tuple-element.32), channel_id=1, source_target_pairs={{4,5},{5,4},{6,7},{7,6},{8,9},{9,8},{10,11},{11,10},{12,13},{13,12... | collective-permute-start | bytes 1572872 | tf_op jit(solution)/shard_map/ppermute | solution.py:186
  66.5 0.7 collective-permute-start.10

commit v16 on v15

--- a/solution.py
+++ b/solution.py
@@ -258,7 +258,6 @@
             row_id,
             [(depth, 2 * width)] + [(width, cands)] * len(rhs_others),
         )
-        shuffled, arrived, whole = lax.optimization_barrier((shuffled, arrived, whole))
         sums = got = swap(shuffled, 1, top)
         bit = 2
         while bit < half:
@@ -266,6 +265,7 @@
             got = swap(shuffle(update, bit, cands), bit, top)
             sums = sums + got
             bit *= 2
+        sums, whole, arrived = lax.optimization_barrier((sums, whole, arrived))
         first_beside = send_down(first, 1, top)
         (bundle,) = call(
             functools.partial(second_kernel, places),
@@ -280,7 +280,6 @@
         late = swap(late, half, beside)
         held = broadcast_outer(bundle, row_id)
         tail = swap(tail, half, evens)
-        held, tail = lax.optimization_barrier((held, tail))
         solved = [held, swap_cores(held)]
 
         pair = jnp.concatenate([first, held], axis=0)

time: 80.5 us -> 79.9 us (level)
  waiting for transfers between devices: 49.4 us -> 47.1 us
  other arithmetic: 0.99 us -> 2 us
    ppermute x9, starting transfers between devices: 18.4 us -> 15.3 us  [swap(): return lax.ppermute(array, AXES, pairs)]
    ppermute x1, starting transfers between devices: 1.68 us -> 4.69 us  [swap_cores(): return lax.ppermute(array, AXES, pairs)]
    ppermute x4, waiting for transfers between devices: 10.4 us -> 8.14 us  [send_down(): return lax.ppermute(array, AXES, pairs)]
    ppermute x1, waiting for transfers between devices: 1.16 us -> 0.01 us  [swap_cores(): return lax.ppermute(array, AXES, pairs)]
    squeeze x1, local copies, waits for them, and re-layouts: 0.04 us -> 1.15 us  [on_device(): block_inverses[0]]
    ppermute x9, waiting for transfers between devices: 37.9 us -> 39 us  [swap(): return lax.ppermute(array, AXES, pairs)]
    select_n x1, other arithmetic: 0.06 us -> 1.02 us  [spread(): jnp.where(digit == step, send_down(array, step * low, have), result)]
    squeeze x1, local copies, waits for them, and re-layouts: 0.97 us -> 0.02 us  [on_device(): factor_panels[0, :, width:2 * width]]
  transfers between devices with their start and end apart: 14 -> 14, of which waited for: 5 -> 4; matrix products, arithmetic and copies ran while one was open for 3% -> 3% of each run, Pallas kernels for 0% -> 1%
where the time goes in v16:
time: 79.9 us; the launch traced here: 79.5 us
  waiting for transfers between devices  47.1 us (59%)
  starting transfers between devices  23.3 us (29%)
  Pallas kernels  4.25 us (5%)
  local copies, waits for them, and re-layouts  2.57 us (3%)
  other arithmetic  2 us (3%)
    ppermute x9, waiting for transfers between devices, swap(): return lax.ppermute(array, AXES, pairs)  39 us
    ppermute x9, starting transfers between devices, swap(): return lax.ppermute(array, AXES, pairs)  15.3 us
    ppermute x4, waiting for transfers between devices, send_down(): return lax.ppermute(array, AXES, pairs)  8.14 us
    ppermute x1, starting transfers between devices, swap_cores(): return lax.ppermute(array, AXES, pairs)  4.69 us
    pallas_call x4, Pallas kernels, call(): pl.pallas_call(kernel, out_shape=[jax.ShapeDtypeStruct(shape, jnp.float32...  4.25 us
    ppermute x4, starting transfers between devices, send_down(): return lax.ppermute(array, AXES, pairs)  3.32 us
  transfers between devices with their start and end apart: 14, of which 4 were waited for; matrix products, arithmetic and copies ran while one was open for 3% of the time, Pallas kernels for 1%

profile of v16, /device:TPU:2, one launch (start us, length us, event | category | flops | bytes accessed | tf_op | source)
XLA Modules:
  0.0 79.5 jit_solution(15559183588229729943)
XLA Ops:
  0.0 0.0 copy-start
  0.0 1.2 %slice_bitcast_fusion.2 = (f32[128,512]{1,0:T(8,128)S(1)}, f32[128,512]{1,0:T(8,128)S(1)}) fusion(f32[2,128,512]{2,1,0:T(8,128)} %param.5), kind=kLoop, calls=%fused_computation.9 | loop fusion | bytes 1048576 | tf_op jit(solution)/shard_map/squeeze | solution.py:242
  1.2 0.2 copy-done
  1.4 0.0 copy-start.1
  1.4 0.1 pad_maximum_fusion.lead
  1.5 0.8 %collective-permute-start = (f32[128,1536]{1,0:T(8,128)S(1)}, f32[128,1536]{1,0:T(8,128)S(1)}, u32[]{:S(2)}, u32[]{:S(2)}) collective-permute-start(f32[128,1536]{1,0:T(8,128)S(1)} %pad_maximum_fusion.lead), channel_id=1, source_target_pairs={{0,2},{1,3},{2,0},{3,1}} | collective-permute-start | bytes 2359304 | tf_op jit(solution)/shard_map/ppermute | solution.py:186
  2.3 0.1 copy-done.1
  2.5 1.5 %collective-permute-start.1 = (f32[1024,128]{1,0:T(8,128)S(1)}, f32[1024,128]{1,0:T(8,128)}, u32[]{:S(2)}, u32[]{:S(2)}) collective-permute-start(f32[1024,128]{1,0:T(8,128)S(1)} %copy-done.1), channel_id=1, source_target_pairs={{0,1},{1,0},{2,3},{3,2}} | collective-permute-start | bytes 1572872 | tf_op jit(solution)/shard_map/ppermute | solution.py:186
  3.9 1.6 %collective-permute-start.3 = (f32[256,1024]{1,0:T(8,128)S(1)}, f32[256,1024]{1,0:T(8,128)}, u32[]{:S(2)}, u32[]{:S(2)}) collective-permute-start(f32[256,1024]{1,0:T(8,128)S(1)} %bitcast.9), channel_id=1, source_target_pairs={{12,14},{13,15},{14,12},{15,13},{20,22},{21,23},{22,20},{23,21},{2... | collective-permute-start | bytes 3145736 | tf_op jit(solution)/shard_map/ppermute | solution.py:186
  5.6 1.0 %fusion.1 = (f32[256,512]{1,0:T(8,128)}, f32[256,512]{1,0:T(8,128)}) fusion(f32[256,1024]{1,0:T(8,128)S(1)} %bitcast.10), kind=kLoop, calls=%fused_computation.10 | loop fusion | bytes 2097152 | tf_op jit(solution)/shard_map/slice | solution.py:248
  6.6 4.5 %collective-permute-start.4 = (f32[256,512]{1,0:T(8,128)}, f32[256,512]{1,0:T(8,128)}, u32[]{:S(2)}, u32[]{:S(2)}) collective-permute-start(f32[256,512]{1,0:T(8,128)} %get-tuple-element.29), channel_id=1, source_target_pairs={{8,10},{9,11},{10,8},{11,9},{16,18},{17,19},{18,16},{19,17},{24,26... | collective-permute-start | bytes 1572872 | tf_op jit(solution)/shard_map/ppermute | solution.py:186
  11.1 0.0 collective-permute-done.far_lead
  11.1 0.0 collective-permute-done.1.refs_0_
  11.1 0.1 shard_map.37
  11.2 0.7 collective-permute-start.2
  11.9 0.7 collective-permute-start.5
  12.6 0.0 collective-permute-done.5.first
  12.6 1.7 %collective-permute-start.11 = (f32[256,1024]{1,0:T(8,128)S(1)}, f32[256,1024]{1,0:T(8,128)}, u32[]{:S(2)}, u32[]{:S(2)}) collective-permute-start(f32[256,1024]{1,0:T(8,128)S(1)} %bitcast.11), channel_id=1, source_target_pairs={{4,6},{5,7},{6,4},{7,5}} | collective-permute-start | bytes 3145736 | tf_op jit(solution)/shard_map/ppermute | solution.py:186
  14.3 24.2 %collective-permute-done.4.early = f32[256,512]{1,0:T(8,128)} collective-permute-done((f32[256,512]{1,0:T(8,128)}, f32[256,512]{1,0:T(8,128)}, u32[]{:S(2)}, u32[]{:S(2)}) %collective-permute-start.4) | collective-permute-done | bytes 524320 | tf_op jit(solution)/shard_map/ppermute | solution.py:186
  38.5 0.0 collective-permute-done.3.whole
  38.5 0.0 collective-permute-done.2.got
  38.5 0.8 shard_map.38
  39.3 0.7 collective-permute-start.6
  40.0 1.3 %collective-permute-start.7 = (f32[256,256]{1,0:T(8,128)}, f32[256,256]{1,0:T(8,128)S(1)}, u32[]{:S(2)}, u32[]{:S(2)}) collective-permute-start(f32[256,256]{1,0:T(8,128)} %shard_map.38), channel_id=1, source_target_pairs={{0,12},{1,13},{2,14},{3,15},{4,8},{5,9},{6,10},{7,11}} | collective-permute-start | bytes 786440 | tf_op jit(solution)/shard_map/ppermute | solution.py:194
  41.3 0.7 collective-permute-start.8
  41.9 1.9 %collective-permute-start.12 = (f32[256,512]{1,0:T(8,128)}, f32[256,512]{1,0:T(8,128)S(1)}, u32[]{:S(2)}, u32[]{:S(2)}) collective-permute-start(f32[256,512]{1,0:T(8,128)} %get-tuple-element.26), channel_id=1, source_target_pairs={{8,10},{9,11},{10,8},{11,9},{16,18},{17,19},{18,16},{19,17},{24,26... | collective-permute-start | bytes 1572872 | tf_op jit(solution)/shard_map/ppermute | solution.py:186
  43.9 0.0 collective-permute-done.6
  43.9 8.1 %collective-permute-done.7 = f32[256,256]{1,0:T(8,128)S(1)} collective-permute-done((f32[256,256]{1,0:T(8,128)}, f32[256,256]{1,0:T(8,128)S(1)}, u32[]{:S(2)}, u32[]{:S(2)}) %collective-permute-start.7) | collective-permute-done | bytes 262176 | tf_op jit(solution)/shard_map/ppermute | solution.py:194
  52.0 0.0 collective-permute-done.8
  52.1 1.0 %select_select_fusion.held = f32[256,256]{1,0:T(8,128)S(1)} fusion(f32[256,256]{1,0:T(8,128)S(1)} %collective-permute-done.6, f32[256,256]{1,0:T(8,128)S(1)} %collective-permute-done.7, f32[256,256]{1,0:T(8,128)S(1)} %collective-permute-done.8, f32[256,256]{1,0:T(8,128)} %shard_map.38, pred[]{:T(512)S(6)} %eq.17, pred[]{:T(512)S(6)} %eq.16, pred[]{:T(512)S(6)} %eq.15), kind=kLoop, calls=%fused_computation.6 | loop fusion | flops 196608 | bytes 1310723 | tf_op jit(solution)/shard_map/jit(_where)/select_n | solution.py:203
  53.1 4.7 %collective-permute-start.10 = (f32[256,256]{1,0:T(8,128)S(1)}, f32[256,256]{1,0:T(8,128)S(1)}, u32[]{:S(2)}, u32[]{:S(2)}) collective-permute-start(f32[256,256]{1,0:T(8,128)S(1)} %select_select_fusion.held), channel_id=1, source_target_pairs={{0,4},{1,5},{2,6},{3,7},{4,0},{5,1},{6,2},{7,3},{8,12},{9,13},{10,... | collective-permute-start | bytes 786440 | tf_op jit(solution)/shard_map/ppermute | solution.py:221
  57.8 1.5 %collective-permute-done.12.tail = f32[256,512]{1,0:T(8,128)S(1)} collective-permute-done((f32[256,512]{1,0:T(8,128)}, f32[256,512]{1,0:T(8,128)S(1)}, u32[]{:S(2)}, u32[]{:S(2)}) %collective-permute-start.12) | collective-permute-done | bytes 524320 | tf_op jit(solution)/shard_map/ppermute | solution.py:186
  59.2 0.0 collective-permute-done.10.got
  59.2 0.0 collective-permute-done.11.beside
  59.2 3.4 %shard_map.40 = (f32[1024,128]{1,0:T(8,128)S(1)}, f32[1024,128]{1,0:T(8,128)}) custom-call(s32[1]{0:T(128)} %bitcast.1.row, f32[256,256]{1,0:T(8,128)S(1)} %select_select_fusion.held, f32[256,256]{1,0:T(8,128)S(1)} %collective-permute-done.10.got, f32[256,1024]{1,0:T(8,128)S(1)} %bitcast.12, f32[256,1024]{1,0:T(8,128)} %collective-permute-done.3.whole, ...), custom_call_target="tpu_custom_call" | custom-call | flops 805306368 | tf_op jit(solution)/shard_map/pallas_call | solution.py:32
  62.6 1.9 %collective-permute-start.13 = (f32[1024,128]{1,0:T(8,128)}, f32[1024,128]{1,0:T(8,128)S(1)}, u32[]{:S(2)}, u32[]{:S(2)}) collective-permute-start(f32[1024,128]{1,0:T(8,128)} %get-tuple-element.28), channel_id=1, source_target_pairs={{4,5},{5,4},{6,7},{7,6},{8,9},{9,8},{10,11},{11,10},{12,13},{13,12... | collective-permute-start | bytes 1572872 | tf_op jit(solution)/shard_map/ppermute | solution.py:186
  64.6 0.7 collective-permute-start.9
  65.3 0.0 collective-permute-done.9.refs_0_
  65.3 0.1 shard_map.39
  65.4 13.2 %collective-permute-done.13 = f32[1024,128]{1,0:T(8,128)S(1)} collective-permute-done((f32[1024,128]{1,0:T(8,128)}, f32[1024,128]{1,0:T(8,128)S(1)}, u32[]{:S(2)}, u32[]{:S(2)}) %collective-permute-start.13) | collective-permute-done | bytes 524320 | tf_op jit(solution)/shard_map/ppermute | solution.py:186
  78.6 0.9 %subtract_select_fusion = f32[1024,128]{1,0:T(8,128)} fusion(f32[1024,128]{1,0:T(8,128)S(1)} %shard_map.39, f32[1024,128]{1,0:T(8,128)S(1)} %get-tuple-element.27, f32[1024,128]{1,0:T(8,128)S(1)} %collective-permute-done.13, pred[]{:T(512)S(6)} %eq.14), kind=kLoop, calls=%fused_computation.4 | loop fusion | flops 262144 | bytes 2097153 | tf_op jit(solution)/shard_map/jit(_where)/select_n | solution.py:307
  (3 shorter events, 0.1 us)
Async XLA Ops:
  0.0 1.4 %copy-start = (f32[2,128,1024]{2,1,0:T(8,128)S(1)}, f32[2,128,1024]{2,1,0:T(8,128)}, u32[]{:S(2)}) copy-start(f32[2,128,1024]{2,1,0:T(8,128)} %param.4) | copy-start | bytes 3145732
  1.4 1.0 %copy-start.1 = (f32[1024,128]{1,0:T(8,128)S(1)}, f32[1024,128]{1,0:T(8,128)}, u32[]{:S(2)}) copy-start(f32[1024,128]{1,0:T(8,128)} %cross.1) | copy-start | bytes 1572868
  1.5 9.6 %collective-permute-start = (f32[128,1536]{1,0:T(8,128)S(1)}, f32[128,1536]{1,0:T(8,128)S(1)}, u32[]{:S(2)}, u32[]{:S(2)}) collective-permute-start(f32[128,1536]{1,0:T(8,128)S(1)} %pad_maximum_fusion.lead), channel_id=1, source_target_pairs={{0,2},{1,3},{2,0},{3,1}} | collective-permute-start | bytes 2359304 | tf_op jit(solution)/shard_map/ppermute | solution.py:186
  2.5 8.7 %collective-permute-start.1 = (f32[1024,128]{1,0:T(8,128)S(1)}, f32[1024,128]{1,0:T(8,128)}, u32[]{:S(2)}, u32[]{:S(2)}) collective-permute-start(f32[1024,128]{1,0:T(8,128)S(1)} %copy-done.1), channel_id=1, source_target_pairs={{0,1},{1,0},{2,3},{3,2}} | collective-permute-start | bytes 1572872 | tf_op jit(solution)/shard_map/ppermute | solution.py:186
  3.9 34.6 %collective-permute-start.3 = (f32[256,1024]{1,0:T(8,128)S(1)}, f32[256,1024]{1,0:T(8,128)}, u32[]{:S(2)}, u32[]{:S(2)}) collective-permute-start(f32[256,1024]{1,0:T(8,128)S(1)} %bitcast.9), channel_id=1, source_target_pairs={{12,14},{13,15},{14,12},{15,13},{20,22},{21,23},{22,20},{23,21},{2... | collective-permute-start | bytes 3145736 | tf_op jit(solution)/shard_map/ppermute | solution.py:186
  6.6 31.9 %collective-permute-start.4 = (f32[256,512]{1,0:T(8,128)}, f32[256,512]{1,0:T(8,128)}, u32[]{:S(2)}, u32[]{:S(2)}) collective-permute-start(f32[256,512]{1,0:T(8,128)} %get-tuple-element.29), channel_id=1, source_target_pairs={{8,10},{9,11},{10,8},{11,9},{16,18},{17,19},{18,16},{19,17},{24,26... | collective-permute-start | bytes 1572872 | tf_op jit(solution)/shard_map/ppermute | solution.py:186
  11.2 27.3 %collective-permute-start.2 = (f32[512,256]{1,0:T(8,128)S(1)}, f32[512,256]{1,0:T(8,128)S(1)}, u32[]{:S(2)}, u32[]{:S(2)}) collective-permute-start(f32[512,256]{1,0:T(8,128)S(1)} %get-tuple-element.21.sent), channel_id=1, source_target_pairs={{0,1},{1,0},{2,3},{3,2}} | collective-permute-start | bytes 1572872 | tf_op jit(solution)/shard_map/ppermute | solution.py:186
  11.9 0.7 collective-permute-start.5
  12.6 46.7 %collective-permute-start.11 = (f32[256,1024]{1,0:T(8,128)S(1)}, f32[256,1024]{1,0:T(8,128)}, u32[]{:S(2)}, u32[]{:S(2)}) collective-permute-start(f32[256,1024]{1,0:T(8,128)S(1)} %bitcast.11), channel_id=1, source_target_pairs={{4,6},{5,7},{6,4},{7,5}} | collective-permute-start | bytes 3145736 | tf_op jit(solution)/shard_map/ppermute | solution.py:186
  39.3 4.6 %collective-permute-start.6 = (f32[256,256]{1,0:T(8,128)}, f32[256,256]{1,0:T(8,128)S(1)}, u32[]{:S(2)}, u32[]{:S(2)}) collective-permute-start(f32[256,256]{1,0:T(8,128)} %shard_map.38), channel_id=1, source_target_pairs={{0,28},{1,29},{2,30},{3,31},{4,24},{5,25},{6,26},{7,27}} | collective-permute-start | bytes 786440 | tf_op jit(solution)/shard_map/ppermute | solution.py:194
  40.0 12.1 %collective-permute-start.7 = (f32[256,256]{1,0:T(8,128)}, f32[256,256]{1,0:T(8,128)S(1)}, u32[]{:S(2)}, u32[]{:S(2)}) collective-permute-start(f32[256,256]{1,0:T(8,128)} %shard_map.38), channel_id=1, source_target_pairs={{0,12},{1,13},{2,14},{3,15},{4,8},{5,9},{6,10},{7,11}} | collective-permute-start | bytes 786440 | tf_op jit(solution)/shard_map/ppermute | solution.py:194
  41.3 10.8 %collective-permute-start.8 = (f32[256,256]{1,0:T(8,128)}, f32[256,256]{1,0:T(8,128)S(1)}, u32[]{:S(2)}, u32[]{:S(2)}) collective-permute-start(f32[256,256]{1,0:T(8,128)} %shard_map.38), channel_id=1, source_target_pairs={{0,20},{1,21},{2,22},{3,23},{4,16},{5,17},{6,18},{7,19}} | collective-permute-start | bytes 786440 | tf_op jit(solution)/shard_map/ppermute | solution.py:194
  41.9 17.3 %collective-permute-start.12 = (f32[256,512]{1,0:T(8,128)}, f32[256,512]{1,0:T(8,128)S(1)}, u32[]{:S(2)}, u32[]{:S(2)}) collective-permute-start(f32[256,512]{1,0:T(8,128)} %get-tuple-element.26), channel_id=1, source_target_pairs={{8,10},{9,11},{10,8},{11,9},{16,18},{17,19},{18,16},{19,17},{24,26... | collective-permute-start | bytes 1572872 | tf_op jit(solution)/shard_map/ppermute | solution.py:186
  53.1 6.2 %collective-permute-start.10 = (f32[256,256]{1,0:T(8,128)S(1)}, f32[256,256]{1,0:T(8,128)S(1)}, u32[]{:S(2)}, u32[]{:S(2)}) collective-permute-start(f32[256,256]{1,0:T(8,128)S(1)} %select_select_fusion.held), channel_id=1, source_target_pairs={{0,4},{1,5},{2,6},{3,7},{4,0},{5,1},{6,2},{7,3},{8,12},{9,13},{10,... | collective-permute-start | bytes 786440 | tf_op jit(solution)/shard_map/ppermute | solution.py:221
  62.6 16.0 %collective-permute-start.13 = (f32[1024,128]{1,0:T(8,128)}, f32[1024,128]{1,0:T(8,128)S(1)}, u32[]{:S(2)}, u32[]{:S(2)}) collective-permute-start(f32[1024,128]{1,0:T(8,128)} %get-tuple-element.28), channel_id=1, source_target_pairs={{4,5},{5,4},{6,7},{7,6},{8,9},{9,8},{10,11},{11,10},{12,13},{13,12... | collective-permute-start | bytes 1572872 | tf_op jit(solution)/shard_map/ppermute | solution.py:186
  64.6 0.7 collective-permute-start.9

commit v17 on v15

--- a/solution.py
+++ b/solution.py
@@ -280,7 +280,6 @@
         late = swap(late, half, beside)
         held = broadcast_outer(bundle, row_id)
         tail = swap(tail, half, evens)
-        held, tail = lax.optimization_barrier((held, tail))
         solved = [held, swap_cores(held)]
 
         pair = jnp.concatenate([first, held], axis=0)

time: 80.5 us -> 79.4 us (0.986)
  waiting for transfers between devices: 49.4 us -> 46.7 us
  other arithmetic: 0.99 us -> 2 us
    ppermute x1, starting transfers between devices: 1.68 us -> 4.69 us  [swap_cores(): return lax.ppermute(array, AXES, pairs)]
    ppermute x9, starting transfers between devices: 18.4 us -> 15.4 us  [swap(): return lax.ppermute(array, AXES, pairs)]
    ppermute x4, waiting for transfers between devices: 10.4 us -> 8.14 us  [send_down(): return lax.ppermute(array, AXES, pairs)]
    ppermute x1, waiting for transfers between devices: 1.16 us -> 0.01 us  [swap_cores(): return lax.ppermute(array, AXES, pairs)]
    select_n x1, other arithmetic: 0.06 us -> 1.02 us  [spread(): jnp.where(digit == step, send_down(array, step * low, have), result)]
  transfers between devices with their start and end apart: 14 -> 14, of which waited for: 5 -> 4; matrix products, arithmetic and copies ran while one was open for 3% -> 4% of each run, Pallas kernels for 0% -> 1%
where the time goes in v17:
time: 79.4 us; the launch traced here: 78.9 us
  waiting for transfers between devices  46.7 us (59%)
  starting transfers between devices  23.4 us (29%)
  Pallas kernels  4.26 us (5%)
  local copies, waits for them, and re-layouts  2.28 us (3%)
  other arithmetic  2 us (3%)
    ppermute x9, waiting for transfers between devices, swap(): return lax.ppermute(array, AXES, pairs)  38.6 us
    ppermute x9, starting transfers between devices, swap(): return lax.ppermute(array, AXES, pairs)  15.4 us
    ppermute x4, waiting for transfers between devices, send_down(): return lax.ppermute(array, AXES, pairs)  8.14 us
    ppermute x1, starting transfers between devices, swap_cores(): return lax.ppermute(array, AXES, pairs)  4.69 us
    pallas_call x4, Pallas kernels, call(): pl.pallas_call(kernel, out_shape=[jax.ShapeDtypeStruct(shape, jnp.float32...  4.26 us
    ppermute x4, starting transfers between devices, send_down(): return lax.ppermute(array, AXES, pairs)  3.32 us
  transfers between devices with their start and end apart: 14, of which 4 were waited for; matrix products, arithmetic and copies ran while one was open for 4% of the time, Pallas kernels for 1%

profile of v17, /device:TPU:2, one launch (start us, length us, event | category | flops | bytes accessed | tf_op | source)
XLA Modules:
  0.0 78.9 jit_solution(13166857810702766182)
XLA Ops:
  0.0 0.0 copy-start.2
  0.0 1.8 %collective-permute-start.3 = (f32[256,1024]{1,0:T(8,128)}, f32[256,1024]{1,0:T(8,128)}, u32[]{:S(2)}, u32[]{:S(2)}) collective-permute-start(f32[256,1024]{1,0:T(8,128)} %bitcast.9), channel_id=1, source_target_pairs={{12,14},{13,15},{14,12},{15,13},{20,22},{21,23},{22,20},{23,21},{2... | collective-permute-start | bytes 3145736 | tf_op jit(solution)/shard_map/ppermute | solution.py:186
  1.8 1.0 %slice_bitcast_fusion.1 = f32[128,512]{1,0:T(8,128)S(1)} fusion(f32[2,128,1024]{2,1,0:T(8,128)} %param.4), kind=kLoop, calls=%fused_computation.8 | loop fusion | bytes 524288 | tf_op jit(solution)/shard_map/squeeze | solution.py:242
  2.8 0.0 copy-done.2
  2.8 0.0 copy-start
  2.8 0.0 copy-start.1
  2.8 0.1 pad_maximum_fusion.lead
  2.9 0.8 %collective-permute-start = (f32[128,1536]{1,0:T(8,128)S(1)}, f32[128,1536]{1,0:T(8,128)S(1)}, u32[]{:S(2)}, u32[]{:S(2)}) collective-permute-start(f32[128,1536]{1,0:T(8,128)S(1)} %pad_maximum_fusion.lead), channel_id=1, source_target_pairs={{0,2},{1,3},{2,0},{3,1}} | collective-permute-start | bytes 2359304 | tf_op jit(solution)/shard_map/ppermute | solution.py:186
  3.7 0.2 copy-done.1
  4.0 1.5 %collective-permute-start.1 = (f32[1024,128]{1,0:T(8,128)S(1)}, f32[1024,128]{1,0:T(8,128)}, u32[]{:S(2)}, u32[]{:S(2)}) collective-permute-start(f32[1024,128]{1,0:T(8,128)S(1)} %copy-done.1), channel_id=1, source_target_pairs={{0,1},{1,0},{2,3},{3,2}} | collective-permute-start | bytes 1572872 | tf_op jit(solution)/shard_map/ppermute | solution.py:186
  5.4 0.0 copy-done
  5.4 1.0 %fusion.1 = (f32[256,512]{1,0:T(8,128)}, f32[256,512]{1,0:T(8,128)}) fusion(f32[256,1024]{1,0:T(8,128)S(1)} %bitcast.10), kind=kLoop, calls=%fused_computation.10 | loop fusion | bytes 2097152 | tf_op jit(solution)/shard_map/slice | solution.py:248
  6.5 4.5 %collective-permute-start.2 = (f32[256,512]{1,0:T(8,128)}, f32[256,512]{1,0:T(8,128)}, u32[]{:S(2)}, u32[]{:S(2)}) collective-permute-start(f32[256,512]{1,0:T(8,128)} %get-tuple-element.29), channel_id=1, source_target_pairs={{8,10},{9,11},{10,8},{11,9},{16,18},{17,19},{18,16},{19,17},{24,26... | collective-permute-start | bytes 1572872 | tf_op jit(solution)/shard_map/ppermute | solution.py:186
  11.0 0.0 collective-permute-done.far_lead
  11.0 0.0 collective-permute-done.1.refs_0_
  11.0 0.1 shard_map.37
  11.1 23.9 %collective-permute-done.2.early = f32[256,512]{1,0:T(8,128)} collective-permute-done((f32[256,512]{1,0:T(8,128)}, f32[256,512]{1,0:T(8,128)}, u32[]{:S(2)}, u32[]{:S(2)}) %collective-permute-start.2) | collective-permute-done | bytes 524320 | tf_op jit(solution)/shard_map/ppermute | solution.py:186
  34.9 0.0 collective-permute-done.3.whole
  34.9 0.7 collective-permute-start.4
  35.6 0.7 collective-permute-start.5
  36.3 0.0 collective-permute-done.5.first
  36.3 1.6 %collective-permute-start.11 = (f32[256,1024]{1,0:T(8,128)S(1)}, f32[256,1024]{1,0:T(8,128)}, u32[]{:S(2)}, u32[]{:S(2)}) collective-permute-start(f32[256,1024]{1,0:T(8,128)S(1)} %bitcast.11), channel_id=1, source_target_pairs={{4,6},{5,7},{6,4},{7,5}} | collective-permute-start | bytes 3145736 | tf_op jit(solution)/shard_map/ppermute | solution.py:186
  38.0 0.0 collective-permute-done.4.got
  38.0 0.8 shard_map.38
  38.7 0.7 collective-permute-start.6
  39.4 1.3 %collective-permute-start.7 = (f32[256,256]{1,0:T(8,128)}, f32[256,256]{1,0:T(8,128)S(1)}, u32[]{:S(2)}, u32[]{:S(2)}) collective-permute-start(f32[256,256]{1,0:T(8,128)} %shard_map.38), channel_id=1, source_target_pairs={{0,12},{1,13},{2,14},{3,15},{4,8},{5,9},{6,10},{7,11}} | collective-permute-start | bytes 786440 | tf_op jit(solution)/shard_map/ppermute | solution.py:194
  40.7 0.7 collective-permute-start.8
  41.4 1.9 %collective-permute-start.12 = (f32[256,512]{1,0:T(8,128)}, f32[256,512]{1,0:T(8,128)S(1)}, u32[]{:S(2)}, u32[]{:S(2)}) collective-permute-start(f32[256,512]{1,0:T(8,128)} %get-tuple-element.26), channel_id=1, source_target_pairs={{8,10},{9,11},{10,8},{11,9},{16,18},{17,19},{18,16},{19,17},{24,26... | collective-permute-start | bytes 1572872 | tf_op jit(solution)/shard_map/ppermute | solution.py:186
  43.4 0.0 collective-permute-done.6
  43.4 8.1 %collective-permute-done.7 = f32[256,256]{1,0:T(8,128)S(1)} collective-permute-done((f32[256,256]{1,0:T(8,128)}, f32[256,256]{1,0:T(8,128)S(1)}, u32[]{:S(2)}, u32[]{:S(2)}) %collective-permute-start.7) | collective-permute-done | bytes 262176 | tf_op jit(solution)/shard_map/ppermute | solution.py:194
  51.5 0.0 collective-permute-done.8
  51.5 1.0 %select_select_fusion.held = f32[256,256]{1,0:T(8,128)S(1)} fusion(f32[256,256]{1,0:T(8,128)S(1)} %collective-permute-done.6, f32[256,256]{1,0:T(8,128)S(1)} %collective-permute-done.7, f32[256,256]{1,0:T(8,128)S(1)} %collective-permute-done.8, f32[256,256]{1,0:T(8,128)} %shard_map.38, pred[]{:T(512)S(6)} %eq.17, pred[]{:T(512)S(6)} %eq.16, pred[]{:T(512)S(6)} %eq.15), kind=kLoop, calls=%fused_computation.6 | loop fusion | flops 196608 | bytes 1310723 | tf_op jit(solution)/shard_map/jit(_where)/select_n | solution.py:203
  52.5 4.7 %collective-permute-start.10 = (f32[256,256]{1,0:T(8,128)S(1)}, f32[256,256]{1,0:T(8,128)S(1)}, u32[]{:S(2)}, u32[]{:S(2)}) collective-permute-start(f32[256,256]{1,0:T(8,128)S(1)} %select_select_fusion.held), channel_id=1, source_target_pairs={{0,4},{1,5},{2,6},{3,7},{4,0},{5,1},{6,2},{7,3},{8,12},{9,13},{10,... | collective-permute-start | bytes 786440 | tf_op jit(solution)/shard_map/ppermute | solution.py:221
  57.2 1.5 %collective-permute-done.12.tail = f32[256,512]{1,0:T(8,128)S(1)} collective-permute-done((f32[256,512]{1,0:T(8,128)}, f32[256,512]{1,0:T(8,128)S(1)}, u32[]{:S(2)}, u32[]{:S(2)}) %collective-permute-start.12) | collective-permute-done | bytes 524320 | tf_op jit(solution)/shard_map/ppermute | solution.py:186
  58.7 0.0 collective-permute-done.10.got
  58.7 0.0 collective-permute-done.11.beside
  58.7 3.4 %shard_map.40 = (f32[1024,128]{1,0:T(8,128)S(1)}, f32[1024,128]{1,0:T(8,128)}) custom-call(s32[1]{0:T(128)} %bitcast.1.row, f32[256,256]{1,0:T(8,128)S(1)} %select_select_fusion.held, f32[256,256]{1,0:T(8,128)S(1)} %collective-permute-done.10.got, f32[256,1024]{1,0:T(8,128)S(1)} %bitcast.12, f32[256,1024]{1,0:T(8,128)} %collective-permute-done.3.whole, ...), custom_call_target="tpu_custom_call" | custom-call | flops 805306368 | tf_op jit(solution)/shard_map/pallas_call | solution.py:32
  62.1 1.9 %collective-permute-start.13 = (f32[1024,128]{1,0:T(8,128)}, f32[1024,128]{1,0:T(8,128)S(1)}, u32[]{:S(2)}, u32[]{:S(2)}) collective-permute-start(f32[1024,128]{1,0:T(8,128)} %get-tuple-element.28), channel_id=1, source_target_pairs={{4,5},{5,4},{6,7},{7,6},{8,9},{9,8},{10,11},{11,10},{12,13},{13,12... | collective-permute-start | bytes 1572872 | tf_op jit(solution)/shard_map/ppermute | solution.py:186
  64.0 0.7 collective-permute-start.9
  64.8 0.0 collective-permute-done.9.refs_0_
  64.8 0.1 shard_map.39
  64.9 13.2 %collective-permute-done.13 = f32[1024,128]{1,0:T(8,128)S(1)} collective-permute-done((f32[1024,128]{1,0:T(8,128)}, f32[1024,128]{1,0:T(8,128)S(1)}, u32[]{:S(2)}, u32[]{:S(2)}) %collective-permute-start.13) | collective-permute-done | bytes 524320 | tf_op jit(solution)/shard_map/ppermute | solution.py:186
  78.1 0.9 %subtract_select_fusion = f32[1024,128]{1,0:T(8,128)} fusion(f32[1024,128]{1,0:T(8,128)S(1)} %shard_map.39, f32[1024,128]{1,0:T(8,128)S(1)} %get-tuple-element.27, f32[1024,128]{1,0:T(8,128)S(1)} %collective-permute-done.13, pred[]{:T(512)S(6)} %eq.14), kind=kLoop, calls=%fused_computation.4 | loop fusion | flops 262144 | bytes 2097153 | tf_op jit(solution)/shard_map/jit(_where)/select_n | solution.py:307
  (3 shorter events, 0.1 us)
Async XLA Ops:
  0.0 2.8 %copy-start.2 = (f32[2,128,512]{2,1,0:T(8,128)S(1)}, f32[2,128,512]{2,1,0:T(8,128)}, u32[]{:S(2)}) copy-start(f32[2,128,512]{2,1,0:T(8,128)} %param.5) | copy-start | bytes 1572868
  0.0 34.9 %collective-permute-start.3 = (f32[256,1024]{1,0:T(8,128)}, f32[256,1024]{1,0:T(8,128)}, u32[]{:S(2)}, u32[]{:S(2)}) collective-permute-start(f32[256,1024]{1,0:T(8,128)} %bitcast.9), channel_id=1, source_target_pairs={{12,14},{13,15},{14,12},{15,13},{20,22},{21,23},{22,20},{23,21},{2... | collective-permute-start | bytes 3145736 | tf_op jit(solution)/shard_map/ppermute | solution.py:186
  2.8 2.6 %copy-start = (f32[2,128,1024]{2,1,0:T(8,128)S(1)}, f32[2,128,1024]{2,1,0:T(8,128)}, u32[]{:S(2)}) copy-start(f32[2,128,1024]{2,1,0:T(8,128)} %param.4) | copy-start | bytes 3145732
  2.8 1.1 %copy-start.1 = (f32[1024,128]{1,0:T(8,128)S(1)}, f32[1024,128]{1,0:T(8,128)}, u32[]{:S(2)}) copy-start(f32[1024,128]{1,0:T(8,128)} %cross.1) | copy-start | bytes 1572868
  2.9 8.1 %collective-permute-start = (f32[128,1536]{1,0:T(8,128)S(1)}, f32[128,1536]{1,0:T(8,128)S(1)}, u32[]{:S(2)}, u32[]{:S(2)}) collective-permute-start(f32[128,1536]{1,0:T(8,128)S(1)} %pad_maximum_fusion.lead), channel_id=1, source_target_pairs={{0,2},{1,3},{2,0},{3,1}} | collective-permute-start | bytes 2359304 | tf_op jit(solution)/shard_map/ppermute | solution.py:186
  4.0 7.0 %collective-permute-start.1 = (f32[1024,128]{1,0:T(8,128)S(1)}, f32[1024,128]{1,0:T(8,128)}, u32[]{:S(2)}, u32[]{:S(2)}) collective-permute-start(f32[1024,128]{1,0:T(8,128)S(1)} %copy-done.1), channel_id=1, source_target_pairs={{0,1},{1,0},{2,3},{3,2}} | collective-permute-start | bytes 1572872 | tf_op jit(solution)/shard_map/ppermute | solution.py:186
  6.5 28.4 %collective-permute-start.2 = (f32[256,512]{1,0:T(8,128)}, f32[256,512]{1,0:T(8,128)}, u32[]{:S(2)}, u32[]{:S(2)}) collective-permute-start(f32[256,512]{1,0:T(8,128)} %get-tuple-element.29), channel_id=1, source_target_pairs={{8,10},{9,11},{10,8},{11,9},{16,18},{17,19},{18,16},{19,17},{24,26... | collective-permute-start | bytes 1572872 | tf_op jit(solution)/shard_map/ppermute | solution.py:186
  34.9 3.0 %collective-permute-start.4 = (f32[512,256]{1,0:T(8,128)S(1)}, f32[512,256]{1,0:T(8,128)S(1)}, u32[]{:S(2)}, u32[]{:S(2)}) collective-permute-start(f32[512,256]{1,0:T(8,128)S(1)} %get-tuple-element.22.sent), channel_id=1, source_target_pairs={{0,1},{1,0},{2,3},{3,2}} | collective-permute-start | bytes 1572872 | tf_op jit(solution)/shard_map/ppermute | solution.py:186
  35.6 0.7 collective-permute-start.5
  36.3 22.4 %collective-permute-start.11 = (f32[256,1024]{1,0:T(8,128)S(1)}, f32[256,1024]{1,0:T(8,128)}, u32[]{:S(2)}, u32[]{:S(2)}) collective-permute-start(f32[256,1024]{1,0:T(8,128)S(1)} %bitcast.11), channel_id=1, source_target_pairs={{4,6},{5,7},{6,4},{7,5}} | collective-permute-start | bytes 3145736 | tf_op jit(solution)/shard_map/ppermute | solution.py:186
  38.7 4.6 %collective-permute-start.6 = (f32[256,256]{1,0:T(8,128)}, f32[256,256]{1,0:T(8,128)S(1)}, u32[]{:S(2)}, u32[]{:S(2)}) collective-permute-start(f32[256,256]{1,0:T(8,128)} %shard_map.38), channel_id=1, source_target_pairs={{0,28},{1,29},{2,30},{3,31},{4,24},{5,25},{6,26},{7,27}} | collective-permute-start | bytes 786440 | tf_op jit(solution)/shard_map/ppermute | solution.py:194
  39.4 12.1 %collective-permute-start.7 = (f32[256,256]{1,0:T(8,128)}, f32[256,256]{1,0:T(8,128)S(1)}, u32[]{:S(2)}, u32[]{:S(2)}) collective-permute-start(f32[256,256]{1,0:T(8,128)} %shard_map.38), channel_id=1, source_target_pairs={{0,12},{1,13},{2,14},{3,15},{4,8},{5,9},{6,10},{7,11}} | collective-permute-start | bytes 786440 | tf_op jit(solution)/shard_map/ppermute | solution.py:194
  40.7 10.8 %collective-permute-start.8 = (f32[256,256]{1,0:T(8,128)}, f32[256,256]{1,0:T(8,128)S(1)}, u32[]{:S(2)}, u32[]{:S(2)}) collective-permute-start(f32[256,256]{1,0:T(8,128)} %shard_map.38), channel_id=1, source_target_pairs={{0,20},{1,21},{2,22},{3,23},{4,16},{5,17},{6,18},{7,19}} | collective-permute-start | bytes 786440 | tf_op jit(solution)/shard_map/ppermute | solution.py:194
  41.4 17.3 %collective-permute-start.12 = (f32[256,512]{1,0:T(8,128)}, f32[256,512]{1,0:T(8,128)S(1)}, u32[]{:S(2)}, u32[]{:S(2)}) collective-permute-start(f32[256,512]{1,0:T(8,128)} %get-tuple-element.26), channel_id=1, source_target_pairs={{8,10},{9,11},{10,8},{11,9},{16,18},{17,19},{18,16},{19,17},{24,26... | collective-permute-start | bytes 1572872 | tf_op jit(solution)/shard_map/ppermute | solution.py:186
  52.5 6.2 %collective-permute-start.10 = (f32[256,256]{1,0:T(8,128)S(1)}, f32[256,256]{1,0:T(8,128)S(1)}, u32[]{:S(2)}, u32[]{:S(2)}) collective-permute-start(f32[256,256]{1,0:T(8,128)S(1)} %select_select_fusion.held), channel_id=1, source_target_pairs={{0,4},{1,5},{2,6},{3,7},{4,0},{5,1},{6,2},{7,3},{8,12},{9,13},{10,... | collective-permute-start | bytes 786440 | tf_op jit(solution)/shard_map/ppermute | solution.py:221
  62.1 16.0 %collective-permute-start.13 = (f32[1024,128]{1,0:T(8,128)}, f32[1024,128]{1,0:T(8,128)S(1)}, u32[]{:S(2)}, u32[]{:S(2)}) collective-permute-start(f32[1024,128]{1,0:T(8,128)} %get-tuple-element.28), channel_id=1, source_target_pairs={{4,5},{5,4},{6,7},{7,6},{8,9},{9,8},{10,11},{11,10},{12,13},{13,12... | collective-permute-start | bytes 1572872 | tf_op jit(solution)/shard_map/ppermute | solution.py:186
  64.0 0.7 collective-permute-start.9

commit v18 on v17

--- a/solution.py
+++ b/solution.py
@@ -127,7 +127,7 @@
                 ]
             )
         sources = [
-            (row[0] == 1, [beside.at[:, part] for part in parts]),
+            (row[0] == 1, [beside, tail]),
             ((row[0] > 1) & ~is_odd, [early, tail]),
             ((row[0] > 1) & is_odd, [whole.at[:, part] for part in parts]),
         ]
@@ -246,7 +246,9 @@
         rhs_others = [swap(rhs, step, top) for step in range(1, half)]
         whole = swap(flat, half, odds)
         arrived = swap(flat[:, :count], half, evens)
-        lead_other, tail = lax.optimization_barrier((lead_other, flat[:, count:]))
+        lead_other, head, tail = lax.optimization_barrier(
+            (lead_other, flat[:, : n_design // 2], flat[:, count:])
+        )
 
         places = [at ^ 1 for at in range(half)]
         first, shuffled = call(
@@ -276,10 +278,11 @@
             row_id,
             [(depth, width)] + [(width, half * cands)] * 2,
         )
-        first_beside, late = lax.optimization_barrier((first_beside, flat))
-        late = swap(late, half, beside)
+        first_beside, head = lax.optimization_barrier((first_beside, head))
+        late = swap(head, half, beside)
         held = broadcast_outer(bundle, row_id)
-        tail = swap(tail, half, evens)
+        held, late = lax.optimization_barrier((held, late))
+        tail = swap(tail, half, [*beside, *evens])
         solved = [held, swap_cores(held)]
 
         pair = jnp.concatenate([first, held], axis=0)

time: 79.4 us -> 78.1 us (0.984)
  other arithmetic: 2 us -> 0.99 us
    select_n x1, other arithmetic: 1.02 us -> 0.06 us  [spread(): jnp.where(digit == step, send_down(array, step * low, have), result)]
  transfers between devices with their start and end apart: 14 -> 14, of which waited for: 4 -> 4; matrix products, arithmetic and copies ran while one was open for 4% -> 3% of each run, Pallas kernels for 1% -> 0%
where the time goes in v18:
time: 78.1 us; the launch traced here: 76.9 us
  waiting for transfers between devices  46.5 us (60%)
  starting transfers between devices  23.2 us (30%)
  Pallas kernels  3.54 us (5%)
  local copies, waits for them, and re-layouts  2.36 us (3%)
  other arithmetic  0.99 us (1%)
    ppermute x9, waiting for transfers between devices, swap(): return lax.ppermute(array, AXES, pairs)  38.5 us
    ppermute x9, starting transfers between devices, swap(): return lax.ppermute(array, AXES, pairs)  15.2 us
    ppermute x4, waiting for transfers between devices, send_down(): return lax.ppermute(array, AXES, pairs)  7.93 us
    ppermute x1, starting transfers between devices, swap_cores(): return lax.ppermute(array, AXES, pairs)  4.69 us
    pallas_call x4, Pallas kernels, call(): pl.pallas_call(kernel, out_shape=[jax.ShapeDtypeStruct(shape, jnp.float32...  3.54 us
    ppermute x4, starting transfers between devices, send_down(): return lax.ppermute(array, AXES, pairs)  3.32 us
  transfers between devices with their start and end apart: 14, of which 4 were waited for; matrix products, arithmetic and copies ran while one was open for 3% of the time, Pallas kernels for 0%

profile of v18, /device:TPU:2, one launch (start us, length us, event | category | flops | bytes accessed | tf_op | source)
XLA Modules:
  0.0 76.9 jit_solution(7068693850063229440)
XLA Ops:
  0.0 0.0 copy-start.4
  0.0 1.8 %collective-permute-start.3 = (f32[256,1024]{1,0:T(8,128)}, f32[256,1024]{1,0:T(8,128)}, u32[]{:S(2)}, u32[]{:S(2)}) collective-permute-start(f32[256,1024]{1,0:T(8,128)} %bitcast.9), channel_id=1, source_target_pairs={{12,14},{13,15},{14,12},{15,13},{20,22},{21,23},{22,20},{23,21},{2... | collective-permute-start | bytes 3145736 | tf_op jit(solution)/shard_map/ppermute | solution.py:186
  1.8 1.0 %slice_bitcast_fusion.1 = f32[128,512]{1,0:T(8,128)S(1)} fusion(f32[2,128,1024]{2,1,0:T(8,128)} %param.4), kind=kLoop, calls=%fused_computation.4 | loop fusion | bytes 524288 | tf_op jit(solution)/shard_map/squeeze | solution.py:242
  2.8 0.0 copy-done.4
  2.8 0.0 copy-start
  2.8 0.0 copy-start.1
  2.8 0.1 pad_maximum_fusion.lead
  2.9 0.8 %collective-permute-start = (f32[128,1536]{1,0:T(8,128)S(1)}, f32[128,1536]{1,0:T(8,128)S(1)}, u32[]{:S(2)}, u32[]{:S(2)}) collective-permute-start(f32[128,1536]{1,0:T(8,128)S(1)} %pad_maximum_fusion.lead), channel_id=1, source_target_pairs={{0,2},{1,3},{2,0},{3,1}} | collective-permute-start | bytes 2359304 | tf_op jit(solution)/shard_map/ppermute | solution.py:186
  3.8 0.2 copy-done.1
  4.0 1.4 %collective-permute-start.1 = (f32[1024,128]{1,0:T(8,128)S(1)}, f32[1024,128]{1,0:T(8,128)}, u32[]{:S(2)}, u32[]{:S(2)}) collective-permute-start(f32[1024,128]{1,0:T(8,128)S(1)} %copy-done.1), channel_id=1, source_target_pairs={{0,1},{1,0},{2,3},{3,2}} | collective-permute-start | bytes 1572872 | tf_op jit(solution)/shard_map/ppermute | solution.py:186
  5.4 0.0 copy-done
  5.4 1.1 %fusion = (f32[256,512]{1,0:T(8,128)}, f32[256,512]{1,0:T(8,128)}) fusion(f32[256,1024]{1,0:T(8,128)S(1)} %bitcast.10), kind=kLoop, calls=%fused_computation.8 | loop fusion | bytes 2097152 | tf_op jit(solution)/shard_map/slice | solution.py:250
  6.5 4.5 %collective-permute-start.2 = (f32[256,512]{1,0:T(8,128)}, f32[256,512]{1,0:T(8,128)}, u32[]{:S(2)}, u32[]{:S(2)}) collective-permute-start(f32[256,512]{1,0:T(8,128)} %get-tuple-element.27), channel_id=1, source_target_pairs={{8,10},{9,11},{10,8},{11,9},{16,18},{17,19},{18,16},{19,17},{24,26... | collective-permute-start | bytes 1572872 | tf_op jit(solution)/shard_map/ppermute | solution.py:186
  11.0 0.0 collective-permute-done.far_lead
  11.0 0.0 collective-permute-done.1.refs_0_
  11.0 0.1 shard_map.37
  11.1 0.0 copy-start.2
  11.1 23.8 %collective-permute-done.2.early = f32[256,512]{1,0:T(8,128)} collective-permute-done((f32[256,512]{1,0:T(8,128)}, f32[256,512]{1,0:T(8,128)}, u32[]{:S(2)}, u32[]{:S(2)}) %collective-permute-start.2) | collective-permute-done | bytes 524320 | tf_op jit(solution)/shard_map/ppermute | solution.py:186
  34.9 0.0 collective-permute-done.3.whole
  34.9 0.7 collective-permute-start.4
  35.6 0.7 collective-permute-start.5
  36.3 0.0 collective-permute-done.5.first
  36.3 1.5 %collective-permute-start.9 = (f32[256,512]{1,0:T(8,128)}, f32[256,512]{1,0:T(8,128)}, u32[]{:S(2)}, u32[]{:S(2)}) collective-permute-start(f32[256,512]{1,0:T(8,128)} %get-tuple-element.27), channel_id=1, source_target_pairs={{4,6},{5,7},{6,4},{7,5}} | collective-permute-start | bytes 1572872 | tf_op jit(solution)/shard_map/ppermute | solution.py:186
  37.8 0.0 collective-permute-done.4.got
  37.8 0.1 shard_map.38
  37.8 0.0 copy-done.2
  37.8 0.7 collective-permute-start.6
  38.5 1.3 %collective-permute-start.7 = (f32[256,256]{1,0:T(8,128)S(1)}, f32[256,256]{1,0:T(8,128)S(1)}, u32[]{:S(2)}, u32[]{:S(2)}) collective-permute-start(f32[256,256]{1,0:T(8,128)S(1)} %shard_map.38), channel_id=1, source_target_pairs={{0,12},{1,13},{2,14},{3,15},{4,8},{5,9},{6,10},{7,11}} | collective-permute-start | bytes 786440 | tf_op jit(solution)/shard_map/ppermute | solution.py:194
  39.8 0.7 collective-permute-start.8
  40.5 1.9 %collective-permute-start.12 = (f32[256,512]{1,0:T(8,128)}, f32[256,512]{1,0:T(8,128)S(1)}, u32[]{:S(2)}, u32[]{:S(2)}) collective-permute-start(f32[256,512]{1,0:T(8,128)} %get-tuple-element.32), channel_id=1, source_target_pairs={{4,6},{5,7},{6,4},{7,5},{8,10},{9,11},{10,8},{11,9},{16,18},{17,19... | collective-permute-start | bytes 1572872 | tf_op jit(solution)/shard_map/ppermute | solution.py:186
  42.5 0.0 collective-permute-done.6
  42.5 7.9 %collective-permute-done.7 = f32[256,256]{1,0:T(8,128)S(1)} collective-permute-done((f32[256,256]{1,0:T(8,128)S(1)}, f32[256,256]{1,0:T(8,128)S(1)}, u32[]{:S(2)}, u32[]{:S(2)}) %collective-permute-start.7) | collective-permute-done | bytes 262176 | tf_op jit(solution)/shard_map/ppermute | solution.py:194
  50.4 0.0 collective-permute-done.8
  50.4 0.1 select_select_fusion.held
  50.5 0.0 copy-start.3
  50.5 0.0 collective-permute-done.9.beside
  50.5 4.7 %collective-permute-start.11 = (f32[256,256]{1,0:T(8,128)S(1)}, f32[256,256]{1,0:T(8,128)S(1)}, u32[]{:S(2)}, u32[]{:S(2)}) collective-permute-start(f32[256,256]{1,0:T(8,128)S(1)} %select_select_fusion.held), channel_id=1, source_target_pairs={{0,4},{1,5},{2,6},{3,7},{4,0},{5,1},{6,2},{7,3},{8,12},{9,13},{10,... | collective-permute-start | bytes 786440 | tf_op jit(solution)/shard_map/ppermute | solution.py:221
  55.2 2.6 %collective-permute-done.12.tail = f32[256,512]{1,0:T(8,128)S(1)} collective-permute-done((f32[256,512]{1,0:T(8,128)}, f32[256,512]{1,0:T(8,128)S(1)}, u32[]{:S(2)}, u32[]{:S(2)}) %collective-permute-start.12) | collective-permute-done | bytes 524320 | tf_op jit(solution)/shard_map/ppermute | solution.py:186
  57.8 0.0 collective-permute-done.11.got
  57.8 3.4 %shard_map.40 = (f32[1024,128]{1,0:T(8,128)S(1)}, f32[1024,128]{1,0:T(8,128)}) custom-call(s32[1]{0:T(128)} %bitcast.1.row, f32[256,256]{1,0:T(8,128)S(1)} %select_select_fusion.held, f32[256,256]{1,0:T(8,128)S(1)} %collective-permute-done.11.got, f32[256,1024]{1,0:T(8,128)S(1)} %bitcast.11, f32[256,1024]{1,0:T(8,128)} %collective-permute-done.3.whole, ...), custom_call_target="tpu_custom_call" | custom-call | flops 805306368 | tf_op jit(solution)/shard_map/pallas_call | solution.py:32
  61.2 1.9 %collective-permute-start.13 = (f32[1024,128]{1,0:T(8,128)}, f32[1024,128]{1,0:T(8,128)S(1)}, u32[]{:S(2)}, u32[]{:S(2)}) collective-permute-start(f32[1024,128]{1,0:T(8,128)} %get-tuple-element.34), channel_id=1, source_target_pairs={{4,5},{5,4},{6,7},{7,6},{8,9},{9,8},{10,11},{11,10},{12,13},{13,12... | collective-permute-start | bytes 1572872 | tf_op jit(solution)/shard_map/ppermute | solution.py:186
  63.1 0.0 copy-done.3
  63.2 0.7 collective-permute-start.10
  63.9 0.0 collective-permute-done.10.refs_0_
  63.9 0.1 shard_map.39
  64.0 12.1 %collective-permute-done.13 = f32[1024,128]{1,0:T(8,128)S(1)} collective-permute-done((f32[1024,128]{1,0:T(8,128)}, f32[1024,128]{1,0:T(8,128)S(1)}, u32[]{:S(2)}, u32[]{:S(2)}) %collective-permute-start.13) | collective-permute-done | bytes 524320 | tf_op jit(solution)/shard_map/ppermute | solution.py:186
  76.0 0.9 %subtract_select_fusion = f32[1024,128]{1,0:T(8,128)} fusion(f32[1024,128]{1,0:T(8,128)S(1)} %shard_map.39, f32[1024,128]{1,0:T(8,128)S(1)} %get-tuple-element.33, f32[1024,128]{1,0:T(8,128)S(1)} %collective-permute-done.13, pred[]{:T(512)S(6)} %eq.14), kind=kLoop, calls=%fused_computation.1 | loop fusion | flops 262144 | bytes 2097153 | tf_op jit(solution)/shard_map/jit(_where)/select_n | solution.py:310
  (4 shorter events, 0.1 us)
Async XLA Ops:
  0.0 2.8 %copy-start.4 = (f32[2,128,512]{2,1,0:T(8,128)S(1)}, f32[2,128,512]{2,1,0:T(8,128)}, u32[]{:S(2)}) copy-start(f32[2,128,512]{2,1,0:T(8,128)} %param.5) | copy-start | bytes 1572868
  0.0 34.9 %collective-permute-start.3 = (f32[256,1024]{1,0:T(8,128)}, f32[256,1024]{1,0:T(8,128)}, u32[]{:S(2)}, u32[]{:S(2)}) collective-permute-start(f32[256,1024]{1,0:T(8,128)} %bitcast.9), channel_id=1, source_target_pairs={{12,14},{13,15},{14,12},{15,13},{20,22},{21,23},{22,20},{23,21},{2... | collective-permute-start | bytes 3145736 | tf_op jit(solution)/shard_map/ppermute | solution.py:186
  2.8 2.6 %copy-start = (f32[2,128,1024]{2,1,0:T(8,128)S(1)}, f32[2,128,1024]{2,1,0:T(8,128)}, u32[]{:S(2)}) copy-start(f32[2,128,1024]{2,1,0:T(8,128)} %param.4) | copy-start | bytes 3145732
  2.8 1.1 %copy-start.1 = (f32[1024,128]{1,0:T(8,128)S(1)}, f32[1024,128]{1,0:T(8,128)}, u32[]{:S(2)}) copy-start(f32[1024,128]{1,0:T(8,128)} %cross.1) | copy-start | bytes 1572868
  2.9 8.1 %collective-permute-start = (f32[128,1536]{1,0:T(8,128)S(1)}, f32[128,1536]{1,0:T(8,128)S(1)}, u32[]{:S(2)}, u32[]{:S(2)}) collective-permute-start(f32[128,1536]{1,0:T(8,128)S(1)} %pad_maximum_fusion.lead), channel_id=1, source_target_pairs={{0,2},{1,3},{2,0},{3,1}} | collective-permute-start | bytes 2359304 | tf_op jit(solution)/shard_map/ppermute | solution.py:186
  4.0 7.0 %collective-permute-start.1 = (f32[1024,128]{1,0:T(8,128)S(1)}, f32[1024,128]{1,0:T(8,128)}, u32[]{:S(2)}, u32[]{:S(2)}) collective-permute-start(f32[1024,128]{1,0:T(8,128)S(1)} %copy-done.1), channel_id=1, source_target_pairs={{0,1},{1,0},{2,3},{3,2}} | collective-permute-start | bytes 1572872 | tf_op jit(solution)/shard_map/ppermute | solution.py:186
  6.5 28.4 %collective-permute-start.2 = (f32[256,512]{1,0:T(8,128)}, f32[256,512]{1,0:T(8,128)}, u32[]{:S(2)}, u32[]{:S(2)}) collective-permute-start(f32[256,512]{1,0:T(8,128)} %get-tuple-element.27), channel_id=1, source_target_pairs={{8,10},{9,11},{10,8},{11,9},{16,18},{17,19},{18,16},{19,17},{24,26... | collective-permute-start | bytes 1572872 | tf_op jit(solution)/shard_map/ppermute | solution.py:186
  11.1 26.8 %copy-start.2 = (f32[256,256]{1,0:T(8,128)}, f32[256,256]{1,0:T(8,128)S(1)}, u32[]{:S(2)}) copy-start(f32[256,256]{1,0:T(8,128)S(1)} %get-tuple-element.23) | copy-start | bytes 786436
  34.9 2.8 %collective-permute-start.4 = (f32[512,256]{1,0:T(8,128)S(1)}, f32[512,256]{1,0:T(8,128)S(1)}, u32[]{:S(2)}, u32[]{:S(2)}) collective-permute-start(f32[512,256]{1,0:T(8,128)S(1)} %get-tuple-element.25.sent), channel_id=1, source_target_pairs={{0,1},{1,0},{2,3},{3,2}} | collective-permute-start | bytes 1572872 | tf_op jit(solution)/shard_map/ppermute | solution.py:186
  35.6 0.7 collective-permute-start.5
  36.3 14.2 %collective-permute-start.9 = (f32[256,512]{1,0:T(8,128)}, f32[256,512]{1,0:T(8,128)}, u32[]{:S(2)}, u32[]{:S(2)}) collective-permute-start(f32[256,512]{1,0:T(8,128)} %get-tuple-element.27), channel_id=1, source_target_pairs={{4,6},{5,7},{6,4},{7,5}} | collective-permute-start | bytes 1572872 | tf_op jit(solution)/shard_map/ppermute | solution.py:186
  37.8 4.6 %collective-permute-start.6 = (f32[256,256]{1,0:T(8,128)S(1)}, f32[256,256]{1,0:T(8,128)S(1)}, u32[]{:S(2)}, u32[]{:S(2)}) collective-permute-start(f32[256,256]{1,0:T(8,128)S(1)} %shard_map.38), channel_id=1, source_target_pairs={{0,28},{1,29},{2,30},{3,31},{4,24},{5,25},{6,26},{7,27}} | collective-permute-start | bytes 786440 | tf_op jit(solution)/shard_map/ppermute | solution.py:194
  38.5 11.9 %collective-permute-start.7 = (f32[256,256]{1,0:T(8,128)S(1)}, f32[256,256]{1,0:T(8,128)S(1)}, u32[]{:S(2)}, u32[]{:S(2)}) collective-permute-start(f32[256,256]{1,0:T(8,128)S(1)} %shard_map.38), channel_id=1, source_target_pairs={{0,12},{1,13},{2,14},{3,15},{4,8},{5,9},{6,10},{7,11}} | collective-permute-start | bytes 786440 | tf_op jit(solution)/shard_map/ppermute | solution.py:194
  39.8 10.6 %collective-permute-start.8 = (f32[256,256]{1,0:T(8,128)S(1)}, f32[256,256]{1,0:T(8,128)S(1)}, u32[]{:S(2)}, u32[]{:S(2)}) collective-permute-start(f32[256,256]{1,0:T(8,128)S(1)} %shard_map.38), channel_id=1, source_target_pairs={{0,20},{1,21},{2,22},{3,23},{4,16},{5,17},{6,18},{7,19}} | collective-permute-start | bytes 786440 | tf_op jit(solution)/shard_map/ppermute | solution.py:194
  40.5 17.3 %collective-permute-start.12 = (f32[256,512]{1,0:T(8,128)}, f32[256,512]{1,0:T(8,128)S(1)}, u32[]{:S(2)}, u32[]{:S(2)}) collective-permute-start(f32[256,512]{1,0:T(8,128)} %get-tuple-element.32), channel_id=1, source_target_pairs={{4,6},{5,7},{6,4},{7,5},{8,10},{9,11},{10,8},{11,9},{16,18},{17,19... | collective-permute-start | bytes 1572872 | tf_op jit(solution)/shard_map/ppermute | solution.py:186
  50.5 12.6 %copy-start.3 = (f32[256,256]{1,0:T(8,128)S(1)}, f32[256,256]{1,0:T(8,128)}, u32[]{:S(2)}) copy-start(f32[256,256]{1,0:T(8,128)} %copy-done.2) | copy-start | bytes 786436
  50.5 7.3 %collective-permute-start.11 = (f32[256,256]{1,0:T(8,128)S(1)}, f32[256,256]{1,0:T(8,128)S(1)}, u32[]{:S(2)}, u32[]{:S(2)}) collective-permute-start(f32[256,256]{1,0:T(8,128)S(1)} %select_select_fusion.held), channel_id=1, source_target_pairs={{0,4},{1,5},{2,6},{3,7},{4,0},{5,1},{6,2},{7,3},{8,12},{9,13},{10,... | collective-permute-start | bytes 786440 | tf_op jit(solution)/shard_map/ppermute | solution.py:221
  61.2 14.8 %collective-permute-start.13 = (f32[1024,128]{1,0:T(8,128)}, f32[1024,128]{1,0:T(8,128)S(1)}, u32[]{:S(2)}, u32[]{:S(2)}) collective-permute-start(f32[1024,128]{1,0:T(8,128)} %get-tuple-element.34), channel_id=1, source_target_pairs={{4,5},{5,4},{6,7},{7,6},{8,9},{9,8},{10,11},{11,10},{12,13},{13,12... | collective-permute-start | bytes 1572872 | tf_op jit(solution)/shard_map/ppermute | solution.py:186
  63.2 0.7 collective-permute-start.10

commit v19 on v17

--- a/solution.py
+++ b/solution.py
@@ -258,7 +258,9 @@
             row_id,
             [(depth, 2 * width)] + [(width, cands)] * len(rhs_others),
         )
-        shuffled, arrived, whole = lax.optimization_barrier((shuffled, arrived, whole))
+        shuffled, first, arrived, whole = lax.optimization_barrier(
+            (shuffled, first, arrived, whole)
+        )
         sums = got = swap(shuffled, 1, top)
         bit = 2
         while bit < half:
@@ -279,6 +281,7 @@
         first_beside, late = lax.optimization_barrier((first_beside, flat))
         late = swap(late, half, beside)
         held = broadcast_outer(bundle, row_id)
+        held, late = lax.optimization_barrier((held, late))
         tail = swap(tail, half, evens)
         solved = [held, swap_cores(held)]
 

time: 79.4 us -> 77.7 us (0.979)
  waiting for transfers between devices: 46.7 us -> 45.4 us
  starting transfers between devices: 23.4 us -> 24.7 us
  other arithmetic: 2 us -> 0.99 us
    ppermute x4, waiting for transfers between devices: 8.14 us -> 6.82 us  [send_down(): return lax.ppermute(array, AXES, pairs)]
    ppermute x1, starting transfers between devices: 4.69 us -> 5.95 us  [swap_cores(): return lax.ppermute(array, AXES, pairs)]
    select_n x1, other arithmetic: 1.02 us -> 0.06 us  [spread(): jnp.where(digit == step, send_down(array, step * low, have), result)]
  transfers between devices with their start and end apart: 14 -> 14, of which waited for: 4 -> 4; matrix products, arithmetic and copies ran while one was open for 4% -> 3% of each run, Pallas kernels for 1% -> 0%
where the time goes in v19:
time: 77.7 us; the launch traced here: 77.2 us
  waiting for transfers between devices  45.4 us (58%)
  starting transfers between devices  24.7 us (32%)
  Pallas kernels  3.54 us (5%)
  local copies, waits for them, and re-layouts  2.34 us (3%)
  other arithmetic  0.99 us (1%)
    ppermute x9, waiting for transfers between devices, swap(): return lax.ppermute(array, AXES, pairs)  38.5 us
    ppermute x9, starting transfers between devices, swap(): return lax.ppermute(array, AXES, pairs)  15.4 us
    ppermute x4, waiting for transfers between devices, send_down(): return lax.ppermute(array, AXES, pairs)  6.82 us
    ppermute x1, starting transfers between devices, swap_cores(): return lax.ppermute(array, AXES, pairs)  5.95 us
    pallas_call x4, Pallas kernels, call(): pl.pallas_call(kernel, out_shape=[jax.ShapeDtypeStruct(shape, jnp.float32...  3.54 us
    ppermute x4, starting transfers between devices, send_down(): return lax.ppermute(array, AXES, pairs)  3.31 us
  transfers between devices with their start and end apart: 14, of which 4 were waited for; matrix products, arithmetic and copies ran while one was open for 3% of the time, Pallas kernels for 0%

profile of v19, /device:TPU:2, one launch (start us, length us, event | category | flops | bytes accessed | tf_op | source)
XLA Modules:
  0.0 77.2 jit_solution(1516304997174022535)
XLA Ops:
  0.0 0.0 copy-start.4
  0.0 1.8 %collective-permute-start.3 = (f32[256,1024]{1,0:T(8,128)}, f32[256,1024]{1,0:T(8,128)}, u32[]{:S(2)}, u32[]{:S(2)}) collective-permute-start(f32[256,1024]{1,0:T(8,128)} %bitcast.9), channel_id=1, source_target_pairs={{12,14},{13,15},{14,12},{15,13},{20,22},{21,23},{22,20},{23,21},{2... | collective-permute-start | bytes 3145736 | tf_op jit(solution)/shard_map/ppermute | solution.py:186
  1.8 1.0 %slice_bitcast_fusion.1 = f32[128,512]{1,0:T(8,128)S(1)} fusion(f32[2,128,1024]{2,1,0:T(8,128)} %param.4), kind=kLoop, calls=%fused_computation.4 | loop fusion | bytes 524288 | tf_op jit(solution)/shard_map/squeeze | solution.py:242
  2.8 0.0 copy-done.4
  2.8 0.0 copy-start
  2.8 0.0 copy-start.1
  2.8 0.1 pad_maximum_fusion.lead
  2.9 0.8 %collective-permute-start = (f32[128,1536]{1,0:T(8,128)S(1)}, f32[128,1536]{1,0:T(8,128)S(1)}, u32[]{:S(2)}, u32[]{:S(2)}) collective-permute-start(f32[128,1536]{1,0:T(8,128)S(1)} %pad_maximum_fusion.lead), channel_id=1, source_target_pairs={{0,2},{1,3},{2,0},{3,1}} | collective-permute-start | bytes 2359304 | tf_op jit(solution)/shard_map/ppermute | solution.py:186
  3.8 0.2 copy-done.1
  4.0 1.4 %collective-permute-start.1 = (f32[1024,128]{1,0:T(8,128)S(1)}, f32[1024,128]{1,0:T(8,128)}, u32[]{:S(2)}, u32[]{:S(2)}) collective-permute-start(f32[1024,128]{1,0:T(8,128)S(1)} %copy-done.1), channel_id=1, source_target_pairs={{0,1},{1,0},{2,3},{3,2}} | collective-permute-start | bytes 1572872 | tf_op jit(solution)/shard_map/ppermute | solution.py:186
  5.4 0.0 copy-done
  5.4 1.1 %fusion = (f32[256,512]{1,0:T(8,128)}, f32[256,512]{1,0:T(8,128)}) fusion(f32[256,1024]{1,0:T(8,128)S(1)} %bitcast.10), kind=kLoop, calls=%fused_computation.8 | loop fusion | bytes 2097152 | tf_op jit(solution)/shard_map/slice | solution.py:248
  6.5 4.5 %collective-permute-start.2 = (f32[256,512]{1,0:T(8,128)}, f32[256,512]{1,0:T(8,128)}, u32[]{:S(2)}, u32[]{:S(2)}) collective-permute-start(f32[256,512]{1,0:T(8,128)} %get-tuple-element.35), channel_id=1, source_target_pairs={{8,10},{9,11},{10,8},{11,9},{16,18},{17,19},{18,16},{19,17},{24,26... | collective-permute-start | bytes 1572872 | tf_op jit(solution)/shard_map/ppermute | solution.py:186
  11.0 0.0 collective-permute-done.far_lead
  11.0 0.0 collective-permute-done.1.refs_0_
  11.0 0.1 shard_map.37
  11.1 0.0 copy-start.2
  11.1 23.9 %collective-permute-done.2.early = f32[256,512]{1,0:T(8,128)} collective-permute-done((f32[256,512]{1,0:T(8,128)}, f32[256,512]{1,0:T(8,128)}, u32[]{:S(2)}, u32[]{:S(2)}) %collective-permute-start.2) | collective-permute-done | bytes 524320 | tf_op jit(solution)/shard_map/ppermute | solution.py:186
  34.9 0.0 collective-permute-done.3.whole
  34.9 0.7 collective-permute-start.5
  35.6 0.7 collective-permute-start.4
  36.3 0.0 collective-permute-done.5.first
  36.3 1.6 %collective-permute-start.9 = (f32[256,1024]{1,0:T(8,128)S(1)}, f32[256,1024]{1,0:T(8,128)}, u32[]{:S(2)}, u32[]{:S(2)}) collective-permute-start(f32[256,1024]{1,0:T(8,128)S(1)} %bitcast.11), channel_id=1, source_target_pairs={{4,6},{5,7},{6,4},{7,5}} | collective-permute-start | bytes 3145736 | tf_op jit(solution)/shard_map/ppermute | solution.py:186
  38.0 0.0 collective-permute-done.4.got
  38.0 0.1 shard_map.38
  38.0 0.0 copy-done.2
  38.0 0.7 collective-permute-start.6
  38.7 1.3 %collective-permute-start.7 = (f32[256,256]{1,0:T(8,128)S(1)}, f32[256,256]{1,0:T(8,128)S(1)}, u32[]{:S(2)}, u32[]{:S(2)}) collective-permute-start(f32[256,256]{1,0:T(8,128)S(1)} %shard_map.38), channel_id=1, source_target_pairs={{0,12},{1,13},{2,14},{3,15},{4,8},{5,9},{6,10},{7,11}} | collective-permute-start | bytes 786440 | tf_op jit(solution)/shard_map/ppermute | solution.py:194
  40.0 0.7 collective-permute-start.8
  40.7 1.9 %collective-permute-start.12 = (f32[256,512]{1,0:T(8,128)}, f32[256,512]{1,0:T(8,128)S(1)}, u32[]{:S(2)}, u32[]{:S(2)}) collective-permute-start(f32[256,512]{1,0:T(8,128)} %get-tuple-element.32), channel_id=1, source_target_pairs={{8,10},{9,11},{10,8},{11,9},{16,18},{17,19},{18,16},{19,17},{24,26... | collective-permute-start | bytes 1572872 | tf_op jit(solution)/shard_map/ppermute | solution.py:186
  42.7 0.0 collective-permute-done.6
  42.7 6.8 %collective-permute-done.7 = f32[256,256]{1,0:T(8,128)S(1)} collective-permute-done((f32[256,256]{1,0:T(8,128)S(1)}, f32[256,256]{1,0:T(8,128)S(1)}, u32[]{:S(2)}, u32[]{:S(2)}) %collective-permute-start.7) | collective-permute-done | bytes 262176 | tf_op jit(solution)/shard_map/ppermute | solution.py:194
  49.5 0.0 collective-permute-done.8
  49.5 0.1 select_select_fusion.held
  49.6 0.0 copy-start.3
  49.6 0.0 collective-permute-done.9.beside
  49.6 5.9 %collective-permute-start.11 = (f32[256,256]{1,0:T(8,128)S(1)}, f32[256,256]{1,0:T(8,128)S(1)}, u32[]{:S(2)}, u32[]{:S(2)}) collective-permute-start(f32[256,256]{1,0:T(8,128)S(1)} %select_select_fusion.held), channel_id=1, source_target_pairs={{0,4},{1,5},{2,6},{3,7},{4,0},{5,1},{6,2},{7,3},{8,12},{9,13},{10,... | collective-permute-start | bytes 786440 | tf_op jit(solution)/shard_map/ppermute | solution.py:221
  55.5 2.5 %collective-permute-done.12.tail = f32[256,512]{1,0:T(8,128)S(1)} collective-permute-done((f32[256,512]{1,0:T(8,128)}, f32[256,512]{1,0:T(8,128)S(1)}, u32[]{:S(2)}, u32[]{:S(2)}) %collective-permute-start.12) | collective-permute-done | bytes 524320 | tf_op jit(solution)/shard_map/ppermute | solution.py:186
  58.0 0.0 collective-permute-done.11.got
  58.0 3.4 %shard_map.40 = (f32[1024,128]{1,0:T(8,128)S(1)}, f32[1024,128]{1,0:T(8,128)}) custom-call(s32[1]{0:T(128)} %bitcast.1.row, f32[256,256]{1,0:T(8,128)S(1)} %select_select_fusion.held, f32[256,256]{1,0:T(8,128)S(1)} %collective-permute-done.11.got, f32[256,1024]{1,0:T(8,128)S(1)} %bitcast.12, f32[256,1024]{1,0:T(8,128)} %collective-permute-done.3.whole, ...), custom_call_target="tpu_custom_call" | custom-call | flops 805306368 | tf_op jit(solution)/shard_map/pallas_call | solution.py:32
  61.4 1.9 %collective-permute-start.13 = (f32[1024,128]{1,0:T(8,128)}, f32[1024,128]{1,0:T(8,128)S(1)}, u32[]{:S(2)}, u32[]{:S(2)}) collective-permute-start(f32[1024,128]{1,0:T(8,128)} %get-tuple-element.34), channel_id=1, source_target_pairs={{4,5},{5,4},{6,7},{7,6},{8,9},{9,8},{10,11},{11,10},{12,13},{13,12... | collective-permute-start | bytes 1572872 | tf_op jit(solution)/shard_map/ppermute | solution.py:186
  63.3 0.0 copy-done.3
  63.4 0.7 collective-permute-start.10
  64.1 0.0 collective-permute-done.10.refs_0_
  64.1 0.1 shard_map.39
  64.2 12.2 %collective-permute-done.13 = f32[1024,128]{1,0:T(8,128)S(1)} collective-permute-done((f32[1024,128]{1,0:T(8,128)}, f32[1024,128]{1,0:T(8,128)S(1)}, u32[]{:S(2)}, u32[]{:S(2)}) %collective-permute-start.13) | collective-permute-done | bytes 524320 | tf_op jit(solution)/shard_map/ppermute | solution.py:186
  76.4 0.9 %subtract_select_fusion = f32[1024,128]{1,0:T(8,128)} fusion(f32[1024,128]{1,0:T(8,128)S(1)} %shard_map.39, f32[1024,128]{1,0:T(8,128)S(1)} %get-tuple-element.33, f32[1024,128]{1,0:T(8,128)S(1)} %collective-permute-done.13, pred[]{:T(512)S(6)} %eq.14), kind=kLoop, calls=%fused_computation.1 | loop fusion | flops 262144 | bytes 2097153 | tf_op jit(solution)/shard_map/jit(_where)/select_n | solution.py:310
  (4 shorter events, 0.1 us)
Async XLA Ops:
  0.0 2.8 %copy-start.4 = (f32[2,128,512]{2,1,0:T(8,128)S(1)}, f32[2,128,512]{2,1,0:T(8,128)}, u32[]{:S(2)}) copy-start(f32[2,128,512]{2,1,0:T(8,128)} %param.5) | copy-start | bytes 1572868
  0.0 34.9 %collective-permute-start.3 = (f32[256,1024]{1,0:T(8,128)}, f32[256,1024]{1,0:T(8,128)}, u32[]{:S(2)}, u32[]{:S(2)}) collective-permute-start(f32[256,1024]{1,0:T(8,128)} %bitcast.9), channel_id=1, source_target_pairs={{12,14},{13,15},{14,12},{15,13},{20,22},{21,23},{22,20},{23,21},{2... | collective-permute-start | bytes 3145736 | tf_op jit(solution)/shard_map/ppermute | solution.py:186
  2.8 2.6 %copy-start = (f32[2,128,1024]{2,1,0:T(8,128)S(1)}, f32[2,128,1024]{2,1,0:T(8,128)}, u32[]{:S(2)}) copy-start(f32[2,128,1024]{2,1,0:T(8,128)} %param.4) | copy-start | bytes 3145732
  2.8 1.1 %copy-start.1 = (f32[1024,128]{1,0:T(8,128)S(1)}, f32[1024,128]{1,0:T(8,128)}, u32[]{:S(2)}) copy-start(f32[1024,128]{1,0:T(8,128)} %cross.1) | copy-start | bytes 1572868
  2.9 8.1 %collective-permute-start = (f32[128,1536]{1,0:T(8,128)S(1)}, f32[128,1536]{1,0:T(8,128)S(1)}, u32[]{:S(2)}, u32[]{:S(2)}) collective-permute-start(f32[128,1536]{1,0:T(8,128)S(1)} %pad_maximum_fusion.lead), channel_id=1, source_target_pairs={{0,2},{1,3},{2,0},{3,1}} | collective-permute-start | bytes 2359304 | tf_op jit(solution)/shard_map/ppermute | solution.py:186
  4.0 7.0 %collective-permute-start.1 = (f32[1024,128]{1,0:T(8,128)S(1)}, f32[1024,128]{1,0:T(8,128)}, u32[]{:S(2)}, u32[]{:S(2)}) collective-permute-start(f32[1024,128]{1,0:T(8,128)S(1)} %copy-done.1), channel_id=1, source_target_pairs={{0,1},{1,0},{2,3},{3,2}} | collective-permute-start | bytes 1572872 | tf_op jit(solution)/shard_map/ppermute | solution.py:186
  6.5 28.5 %collective-permute-start.2 = (f32[256,512]{1,0:T(8,128)}, f32[256,512]{1,0:T(8,128)}, u32[]{:S(2)}, u32[]{:S(2)}) collective-permute-start(f32[256,512]{1,0:T(8,128)} %get-tuple-element.35), channel_id=1, source_target_pairs={{8,10},{9,11},{10,8},{11,9},{16,18},{17,19},{18,16},{19,17},{24,26... | collective-permute-start | bytes 1572872 | tf_op jit(solution)/shard_map/ppermute | solution.py:186
  11.1 27.0 %copy-start.2 = (f32[256,256]{1,0:T(8,128)}, f32[256,256]{1,0:T(8,128)S(1)}, u32[]{:S(2)}) copy-start(f32[256,256]{1,0:T(8,128)S(1)} %get-tuple-element.25) | copy-start | bytes 786436
  34.9 1.4 %collective-permute-start.5 = (f32[256,256]{1,0:T(8,128)S(1)}, f32[256,256]{1,0:T(8,128)S(1)}, u32[]{:S(2)}, u32[]{:S(2)}) collective-permute-start(f32[256,256]{1,0:T(8,128)S(1)} %get-tuple-element.25), channel_id=1, source_target_pairs={{0,4},{1,5},{2,6},{3,7}} | collective-permute-start | bytes 786440 | tf_op jit(solution)/shard_map/ppermute | solution.py:194
  35.6 2.4 %collective-permute-start.4 = (f32[512,256]{1,0:T(8,128)S(1)}, f32[512,256]{1,0:T(8,128)S(1)}, u32[]{:S(2)}, u32[]{:S(2)}) collective-permute-start(f32[512,256]{1,0:T(8,128)S(1)} %get-tuple-element.26.sent), channel_id=1, source_target_pairs={{0,1},{1,0},{2,3},{3,2}} | collective-permute-start | bytes 1572872 | tf_op jit(solution)/shard_map/ppermute | solution.py:186
  36.3 13.3 %collective-permute-start.9 = (f32[256,1024]{1,0:T(8,128)S(1)}, f32[256,1024]{1,0:T(8,128)}, u32[]{:S(2)}, u32[]{:S(2)}) collective-permute-start(f32[256,1024]{1,0:T(8,128)S(1)} %bitcast.11), channel_id=1, source_target_pairs={{4,6},{5,7},{6,4},{7,5}} | collective-permute-start | bytes 3145736 | tf_op jit(solution)/shard_map/ppermute | solution.py:186
  38.0 4.6 %collective-permute-start.6 = (f32[256,256]{1,0:T(8,128)S(1)}, f32[256,256]{1,0:T(8,128)S(1)}, u32[]{:S(2)}, u32[]{:S(2)}) collective-permute-start(f32[256,256]{1,0:T(8,128)S(1)} %shard_map.38), channel_id=1, source_target_pairs={{0,28},{1,29},{2,30},{3,31},{4,24},{5,25},{6,26},{7,27}} | collective-permute-start | bytes 786440 | tf_op jit(solution)/shard_map/ppermute | solution.py:194
  38.7 10.8 %collective-permute-start.7 = (f32[256,256]{1,0:T(8,128)S(1)}, f32[256,256]{1,0:T(8,128)S(1)}, u32[]{:S(2)}, u32[]{:S(2)}) collective-permute-start(f32[256,256]{1,0:T(8,128)S(1)} %shard_map.38), channel_id=1, source_target_pairs={{0,12},{1,13},{2,14},{3,15},{4,8},{5,9},{6,10},{7,11}} | collective-permute-start | bytes 786440 | tf_op jit(solution)/shard_map/ppermute | solution.py:194
  40.0 9.5 %collective-permute-start.8 = (f32[256,256]{1,0:T(8,128)S(1)}, f32[256,256]{1,0:T(8,128)S(1)}, u32[]{:S(2)}, u32[]{:S(2)}) collective-permute-start(f32[256,256]{1,0:T(8,128)S(1)} %shard_map.38), channel_id=1, source_target_pairs={{0,20},{1,21},{2,22},{3,23},{4,16},{5,17},{6,18},{7,19}} | collective-permute-start | bytes 786440 | tf_op jit(solution)/shard_map/ppermute | solution.py:194
  40.7 17.3 %collective-permute-start.12 = (f32[256,512]{1,0:T(8,128)}, f32[256,512]{1,0:T(8,128)S(1)}, u32[]{:S(2)}, u32[]{:S(2)}) collective-permute-start(f32[256,512]{1,0:T(8,128)} %get-tuple-element.32), channel_id=1, source_target_pairs={{8,10},{9,11},{10,8},{11,9},{16,18},{17,19},{18,16},{19,17},{24,26... | collective-permute-start | bytes 1572872 | tf_op jit(solution)/shard_map/ppermute | solution.py:186
  49.6 13.7 %copy-start.3 = (f32[256,256]{1,0:T(8,128)S(1)}, f32[256,256]{1,0:T(8,128)}, u32[]{:S(2)}) copy-start(f32[256,256]{1,0:T(8,128)} %copy-done.2) | copy-start | bytes 786436
  49.6 8.4 %collective-permute-start.11 = (f32[256,256]{1,0:T(8,128)S(1)}, f32[256,256]{1,0:T(8,128)S(1)}, u32[]{:S(2)}, u32[]{:S(2)}) collective-permute-start(f32[256,256]{1,0:T(8,128)S(1)} %select_select_fusion.held), channel_id=1, source_target_pairs={{0,4},{1,5},{2,6},{3,7},{4,0},{5,1},{6,2},{7,3},{8,12},{9,13},{10,... | collective-permute-start | bytes 786440 | tf_op jit(solution)/shard_map/ppermute | solution.py:221
  61.4 15.0 %collective-permute-start.13 = (f32[1024,128]{1,0:T(8,128)}, f32[1024,128]{1,0:T(8,128)S(1)}, u32[]{:S(2)}, u32[]{:S(2)}) collective-permute-start(f32[1024,128]{1,0:T(8,128)} %get-tuple-element.34), channel_id=1, source_target_pairs={{4,5},{5,4},{6,7},{7,6},{8,9},{9,8},{10,11},{11,10},{12,13},{13,12... | collective-permute-start | bytes 1572872 | tf_op jit(solution)/shard_map/ppermute | solution.py:186
  63.4 0.7 collective-permute-start.10

commit v20 on v19

--- a/solution.py
+++ b/solution.py
@@ -7,6 +7,7 @@
 from jax.sharding import PartitionSpec as P
 
 AXES = ("rows", "cols")
+CUT = 5
 LIMIT = 12 * 1024 * 1024
 
 
@@ -106,50 +107,52 @@
         copy.wait()
 
 
-def rows_kernel(row, held, got, flat, whole, early, beside, tail, cross, own, send, *refs):
+def rows_kernel(rows, row, held, got, flat, whole, early, beside, tail, cross, own, send, *refs):
     mine, other, base, sems = refs
-    n_design, cands = base.shape
+    cands = base.shape[1]
     depth = held.shape[0] // 2
-    parts = [slice(at * n_design // 2, (at + 1) * n_design // 2) for at in range(2)]
+    start, stop = rows
+    middle = early.shape[1]
     is_odd = row[0] % 2 == 1
 
-    def fetch(at, source):
-        return pltpu.make_async_copy(source, other.at[:, parts[at]], sems.at[at])
+    def fetch(source, low, high):
+        place = other.at[:, low - start : high - start]
+        return pltpu.make_async_copy(source, place, sems.at[0])
+
+    pieces = []
+    if start < middle:
+        low, high = start, min(stop, middle)
+        pieces.append((early.at[:, low:high], low, high))
+    if stop > middle:
+        low, high = max(start, middle), stop
+        pieces.append((tail.at[:, low - middle : high - middle], low, high))
 
     @pl.when(row[0] > 0)
     def _():
-        copies = []
-        for at, part in enumerate(parts):
-            copies.append(
-                [
-                    pltpu.make_async_copy(flat.at[:, part], mine.at[:, part], sems.at[2 + at]),
-                    pltpu.make_async_copy(cross.at[part], base.at[part], sems.at[4 + at]),
-                ]
-            )
-        sources = [
-            (row[0] == 1, [beside.at[:, part] for part in parts]),
-            ((row[0] > 1) & ~is_odd, [early, tail]),
-            ((row[0] > 1) & is_odd, [whole.at[:, part] for part in parts]),
-        ]
-        for at in range(2):
-            for chosen, pieces in sources:
-                pl.when(chosen)(lambda at=at, pieces=pieces: fetch(at, pieces[at]).start())
-            for copy in copies[at]:
-                copy.start()
+        part = slice(start, stop)
+        arrivals = fetch(whole.at[:, part], start, stop)
+        copies = [
+            pltpu.make_async_copy(flat.at[:, part], mine, sems.at[1]),
+            pltpu.make_async_copy(cross.at[part], base, sems.at[2]),
+        ]
+        pl.when((row[0] > 1) & is_odd)(arrivals.start)
+        pl.when(row[0] == 1)(fetch(beside.at[:, part], start, stop).start)
+        for piece in pieces:
+            pl.when((row[0] > 1) & ~is_odd)(fetch(*piece).start)
+        for copy in copies:
+            copy.start()
         has_first = (row[0] == 1) | ((row[0] > 1) & ~is_odd)
         first = jnp.where(has_first, held[...], got[...])
         second = jnp.where(has_first, got[...], held[...])
         solved = jnp.concatenate(
             [first[:depth], second[:depth], first[depth:], second[depth:]], axis=0
         )
-        for at, part in enumerate(parts):
-            fetch(at, whole.at[:, part]).wait()
-            for copy in copies[at]:
-                copy.wait()
-            factors = jnp.concatenate([mine[:, part], other[:, part]], axis=0)
-            partial = dot(solved, factors, 0)
-            own[part] = base[part] - partial[:cands].T
-            send[part] = partial[cands:].T
+        for copy in [arrivals, *copies]:
+            copy.wait()
+        factors = jnp.concatenate([mine[...], other[...]], axis=0)
+        partial = dot(solved, factors, 0)
+        own[...] = base[...] - partial[:cands].T
+        send[...] = partial[cands:].T
 
 
 def top_kernel(offsets, col, pair, *refs):
@@ -296,17 +299,23 @@
             flag=col_id,
         )
 
-        fresh, send = call(
-            rows_kernel,
-            [(n_design, cands), (n_design, (half - 1) * cands)],
-            6 * n_design * 4 * depth * half * cands,
-            solved,
-            [flat, whole, arrived, late, tail, cross_kernel],
-            row_id,
-            [(2 * depth, n_design)] * 2 + [(n_design, cands)],
-        )
-        for step in range(1, half):
-            fresh = fresh - swap(block(send, step - 1, cands), step, range(1, n_rows))
+        fresh = []
+        for rows in ((0, CUT * n_design // 8), (CUT * n_design // 8, n_design)):
+            size = rows[1] - rows[0]
+            own, send = call(
+                functools.partial(rows_kernel, rows),
+                [(size, cands), (size, (half - 1) * cands)],
+                6 * size * 4 * depth * half * cands,
+                solved,
+                [flat, whole, arrived, late, tail, cross_kernel],
+                row_id,
+                [(2 * depth, size)] * 2 + [(size, cands)],
+            )
+            solved[0], send = lax.optimization_barrier((solved[0], send))
+            for step in range(1, half):
+                own = own - swap(block(send, step - 1, cands), step, range(1, n_rows))
+            fresh.append(own)
+        fresh = jnp.concatenate(fresh, axis=0)
         return jnp.where(row_id == 0, top_rows, fresh)
 
     return on_device

time: 77.7 us -> 80 us (1.030)
  waiting for transfers between devices: 45.4 us -> 35.9 us
  starting transfers between devices: 24.7 us -> 29.6 us
  Pallas kernels: 3.54 us -> 7.07 us
  other arithmetic: 0.99 us -> 2.95 us
  local copies, waits for them, and re-layouts: 2.34 us -> 3.57 us
    ppermute x9 -> x10, waiting for transfers between devices: 38.5 us -> 28.8 us  [swap(): return lax.ppermute(array, AXES, pairs)]
    ppermute x9 -> x10, starting transfers between devices: 15.4 us -> 20 us  [swap(): return lax.ppermute(array, AXES, pairs)]
    pallas_call x4 -> x5, Pallas kernels: 3.54 us -> 7.07 us  [call(): pl.pallas_call(kernel, out_shape=[jax.ShapeDtypeStruct(shape, jnp.float32...]
    sub x0 -> x2, other arithmetic: none -> 1.03 us  [on_device(): own = own - swap(block(send, step - 1, cands), step, range(1, n_rows))]
    select_n x1, other arithmetic: 0.06 us -> 1.02 us  [spread(): jnp.where(digit == step, send_down(array, step * low, have), result)]
  transfers between devices with their start and end apart: 14 -> 15, of which waited for: 4 -> 5; matrix products, arithmetic and copies ran while one was open for 3% -> 5% of each run, Pallas kernels for 0% -> 5%
where the time goes in v20:
time: 80 us; the launch traced here: 79.4 us
  waiting for transfers between devices  35.9 us (45%)
  starting transfers between devices  29.6 us (37%)
  Pallas kernels  7.07 us (9%)
  local copies, waits for them, and re-layouts  3.57 us (4%)
  other arithmetic  2.95 us (4%)
    ppermute x10, waiting for transfers between devices, swap(): return lax.ppermute(array, AXES, pairs)  28.8 us
    ppermute x10, starting transfers between devices, swap(): return lax.ppermute(array, AXES, pairs)  20 us
    pallas_call x5, Pallas kernels, call(): pl.pallas_call(kernel, out_shape=[jax.ShapeDtypeStruct(shape, jnp.float32...  7.07 us
    ppermute x4, waiting for transfers between devices, send_down(): return lax.ppermute(array, AXES, pairs)  7.02 us
    ppermute x1, starting transfers between devices, swap_cores(): return lax.ppermute(array, AXES, pairs)  6.29 us
    ppermute x4, starting transfers between devices, send_down(): return lax.ppermute(array, AXES, pairs)  3.31 us
  transfers between devices with their start and end apart: 15, of which 5 were waited for; matrix products, arithmetic and copies ran while one was open for 5% of the time, Pallas kernels for 5%

profile of v20, /device:TPU:2, one launch (start us, length us, event | category | flops | bytes accessed | tf_op | source)
XLA Modules:
  0.0 79.4 jit_solution(4856867110384063062)
XLA Ops:
  0.0 0.8 %collective-permute-start.3 = (f32[256,1024]{1,0:T(8,128)}, f32[256,1024]{1,0:T(8,128)S(1)}, u32[]{:S(2)}, u32[]{:S(2)}) collective-permute-start(f32[256,1024]{1,0:T(8,128)} %bitcast.9), channel_id=1, source_target_pairs={{12,14},{13,15},{14,12},{15,13},{20,22},{21,23},{22,20},{23,21},{2... | collective-permute-start | bytes 3145736 | tf_op jit(solution)/shard_map/ppermute | solution.py:189
  0.9 1.0 %slice_bitcast_fusion.1 = f32[128,512]{1,0:T(8,128)S(1)} fusion(f32[2,128,1024]{2,1,0:T(8,128)} %param.4), kind=kLoop, calls=%fused_computation.4 | loop fusion | bytes 524288 | tf_op jit(solution)/shard_map/squeeze | solution.py:245
  1.9 0.0 copy-start
  1.9 0.0 copy-start.1
  1.9 0.1 pad_maximum_fusion.lead
  2.0 1.7 %collective-permute-start = (f32[128,1536]{1,0:T(8,128)S(1)}, f32[128,1536]{1,0:T(8,128)}, u32[]{:S(2)}, u32[]{:S(2)}) collective-permute-start(f32[128,1536]{1,0:T(8,128)S(1)} %pad_maximum_fusion.lead), channel_id=1, source_target_pairs={{0,2},{1,3},{2,0},{3,1}} | collective-permute-start | bytes 2359304 | tf_op jit(solution)/shard_map/ppermute | solution.py:189
  3.7 1.5 %collective-permute-start.1 = (f32[1024,128]{1,0:T(8,128)S(1)}, f32[1024,128]{1,0:T(8,128)}, u32[]{:S(2)}, u32[]{:S(2)}) collective-permute-start(f32[1024,128]{1,0:T(8,128)S(1)} %copy-done.1), channel_id=1, source_target_pairs={{0,1},{1,0},{2,3},{3,2}} | collective-permute-start | bytes 1572872 | tf_op jit(solution)/shard_map/ppermute | solution.py:189
  5.1 1.1 %fusion = (f32[256,512]{1,0:T(8,128)}, f32[256,512]{1,0:T(8,128)}) fusion(f32[256,1024]{1,0:T(8,128)S(1)} %bitcast.10), kind=kLoop, calls=%fused_computation.8 | loop fusion | bytes 2097152 | tf_op jit(solution)/shard_map/slice | solution.py:251
  6.2 4.5 %collective-permute-start.2 = (f32[256,512]{1,0:T(8,128)}, f32[256,512]{1,0:T(8,128)}, u32[]{:S(2)}, u32[]{:S(2)}) collective-permute-start(f32[256,512]{1,0:T(8,128)} %get-tuple-element.45), channel_id=1, source_target_pairs={{8,10},{9,11},{10,8},{11,9},{16,18},{17,19},{18,16},{19,17},{24,26... | collective-permute-start | bytes 1572872 | tf_op jit(solution)/shard_map/ppermute | solution.py:189
  10.7 0.0 collective-permute-done.far_lead
  10.7 0.0 collective-permute-done.1.refs_0_
  10.7 0.1 shard_map.37
  10.8 24.1 %collective-permute-done.2.early = f32[256,512]{1,0:T(8,128)} collective-permute-done((f32[256,512]{1,0:T(8,128)}, f32[256,512]{1,0:T(8,128)}, u32[]{:S(2)}, u32[]{:S(2)}) %collective-permute-start.2) | collective-permute-done | bytes 524320 | tf_op jit(solution)/shard_map/ppermute | solution.py:189
  34.9 0.0 collective-permute-done.3.whole
  34.9 0.7 collective-permute-start.5
  35.6 0.7 collective-permute-start.4
  36.3 0.0 collective-permute-done.5.first
  36.3 1.7 %collective-permute-start.9 = (f32[256,1024]{1,0:T(8,128)S(1)}, f32[256,1024]{1,0:T(8,128)}, u32[]{:S(2)}, u32[]{:S(2)}) collective-permute-start(f32[256,1024]{1,0:T(8,128)S(1)} %bitcast.11), channel_id=1, source_target_pairs={{4,6},{5,7},{6,4},{7,5}} | collective-permute-start | bytes 3145736 | tf_op jit(solution)/shard_map/ppermute | solution.py:189
  38.0 0.0 collective-permute-done.4.got
  38.0 0.8 shard_map.38
  38.8 0.0 copy-done.4
  38.8 0.7 collective-permute-start.6
  39.5 1.3 %collective-permute-start.7 = (f32[256,256]{1,0:T(8,128)}, f32[256,256]{1,0:T(8,128)S(1)}, u32[]{:S(2)}, u32[]{:S(2)}) collective-permute-start(f32[256,256]{1,0:T(8,128)} %shard_map.38), channel_id=1, source_target_pairs={{0,12},{1,13},{2,14},{3,15},{4,8},{5,9},{6,10},{7,11}} | collective-permute-start | bytes 786440 | tf_op jit(solution)/shard_map/ppermute | solution.py:197
  40.8 0.7 collective-permute-start.8
  41.4 1.9 %collective-permute-start.12 = (f32[256,512]{1,0:T(8,128)}, f32[256,512]{1,0:T(8,128)}, u32[]{:S(2)}, u32[]{:S(2)}) collective-permute-start(f32[256,512]{1,0:T(8,128)} %get-tuple-element.37), channel_id=1, source_target_pairs={{8,10},{9,11},{10,8},{11,9},{16,18},{17,19},{18,16},{19,17},{24,26... | collective-permute-start | bytes 1572872 | tf_op jit(solution)/shard_map/ppermute | solution.py:189
  43.4 0.0 copy-start.5
  43.4 0.0 collective-permute-done.6
  43.4 7.0 %collective-permute-done.7 = f32[256,256]{1,0:T(8,128)S(1)} collective-permute-done((f32[256,256]{1,0:T(8,128)}, f32[256,256]{1,0:T(8,128)S(1)}, u32[]{:S(2)}, u32[]{:S(2)}) %collective-permute-start.7) | collective-permute-done | bytes 262176 | tf_op jit(solution)/shard_map/ppermute | solution.py:197
  50.4 0.0 collective-permute-done.8
  50.4 1.0 %select_select_fusion.held = f32[256,256]{1,0:T(8,128)S(1)} fusion(f32[256,256]{1,0:T(8,128)S(1)} %collective-permute-done.6, f32[256,256]{1,0:T(8,128)S(1)} %collective-permute-done.7, f32[256,256]{1,0:T(8,128)S(1)} %collective-permute-done.8, f32[256,256]{1,0:T(8,128)} %shard_map.38, pred[]{:T(512)S(6)} %eq.17, pred[]{:T(512)S(6)} %eq.16, pred[]{:T(512)S(6)} %eq.15), kind=kLoop, calls=%fused_computation.2 | loop fusion | flops 196608 | bytes 1310723 | tf_op jit(solution)/shard_map/jit(_where)/select_n | solution.py:206
  51.5 0.0 collective-permute-done.9.beside
  51.5 6.3 %collective-permute-start.11 = (f32[256,256]{1,0:T(8,128)S(1)}, f32[256,256]{1,0:T(8,128)S(1)}, u32[]{:S(2)}, u32[]{:S(2)}) collective-permute-start(f32[256,256]{1,0:T(8,128)S(1)} %select_select_fusion.held), channel_id=1, source_target_pairs={{0,4},{1,5},{2,6},{3,7},{4,0},{5,1},{6,2},{7,3},{8,12},{9,13},{10,... | collective-permute-start | bytes 786440 | tf_op jit(solution)/shard_map/ppermute | solution.py:224
  57.8 1.1 %collective-permute-done.12.tail = f32[256,512]{1,0:T(8,128)} collective-permute-done((f32[256,512]{1,0:T(8,128)}, f32[256,512]{1,0:T(8,128)}, u32[]{:S(2)}, u32[]{:S(2)}) %collective-permute-start.12) | collective-permute-done | bytes 524320 | tf_op jit(solution)/shard_map/ppermute | solution.py:189
  58.8 0.1 collective-permute-done.11.got
  58.9 2.8 %shard_map.40 = (f32[640,128]{1,0:T(8,128)S(1)}, f32[640,128]{1,0:T(8,128)}) custom-call(s32[1]{0:T(128)} %bitcast.1.row, f32[256,256]{1,0:T(8,128)S(1)} %select_select_fusion.held, f32[256,256]{1,0:T(8,128)S(1)} %collective-permute-done.11.got, f32[256,1024]{1,0:T(8,128)S(1)} %bitcast.12, f32[256,1024]{1,0:T(8,128)S(1)} %collective-permute-done.3.whole, ...), custom_call_target="tpu_custom_call" | custom-call | flops 503316480 | tf_op jit(solution)/shard_map/pallas_call | solution.py:33
  61.7 2.7 %collective-permute-start.13 = (f32[640,128]{1,0:T(8,128)}, f32[640,128]{1,0:T(8,128)}, u32[]{:S(2)}, u32[]{:S(2)}) collective-permute-start(f32[640,128]{1,0:T(8,128)} %get-tuple-element.40), channel_id=1, source_target_pairs={{4,5},{5,4},{6,7},{7,6},{8,9},{9,8},{10,11},{11,10},{12,13},{13,12... | collective-permute-start | bytes 983048 | tf_op jit(solution)/shard_map/ppermute | solution.py:189
  64.5 0.8 slice.26
  65.3 1.4 %collective-permute-start.10 = (f32[512,128]{1,0:T(8,128)}, f32[512,128]{1,0:T(8,128)}, u32[]{:S(2)}, u32[]{:S(2)}) collective-permute-start(f32[512,128]{1,0:T(8,128)} %slice.26), channel_id=1, source_target_pairs={{0,1},{1,0},{2,3},{3,2}} | collective-permute-start | bytes 786440 | tf_op jit(solution)/shard_map/ppermute | solution.py:189
  66.6 2.4 %shard_map.41 = (f32[384,128]{1,0:T(8,128)S(1)}, f32[384,128]{1,0:T(8,128)}) custom-call(s32[1]{0:T(128)} %bitcast.1.row, f32[256,256]{1,0:T(8,128)S(1)} %select_select_fusion.held, f32[256,256]{1,0:T(8,128)S(1)} %collective-permute-done.11.got, f32[256,1024]{1,0:T(8,128)S(1)} %bitcast.13, f32[256,1024]{1,0:T(8,128)S(1)} %collective-permute-done.3.whole, ...), custom_call_target="tpu_custom_call" | custom-call | flops 301989888 | tf_op jit(solution)/shard_map/pallas_call | solution.py:33
  69.1 0.7 copy-done.6
  69.7 3.1 %collective-permute-start.14 = (f32[384,128]{1,0:T(8,128)}, f32[384,128]{1,0:T(8,128)S(1)}, u32[]{:S(2)}, u32[]{:S(2)}) collective-permute-start(f32[384,128]{1,0:T(8,128)} %get-tuple-element.44), channel_id=1, source_target_pairs={{4,5},{5,4},{6,7},{7,6},{8,9},{9,8},{10,11},{11,10},{12,13},{13,12... | collective-permute-start | bytes 589832 | tf_op jit(solution)/shard_map/ppermute | solution.py:189
  72.8 0.0 collective-permute-done.10.refs_0_
  72.8 0.0 copy-start.7
  72.9 1.0 %shard_map.39 = f32[1024,128]{1,0:T(8,128)S(1)} custom-call(s32[1]{0:T(128)} %bitcast.col, f32[512,256]{1,0:T(8,128)S(1)} %constant_dynamic-update-slice_fusion.pair, f32[512,128]{1,0:T(8,128)} %collective-permute-done.10.refs_0_), custom_call_target="tpu_custom_call" | custom-call | tf_op jit(solution)/shard_map/pallas_call | solution.py:33
  73.9 3.6 %collective-permute-done.14 = f32[384,128]{1,0:T(8,128)S(1)} collective-permute-done((f32[384,128]{1,0:T(8,128)}, f32[384,128]{1,0:T(8,128)S(1)}, u32[]{:S(2)}, u32[]{:S(2)}) %collective-permute-start.14) | collective-permute-done | bytes 196640 | tf_op jit(solution)/shard_map/ppermute | solution.py:189
  77.5 0.0 collective-permute-done.13
  77.5 1.0 %sub.11 = f32[640,128]{1,0:T(8,128)S(1)} subtract(f32[640,128]{1,0:T(8,128)S(1)} %copy-done.3, f32[640,128]{1,0:T(8,128)} %collective-permute-done.13) | non-fusion elementwise | flops 81920 | bytes 983040 | tf_op jit(solution)/shard_map/sub | solution.py:316
  78.6 0.9 %maximum_select_fusion = f32[1024,128]{1,0:T(8,128)} fusion(f32[1024,128]{1,0:T(8,128)S(1)} %shard_map.39, f32[384,128]{1,0:T(8,128)S(1)} %sub.12, f32[640,128]{1,0:T(8,128)S(1)} %sub.11, pred[]{:T(512)S(6)} %eq.14), kind=kLoop, calls=%fused_computation.1 | loop fusion | flops 262144 | bytes 1572865 | tf_op jit(solution)/shard_map/jit(_where)/select_n | solution.py:319
  (16 shorter events, 0.1 us)
Async XLA Ops:
  0.0 1.8 %copy-start.8 = (f32[2,128,512]{2,1,0:T(8,128)S(1)}, f32[2,128,512]{2,1,0:T(8,128)}, u32[]{:S(2)}) copy-start(f32[2,128,512]{2,1,0:T(8,128)} %param.5) | copy-start | bytes 1572868
  0.0 34.9 %collective-permute-start.3 = (f32[256,1024]{1,0:T(8,128)}, f32[256,1024]{1,0:T(8,128)S(1)}, u32[]{:S(2)}, u32[]{:S(2)}) collective-permute-start(f32[256,1024]{1,0:T(8,128)} %bitcast.9), channel_id=1, source_target_pairs={{12,14},{13,15},{14,12},{15,13},{20,22},{21,23},{22,20},{23,21},{2... | collective-permute-start | bytes 3145736 | tf_op jit(solution)/shard_map/ppermute | solution.py:189
  1.9 3.2 %copy-start = (f32[2,128,1024]{2,1,0:T(8,128)S(1)}, f32[2,128,1024]{2,1,0:T(8,128)}, u32[]{:S(2)}) copy-start(f32[2,128,1024]{2,1,0:T(8,128)} %param.4) | copy-start | bytes 3145732
  1.9 1.8 %copy-start.1 = (f32[1024,128]{1,0:T(8,128)S(1)}, f32[1024,128]{1,0:T(8,128)}, u32[]{:S(2)}) copy-start(f32[1024,128]{1,0:T(8,128)} %cross.3) | copy-start | bytes 1572868
  2.0 8.7 %collective-permute-start = (f32[128,1536]{1,0:T(8,128)S(1)}, f32[128,1536]{1,0:T(8,128)}, u32[]{:S(2)}, u32[]{:S(2)}) collective-permute-start(f32[128,1536]{1,0:T(8,128)S(1)} %pad_maximum_fusion.lead), channel_id=1, source_target_pairs={{0,2},{1,3},{2,0},{3,1}} | collective-permute-start | bytes 2359304 | tf_op jit(solution)/shard_map/ppermute | solution.py:189
  3.7 7.1 %collective-permute-start.1 = (f32[1024,128]{1,0:T(8,128)S(1)}, f32[1024,128]{1,0:T(8,128)}, u32[]{:S(2)}, u32[]{:S(2)}) collective-permute-start(f32[1024,128]{1,0:T(8,128)S(1)} %copy-done.1), channel_id=1, source_target_pairs={{0,1},{1,0},{2,3},{3,2}} | collective-permute-start | bytes 1572872 | tf_op jit(solution)/shard_map/ppermute | solution.py:189
  6.2 28.7 %collective-permute-start.2 = (f32[256,512]{1,0:T(8,128)}, f32[256,512]{1,0:T(8,128)}, u32[]{:S(2)}, u32[]{:S(2)}) collective-permute-start(f32[256,512]{1,0:T(8,128)} %get-tuple-element.45), channel_id=1, source_target_pairs={{8,10},{9,11},{10,8},{11,9},{16,18},{17,19},{18,16},{19,17},{24,26... | collective-permute-start | bytes 1572872 | tf_op jit(solution)/shard_map/ppermute | solution.py:189
  10.8 28.0 %copy-start.4 = (f32[256,256]{1,0:T(8,128)}, f32[256,256]{1,0:T(8,128)S(1)}, u32[]{:S(2)}) copy-start(f32[256,256]{1,0:T(8,128)S(1)} %get-tuple-element.30) | copy-start | bytes 786436
  34.9 1.4 %collective-permute-start.5 = (f32[256,256]{1,0:T(8,128)S(1)}, f32[256,256]{1,0:T(8,128)S(1)}, u32[]{:S(2)}, u32[]{:S(2)}) collective-permute-start(f32[256,256]{1,0:T(8,128)S(1)} %get-tuple-element.30), channel_id=1, source_target_pairs={{0,4},{1,5},{2,6},{3,7}} | collective-permute-start | bytes 786440 | tf_op jit(solution)/shard_map/ppermute | solution.py:197
  35.6 2.4 %collective-permute-start.4 = (f32[512,256]{1,0:T(8,128)S(1)}, f32[512,256]{1,0:T(8,128)S(1)}, u32[]{:S(2)}, u32[]{:S(2)}) collective-permute-start(f32[512,256]{1,0:T(8,128)S(1)} %get-tuple-element.31.sent), channel_id=1, source_target_pairs={{0,1},{1,0},{2,3},{3,2}} | collective-permute-start | bytes 1572872 | tf_op jit(solution)/shard_map/ppermute | solution.py:189
  36.3 15.2 %collective-permute-start.9 = (f32[256,1024]{1,0:T(8,128)S(1)}, f32[256,1024]{1,0:T(8,128)}, u32[]{:S(2)}, u32[]{:S(2)}) collective-permute-start(f32[256,1024]{1,0:T(8,128)S(1)} %bitcast.11), channel_id=1, source_target_pairs={{4,6},{5,7},{6,4},{7,5}} | collective-permute-start | bytes 3145736 | tf_op jit(solution)/shard_map/ppermute | solution.py:189
  38.8 4.6 %collective-permute-start.6 = (f32[256,256]{1,0:T(8,128)}, f32[256,256]{1,0:T(8,128)S(1)}, u32[]{:S(2)}, u32[]{:S(2)}) collective-permute-start(f32[256,256]{1,0:T(8,128)} %shard_map.38), channel_id=1, source_target_pairs={{0,28},{1,29},{2,30},{3,31},{4,24},{5,25},{6,26},{7,27}} | collective-permute-start | bytes 786440 | tf_op jit(solution)/shard_map/ppermute | solution.py:197
  39.5 11.0 %collective-permute-start.7 = (f32[256,256]{1,0:T(8,128)}, f32[256,256]{1,0:T(8,128)S(1)}, u32[]{:S(2)}, u32[]{:S(2)}) collective-permute-start(f32[256,256]{1,0:T(8,128)} %shard_map.38), channel_id=1, source_target_pairs={{0,12},{1,13},{2,14},{3,15},{4,8},{5,9},{6,10},{7,11}} | collective-permute-start | bytes 786440 | tf_op jit(solution)/shard_map/ppermute | solution.py:197
  40.8 9.7 %collective-permute-start.8 = (f32[256,256]{1,0:T(8,128)}, f32[256,256]{1,0:T(8,128)S(1)}, u32[]{:S(2)}, u32[]{:S(2)}) collective-permute-start(f32[256,256]{1,0:T(8,128)} %shard_map.38), channel_id=1, source_target_pairs={{0,20},{1,21},{2,22},{3,23},{4,16},{5,17},{6,18},{7,19}} | collective-permute-start | bytes 786440 | tf_op jit(solution)/shard_map/ppermute | solution.py:197
  41.4 17.4 %collective-permute-start.12 = (f32[256,512]{1,0:T(8,128)}, f32[256,512]{1,0:T(8,128)}, u32[]{:S(2)}, u32[]{:S(2)}) collective-permute-start(f32[256,512]{1,0:T(8,128)} %get-tuple-element.37), channel_id=1, source_target_pairs={{8,10},{9,11},{10,8},{11,9},{16,18},{17,19},{18,16},{19,17},{24,26... | collective-permute-start | bytes 1572872 | tf_op jit(solution)/shard_map/ppermute | solution.py:189
  43.4 14.4 %copy-start.5 = (f32[256,256]{1,0:T(8,128)S(1)}, f32[256,256]{1,0:T(8,128)}, u32[]{:S(2)}) copy-start(f32[256,256]{1,0:T(8,128)} %copy-done.4) | copy-start | bytes 786436
  51.5 7.5 %collective-permute-start.11 = (f32[256,256]{1,0:T(8,128)S(1)}, f32[256,256]{1,0:T(8,128)S(1)}, u32[]{:S(2)}, u32[]{:S(2)}) collective-permute-start(f32[256,256]{1,0:T(8,128)S(1)} %select_select_fusion.held), channel_id=1, source_target_pairs={{0,4},{1,5},{2,6},{3,7},{4,0},{5,1},{6,2},{7,3},{8,12},{9,13},{10,... | collective-permute-start | bytes 786440 | tf_op jit(solution)/shard_map/ppermute | solution.py:224
  61.7 3.5 %copy-start.2 = (f32[640,128]{1,0:T(8,128)}, f32[640,128]{1,0:T(8,128)S(1)}, u32[]{:S(2)}) copy-start(f32[640,128]{1,0:T(8,128)S(1)} %get-tuple-element.38) | copy-start | bytes 983044
  61.7 15.8 %collective-permute-start.13 = (f32[640,128]{1,0:T(8,128)}, f32[640,128]{1,0:T(8,128)}, u32[]{:S(2)}, u32[]{:S(2)}) collective-permute-start(f32[640,128]{1,0:T(8,128)} %get-tuple-element.40), channel_id=1, source_target_pairs={{4,5},{5,4},{6,7},{7,6},{8,9},{9,8},{10,11},{11,10},{12,13},{13,12... | collective-permute-start | bytes 983048 | tf_op jit(solution)/shard_map/ppermute | solution.py:189
  65.3 7.6 %collective-permute-start.10 = (f32[512,128]{1,0:T(8,128)}, f32[512,128]{1,0:T(8,128)}, u32[]{:S(2)}, u32[]{:S(2)}) collective-permute-start(f32[512,128]{1,0:T(8,128)} %slice.26), channel_id=1, source_target_pairs={{0,1},{1,0},{2,3},{3,2}} | collective-permute-start | bytes 786440 | tf_op jit(solution)/shard_map/ppermute | solution.py:189
  69.1 0.7 copy-start.6
  69.7 7.8 %collective-permute-start.14 = (f32[384,128]{1,0:T(8,128)}, f32[384,128]{1,0:T(8,128)S(1)}, u32[]{:S(2)}, u32[]{:S(2)}) collective-permute-start(f32[384,128]{1,0:T(8,128)} %get-tuple-element.44), channel_id=1, source_target_pairs={{4,5},{5,4},{6,7},{7,6},{8,9},{9,8},{10,11},{11,10},{12,13},{13,12... | collective-permute-start | bytes 589832 | tf_op jit(solution)/shard_map/ppermute | solution.py:189
  72.8 4.6 %copy-start.7 = (f32[384,128]{1,0:T(8,128)S(1)}, f32[384,128]{1,0:T(8,128)}, u32[]{:S(2)}) copy-start(f32[384,128]{1,0:T(8,128)} %copy-done.6) | copy-start | bytes 589828
  73.9 3.6 %copy-start.3 = (f32[640,128]{1,0:T(8,128)S(1)}, f32[640,128]{1,0:T(8,128)}, u32[]{:S(2)}) copy-start(f32[640,128]{1,0:T(8,128)} %copy-done.2) | copy-start | bytes 983044

commit v21 on v19

--- a/solution.py
+++ b/solution.py
@@ -106,8 +106,8 @@
         copy.wait()
 
 
-def rows_kernel(row, held, got, flat, whole, early, beside, tail, cross, own, send, *refs):
-    mine, other, base, sems = refs
+def rows_kernel(row, held, got, mine, base, whole, early, beside, tail, own, send, *refs):
+    other, sems = refs
     n_design, cands = base.shape
     depth = held.shape[0] // 2
     parts = [slice(at * n_design // 2, (at + 1) * n_design // 2) for at in range(2)]
@@ -118,14 +118,6 @@
 
     @pl.when(row[0] > 0)
     def _():
-        copies = []
-        for at, part in enumerate(parts):
-            copies.append(
-                [
-                    pltpu.make_async_copy(flat.at[:, part], mine.at[:, part], sems.at[2 + at]),
-                    pltpu.make_async_copy(cross.at[part], base.at[part], sems.at[4 + at]),
-                ]
-            )
         sources = [
             (row[0] == 1, [beside.at[:, part] for part in parts]),
             ((row[0] > 1) & ~is_odd, [early, tail]),
@@ -134,8 +126,6 @@
         for at in range(2):
             for chosen, pieces in sources:
                 pl.when(chosen)(lambda at=at, pieces=pieces: fetch(at, pieces[at]).start())
-            for copy in copies[at]:
-                copy.start()
         has_first = (row[0] == 1) | ((row[0] > 1) & ~is_odd)
         first = jnp.where(has_first, held[...], got[...])
         second = jnp.where(has_first, got[...], held[...])
@@ -144,8 +134,6 @@
         )
         for at, part in enumerate(parts):
             fetch(at, whole.at[:, part]).wait()
-            for copy in copies[at]:
-                copy.wait()
             factors = jnp.concatenate([mine[:, part], other[:, part]], axis=0)
             partial = dot(solved, factors, 0)
             own[part] = base[part] - partial[:cands].T
@@ -300,10 +288,10 @@
             rows_kernel,
             [(n_design, cands), (n_design, (half - 1) * cands)],
             6 * n_design * 4 * depth * half * cands,
-            solved,
-            [flat, whole, arrived, late, tail, cross_kernel],
+            [*solved, flat, cross_kernel],
+            [whole, arrived, late, tail],
             row_id,
-            [(2 * depth, n_design)] * 2 + [(n_design, cands)],
+            [(2 * depth, n_design)],
         )
         for step in range(1, half):
             fresh = fresh - swap(block(send, step - 1, cands), step, range(1, n_rows))

time: 77.7 us -> 77.6 us (level)
  no operation moved by 1% of the time
where the time goes in v21:
time: 77.6 us; the launch traced here: 77.2 us
  waiting for transfers between devices  45.4 us (59%)
  starting transfers between devices  24.7 us (32%)
  Pallas kernels  3.53 us (5%)
  local copies, waits for them, and re-layouts  2.34 us (3%)
  other arithmetic  0.99 us (1%)
    ppermute x9, waiting for transfers between devices, swap(): return lax.ppermute(array, AXES, pairs)  38.5 us
    ppermute x9, starting transfers between devices, swap(): return lax.ppermute(array, AXES, pairs)  15.4 us
    ppermute x4, waiting for transfers between devices, send_down(): return lax.ppermute(array, AXES, pairs)  6.82 us
    ppermute x1, starting transfers between devices, swap_cores(): return lax.ppermute(array, AXES, pairs)  5.95 us
    pallas_call x4, Pallas kernels, call(): pl.pallas_call(kernel, out_shape=[jax.ShapeDtypeStruct(shape, jnp.float32...  3.53 us
    ppermute x4, starting transfers between devices, send_down(): return lax.ppermute(array, AXES, pairs)  3.31 us
  transfers between devices with their start and end apart: 14, of which 4 were waited for; matrix products, arithmetic and copies ran while one was open for 3% of the time, Pallas kernels for 0%

profile of v21, /device:TPU:2, one launch (start us, length us, event | category | flops | bytes accessed | tf_op | source)
XLA Modules:
  0.0 77.2 jit_solution(18073427388239332487)
XLA Ops:
  0.0 0.0 copy-start.4
  0.0 1.8 %collective-permute-start.3 = (f32[256,1024]{1,0:T(8,128)}, f32[256,1024]{1,0:T(8,128)}, u32[]{:S(2)}, u32[]{:S(2)}) collective-permute-start(f32[256,1024]{1,0:T(8,128)} %bitcast.9), channel_id=1, source_target_pairs={{12,14},{13,15},{14,12},{15,13},{20,22},{21,23},{22,20},{23,21},{2... | collective-permute-start | bytes 3145736 | tf_op jit(solution)/shard_map/ppermute | solution.py:174
  1.8 1.0 %slice_bitcast_fusion.1 = f32[128,512]{1,0:T(8,128)S(1)} fusion(f32[2,128,1024]{2,1,0:T(8,128)} %param.4), kind=kLoop, calls=%fused_computation.4 | loop fusion | bytes 524288 | tf_op jit(solution)/shard_map/squeeze | solution.py:230
  2.8 0.0 copy-done.4
  2.8 0.0 copy-start
  2.8 0.0 copy-start.1
  2.8 0.1 pad_maximum_fusion.lead
  2.9 0.8 %collective-permute-start = (f32[128,1536]{1,0:T(8,128)S(1)}, f32[128,1536]{1,0:T(8,128)S(1)}, u32[]{:S(2)}, u32[]{:S(2)}) collective-permute-start(f32[128,1536]{1,0:T(8,128)S(1)} %pad_maximum_fusion.lead), channel_id=1, source_target_pairs={{0,2},{1,3},{2,0},{3,1}} | collective-permute-start | bytes 2359304 | tf_op jit(solution)/shard_map/ppermute | solution.py:174
  3.8 0.2 copy-done.1
  4.0 1.4 %collective-permute-start.1 = (f32[1024,128]{1,0:T(8,128)S(1)}, f32[1024,128]{1,0:T(8,128)}, u32[]{:S(2)}, u32[]{:S(2)}) collective-permute-start(f32[1024,128]{1,0:T(8,128)S(1)} %copy-done.1), channel_id=1, source_target_pairs={{0,1},{1,0},{2,3},{3,2}} | collective-permute-start | bytes 1572872 | tf_op jit(solution)/shard_map/ppermute | solution.py:174
  5.4 0.0 copy-done
  5.4 1.1 %fusion = (f32[256,512]{1,0:T(8,128)}, f32[256,512]{1,0:T(8,128)}) fusion(f32[256,1024]{1,0:T(8,128)S(1)} %bitcast.10), kind=kLoop, calls=%fused_computation.8 | loop fusion | bytes 2097152 | tf_op jit(solution)/shard_map/slice | solution.py:236
  6.5 4.5 %collective-permute-start.2 = (f32[256,512]{1,0:T(8,128)}, f32[256,512]{1,0:T(8,128)}, u32[]{:S(2)}, u32[]{:S(2)}) collective-permute-start(f32[256,512]{1,0:T(8,128)} %get-tuple-element.35), channel_id=1, source_target_pairs={{8,10},{9,11},{10,8},{11,9},{16,18},{17,19},{18,16},{19,17},{24,26... | collective-permute-start | bytes 1572872 | tf_op jit(solution)/shard_map/ppermute | solution.py:174
  11.0 0.0 collective-permute-done.far_lead
  11.0 0.0 collective-permute-done.1.refs_0_
  11.0 0.1 shard_map.37
  11.1 0.0 copy-start.2
  11.1 23.9 %collective-permute-done.2.early = f32[256,512]{1,0:T(8,128)} collective-permute-done((f32[256,512]{1,0:T(8,128)}, f32[256,512]{1,0:T(8,128)}, u32[]{:S(2)}, u32[]{:S(2)}) %collective-permute-start.2) | collective-permute-done | bytes 524320 | tf_op jit(solution)/shard_map/ppermute | solution.py:174
  34.9 0.0 collective-permute-done.3.whole
  34.9 0.7 collective-permute-start.5
  35.6 0.7 collective-permute-start.4
  36.3 0.0 collective-permute-done.5.first
  36.3 1.6 %collective-permute-start.9 = (f32[256,1024]{1,0:T(8,128)S(1)}, f32[256,1024]{1,0:T(8,128)}, u32[]{:S(2)}, u32[]{:S(2)}) collective-permute-start(f32[256,1024]{1,0:T(8,128)S(1)} %bitcast.11), channel_id=1, source_target_pairs={{4,6},{5,7},{6,4},{7,5}} | collective-permute-start | bytes 3145736 | tf_op jit(solution)/shard_map/ppermute | solution.py:174
  38.0 0.0 collective-permute-done.4.got
  38.0 0.1 shard_map.38
  38.0 0.0 copy-done.2
  38.0 0.7 collective-permute-start.6
  38.7 1.3 %collective-permute-start.7 = (f32[256,256]{1,0:T(8,128)S(1)}, f32[256,256]{1,0:T(8,128)S(1)}, u32[]{:S(2)}, u32[]{:S(2)}) collective-permute-start(f32[256,256]{1,0:T(8,128)S(1)} %shard_map.38), channel_id=1, source_target_pairs={{0,12},{1,13},{2,14},{3,15},{4,8},{5,9},{6,10},{7,11}} | collective-permute-start | bytes 786440 | tf_op jit(solution)/shard_map/ppermute | solution.py:182
  40.0 0.7 collective-permute-start.8
  40.7 1.9 %collective-permute-start.12 = (f32[256,512]{1,0:T(8,128)}, f32[256,512]{1,0:T(8,128)S(1)}, u32[]{:S(2)}, u32[]{:S(2)}) collective-permute-start(f32[256,512]{1,0:T(8,128)} %get-tuple-element.32), channel_id=1, source_target_pairs={{8,10},{9,11},{10,8},{11,9},{16,18},{17,19},{18,16},{19,17},{24,26... | collective-permute-start | bytes 1572872 | tf_op jit(solution)/shard_map/ppermute | solution.py:174
  42.7 0.0 collective-permute-done.6
  42.7 6.8 %collective-permute-done.7 = f32[256,256]{1,0:T(8,128)S(1)} collective-permute-done((f32[256,256]{1,0:T(8,128)S(1)}, f32[256,256]{1,0:T(8,128)S(1)}, u32[]{:S(2)}, u32[]{:S(2)}) %collective-permute-start.7) | collective-permute-done | bytes 262176 | tf_op jit(solution)/shard_map/ppermute | solution.py:182
  49.5 0.0 collective-permute-done.8
  49.5 0.1 select_select_fusion.held
  49.6 0.0 copy-start.3
  49.6 0.0 collective-permute-done.9.beside
  49.6 5.9 %collective-permute-start.11 = (f32[256,256]{1,0:T(8,128)S(1)}, f32[256,256]{1,0:T(8,128)S(1)}, u32[]{:S(2)}, u32[]{:S(2)}) collective-permute-start(f32[256,256]{1,0:T(8,128)S(1)} %select_select_fusion.held), channel_id=1, source_target_pairs={{0,4},{1,5},{2,6},{3,7},{4,0},{5,1},{6,2},{7,3},{8,12},{9,13},{10,... | collective-permute-start | bytes 786440 | tf_op jit(solution)/shard_map/ppermute | solution.py:209
  55.5 2.5 %collective-permute-done.12.tail = f32[256,512]{1,0:T(8,128)S(1)} collective-permute-done((f32[256,512]{1,0:T(8,128)}, f32[256,512]{1,0:T(8,128)S(1)}, u32[]{:S(2)}, u32[]{:S(2)}) %collective-permute-start.12) | collective-permute-done | bytes 524320 | tf_op jit(solution)/shard_map/ppermute | solution.py:174
  58.0 0.0 collective-permute-done.11.got
  58.0 3.4 %shard_map.40 = (f32[1024,128]{1,0:T(8,128)S(1)}, f32[1024,128]{1,0:T(8,128)}) custom-call(s32[1]{0:T(128)} %bitcast.1.row, f32[256,256]{1,0:T(8,128)S(1)} %select_select_fusion.held, f32[256,256]{1,0:T(8,128)S(1)} %collective-permute-done.11.got, f32[256,1024]{1,0:T(8,128)S(1)} %bitcast.12, f32[1024,128]{1,0:T(8,128)S(1)} %copy-done.1, ...), custom_call_target="tpu_custom_call" | custom-call | flops 805306368 | tf_op jit(solution)/shard_map/pallas_call | solution.py:32
  61.4 1.9 %collective-permute-start.13 = (f32[1024,128]{1,0:T(8,128)}, f32[1024,128]{1,0:T(8,128)S(1)}, u32[]{:S(2)}, u32[]{:S(2)}) collective-permute-start(f32[1024,128]{1,0:T(8,128)} %get-tuple-element.34), channel_id=1, source_target_pairs={{4,5},{5,4},{6,7},{7,6},{8,9},{9,8},{10,11},{11,10},{12,13},{13,12... | collective-permute-start | bytes 1572872 | tf_op jit(solution)/shard_map/ppermute | solution.py:174
  63.3 0.0 copy-done.3
  63.4 0.7 collective-permute-start.10
  64.1 0.0 collective-permute-done.10.refs_0_
  64.1 0.1 shard_map.39
  64.2 12.2 %collective-permute-done.13 = f32[1024,128]{1,0:T(8,128)S(1)} collective-permute-done((f32[1024,128]{1,0:T(8,128)}, f32[1024,128]{1,0:T(8,128)S(1)}, u32[]{:S(2)}, u32[]{:S(2)}) %collective-permute-start.13) | collective-permute-done | bytes 524320 | tf_op jit(solution)/shard_map/ppermute | solution.py:174
  76.4 0.9 %subtract_select_fusion = f32[1024,128]{1,0:T(8,128)} fusion(f32[1024,128]{1,0:T(8,128)S(1)} %shard_map.39, f32[1024,128]{1,0:T(8,128)S(1)} %get-tuple-element.33, f32[1024,128]{1,0:T(8,128)S(1)} %collective-permute-done.13, pred[]{:T(512)S(6)} %eq.14), kind=kLoop, calls=%fused_computation.1 | loop fusion | flops 262144 | bytes 2097153 | tf_op jit(solution)/shard_map/jit(_where)/select_n | solution.py:298
  (4 shorter events, 0.1 us)
Async XLA Ops:
  0.0 2.8 %copy-start.4 = (f32[2,128,512]{2,1,0:T(8,128)S(1)}, f32[2,128,512]{2,1,0:T(8,128)}, u32[]{:S(2)}) copy-start(f32[2,128,512]{2,1,0:T(8,128)} %param.5) | copy-start | bytes 1572868
  0.0 34.9 %collective-permute-start.3 = (f32[256,1024]{1,0:T(8,128)}, f32[256,1024]{1,0:T(8,128)}, u32[]{:S(2)}, u32[]{:S(2)}) collective-permute-start(f32[256,1024]{1,0:T(8,128)} %bitcast.9), channel_id=1, source_target_pairs={{12,14},{13,15},{14,12},{15,13},{20,22},{21,23},{22,20},{23,21},{2... | collective-permute-start | bytes 3145736 | tf_op jit(solution)/shard_map/ppermute | solution.py:174
  2.8 2.6 %copy-start = (f32[2,128,1024]{2,1,0:T(8,128)S(1)}, f32[2,128,1024]{2,1,0:T(8,128)}, u32[]{:S(2)}) copy-start(f32[2,128,1024]{2,1,0:T(8,128)} %param.4) | copy-start | bytes 3145732
  2.8 1.1 %copy-start.1 = (f32[1024,128]{1,0:T(8,128)S(1)}, f32[1024,128]{1,0:T(8,128)}, u32[]{:S(2)}) copy-start(f32[1024,128]{1,0:T(8,128)} %base.1) | copy-start | bytes 1572868
  2.9 8.1 %collective-permute-start = (f32[128,1536]{1,0:T(8,128)S(1)}, f32[128,1536]{1,0:T(8,128)S(1)}, u32[]{:S(2)}, u32[]{:S(2)}) collective-permute-start(f32[128,1536]{1,0:T(8,128)S(1)} %pad_maximum_fusion.lead), channel_id=1, source_target_pairs={{0,2},{1,3},{2,0},{3,1}} | collective-permute-start | bytes 2359304 | tf_op jit(solution)/shard_map/ppermute | solution.py:174
  4.0 7.0 %collective-permute-start.1 = (f32[1024,128]{1,0:T(8,128)S(1)}, f32[1024,128]{1,0:T(8,128)}, u32[]{:S(2)}, u32[]{:S(2)}) collective-permute-start(f32[1024,128]{1,0:T(8,128)S(1)} %copy-done.1), channel_id=1, source_target_pairs={{0,1},{1,0},{2,3},{3,2}} | collective-permute-start | bytes 1572872 | tf_op jit(solution)/shard_map/ppermute | solution.py:174
  6.5 28.5 %collective-permute-start.2 = (f32[256,512]{1,0:T(8,128)}, f32[256,512]{1,0:T(8,128)}, u32[]{:S(2)}, u32[]{:S(2)}) collective-permute-start(f32[256,512]{1,0:T(8,128)} %get-tuple-element.35), channel_id=1, source_target_pairs={{8,10},{9,11},{10,8},{11,9},{16,18},{17,19},{18,16},{19,17},{24,26... | collective-permute-start | bytes 1572872 | tf_op jit(solution)/shard_map/ppermute | solution.py:174
  11.1 27.0 %copy-start.2 = (f32[256,256]{1,0:T(8,128)}, f32[256,256]{1,0:T(8,128)S(1)}, u32[]{:S(2)}) copy-start(f32[256,256]{1,0:T(8,128)S(1)} %get-tuple-element.25) | copy-start | bytes 786436
  34.9 1.4 %collective-permute-start.5 = (f32[256,256]{1,0:T(8,128)S(1)}, f32[256,256]{1,0:T(8,128)S(1)}, u32[]{:S(2)}, u32[]{:S(2)}) collective-permute-start(f32[256,256]{1,0:T(8,128)S(1)} %get-tuple-element.25), channel_id=1, source_target_pairs={{0,4},{1,5},{2,6},{3,7}} | collective-permute-start | bytes 786440 | tf_op jit(solution)/shard_map/ppermute | solution.py:182
  35.6 2.4 %collective-permute-start.4 = (f32[512,256]{1,0:T(8,128)S(1)}, f32[512,256]{1,0:T(8,128)S(1)}, u32[]{:S(2)}, u32[]{:S(2)}) collective-permute-start(f32[512,256]{1,0:T(8,128)S(1)} %get-tuple-element.26.sent), channel_id=1, source_target_pairs={{0,1},{1,0},{2,3},{3,2}} | collective-permute-start | bytes 1572872 | tf_op jit(solution)/shard_map/ppermute | solution.py:174
  36.3 13.3 %collective-permute-start.9 = (f32[256,1024]{1,0:T(8,128)S(1)}, f32[256,1024]{1,0:T(8,128)}, u32[]{:S(2)}, u32[]{:S(2)}) collective-permute-start(f32[256,1024]{1,0:T(8,128)S(1)} %bitcast.11), channel_id=1, source_target_pairs={{4,6},{5,7},{6,4},{7,5}} | collective-permute-start | bytes 3145736 | tf_op jit(solution)/shard_map/ppermute | solution.py:174
  38.0 4.6 %collective-permute-start.6 = (f32[256,256]{1,0:T(8,128)S(1)}, f32[256,256]{1,0:T(8,128)S(1)}, u32[]{:S(2)}, u32[]{:S(2)}) collective-permute-start(f32[256,256]{1,0:T(8,128)S(1)} %shard_map.38), channel_id=1, source_target_pairs={{0,28},{1,29},{2,30},{3,31},{4,24},{5,25},{6,26},{7,27}} | collective-permute-start | bytes 786440 | tf_op jit(solution)/shard_map/ppermute | solution.py:182
  38.7 10.8 %collective-permute-start.7 = (f32[256,256]{1,0:T(8,128)S(1)}, f32[256,256]{1,0:T(8,128)S(1)}, u32[]{:S(2)}, u32[]{:S(2)}) collective-permute-start(f32[256,256]{1,0:T(8,128)S(1)} %shard_map.38), channel_id=1, source_target_pairs={{0,12},{1,13},{2,14},{3,15},{4,8},{5,9},{6,10},{7,11}} | collective-permute-start | bytes 786440 | tf_op jit(solution)/shard_map/ppermute | solution.py:182
  40.0 9.5 %collective-permute-start.8 = (f32[256,256]{1,0:T(8,128)S(1)}, f32[256,256]{1,0:T(8,128)S(1)}, u32[]{:S(2)}, u32[]{:S(2)}) collective-permute-start(f32[256,256]{1,0:T(8,128)S(1)} %shard_map.38), channel_id=1, source_target_pairs={{0,20},{1,21},{2,22},{3,23},{4,16},{5,17},{6,18},{7,19}} | collective-permute-start | bytes 786440 | tf_op jit(solution)/shard_map/ppermute | solution.py:182
  40.7 17.3 %collective-permute-start.12 = (f32[256,512]{1,0:T(8,128)}, f32[256,512]{1,0:T(8,128)S(1)}, u32[]{:S(2)}, u32[]{:S(2)}) collective-permute-start(f32[256,512]{1,0:T(8,128)} %get-tuple-element.32), channel_id=1, source_target_pairs={{8,10},{9,11},{10,8},{11,9},{16,18},{17,19},{18,16},{19,17},{24,26... | collective-permute-start | bytes 1572872 | tf_op jit(solution)/shard_map/ppermute | solution.py:174
  49.6 13.7 %copy-start.3 = (f32[256,256]{1,0:T(8,128)S(1)}, f32[256,256]{1,0:T(8,128)}, u32[]{:S(2)}) copy-start(f32[256,256]{1,0:T(8,128)} %copy-done.2) | copy-start | bytes 786436
  49.6 8.4 %collective-permute-start.11 = (f32[256,256]{1,0:T(8,128)S(1)}, f32[256,256]{1,0:T(8,128)S(1)}, u32[]{:S(2)}, u32[]{:S(2)}) collective-permute-start(f32[256,256]{1,0:T(8,128)S(1)} %select_select_fusion.held), channel_id=1, source_target_pairs={{0,4},{1,5},{2,6},{3,7},{4,0},{5,1},{6,2},{7,3},{8,12},{9,13},{10,... | collective-permute-start | bytes 786440 | tf_op jit(solution)/shard_map/ppermute | solution.py:209
  61.4 15.0 %collective-permute-start.13 = (f32[1024,128]{1,0:T(8,128)}, f32[1024,128]{1,0:T(8,128)S(1)}, u32[]{:S(2)}, u32[]{:S(2)}) collective-permute-start(f32[1024,128]{1,0:T(8,128)} %get-tuple-element.34), channel_id=1, source_target_pairs={{4,5},{5,4},{6,7},{7,6},{8,9},{9,8},{10,11},{11,10},{12,13},{13,12... | collective-permute-start | bytes 1572872 | tf_op jit(solution)/shard_map/ppermute | solution.py:174
  63.4 0.7 collective-permute-start.10

commit v22 on v19

--- a/solution.py
+++ b/solution.py
@@ -199,7 +199,7 @@
     def spread(array, row_id, low, radix, have):
         digit = (row_id // low) % radix
         result = array
-        for step in (2, 1, 3) if radix == 4 else range(1, radix):
+        for step in (2, 3, 1) if radix == 4 else range(1, radix):
             result = jnp.where(digit == step, send_down(array, step * low, have), result)
         return result, [target(row, step * low) for row in have for step in range(radix)]
 

time: 77.7 us -> 77.6 us (level)
  the two profiles are of different devices: /device:TPU:2 before, /device:TPU:6 now
where the time goes in v22:
time: 77.6 us; the launch traced here: 77.2 us
  waiting for transfers between devices  44.4 us (57%)
  starting transfers between devices  25.6 us (33%)
  Pallas kernels  3.54 us (5%)
  local copies, waits for them, and re-layouts  2.34 us (3%)
  other arithmetic  0.99 us (1%)
    ppermute x9, waiting for transfers between devices, swap(): return lax.ppermute(array, AXES, pairs)  38.5 us
    ppermute x9, starting transfers between devices, swap(): return lax.ppermute(array, AXES, pairs)  15.4 us
    ppermute x1, starting transfers between devices, swap_cores(): return lax.ppermute(array, AXES, pairs)  6.9 us
    ppermute x4, waiting for transfers between devices, send_down(): return lax.ppermute(array, AXES, pairs)  5.81 us
    pallas_call x4, Pallas kernels, call(): pl.pallas_call(kernel, out_shape=[jax.ShapeDtypeStruct(shape, jnp.float32...  3.54 us
    ppermute x4, starting transfers between devices, send_down(): return lax.ppermute(array, AXES, pairs)  3.31 us
  transfers between devices with their start and end apart: 14, of which 4 were waited for; matrix products, arithmetic and copies ran while one was open for 3% of the time, Pallas kernels for 0%

profile of v22, /device:TPU:6, one launch (start us, length us, event | category | flops | bytes accessed | tf_op | source)
XLA Modules:
  0.0 77.2 jit_solution(560248219474397023)
XLA Ops:
  0.0 0.0 copy-start.4
  0.0 1.8 %collective-permute-start.3 = (f32[256,1024]{1,0:T(8,128)}, f32[256,1024]{1,0:T(8,128)}, u32[]{:S(2)}, u32[]{:S(2)}) collective-permute-start(f32[256,1024]{1,0:T(8,128)} %bitcast.9), channel_id=1, source_target_pairs={{12,14},{13,15},{14,12},{15,13},{20,22},{21,23},{22,20},{23,21},{2... | collective-permute-start | bytes 3145736 | tf_op jit(solution)/shard_map/ppermute | solution.py:186
  1.8 1.0 %slice_bitcast_fusion.1 = f32[128,512]{1,0:T(8,128)S(1)} fusion(f32[2,128,1024]{2,1,0:T(8,128)} %param.4), kind=kLoop, calls=%fused_computation.4 | loop fusion | bytes 524288 | tf_op jit(solution)/shard_map/squeeze | solution.py:242
  2.8 0.0 copy-done.4
  2.8 0.0 copy-start
  2.8 0.0 copy-start.1
  2.8 0.1 pad_maximum_fusion.lead
  2.9 0.8 %collective-permute-start = (f32[128,1536]{1,0:T(8,128)S(1)}, f32[128,1536]{1,0:T(8,128)S(1)}, u32[]{:S(2)}, u32[]{:S(2)}) collective-permute-start(f32[128,1536]{1,0:T(8,128)S(1)} %pad_maximum_fusion.lead), channel_id=1, source_target_pairs={{0,2},{1,3},{2,0},{3,1}} | collective-permute-start | bytes 2359304 | tf_op jit(solution)/shard_map/ppermute | solution.py:186
  3.8 0.2 copy-done.1
  4.0 1.4 %collective-permute-start.1 = (f32[1024,128]{1,0:T(8,128)S(1)}, f32[1024,128]{1,0:T(8,128)}, u32[]{:S(2)}, u32[]{:S(2)}) collective-permute-start(f32[1024,128]{1,0:T(8,128)S(1)} %copy-done.1), channel_id=1, source_target_pairs={{0,1},{1,0},{2,3},{3,2}} | collective-permute-start | bytes 1572872 | tf_op jit(solution)/shard_map/ppermute | solution.py:186
  5.4 0.0 copy-done
  5.4 1.1 %fusion = (f32[256,512]{1,0:T(8,128)}, f32[256,512]{1,0:T(8,128)}) fusion(f32[256,1024]{1,0:T(8,128)S(1)} %bitcast.10), kind=kLoop, calls=%fused_computation.8 | loop fusion | bytes 2097152 | tf_op jit(solution)/shard_map/slice | solution.py:248
  6.5 4.5 %collective-permute-start.2 = (f32[256,512]{1,0:T(8,128)}, f32[256,512]{1,0:T(8,128)}, u32[]{:S(2)}, u32[]{:S(2)}) collective-permute-start(f32[256,512]{1,0:T(8,128)} %get-tuple-element.35), channel_id=1, source_target_pairs={{8,10},{9,11},{10,8},{11,9},{16,18},{17,19},{18,16},{19,17},{24,26... | collective-permute-start | bytes 1572872 | tf_op jit(solution)/shard_map/ppermute | solution.py:186
  11.0 0.0 collective-permute-done.far_lead
  11.0 0.0 collective-permute-done.1.refs_0_
  11.0 0.1 shard_map.37
  11.1 0.0 copy-start.2
  11.1 23.9 %collective-permute-done.2.early = f32[256,512]{1,0:T(8,128)} collective-permute-done((f32[256,512]{1,0:T(8,128)}, f32[256,512]{1,0:T(8,128)}, u32[]{:S(2)}, u32[]{:S(2)}) %collective-permute-start.2) | collective-permute-done | bytes 524320 | tf_op jit(solution)/shard_map/ppermute | solution.py:186
  34.9 0.0 collective-permute-done.3.whole
  34.9 0.7 collective-permute-start.5
  35.6 0.7 collective-permute-start.4
  36.3 0.0 collective-permute-done.5.first
  36.3 1.6 %collective-permute-start.9 = (f32[256,1024]{1,0:T(8,128)S(1)}, f32[256,1024]{1,0:T(8,128)}, u32[]{:S(2)}, u32[]{:S(2)}) collective-permute-start(f32[256,1024]{1,0:T(8,128)S(1)} %bitcast.11), channel_id=1, source_target_pairs={{4,6},{5,7},{6,4},{7,5}} | collective-permute-start | bytes 3145736 | tf_op jit(solution)/shard_map/ppermute | solution.py:186
  38.0 0.0 collective-permute-done.4.got
  38.0 0.1 shard_map.38
  38.0 0.0 copy-done.2
  38.0 0.7 collective-permute-start.6
  38.7 1.3 %collective-permute-start.7 = (f32[256,256]{1,0:T(8,128)S(1)}, f32[256,256]{1,0:T(8,128)S(1)}, u32[]{:S(2)}, u32[]{:S(2)}) collective-permute-start(f32[256,256]{1,0:T(8,128)S(1)} %shard_map.38), channel_id=1, source_target_pairs={{0,28},{1,29},{2,30},{3,31},{4,24},{5,25},{6,26},{7,27}} | collective-permute-start | bytes 786440 | tf_op jit(solution)/shard_map/ppermute | solution.py:194
  40.0 0.7 collective-permute-start.8
  40.7 1.9 %collective-permute-start.12 = (f32[256,512]{1,0:T(8,128)}, f32[256,512]{1,0:T(8,128)S(1)}, u32[]{:S(2)}, u32[]{:S(2)}) collective-permute-start(f32[256,512]{1,0:T(8,128)} %get-tuple-element.32), channel_id=1, source_target_pairs={{8,10},{9,11},{10,8},{11,9},{16,18},{17,19},{18,16},{19,17},{24,26... | collective-permute-start | bytes 1572872 | tf_op jit(solution)/shard_map/ppermute | solution.py:186
  42.7 0.0 collective-permute-done.6
  42.7 5.8 %collective-permute-done.7 = f32[256,256]{1,0:T(8,128)S(1)} collective-permute-done((f32[256,256]{1,0:T(8,128)S(1)}, f32[256,256]{1,0:T(8,128)S(1)}, u32[]{:S(2)}, u32[]{:S(2)}) %collective-permute-start.7) | collective-permute-done | bytes 262176 | tf_op jit(solution)/shard_map/ppermute | solution.py:194
  48.5 0.0 collective-permute-done.8
  48.5 0.1 select_select_fusion.held
  48.5 0.0 copy-start.3
  48.6 0.0 collective-permute-done.9.beside
  48.6 6.9 %collective-permute-start.11 = (f32[256,256]{1,0:T(8,128)S(1)}, f32[256,256]{1,0:T(8,128)S(1)}, u32[]{:S(2)}, u32[]{:S(2)}) collective-permute-start(f32[256,256]{1,0:T(8,128)S(1)} %select_select_fusion.held), channel_id=1, source_target_pairs={{0,4},{1,5},{2,6},{3,7},{4,0},{5,1},{6,2},{7,3},{8,12},{9,13},{10,... | collective-permute-start | bytes 786440 | tf_op jit(solution)/shard_map/ppermute | solution.py:221
  55.5 2.5 %collective-permute-done.12.tail = f32[256,512]{1,0:T(8,128)S(1)} collective-permute-done((f32[256,512]{1,0:T(8,128)}, f32[256,512]{1,0:T(8,128)S(1)}, u32[]{:S(2)}, u32[]{:S(2)}) %collective-permute-start.12) | collective-permute-done | bytes 524320 | tf_op jit(solution)/shard_map/ppermute | solution.py:186
  58.0 0.0 collective-permute-done.11.got
  58.0 3.4 %shard_map.40 = (f32[1024,128]{1,0:T(8,128)S(1)}, f32[1024,128]{1,0:T(8,128)}) custom-call(s32[1]{0:T(128)} %bitcast.1.row, f32[256,256]{1,0:T(8,128)S(1)} %select_select_fusion.held, f32[256,256]{1,0:T(8,128)S(1)} %collective-permute-done.11.got, f32[256,1024]{1,0:T(8,128)S(1)} %bitcast.12, f32[256,1024]{1,0:T(8,128)} %collective-permute-done.3.whole, ...), custom_call_target="tpu_custom_call" | custom-call | flops 805306368 | tf_op jit(solution)/shard_map/pallas_call | solution.py:32
  61.4 1.9 %collective-permute-start.13 = (f32[1024,128]{1,0:T(8,128)}, f32[1024,128]{1,0:T(8,128)S(1)}, u32[]{:S(2)}, u32[]{:S(2)}) collective-permute-start(f32[1024,128]{1,0:T(8,128)} %get-tuple-element.34), channel_id=1, source_target_pairs={{4,5},{5,4},{6,7},{7,6},{8,9},{9,8},{10,11},{11,10},{12,13},{13,12... | collective-permute-start | bytes 1572872 | tf_op jit(solution)/shard_map/ppermute | solution.py:186
  63.3 0.0 copy-done.3
  63.4 0.7 collective-permute-start.10
  64.1 0.0 collective-permute-done.10.refs_0_
  64.1 0.1 shard_map.39
  64.2 12.1 %collective-permute-done.13 = f32[1024,128]{1,0:T(8,128)S(1)} collective-permute-done((f32[1024,128]{1,0:T(8,128)}, f32[1024,128]{1,0:T(8,128)S(1)}, u32[]{:S(2)}, u32[]{:S(2)}) %collective-permute-start.13) | collective-permute-done | bytes 524320 | tf_op jit(solution)/shard_map/ppermute | solution.py:186
  76.3 0.9 %subtract_select_fusion = f32[1024,128]{1,0:T(8,128)} fusion(f32[1024,128]{1,0:T(8,128)S(1)} %shard_map.39, f32[1024,128]{1,0:T(8,128)S(1)} %get-tuple-element.33, f32[1024,128]{1,0:T(8,128)S(1)} %collective-permute-done.13, pred[]{:T(512)S(6)} %eq.14), kind=kLoop, calls=%fused_computation.1 | loop fusion | flops 262144 | bytes 2097153 | tf_op jit(solution)/shard_map/jit(_where)/select_n | solution.py:310
  (4 shorter events, 0.1 us)
Async XLA Ops:
  0.0 2.8 %copy-start.4 = (f32[2,128,512]{2,1,0:T(8,128)S(1)}, f32[2,128,512]{2,1,0:T(8,128)}, u32[]{:S(2)}) copy-start(f32[2,128,512]{2,1,0:T(8,128)} %param.5) | copy-start | bytes 1572868
  0.0 34.9 %collective-permute-start.3 = (f32[256,1024]{1,0:T(8,128)}, f32[256,1024]{1,0:T(8,128)}, u32[]{:S(2)}, u32[]{:S(2)}) collective-permute-start(f32[256,1024]{1,0:T(8,128)} %bitcast.9), channel_id=1, source_target_pairs={{12,14},{13,15},{14,12},{15,13},{20,22},{21,23},{22,20},{23,21},{2... | collective-permute-start | bytes 3145736 | tf_op jit(solution)/shard_map/ppermute | solution.py:186
  2.8 2.6 %copy-start = (f32[2,128,1024]{2,1,0:T(8,128)S(1)}, f32[2,128,1024]{2,1,0:T(8,128)}, u32[]{:S(2)}) copy-start(f32[2,128,1024]{2,1,0:T(8,128)} %param.4) | copy-start | bytes 3145732
  2.8 1.1 %copy-start.1 = (f32[1024,128]{1,0:T(8,128)S(1)}, f32[1024,128]{1,0:T(8,128)}, u32[]{:S(2)}) copy-start(f32[1024,128]{1,0:T(8,128)} %cross.1) | copy-start | bytes 1572868
  2.9 8.1 %collective-permute-start = (f32[128,1536]{1,0:T(8,128)S(1)}, f32[128,1536]{1,0:T(8,128)S(1)}, u32[]{:S(2)}, u32[]{:S(2)}) collective-permute-start(f32[128,1536]{1,0:T(8,128)S(1)} %pad_maximum_fusion.lead), channel_id=1, source_target_pairs={{0,2},{1,3},{2,0},{3,1}} | collective-permute-start | bytes 2359304 | tf_op jit(solution)/shard_map/ppermute | solution.py:186
  4.0 7.0 %collective-permute-start.1 = (f32[1024,128]{1,0:T(8,128)S(1)}, f32[1024,128]{1,0:T(8,128)}, u32[]{:S(2)}, u32[]{:S(2)}) collective-permute-start(f32[1024,128]{1,0:T(8,128)S(1)} %copy-done.1), channel_id=1, source_target_pairs={{0,1},{1,0},{2,3},{3,2}} | collective-permute-start | bytes 1572872 | tf_op jit(solution)/shard_map/ppermute | solution.py:186
  6.5 28.5 %collective-permute-start.2 = (f32[256,512]{1,0:T(8,128)}, f32[256,512]{1,0:T(8,128)}, u32[]{:S(2)}, u32[]{:S(2)}) collective-permute-start(f32[256,512]{1,0:T(8,128)} %get-tuple-element.35), channel_id=1, source_target_pairs={{8,10},{9,11},{10,8},{11,9},{16,18},{17,19},{18,16},{19,17},{24,26... | collective-permute-start | bytes 1572872 | tf_op jit(solution)/shard_map/ppermute | solution.py:186
  11.1 27.0 %copy-start.2 = (f32[256,256]{1,0:T(8,128)}, f32[256,256]{1,0:T(8,128)S(1)}, u32[]{:S(2)}) copy-start(f32[256,256]{1,0:T(8,128)S(1)} %get-tuple-element.25) | copy-start | bytes 786436
  34.9 1.4 %collective-permute-start.5 = (f32[256,256]{1,0:T(8,128)S(1)}, f32[256,256]{1,0:T(8,128)S(1)}, u32[]{:S(2)}, u32[]{:S(2)}) collective-permute-start(f32[256,256]{1,0:T(8,128)S(1)} %get-tuple-element.25), channel_id=1, source_target_pairs={{0,4},{1,5},{2,6},{3,7}} | collective-permute-start | bytes 786440 | tf_op jit(solution)/shard_map/ppermute | solution.py:194
  35.6 2.4 %collective-permute-start.4 = (f32[512,256]{1,0:T(8,128)S(1)}, f32[512,256]{1,0:T(8,128)S(1)}, u32[]{:S(2)}, u32[]{:S(2)}) collective-permute-start(f32[512,256]{1,0:T(8,128)S(1)} %get-tuple-element.26.sent), channel_id=1, source_target_pairs={{0,1},{1,0},{2,3},{3,2}} | collective-permute-start | bytes 1572872 | tf_op jit(solution)/shard_map/ppermute | solution.py:186
  36.3 12.2 %collective-permute-start.9 = (f32[256,1024]{1,0:T(8,128)S(1)}, f32[256,1024]{1,0:T(8,128)}, u32[]{:S(2)}, u32[]{:S(2)}) collective-permute-start(f32[256,1024]{1,0:T(8,128)S(1)} %bitcast.11), channel_id=1, source_target_pairs={{4,6},{5,7},{6,4},{7,5}} | collective-permute-start | bytes 3145736 | tf_op jit(solution)/shard_map/ppermute | solution.py:186
  38.0 4.6 %collective-permute-start.6 = (f32[256,256]{1,0:T(8,128)S(1)}, f32[256,256]{1,0:T(8,128)S(1)}, u32[]{:S(2)}, u32[]{:S(2)}) collective-permute-start(f32[256,256]{1,0:T(8,128)S(1)} %shard_map.38), channel_id=1, source_target_pairs={{0,12},{1,13},{2,14},{3,15},{4,8},{5,9},{6,10},{7,11}} | collective-permute-start | bytes 786440 | tf_op jit(solution)/shard_map/ppermute | solution.py:194
  38.7 9.8 %collective-permute-start.7 = (f32[256,256]{1,0:T(8,128)S(1)}, f32[256,256]{1,0:T(8,128)S(1)}, u32[]{:S(2)}, u32[]{:S(2)}) collective-permute-start(f32[256,256]{1,0:T(8,128)S(1)} %shard_map.38), channel_id=1, source_target_pairs={{0,28},{1,29},{2,30},{3,31},{4,24},{5,25},{6,26},{7,27}} | collective-permute-start | bytes 786440 | tf_op jit(solution)/shard_map/ppermute | solution.py:194
  40.0 8.5 %collective-permute-start.8 = (f32[256,256]{1,0:T(8,128)S(1)}, f32[256,256]{1,0:T(8,128)S(1)}, u32[]{:S(2)}, u32[]{:S(2)}) collective-permute-start(f32[256,256]{1,0:T(8,128)S(1)} %shard_map.38), channel_id=1, source_target_pairs={{0,20},{1,21},{2,22},{3,23},{4,16},{5,17},{6,18},{7,19}} | collective-permute-start | bytes 786440 | tf_op jit(solution)/shard_map/ppermute | solution.py:194
  40.7 17.3 %collective-permute-start.12 = (f32[256,512]{1,0:T(8,128)}, f32[256,512]{1,0:T(8,128)S(1)}, u32[]{:S(2)}, u32[]{:S(2)}) collective-permute-start(f32[256,512]{1,0:T(8,128)} %get-tuple-element.32), channel_id=1, source_target_pairs={{8,10},{9,11},{10,8},{11,9},{16,18},{17,19},{18,16},{19,17},{24,26... | collective-permute-start | bytes 1572872 | tf_op jit(solution)/shard_map/ppermute | solution.py:186
  48.5 14.8 %copy-start.3 = (f32[256,256]{1,0:T(8,128)S(1)}, f32[256,256]{1,0:T(8,128)}, u32[]{:S(2)}) copy-start(f32[256,256]{1,0:T(8,128)} %copy-done.2) | copy-start | bytes 786436
  48.6 9.4 %collective-permute-start.11 = (f32[256,256]{1,0:T(8,128)S(1)}, f32[256,256]{1,0:T(8,128)S(1)}, u32[]{:S(2)}, u32[]{:S(2)}) collective-permute-start(f32[256,256]{1,0:T(8,128)S(1)} %select_select_fusion.held), channel_id=1, source_target_pairs={{0,4},{1,5},{2,6},{3,7},{4,0},{5,1},{6,2},{7,3},{8,12},{9,13},{10,... | collective-permute-start | bytes 786440 | tf_op jit(solution)/shard_map/ppermute | solution.py:221
  61.4 14.9 %collective-permute-start.13 = (f32[1024,128]{1,0:T(8,128)}, f32[1024,128]{1,0:T(8,128)S(1)}, u32[]{:S(2)}, u32[]{:S(2)}) collective-permute-start(f32[1024,128]{1,0:T(8,128)} %get-tuple-element.34), channel_id=1, source_target_pairs={{4,5},{5,4},{6,7},{7,6},{8,9},{9,8},{10,11},{11,10},{12,13},{13,12... | collective-permute-start | bytes 1572872 | tf_op jit(solution)/shard_map/ppermute | solution.py:186
  63.4 0.7 collective-permute-start.10

commit v23 on v19

--- a/solution.py
+++ b/solution.py
@@ -23,7 +23,9 @@
 
     left_high, left_low = split(left)
     right_high, right_low = split(right)
-    return one(left_high, right_high) + (one(left_high, right_low) + one(left_low, right_high))
+    both = one(jnp.concatenate([left_high, left_low], axis=1 - left_dim), right_high)
+    count = both.shape[0] // 2
+    return both[:count] + (one(left_high, right_low) + both[count:])
 
 
 def call(kernel, shapes, flops, near, far=(), flag=None, scratch=()):

time: 77.7 us -> 77.6 us (level)
  no operation moved by 1% of the time
where the time goes in v23:
time: 77.6 us; the launch traced here: 77.2 us
  waiting for transfers between devices  45.4 us (59%)
  starting transfers between devices  24.7 us (32%)
  Pallas kernels  3.52 us (5%)
  local copies, waits for them, and re-layouts  2.34 us (3%)
  other arithmetic  0.99 us (1%)
    ppermute x9, waiting for transfers between devices, swap(): return lax.ppermute(array, AXES, pairs)  38.5 us
    ppermute x9, starting transfers between devices, swap(): return lax.ppermute(array, AXES, pairs)  15.4 us
    ppermute x4, waiting for transfers between devices, send_down(): return lax.ppermute(array, AXES, pairs)  6.82 us
    ppermute x1, starting transfers between devices, swap_cores(): return lax.ppermute(array, AXES, pairs)  5.92 us
    pallas_call x4, Pallas kernels, call(): pl.pallas_call(kernel, out_shape=[jax.ShapeDtypeStruct(shape, jnp.float32...  3.52 us
    ppermute x4, starting transfers between devices, send_down(): return lax.ppermute(array, AXES, pairs)  3.31 us
  transfers between devices with their start and end apart: 14, of which 4 were waited for; matrix products, arithmetic and copies ran while one was open for 3% of the time, Pallas kernels for 0%

profile of v23, /device:TPU:2, one launch (start us, length us, event | category | flops | bytes accessed | tf_op | source)
XLA Modules:
  0.0 77.2 jit_solution(12919690505240313140)
XLA Ops:
  0.0 0.0 copy-start.4
  0.0 1.8 %collective-permute-start.3 = (f32[256,1024]{1,0:T(8,128)}, f32[256,1024]{1,0:T(8,128)}, u32[]{:S(2)}, u32[]{:S(2)}) collective-permute-start(f32[256,1024]{1,0:T(8,128)} %bitcast.9), channel_id=1, source_target_pairs={{12,14},{13,15},{14,12},{15,13},{20,22},{21,23},{22,20},{23,21},{2... | collective-permute-start | bytes 3145736 | tf_op jit(solution)/shard_map/ppermute | solution.py:188
  1.8 1.0 %slice_bitcast_fusion.1 = f32[128,512]{1,0:T(8,128)S(1)} fusion(f32[2,128,1024]{2,1,0:T(8,128)} %param.4), kind=kLoop, calls=%fused_computation.4 | loop fusion | bytes 524288 | tf_op jit(solution)/shard_map/squeeze | solution.py:244
  2.8 0.0 copy-done.4
  2.8 0.0 copy-start
  2.8 0.0 copy-start.1
  2.8 0.1 pad_maximum_fusion.lead
  2.9 0.8 %collective-permute-start = (f32[128,1536]{1,0:T(8,128)S(1)}, f32[128,1536]{1,0:T(8,128)S(1)}, u32[]{:S(2)}, u32[]{:S(2)}) collective-permute-start(f32[128,1536]{1,0:T(8,128)S(1)} %pad_maximum_fusion.lead), channel_id=1, source_target_pairs={{0,2},{1,3},{2,0},{3,1}} | collective-permute-start | bytes 2359304 | tf_op jit(solution)/shard_map/ppermute | solution.py:188
  3.8 0.2 copy-done.1
  4.0 1.4 %collective-permute-start.1 = (f32[1024,128]{1,0:T(8,128)S(1)}, f32[1024,128]{1,0:T(8,128)}, u32[]{:S(2)}, u32[]{:S(2)}) collective-permute-start(f32[1024,128]{1,0:T(8,128)S(1)} %copy-done.1), channel_id=1, source_target_pairs={{0,1},{1,0},{2,3},{3,2}} | collective-permute-start | bytes 1572872 | tf_op jit(solution)/shard_map/ppermute | solution.py:188
  5.4 0.0 copy-done
  5.4 1.1 %fusion = (f32[256,512]{1,0:T(8,128)}, f32[256,512]{1,0:T(8,128)}) fusion(f32[256,1024]{1,0:T(8,128)S(1)} %bitcast.10), kind=kLoop, calls=%fused_computation.8 | loop fusion | bytes 2097152 | tf_op jit(solution)/shard_map/slice | solution.py:250
  6.5 4.5 %collective-permute-start.2 = (f32[256,512]{1,0:T(8,128)}, f32[256,512]{1,0:T(8,128)}, u32[]{:S(2)}, u32[]{:S(2)}) collective-permute-start(f32[256,512]{1,0:T(8,128)} %get-tuple-element.35), channel_id=1, source_target_pairs={{8,10},{9,11},{10,8},{11,9},{16,18},{17,19},{18,16},{19,17},{24,26... | collective-permute-start | bytes 1572872 | tf_op jit(solution)/shard_map/ppermute | solution.py:188
  11.0 0.0 collective-permute-done.far_lead
  11.0 0.0 collective-permute-done.1.refs_0_
  11.0 0.1 shard_map.37
  11.1 0.0 copy-start.2
  11.1 23.9 %collective-permute-done.2.early = f32[256,512]{1,0:T(8,128)} collective-permute-done((f32[256,512]{1,0:T(8,128)}, f32[256,512]{1,0:T(8,128)}, u32[]{:S(2)}, u32[]{:S(2)}) %collective-permute-start.2) | collective-permute-done | bytes 524320 | tf_op jit(solution)/shard_map/ppermute | solution.py:188
  34.9 0.0 collective-permute-done.3.whole
  34.9 0.7 collective-permute-start.5
  35.6 0.7 collective-permute-start.4
  36.3 0.0 collective-permute-done.5.first
  36.3 1.6 %collective-permute-start.9 = (f32[256,1024]{1,0:T(8,128)S(1)}, f32[256,1024]{1,0:T(8,128)}, u32[]{:S(2)}, u32[]{:S(2)}) collective-permute-start(f32[256,1024]{1,0:T(8,128)S(1)} %bitcast.11), channel_id=1, source_target_pairs={{4,6},{5,7},{6,4},{7,5}} | collective-permute-start | bytes 3145736 | tf_op jit(solution)/shard_map/ppermute | solution.py:188
  38.0 0.0 collective-permute-done.4.got
  38.0 0.1 shard_map.38
  38.0 0.0 copy-done.2
  38.0 0.7 collective-permute-start.6
  38.7 1.3 %collective-permute-start.7 = (f32[256,256]{1,0:T(8,128)S(1)}, f32[256,256]{1,0:T(8,128)S(1)}, u32[]{:S(2)}, u32[]{:S(2)}) collective-permute-start(f32[256,256]{1,0:T(8,128)S(1)} %shard_map.38), channel_id=1, source_target_pairs={{0,12},{1,13},{2,14},{3,15},{4,8},{5,9},{6,10},{7,11}} | collective-permute-start | bytes 786440 | tf_op jit(solution)/shard_map/ppermute | solution.py:196
  40.0 0.7 collective-permute-start.8
  40.7 1.9 %collective-permute-start.12 = (f32[256,512]{1,0:T(8,128)}, f32[256,512]{1,0:T(8,128)S(1)}, u32[]{:S(2)}, u32[]{:S(2)}) collective-permute-start(f32[256,512]{1,0:T(8,128)} %get-tuple-element.32), channel_id=1, source_target_pairs={{8,10},{9,11},{10,8},{11,9},{16,18},{17,19},{18,16},{19,17},{24,26... | collective-permute-start | bytes 1572872 | tf_op jit(solution)/shard_map/ppermute | solution.py:188
  42.7 0.0 collective-permute-done.6
  42.7 6.8 %collective-permute-done.7 = f32[256,256]{1,0:T(8,128)S(1)} collective-permute-done((f32[256,256]{1,0:T(8,128)S(1)}, f32[256,256]{1,0:T(8,128)S(1)}, u32[]{:S(2)}, u32[]{:S(2)}) %collective-permute-start.7) | collective-permute-done | bytes 262176 | tf_op jit(solution)/shard_map/ppermute | solution.py:196
  49.5 0.0 collective-permute-done.8
  49.5 0.1 select_select_fusion.held
  49.6 0.0 copy-start.3
  49.6 0.0 collective-permute-done.9.beside
  49.6 5.9 %collective-permute-start.11 = (f32[256,256]{1,0:T(8,128)S(1)}, f32[256,256]{1,0:T(8,128)S(1)}, u32[]{:S(2)}, u32[]{:S(2)}) collective-permute-start(f32[256,256]{1,0:T(8,128)S(1)} %select_select_fusion.held), channel_id=1, source_target_pairs={{0,4},{1,5},{2,6},{3,7},{4,0},{5,1},{6,2},{7,3},{8,12},{9,13},{10,... | collective-permute-start | bytes 786440 | tf_op jit(solution)/shard_map/ppermute | solution.py:223
  55.5 2.5 %collective-permute-done.12.tail = f32[256,512]{1,0:T(8,128)S(1)} collective-permute-done((f32[256,512]{1,0:T(8,128)}, f32[256,512]{1,0:T(8,128)S(1)}, u32[]{:S(2)}, u32[]{:S(2)}) %collective-permute-start.12) | collective-permute-done | bytes 524320 | tf_op jit(solution)/shard_map/ppermute | solution.py:188
  58.0 0.0 collective-permute-done.11.got
  58.0 3.3 %shard_map.40 = (f32[1024,128]{1,0:T(8,128)S(1)}, f32[1024,128]{1,0:T(8,128)}) custom-call(s32[1]{0:T(128)} %bitcast.1.row, f32[256,256]{1,0:T(8,128)S(1)} %select_select_fusion.held, f32[256,256]{1,0:T(8,128)S(1)} %collective-permute-done.11.got, f32[256,1024]{1,0:T(8,128)S(1)} %bitcast.12, f32[256,1024]{1,0:T(8,128)} %collective-permute-done.3.whole, ...), custom_call_target="tpu_custom_call" | custom-call | flops 805306368 | tf_op jit(solution)/shard_map/pallas_call | solution.py:34
  61.4 1.9 %collective-permute-start.13 = (f32[1024,128]{1,0:T(8,128)}, f32[1024,128]{1,0:T(8,128)S(1)}, u32[]{:S(2)}, u32[]{:S(2)}) collective-permute-start(f32[1024,128]{1,0:T(8,128)} %get-tuple-element.34), channel_id=1, source_target_pairs={{4,5},{5,4},{6,7},{7,6},{8,9},{9,8},{10,11},{11,10},{12,13},{13,12... | collective-permute-start | bytes 1572872 | tf_op jit(solution)/shard_map/ppermute | solution.py:188
  63.3 0.0 copy-done.3
  63.4 0.7 collective-permute-start.10
  64.1 0.0 collective-permute-done.10.refs_0_
  64.1 0.1 shard_map.39
  64.1 12.2 %collective-permute-done.13 = f32[1024,128]{1,0:T(8,128)S(1)} collective-permute-done((f32[1024,128]{1,0:T(8,128)}, f32[1024,128]{1,0:T(8,128)S(1)}, u32[]{:S(2)}, u32[]{:S(2)}) %collective-permute-start.13) | collective-permute-done | bytes 524320 | tf_op jit(solution)/shard_map/ppermute | solution.py:188
  76.3 0.9 %subtract_select_fusion = f32[1024,128]{1,0:T(8,128)} fusion(f32[1024,128]{1,0:T(8,128)S(1)} %shard_map.39, f32[1024,128]{1,0:T(8,128)S(1)} %get-tuple-element.33, f32[1024,128]{1,0:T(8,128)S(1)} %collective-permute-done.13, pred[]{:T(512)S(6)} %eq.14), kind=kLoop, calls=%fused_computation.1 | loop fusion | flops 262144 | bytes 2097153 | tf_op jit(solution)/shard_map/jit(_where)/select_n | solution.py:312
  (4 shorter events, 0.1 us)
Async XLA Ops:
  0.0 2.8 %copy-start.4 = (f32[2,128,512]{2,1,0:T(8,128)S(1)}, f32[2,128,512]{2,1,0:T(8,128)}, u32[]{:S(2)}) copy-start(f32[2,128,512]{2,1,0:T(8,128)} %param.5) | copy-start | bytes 1572868
  0.0 34.9 %collective-permute-start.3 = (f32[256,1024]{1,0:T(8,128)}, f32[256,1024]{1,0:T(8,128)}, u32[]{:S(2)}, u32[]{:S(2)}) collective-permute-start(f32[256,1024]{1,0:T(8,128)} %bitcast.9), channel_id=1, source_target_pairs={{12,14},{13,15},{14,12},{15,13},{20,22},{21,23},{22,20},{23,21},{2... | collective-permute-start | bytes 3145736 | tf_op jit(solution)/shard_map/ppermute | solution.py:188
  2.8 2.6 %copy-start = (f32[2,128,1024]{2,1,0:T(8,128)S(1)}, f32[2,128,1024]{2,1,0:T(8,128)}, u32[]{:S(2)}) copy-start(f32[2,128,1024]{2,1,0:T(8,128)} %param.4) | copy-start | bytes 3145732
  2.8 1.1 %copy-start.1 = (f32[1024,128]{1,0:T(8,128)S(1)}, f32[1024,128]{1,0:T(8,128)}, u32[]{:S(2)}) copy-start(f32[1024,128]{1,0:T(8,128)} %cross.1) | copy-start | bytes 1572868
  2.9 8.1 %collective-permute-start = (f32[128,1536]{1,0:T(8,128)S(1)}, f32[128,1536]{1,0:T(8,128)S(1)}, u32[]{:S(2)}, u32[]{:S(2)}) collective-permute-start(f32[128,1536]{1,0:T(8,128)S(1)} %pad_maximum_fusion.lead), channel_id=1, source_target_pairs={{0,2},{1,3},{2,0},{3,1}} | collective-permute-start | bytes 2359304 | tf_op jit(solution)/shard_map/ppermute | solution.py:188
  4.0 7.0 %collective-permute-start.1 = (f32[1024,128]{1,0:T(8,128)S(1)}, f32[1024,128]{1,0:T(8,128)}, u32[]{:S(2)}, u32[]{:S(2)}) collective-permute-start(f32[1024,128]{1,0:T(8,128)S(1)} %copy-done.1), channel_id=1, source_target_pairs={{0,1},{1,0},{2,3},{3,2}} | collective-permute-start | bytes 1572872 | tf_op jit(solution)/shard_map/ppermute | solution.py:188
  6.5 28.5 %collective-permute-start.2 = (f32[256,512]{1,0:T(8,128)}, f32[256,512]{1,0:T(8,128)}, u32[]{:S(2)}, u32[]{:S(2)}) collective-permute-start(f32[256,512]{1,0:T(8,128)} %get-tuple-element.35), channel_id=1, source_target_pairs={{8,10},{9,11},{10,8},{11,9},{16,18},{17,19},{18,16},{19,17},{24,26... | collective-permute-start | bytes 1572872 | tf_op jit(solution)/shard_map/ppermute | solution.py:188
  11.1 27.0 %copy-start.2 = (f32[256,256]{1,0:T(8,128)}, f32[256,256]{1,0:T(8,128)S(1)}, u32[]{:S(2)}) copy-start(f32[256,256]{1,0:T(8,128)S(1)} %get-tuple-element.25) | copy-start | bytes 786436
  34.9 1.4 %collective-permute-start.5 = (f32[256,256]{1,0:T(8,128)S(1)}, f32[256,256]{1,0:T(8,128)S(1)}, u32[]{:S(2)}, u32[]{:S(2)}) collective-permute-start(f32[256,256]{1,0:T(8,128)S(1)} %get-tuple-element.25), channel_id=1, source_target_pairs={{0,4},{1,5},{2,6},{3,7}} | collective-permute-start | bytes 786440 | tf_op jit(solution)/shard_map/ppermute | solution.py:196
  35.6 2.4 %collective-permute-start.4 = (f32[512,256]{1,0:T(8,128)S(1)}, f32[512,256]{1,0:T(8,128)S(1)}, u32[]{:S(2)}, u32[]{:S(2)}) collective-permute-start(f32[512,256]{1,0:T(8,128)S(1)} %get-tuple-element.26.sent), channel_id=1, source_target_pairs={{0,1},{1,0},{2,3},{3,2}} | collective-permute-start | bytes 1572872 | tf_op jit(solution)/shard_map/ppermute | solution.py:188
  36.3 13.3 %collective-permute-start.9 = (f32[256,1024]{1,0:T(8,128)S(1)}, f32[256,1024]{1,0:T(8,128)}, u32[]{:S(2)}, u32[]{:S(2)}) collective-permute-start(f32[256,1024]{1,0:T(8,128)S(1)} %bitcast.11), channel_id=1, source_target_pairs={{4,6},{5,7},{6,4},{7,5}} | collective-permute-start | bytes 3145736 | tf_op jit(solution)/shard_map/ppermute | solution.py:188
  38.0 4.6 %collective-permute-start.6 = (f32[256,256]{1,0:T(8,128)S(1)}, f32[256,256]{1,0:T(8,128)S(1)}, u32[]{:S(2)}, u32[]{:S(2)}) collective-permute-start(f32[256,256]{1,0:T(8,128)S(1)} %shard_map.38), channel_id=1, source_target_pairs={{0,28},{1,29},{2,30},{3,31},{4,24},{5,25},{6,26},{7,27}} | collective-permute-start | bytes 786440 | tf_op jit(solution)/shard_map/ppermute | solution.py:196
  38.7 10.8 %collective-permute-start.7 = (f32[256,256]{1,0:T(8,128)S(1)}, f32[256,256]{1,0:T(8,128)S(1)}, u32[]{:S(2)}, u32[]{:S(2)}) collective-permute-start(f32[256,256]{1,0:T(8,128)S(1)} %shard_map.38), channel_id=1, source_target_pairs={{0,12},{1,13},{2,14},{3,15},{4,8},{5,9},{6,10},{7,11}} | collective-permute-start | bytes 786440 | tf_op jit(solution)/shard_map/ppermute | solution.py:196
  40.0 9.5 %collective-permute-start.8 = (f32[256,256]{1,0:T(8,128)S(1)}, f32[256,256]{1,0:T(8,128)S(1)}, u32[]{:S(2)}, u32[]{:S(2)}) collective-permute-start(f32[256,256]{1,0:T(8,128)S(1)} %shard_map.38), channel_id=1, source_target_pairs={{0,20},{1,21},{2,22},{3,23},{4,16},{5,17},{6,18},{7,19}} | collective-permute-start | bytes 786440 | tf_op jit(solution)/shard_map/ppermute | solution.py:196
  40.7 17.3 %collective-permute-start.12 = (f32[256,512]{1,0:T(8,128)}, f32[256,512]{1,0:T(8,128)S(1)}, u32[]{:S(2)}, u32[]{:S(2)}) collective-permute-start(f32[256,512]{1,0:T(8,128)} %get-tuple-element.32), channel_id=1, source_target_pairs={{8,10},{9,11},{10,8},{11,9},{16,18},{17,19},{18,16},{19,17},{24,26... | collective-permute-start | bytes 1572872 | tf_op jit(solution)/shard_map/ppermute | solution.py:188
  49.6 13.7 %copy-start.3 = (f32[256,256]{1,0:T(8,128)S(1)}, f32[256,256]{1,0:T(8,128)}, u32[]{:S(2)}) copy-start(f32[256,256]{1,0:T(8,128)} %copy-done.2) | copy-start | bytes 786436
  49.6 8.4 %collective-permute-start.11 = (f32[256,256]{1,0:T(8,128)S(1)}, f32[256,256]{1,0:T(8,128)S(1)}, u32[]{:S(2)}, u32[]{:S(2)}) collective-permute-start(f32[256,256]{1,0:T(8,128)S(1)} %select_select_fusion.held), channel_id=1, source_target_pairs={{0,4},{1,5},{2,6},{3,7},{4,0},{5,1},{6,2},{7,3},{8,12},{9,13},{10,... | collective-permute-start | bytes 786440 | tf_op jit(solution)/shard_map/ppermute | solution.py:223
  61.4 15.0 %collective-permute-start.13 = (f32[1024,128]{1,0:T(8,128)}, f32[1024,128]{1,0:T(8,128)S(1)}, u32[]{:S(2)}, u32[]{:S(2)}) collective-permute-start(f32[1024,128]{1,0:T(8,128)} %get-tuple-element.34), channel_id=1, source_target_pairs={{4,5},{5,4},{6,7},{7,6},{8,9},{9,8},{10,11},{11,10},{12,13},{13,12... | collective-permute-start | bytes 1572872 | tf_op jit(solution)/shard_map/ppermute | solution.py:188
  63.4 0.7 collective-permute-start.10

commit v24 on v22

--- a/solution.py
+++ b/solution.py
@@ -199,7 +199,7 @@
     def spread(array, row_id, low, radix, have):
         digit = (row_id // low) % radix
         result = array
-        for step in (2, 3, 1) if radix == 4 else range(1, radix):
+        for step in (3, 1, 2) if radix == 4 else range(1, radix):
             result = jnp.where(digit == step, send_down(array, step * low, have), result)
         return result, [target(row, step * low) for row in have for step in range(radix)]
 

time: 77.6 us -> 78.9 us (1.017)
  starting transfers between devices: 25.6 us -> 26.6 us
    ppermute x4, waiting for transfers between devices: 5.81 us -> 7.14 us  [send_down(): return lax.ppermute(array, AXES, pairs)]
    ppermute x9, waiting for transfers between devices: 38.5 us -> 37.5 us  [swap(): return lax.ppermute(array, AXES, pairs)]
    ppermute x9, starting transfers between devices: 15.4 us -> 16.4 us  [swap(): return lax.ppermute(array, AXES, pairs)]
where the time goes in v24:
time: 78.9 us; the launch traced here: 78.5 us
  waiting for transfers between devices  44.7 us (57%)
  starting transfers between devices  26.6 us (34%)
  Pallas kernels  3.54 us (4%)
  local copies, waits for them, and re-layouts  2.34 us (3%)
  other arithmetic  0.99 us (1%)
    ppermute x9, waiting for transfers between devices, swap(): return lax.ppermute(array, AXES, pairs)  37.5 us
    ppermute x9, starting transfers between devices, swap(): return lax.ppermute(array, AXES, pairs)  16.4 us
    ppermute x4, waiting for transfers between devices, send_down(): return lax.ppermute(array, AXES, pairs)  7.14 us
    ppermute x1, starting transfers between devices, swap_cores(): return lax.ppermute(array, AXES, pairs)  6.88 us
    pallas_call x4, Pallas kernels, call(): pl.pallas_call(kernel, out_shape=[jax.ShapeDtypeStruct(shape, jnp.float32...  3.54 us
    ppermute x4, starting transfers between devices, send_down(): return lax.ppermute(array, AXES, pairs)  3.31 us
  transfers between devices with their start and end apart: 14, of which 4 were waited for; matrix products, arithmetic and copies ran while one was open for 3% of the time, Pallas kernels for 0%

profile of v24, /device:TPU:6, one launch (start us, length us, event | category | flops | bytes accessed | tf_op | source)
XLA Modules:
  0.0 78.5 jit_solution(13197384270863968754)
XLA Ops:
  0.0 0.0 copy-start.4
  0.0 1.8 %collective-permute-start.3 = (f32[256,1024]{1,0:T(8,128)}, f32[256,1024]{1,0:T(8,128)}, u32[]{:S(2)}, u32[]{:S(2)}) collective-permute-start(f32[256,1024]{1,0:T(8,128)} %bitcast.9), channel_id=1, source_target_pairs={{12,14},{13,15},{14,12},{15,13},{20,22},{21,23},{22,20},{23,21},{2... | collective-permute-start | bytes 3145736 | tf_op jit(solution)/shard_map/ppermute | solution.py:186
  1.8 1.0 %slice_bitcast_fusion.1 = f32[128,512]{1,0:T(8,128)S(1)} fusion(f32[2,128,1024]{2,1,0:T(8,128)} %param.4), kind=kLoop, calls=%fused_computation.4 | loop fusion | bytes 524288 | tf_op jit(solution)/shard_map/squeeze | solution.py:242
  2.8 0.0 copy-done.4
  2.8 0.0 copy-start
  2.8 0.0 copy-start.1
  2.8 0.1 pad_maximum_fusion.lead
  2.9 0.8 %collective-permute-start = (f32[128,1536]{1,0:T(8,128)S(1)}, f32[128,1536]{1,0:T(8,128)S(1)}, u32[]{:S(2)}, u32[]{:S(2)}) collective-permute-start(f32[128,1536]{1,0:T(8,128)S(1)} %pad_maximum_fusion.lead), channel_id=1, source_target_pairs={{0,2},{1,3},{2,0},{3,1}} | collective-permute-start | bytes 2359304 | tf_op jit(solution)/shard_map/ppermute | solution.py:186
  3.8 0.2 copy-done.1
  4.0 1.4 %collective-permute-start.1 = (f32[1024,128]{1,0:T(8,128)S(1)}, f32[1024,128]{1,0:T(8,128)}, u32[]{:S(2)}, u32[]{:S(2)}) collective-permute-start(f32[1024,128]{1,0:T(8,128)S(1)} %copy-done.1), channel_id=1, source_target_pairs={{0,1},{1,0},{2,3},{3,2}} | collective-permute-start | bytes 1572872 | tf_op jit(solution)/shard_map/ppermute | solution.py:186
  5.4 0.0 copy-done
  5.4 1.1 %fusion = (f32[256,512]{1,0:T(8,128)}, f32[256,512]{1,0:T(8,128)}) fusion(f32[256,1024]{1,0:T(8,128)S(1)} %bitcast.10), kind=kLoop, calls=%fused_computation.8 | loop fusion | bytes 2097152 | tf_op jit(solution)/shard_map/slice | solution.py:248
  6.5 4.5 %collective-permute-start.2 = (f32[256,512]{1,0:T(8,128)}, f32[256,512]{1,0:T(8,128)}, u32[]{:S(2)}, u32[]{:S(2)}) collective-permute-start(f32[256,512]{1,0:T(8,128)} %get-tuple-element.35), channel_id=1, source_target_pairs={{8,10},{9,11},{10,8},{11,9},{16,18},{17,19},{18,16},{19,17},{24,26... | collective-permute-start | bytes 1572872 | tf_op jit(solution)/shard_map/ppermute | solution.py:186
  11.0 0.0 collective-permute-done.far_lead
  11.0 0.0 collective-permute-done.1.refs_0_
  11.0 0.1 shard_map.37
  11.1 0.0 copy-start.2
  11.1 23.9 %collective-permute-done.2.early = f32[256,512]{1,0:T(8,128)} collective-permute-done((f32[256,512]{1,0:T(8,128)}, f32[256,512]{1,0:T(8,128)}, u32[]{:S(2)}, u32[]{:S(2)}) %collective-permute-start.2) | collective-permute-done | bytes 524320 | tf_op jit(solution)/shard_map/ppermute | solution.py:186
  34.9 0.0 collective-permute-done.3.whole
  34.9 0.7 collective-permute-start.5
  35.6 0.7 collective-permute-start.4
  36.3 0.0 collective-permute-done.5.first
  36.3 1.6 %collective-permute-start.9 = (f32[256,1024]{1,0:T(8,128)S(1)}, f32[256,1024]{1,0:T(8,128)}, u32[]{:S(2)}, u32[]{:S(2)}) collective-permute-start(f32[256,1024]{1,0:T(8,128)S(1)} %bitcast.11), channel_id=1, source_target_pairs={{4,6},{5,7},{6,4},{7,5}} | collective-permute-start | bytes 3145736 | tf_op jit(solution)/shard_map/ppermute | solution.py:186
  38.0 0.0 collective-permute-done.4.got
  38.0 0.1 shard_map.38
  38.0 0.0 copy-done.2
  38.0 0.7 collective-permute-start.6
  38.7 0.7 collective-permute-start.7
  39.4 1.3 %collective-permute-start.8 = (f32[256,256]{1,0:T(8,128)S(1)}, f32[256,256]{1,0:T(8,128)S(1)}, u32[]{:S(2)}, u32[]{:S(2)}) collective-permute-start(f32[256,256]{1,0:T(8,128)S(1)} %shard_map.38), channel_id=1, source_target_pairs={{0,28},{1,29},{2,30},{3,31},{4,24},{5,25},{6,26},{7,27}} | collective-permute-start | bytes 786440 | tf_op jit(solution)/shard_map/ppermute | solution.py:194
  40.7 1.9 %collective-permute-start.12 = (f32[256,512]{1,0:T(8,128)}, f32[256,512]{1,0:T(8,128)S(1)}, u32[]{:S(2)}, u32[]{:S(2)}) collective-permute-start(f32[256,512]{1,0:T(8,128)} %get-tuple-element.32), channel_id=1, source_target_pairs={{8,10},{9,11},{10,8},{11,9},{16,18},{17,19},{18,16},{19,17},{24,26... | collective-permute-start | bytes 1572872 | tf_op jit(solution)/shard_map/ppermute | solution.py:186
  42.7 0.0 collective-permute-done.6
  42.7 0.0 collective-permute-done.7
  42.7 7.1 %collective-permute-done.8 = f32[256,256]{1,0:T(8,128)S(1)} collective-permute-done((f32[256,256]{1,0:T(8,128)S(1)}, f32[256,256]{1,0:T(8,128)S(1)}, u32[]{:S(2)}, u32[]{:S(2)}) %collective-permute-start.8) | collective-permute-done | bytes 262176 | tf_op jit(solution)/shard_map/ppermute | solution.py:194
  49.8 0.1 select_select_fusion.held
  49.9 0.0 copy-start.3
  49.9 0.0 collective-permute-done.9.beside
  49.9 6.9 %collective-permute-start.11 = (f32[256,256]{1,0:T(8,128)S(1)}, f32[256,256]{1,0:T(8,128)S(1)}, u32[]{:S(2)}, u32[]{:S(2)}) collective-permute-start(f32[256,256]{1,0:T(8,128)S(1)} %select_select_fusion.held), channel_id=1, source_target_pairs={{0,4},{1,5},{2,6},{3,7},{4,0},{5,1},{6,2},{7,3},{8,12},{9,13},{10,... | collective-permute-start | bytes 786440 | tf_op jit(solution)/shard_map/ppermute | solution.py:221
  56.8 1.2 %collective-permute-done.12.tail = f32[256,512]{1,0:T(8,128)S(1)} collective-permute-done((f32[256,512]{1,0:T(8,128)}, f32[256,512]{1,0:T(8,128)S(1)}, u32[]{:S(2)}, u32[]{:S(2)}) %collective-permute-start.12) | collective-permute-done | bytes 524320 | tf_op jit(solution)/shard_map/ppermute | solution.py:186
  58.0 0.0 collective-permute-done.11.got
  58.0 3.4 %shard_map.40 = (f32[1024,128]{1,0:T(8,128)S(1)}, f32[1024,128]{1,0:T(8,128)}) custom-call(s32[1]{0:T(128)} %bitcast.1.row, f32[256,256]{1,0:T(8,128)S(1)} %select_select_fusion.held, f32[256,256]{1,0:T(8,128)S(1)} %collective-permute-done.11.got, f32[256,1024]{1,0:T(8,128)S(1)} %bitcast.12, f32[256,1024]{1,0:T(8,128)} %collective-permute-done.3.whole, ...), custom_call_target="tpu_custom_call" | custom-call | flops 805306368 | tf_op jit(solution)/shard_map/pallas_call | solution.py:32
  61.4 2.9 %collective-permute-start.13 = (f32[1024,128]{1,0:T(8,128)}, f32[1024,128]{1,0:T(8,128)S(1)}, u32[]{:S(2)}, u32[]{:S(2)}) collective-permute-start(f32[1024,128]{1,0:T(8,128)} %get-tuple-element.34), channel_id=1, source_target_pairs={{4,5},{5,4},{6,7},{7,6},{8,9},{9,8},{10,11},{11,10},{12,13},{13,12... | collective-permute-start | bytes 1572872 | tf_op jit(solution)/shard_map/ppermute | solution.py:186
  64.3 0.0 copy-done.3
  64.4 0.7 collective-permute-start.10
  65.1 0.0 collective-permute-done.10.refs_0_
  65.1 0.1 shard_map.39
  65.2 12.5 %collective-permute-done.13 = f32[1024,128]{1,0:T(8,128)S(1)} collective-permute-done((f32[1024,128]{1,0:T(8,128)}, f32[1024,128]{1,0:T(8,128)S(1)}, u32[]{:S(2)}, u32[]{:S(2)}) %collective-permute-start.13) | collective-permute-done | bytes 524320 | tf_op jit(solution)/shard_map/ppermute | solution.py:186
  77.6 0.9 %subtract_select_fusion = f32[1024,128]{1,0:T(8,128)} fusion(f32[1024,128]{1,0:T(8,128)S(1)} %shard_map.39, f32[1024,128]{1,0:T(8,128)S(1)} %get-tuple-element.33, f32[1024,128]{1,0:T(8,128)S(1)} %collective-permute-done.13, pred[]{:T(512)S(6)} %eq.14), kind=kLoop, calls=%fused_computation.1 | loop fusion | flops 262144 | bytes 2097153 | tf_op jit(solution)/shard_map/jit(_where)/select_n | solution.py:310
  (4 shorter events, 0.1 us)
Async XLA Ops:
  0.0 2.8 %copy-start.4 = (f32[2,128,512]{2,1,0:T(8,128)S(1)}, f32[2,128,512]{2,1,0:T(8,128)}, u32[]{:S(2)}) copy-start(f32[2,128,512]{2,1,0:T(8,128)} %param.5) | copy-start | bytes 1572868
  0.0 34.9 %collective-permute-start.3 = (f32[256,1024]{1,0:T(8,128)}, f32[256,1024]{1,0:T(8,128)}, u32[]{:S(2)}, u32[]{:S(2)}) collective-permute-start(f32[256,1024]{1,0:T(8,128)} %bitcast.9), channel_id=1, source_target_pairs={{12,14},{13,15},{14,12},{15,13},{20,22},{21,23},{22,20},{23,21},{2... | collective-permute-start | bytes 3145736 | tf_op jit(solution)/shard_map/ppermute | solution.py:186
  2.8 2.6 %copy-start = (f32[2,128,1024]{2,1,0:T(8,128)S(1)}, f32[2,128,1024]{2,1,0:T(8,128)}, u32[]{:S(2)}) copy-start(f32[2,128,1024]{2,1,0:T(8,128)} %param.4) | copy-start | bytes 3145732
  2.8 1.1 %copy-start.1 = (f32[1024,128]{1,0:T(8,128)S(1)}, f32[1024,128]{1,0:T(8,128)}, u32[]{:S(2)}) copy-start(f32[1024,128]{1,0:T(8,128)} %cross.1) | copy-start | bytes 1572868
  2.9 8.1 %collective-permute-start = (f32[128,1536]{1,0:T(8,128)S(1)}, f32[128,1536]{1,0:T(8,128)S(1)}, u32[]{:S(2)}, u32[]{:S(2)}) collective-permute-start(f32[128,1536]{1,0:T(8,128)S(1)} %pad_maximum_fusion.lead), channel_id=1, source_target_pairs={{0,2},{1,3},{2,0},{3,1}} | collective-permute-start | bytes 2359304 | tf_op jit(solution)/shard_map/ppermute | solution.py:186
  4.0 7.0 %collective-permute-start.1 = (f32[1024,128]{1,0:T(8,128)S(1)}, f32[1024,128]{1,0:T(8,128)}, u32[]{:S(2)}, u32[]{:S(2)}) collective-permute-start(f32[1024,128]{1,0:T(8,128)S(1)} %copy-done.1), channel_id=1, source_target_pairs={{0,1},{1,0},{2,3},{3,2}} | collective-permute-start | bytes 1572872 | tf_op jit(solution)/shard_map/ppermute | solution.py:186
  6.5 28.5 %collective-permute-start.2 = (f32[256,512]{1,0:T(8,128)}, f32[256,512]{1,0:T(8,128)}, u32[]{:S(2)}, u32[]{:S(2)}) collective-permute-start(f32[256,512]{1,0:T(8,128)} %get-tuple-element.35), channel_id=1, source_target_pairs={{8,10},{9,11},{10,8},{11,9},{16,18},{17,19},{18,16},{19,17},{24,26... | collective-permute-start | bytes 1572872 | tf_op jit(solution)/shard_map/ppermute | solution.py:186
  11.1 27.0 %copy-start.2 = (f32[256,256]{1,0:T(8,128)}, f32[256,256]{1,0:T(8,128)S(1)}, u32[]{:S(2)}) copy-start(f32[256,256]{1,0:T(8,128)S(1)} %get-tuple-element.25) | copy-start | bytes 786436
  34.9 1.4 %collective-permute-start.5 = (f32[256,256]{1,0:T(8,128)S(1)}, f32[256,256]{1,0:T(8,128)S(1)}, u32[]{:S(2)}, u32[]{:S(2)}) collective-permute-start(f32[256,256]{1,0:T(8,128)S(1)} %get-tuple-element.25), channel_id=1, source_target_pairs={{0,4},{1,5},{2,6},{3,7}} | collective-permute-start | bytes 786440 | tf_op jit(solution)/shard_map/ppermute | solution.py:194
  35.6 2.4 %collective-permute-start.4 = (f32[512,256]{1,0:T(8,128)S(1)}, f32[512,256]{1,0:T(8,128)S(1)}, u32[]{:S(2)}, u32[]{:S(2)}) collective-permute-start(f32[512,256]{1,0:T(8,128)S(1)} %get-tuple-element.26.sent), channel_id=1, source_target_pairs={{0,1},{1,0},{2,3},{3,2}} | collective-permute-start | bytes 1572872 | tf_op jit(solution)/shard_map/ppermute | solution.py:186
  36.3 13.6 %collective-permute-start.9 = (f32[256,1024]{1,0:T(8,128)S(1)}, f32[256,1024]{1,0:T(8,128)}, u32[]{:S(2)}, u32[]{:S(2)}) collective-permute-start(f32[256,1024]{1,0:T(8,128)S(1)} %bitcast.11), channel_id=1, source_target_pairs={{4,6},{5,7},{6,4},{7,5}} | collective-permute-start | bytes 3145736 | tf_op jit(solution)/shard_map/ppermute | solution.py:186
  38.0 4.6 %collective-permute-start.6 = (f32[256,256]{1,0:T(8,128)S(1)}, f32[256,256]{1,0:T(8,128)S(1)}, u32[]{:S(2)}, u32[]{:S(2)}) collective-permute-start(f32[256,256]{1,0:T(8,128)S(1)} %shard_map.38), channel_id=1, source_target_pairs={{0,20},{1,21},{2,22},{3,23},{4,16},{5,17},{6,18},{7,19}} | collective-permute-start | bytes 786440 | tf_op jit(solution)/shard_map/ppermute | solution.py:194
  38.7 4.0 %collective-permute-start.7 = (f32[256,256]{1,0:T(8,128)S(1)}, f32[256,256]{1,0:T(8,128)S(1)}, u32[]{:S(2)}, u32[]{:S(2)}) collective-permute-start(f32[256,256]{1,0:T(8,128)S(1)} %shard_map.38), channel_id=1, source_target_pairs={{0,12},{1,13},{2,14},{3,15},{4,8},{5,9},{6,10},{7,11}} | collective-permute-start | bytes 786440 | tf_op jit(solution)/shard_map/ppermute | solution.py:194
  39.4 10.4 %collective-permute-start.8 = (f32[256,256]{1,0:T(8,128)S(1)}, f32[256,256]{1,0:T(8,128)S(1)}, u32[]{:S(2)}, u32[]{:S(2)}) collective-permute-start(f32[256,256]{1,0:T(8,128)S(1)} %shard_map.38), channel_id=1, source_target_pairs={{0,28},{1,29},{2,30},{3,31},{4,24},{5,25},{6,26},{7,27}} | collective-permute-start | bytes 786440 | tf_op jit(solution)/shard_map/ppermute | solution.py:194
  40.7 17.3 %collective-permute-start.12 = (f32[256,512]{1,0:T(8,128)}, f32[256,512]{1,0:T(8,128)S(1)}, u32[]{:S(2)}, u32[]{:S(2)}) collective-permute-start(f32[256,512]{1,0:T(8,128)} %get-tuple-element.32), channel_id=1, source_target_pairs={{8,10},{9,11},{10,8},{11,9},{16,18},{17,19},{18,16},{19,17},{24,26... | collective-permute-start | bytes 1572872 | tf_op jit(solution)/shard_map/ppermute | solution.py:186
  49.9 14.4 %copy-start.3 = (f32[256,256]{1,0:T(8,128)S(1)}, f32[256,256]{1,0:T(8,128)}, u32[]{:S(2)}) copy-start(f32[256,256]{1,0:T(8,128)} %copy-done.2) | copy-start | bytes 786436
  49.9 8.1 %collective-permute-start.11 = (f32[256,256]{1,0:T(8,128)S(1)}, f32[256,256]{1,0:T(8,128)S(1)}, u32[]{:S(2)}, u32[]{:S(2)}) collective-permute-start(f32[256,256]{1,0:T(8,128)S(1)} %select_select_fusion.held), channel_id=1, source_target_pairs={{0,4},{1,5},{2,6},{3,7},{4,0},{5,1},{6,2},{7,3},{8,12},{9,13},{10,... | collective-permute-start | bytes 786440 | tf_op jit(solution)/shard_map/ppermute | solution.py:221
  61.4 16.2 %collective-permute-start.13 = (f32[1024,128]{1,0:T(8,128)}, f32[1024,128]{1,0:T(8,128)S(1)}, u32[]{:S(2)}, u32[]{:S(2)}) collective-permute-start(f32[1024,128]{1,0:T(8,128)} %get-tuple-element.34), channel_id=1, source_target_pairs={{4,5},{5,4},{6,7},{7,6},{8,9},{9,8},{10,11},{11,10},{12,13},{13,12... | collective-permute-start | bytes 1572872 | tf_op jit(solution)/shard_map/ppermute | solution.py:186
  64.4 0.7 collective-permute-start.10
